TPU v7x, 32 devices: a whole 2x2x4 slice. The times are simulated.
32 devices in a mesh: rep: 2 (over core), fsdp: 16 (over z, y, x).
Axes of the slice: x: 2, y: 2, z: 4, core: 2. Of those that a mesh axis runs over, the one named last changes fastest.
Arguments:
- acts: bfloat16 [2, 2048, 8192], P('rep', 'fsdp'), may hold values from -6 to 6
- value_cots: bfloat16 [2, 2048, 512], P('rep', 'fsdp'), may hold values from -0.059814453 to 0.059814453
- inner_weights: float32 [2, 8192, 512], P('rep', 'fsdp'), may hold values from -0.0625 to 0.0625
- first_moment: float32 [2, 8192, 512], P('rep', 'fsdp'), may hold values from -1.8 to 1.8
- second_moment: float32 [2, 8192, 512], P('rep', 'fsdp'), may hold values from 0.01 to 1
- anchor: float32 [8192, 512], P('fsdp'), may hold values from -0.0625 to 0.0625
- outer_momentum: float32 [8192, 512], P('fsdp'), may hold values from -0.06 to 0.06
Outputs:
- first_next: float32 [2, 8192, 512], P('rep', 'fsdp')
- values_next: bfloat16 [2, 2048, 512], P('rep', 'fsdp')
All inputs are finite; a program needn't handle non-finite values.
Results may differ from a plain program's by a relative error of at most 0.0049.
Values may be sent and summed in bfloat16 or wider, within the bound.
No kernel may reach another device: no remote copies, remote signals or barrier semaphores. Data moves between devices by JAX's collectives and lax.ppermute only.
A program may use at most 64 MiB of HBM per device.

v0:
```python
import jax
import jax.numpy as jnp
from jax import lax
from jax.sharding import PartitionSpec as P

decay_first = 0.9
decay_second = 0.95
inner_rate = 0.006
epsilon = 1e-08
outer_rate = 0.7
outer_decay = 0.9


def outer_update(average, anchor_rows, momentum_rows):
    velocity = outer_decay * momentum_rows + average
    return (anchor_rows - outer_rate * (average + outer_decay * velocity)).astype(jnp.bfloat16)


def on_device(acts, value_cots, inner_weights, first_moment, second_moment, anchor, outer_momentum):
    tokens_local = acts[0]
    cots_local = value_cots[0]
    rep_count = lax.axis_size("rep")
    feature_split = lax.all_to_all(tokens_local, "fsdp", split_axis=1, concat_axis=0, tiled=True)
    columns = feature_split
    gradient = lax.dot_general(
        columns,
        lax.all_gather(cots_local, "fsdp", axis=0, tiled=True),
        (((0,), (0,)), ((), ())),
        preferred_element_type=jnp.float32,
    )
    first_next = decay_first * first_moment[0] + (1.0 - decay_first) * gradient
    second_next = decay_second * second_moment[0] + (1.0 - decay_second) * gradient * gradient
    stepped = inner_weights[0] - inner_rate * first_next / (jnp.sqrt(second_next) + epsilon)
    drift = anchor - stepped
    summed_drift = lax.psum(drift, "rep")
    weights_next = outer_update(summed_drift / rep_count, anchor, outer_momentum)
    columns = tokens_local
    values = jnp.dot(
        columns,
        lax.all_gather(weights_next, "fsdp", axis=0, tiled=True),
        preferred_element_type=jnp.float32,
    )
    return (first_next[None], values.astype(jnp.bfloat16)[None])


def solution(mesh):
    placed = (
        P("rep", "fsdp", None),
        P("rep", "fsdp", None),
        P("rep", "fsdp", None),
        P("rep", "fsdp", None),
        P("rep", "fsdp", None),
        P("fsdp", None),
        P("fsdp", None),
    )
    return jax.shard_map(
        on_device,
        mesh=mesh,
        in_specs=placed,
        out_specs=(P("rep", "fsdp", None), P("rep", "fsdp", None)),
        check_vma=False,
    )
```

profile of v0, /device:TPU:0, one launch (start us, length us, event | category | flops | bytes accessed | tf_op | source)
XLA Modules:
  0.0 252.8 jit_solution(8956887058402216352)
XLA Ops:
  7.2 4.1 %copy.11 = bf16[1,128,8192]{1,2,0:T(8,128)(2,1)} copy(bf16[1,128,8192]{2,1,0:T(8,128)(2,1)} %param.7) | data formatting | bytes 4194304 | tf_op args[0]
  11.2 8.3 %all-to-all-start = ((bf16[128,16,512]{0,2,1:T(8,128)(2,1)}), bf16[128,16,512]{0,2,1:T(8,128)(2,1)S(1)}, u32[]{:S(2)}, u32[]{:S(2)}) async-start(bf16[128,16,512]{0,2,1:T(8,128)(2,1)} %bitcast.34), calls=%async_computation | async-start | bytes 4194304 | tf_op jit(solution)/shard_map/all_to_all | solution.py:23
  19.6 0.0 all-gather.6.cloned.1.call-start
  19.6 0.7 all-gather.6.cloned.1.call-update
  20.3 0.0 all-reduce.2.cloned.1.call-start
  20.3 45.9 %all-to-all-done = bf16[128,16,512]{0,2,1:T(8,128)(2,1)S(1)} async-done(((bf16[128,16,512]{0,2,1:T(8,128)(2,1)}), bf16[128,16,512]{0,2,1:T(8,128)(2,1)S(1)}, u32[]{:S(2)}, u32[]{:S(2)}) %all-to-all-start) | async-done | bytes 2097184 | tf_op jit(solution)/shard_map/all_to_all | solution.py:23
  66.3 0.0 copy-start.1
  66.3 2.6 %copy.12 = bf16[16,128,512]{2,1,0:T(8,128)(2,1)} copy(bf16[16,128,512]{1,2,0:T(8,128)(2,1)S(1)} %bitcast.33) | data formatting | bytes 4194304 | tf_op jit(solution)/shard_map/all_to_all | solution.py:23
  68.8 29.0 %all-gather.6.cloned.1.call-done = bf16[1,2048,512]{2,1,0:T(8,128)(2,1)} async-done(((bf16[1,128,512]{2,1,0:T(8,128)(2,1)}), bf16[1,2048,512]{2,1,0:T(8,128)(2,1)}) %all-gather.6.cloned.1.call-update) | async-done | bytes 2097168 | tf_op jit(solution)/shard_map/all_gather | solution.py:27
  97.9 0.0 copy-done.1
  97.9 6.2 %fusion.15 = (f32[512,512]{1,0:T(8,128)}, f32[1,512,512]{2,1,0:T(8,128)}) fusion(f32[512,512]{1,0:T(8,128)S(1)} %copy-done.1, f32[1,512,512]{2,1,0:T(8,128)} %param.9, f32[1,512,512]{2,1,0:T(8,128)} %param.11, f32[1,512,512]{2,1,0:T(8,128)} %param.10, bf16[2048,512]{1,0:T(8,128)(2,1)} %bitcast.35, bf16[1,2048,512]{2,1,0:T(8,128)(2,1)} %all-gather.6.cloned.1.call-done), kind=kOutput, calls=%fused_computation.12 | convolution fusion | flops 1076887552 | bytes 10485760 | tf_op jit(solution)/shard_map/dot_general | solution.py:25
  104.1 0.0 all-reduce.2.cloned.1.call-update
  104.1 0.0 copy-start
  104.1 0.0 all-gather.4.cloned.1.call-start
  104.2 18.3 %all-reduce.2.cloned.1.call-done = f32[512,512]{1,0:T(8,128)} async-done(((f32[512,512]{1,0:T(8,128)}), f32[512,512]{1,0:T(8,128)}) %all-reduce.2.cloned.1.call-update) | async-done | bytes 1048592 | tf_op jit(solution)/shard_map/psum | solution.py:35
  122.5 2.8 %subtract_convert_fusion = bf16[512,512]{1,0:T(8,128)(2,1)} fusion(f32[512,512]{1,0:T(8,128)S(1)} %copy-done.1, f32[512,512]{1,0:T(8,128)} %param.13, f32[512,512]{1,0:T(8,128)} %all-reduce.2.cloned.1.call-done), kind=kLoop, calls=%fused_computation.14 | loop fusion | flops 2097152 | bytes 3670016 | tf_op jit(solution)/shard_map/convert_element_type | solution.py:16
  125.3 0.0 all-gather.4.cloned.1.call-update
  125.3 114.4 %all-gather.4.cloned.1.call-done = bf16[8192,512]{1,0:T(8,128)(2,1)} async-done(((bf16[512,512]{1,0:T(8,128)(2,1)}), bf16[8192,512]{1,0:T(8,128)(2,1)}) %all-gather.4.cloned.1.call-update) | async-done | bytes 8388624 | tf_op jit(solution)/shard_map/all_gather | solution.py:40
  239.7 0.0 copy-done
  239.7 5.8 %fusion.7 = bf16[1,128,512]{1,2,0:T(8,128)(2,1)S(1)} fusion(bf16[8192,512]{1,0:T(8,128)(2,1)} %all-gather.4.cloned.1.call-done, bf16[1,128,8192]{2,1,0:T(8,128)(2,1)S(1)} %copy-done), kind=kOutput, calls=%fused_computation.6 | convolution fusion | flops 1073807360 | bytes 10616832 | tf_op jit(solution)/shard_map/dot_general | solution.py:38
  245.5 0.8 copy.13
Async XLA Ops:
  11.2 55.0 %all-to-all-start = ((bf16[128,16,512]{0,2,1:T(8,128)(2,1)}), bf16[128,16,512]{0,2,1:T(8,128)(2,1)S(1)}, u32[]{:S(2)}, u32[]{:S(2)}) async-start(bf16[128,16,512]{0,2,1:T(8,128)(2,1)} %bitcast.34), calls=%async_computation | async-start | bytes 4194304 | tf_op jit(solution)/shard_map/all_to_all | solution.py:23
  19.6 78.3 %all-gather.6.cloned.1.call-start = ((), (), s32[]{:S(2)}) async-start(), calls=%async_computation.3 | async-start | bytes 2228224 | tf_op jit(solution)/shard_map/all_gather | solution.py:27
  20.3 102.2 %all-reduce.2.cloned.1.call-start = ((), (), s32[]{:S(2)}) async-start(), calls=%async_computation.1 | async-start | bytes 2097152 | tf_op jit(solution)/shard_map/psum | solution.py:35
  66.3 31.6 %copy-start.1 = (f32[512,512]{1,0:T(8,128)S(1)}, f32[512,512]{1,0:T(8,128)}, u32[]{:S(2)}) copy-start(f32[512,512]{1,0:T(8,128)} %param.12) | copy-start | bytes 3145732
  104.1 135.6 %copy-start = (bf16[1,128,8192]{2,1,0:T(8,128)(2,1)S(1)}, bf16[1,128,8192]{2,1,0:T(8,128)(2,1)}, u32[]{:S(2)}) copy-start(bf16[1,128,8192]{2,1,0:T(8,128)(2,1)} %param.7) | copy-start | bytes 6291460
  104.1 135.6 %all-gather.4.cloned.1.call-start = ((), (), s32[]{:S(2)}) async-start(), calls=%async_computation.2 | async-start | bytes 8912896 | tf_op jit(solution)/shard_map/all_gather | solution.py:40
Sparse Core Ops, SparseCore 0:
  23.2 74.6 all-gather.5
  104.2 18.2 all-reduce.1
  125.7 114.0 all-gather.3
where the time goes:
time: 253 us
  waiting for transfers between devices  208 us (82%)
  between operations  13.8 us (5%)
  matrix products  12 us (5%)
  starting transfers between devices  8.43 us (3%)
  local copies, waits for them, and re-layouts  7.45 us (3%)
  other arithmetic  2.75 us (1%)
    all_gather x1, waiting for transfers between devices, on_device(): lax.all_gather(weights_next, 'fsdp', axis=0, tiled=True)  114 us
    all_to_all x1, waiting for transfers between devices, on_device(): lax.all_to_all(tokens_local, 'fsdp', split_axis=1, concat_axis=0, tiled=T...  45.9 us
    all_gather x1, waiting for transfers between devices, on_device(): lax.all_gather(cots_local, 'fsdp', axis=0, tiled=True)  29 us
    psum x1, waiting for transfers between devices, on_device(): summed_drift = lax.psum(drift, 'rep')  18.3 us
    all_to_all x1, starting transfers between devices, on_device(): lax.all_to_all(tokens_local, 'fsdp', split_axis=1, concat_axis=0, tiled=T...  8.31 us
    dot_general x1, matrix products, on_device(): lax.dot_general(columns, lax.all_gather(cots_local, 'fsdp', axis=0, tiled...  6.22 us
    dot_general x1, matrix products, on_device(): jnp.dot(columns, lax.all_gather(weights_next, 'fsdp', axis=0, tiled=True)...  5.76 us
  transfers between devices with their start and end apart: 4, of which 4 were waited for; matrix products, arithmetic and copies ran while one was open for 1% of the time, Pallas kernels for 0%

commit v1 on v0

v1 whole, which is shorter than its diff:
```python
from functools import partial

import jax
import jax.numpy as jnp
from jax import lax
from jax.experimental import pallas as pl
from jax.experimental.pallas import tpu as pltpu
from jax.sharding import PartitionSpec as P

decay_first = 0.9
decay_second = 0.95
inner_rate = 0.006
epsilon = 1e-08
outer_rate = 0.7
outer_decay = 0.9

PLANES = 4
CONTRACT_ROWS = (((0,), (0,)), ((), ()))
VMEM_BYTES = 40 * 1024 * 1024


def outer_update(average, anchor_rows, momentum_rows):
    velocity = outer_decay * momentum_rows + average
    return (anchor_rows - outer_rate * (average + outer_decay * velocity)).astype(jnp.bfloat16)


def inner_update(gradient, inner_weights, first_moment, second_moment, anchor):
    first_next = decay_first * first_moment + (1.0 - decay_first) * gradient
    second_next = decay_second * second_moment + (1.0 - decay_second) * gradient * gradient
    stepped = inner_weights - inner_rate * first_next / (jnp.sqrt(second_next) + epsilon)
    return first_next, anchor - stepped


def general(acts, value_cots, inner_weights, first_moment, second_moment, anchor, outer_momentum):
    tokens_local = acts[0]
    columns = lax.all_to_all(tokens_local, "fsdp", split_axis=1, concat_axis=0, tiled=True)
    cots = lax.all_gather(value_cots[0], "fsdp", axis=0, tiled=True)
    gradient = lax.dot_general(columns, cots, CONTRACT_ROWS, preferred_element_type=jnp.float32)
    first_next, drift = inner_update(gradient, inner_weights[0], first_moment[0], second_moment[0], anchor)
    average = lax.psum(drift, "rep") / lax.axis_size("rep")
    weights_next = outer_update(average, anchor, outer_momentum)
    gathered = lax.all_gather(weights_next, "fsdp", axis=0, tiled=True)
    values = jnp.dot(tokens_local, gathered, preferred_element_type=jnp.float32)
    return (first_next[None], values.astype(jnp.bfloat16)[None])


def repack_kernel(inner, rows, acts_ref, cots_ref, *refs):
    firsts, rests, sems = refs[:inner], refs[inner : 2 * inner], refs[-1]
    tokens = acts_ref.shape[0]
    f = lax.axis_index("fsdp")
    o, i = f // inner, lax.rem(f, inner)
    copies = []
    for k in range(inner):
        place = (i // 2 + k // 2 - 2 * (i // 2) * (k // 2)) * 2 + (lax.rem(i, 2) + k % 2 - 2 * lax.rem(i, 2) * (k % 2))
        for slot, t in enumerate((3, 2, 1, 0)):
            plane = jnp.where(o < PLANES // 2, t, PLANES - 1 - t)
            start = pl.multiple_of((plane * inner + place) * rows, rows)
            to = firsts[k].at[pl.ds(0, tokens)] if slot == 0 else rests[k].at[pl.ds((slot - 1) * tokens, tokens)]
            copies.append(pltpu.make_async_copy(acts_ref.at[:, pl.ds(start, rows)], to, sems.at[len(copies)]))
        copies.append(pltpu.make_async_copy(cots_ref, firsts[k].at[pl.ds(tokens, tokens)], sems.at[len(copies)]))
    for copy in copies:
        copy.start()
    for copy in copies:
        copy.wait()


def repack(tokens_local, cots_local, inner, rows):
    tokens, _ = tokens_local.shape
    out = [jax.ShapeDtypeStruct((2 * tokens, rows), jnp.bfloat16)] * inner
    out += [jax.ShapeDtypeStruct((3 * tokens, rows), jnp.bfloat16)] * inner
    got = pl.pallas_call(
        partial(repack_kernel, inner, rows),
        out_shape=out,
        in_specs=[pl.BlockSpec(memory_space=pl.ANY)] * 2,
        out_specs=[pl.BlockSpec(memory_space=pl.ANY)] * (2 * inner),
        scratch_shapes=[pltpu.SemaphoreType.DMA((5 * inner,))],
        name="repack",
    )(tokens_local, cots_local)
    return got[:inner], got[inner:]


def first_partial_kernel(inner, tokens, *refs):
    firsts, total_ref, sent_ref = refs[:inner], refs[inner], refs[inner + 1]
    columns = jnp.concatenate([ref[:tokens] for ref in firsts], axis=0)
    cots = jnp.concatenate([ref[tokens:] for ref in firsts], axis=0)
    total = lax.dot_general(columns, cots, CONTRACT_ROWS, preferred_element_type=jnp.float32)
    total_ref[...] = total
    sent_ref[...] = total.astype(jnp.bfloat16)


def rest_partial_kernel(inner, tokens, *refs):
    firsts, rests, outs = refs[:inner], refs[inner : 2 * inner], refs[2 * inner :]
    cots = jnp.concatenate([ref[tokens:] for ref in firsts], axis=0)
    for slot in range(3):
        columns = jnp.concatenate([ref[slot * tokens : (slot + 1) * tokens] for ref in rests], axis=0)
        total = lax.dot_general(columns, cots, CONTRACT_ROWS, preferred_element_type=jnp.float32)
        outs[slot][...] = total
        if slot < 2:
            outs[3 + slot][...] = total.astype(jnp.bfloat16)


def values_kernel(inner, tokens, rows, *refs):
    firsts, rests = refs[:inner], refs[inner : 2 * inner]
    mine_ref, other_ref, mine2_ref, other2_ref, mine3_ref, other3_ref = refs[2 * inner : 2 * inner + 6]
    own_ref, sent_refs, weights = refs[2 * inner + 6], refs[2 * inner + 7 : -1], refs[-1]
    half = rows // 2
    o, r = lax.axis_index("fsdp") // inner, lax.axis_index("rep")
    near = jnp.where(o < PLANES // 2, o, PLANES - 1 - o)

    def put(t, which, value):
        weights[pl.ds(pl.multiple_of(t * rows + which * half, half), half), :] = value

    for slot, t in ((0, near), (1, 1 - near)):
        put(t, r, mine_ref[slot])
        put(t, 1 - r, other_ref[slot])
    put(2, r, mine2_ref[...])
    put(2, 1 - r, other2_ref[...])
    put(3, r, mine3_ref[...])
    put(3, 1 - r, other3_ref[...])
    for k in range(inner):
        total = jnp.dot(firsts[k][:tokens], weights[3 * rows :], preferred_element_type=jnp.float32)
        for slot, t in enumerate((2, 1, 0)):
            total += jnp.dot(
                rests[k][slot * tokens : (slot + 1) * tokens],
                weights[t * rows : (t + 1) * rows],
                preferred_element_type=jnp.float32,
            )
        if k == 0:
            own_ref[...] = total
        else:
            sent_refs[k - 1][...] = total.astype(jnp.bfloat16)


def call(kernel, name, out, inputs, flops, scratch=()):
    moved = sum(x.size * x.dtype.itemsize for x in list(inputs) + list(out))
    return pl.pallas_call(
        kernel,
        out_shape=out,
        in_specs=[pl.BlockSpec(memory_space=pltpu.VMEM)] * len(inputs),
        out_specs=[pl.BlockSpec(memory_space=pltpu.VMEM)] * len(out),
        scratch_shapes=list(scratch),
        compiler_params=pltpu.CompilerParams(vmem_limit_bytes=VMEM_BYTES),
        cost_estimate=pl.CostEstimate(flops=flops, bytes_accessed=moved, transcendentals=0),
        name=name,
    )(*inputs)


def on_device(acts, value_cots, inner_weights, first_moment, second_moment, anchor, outer_momentum):
    inner = lax.axis_size("fsdp") // PLANES
    rows, width = anchor.shape
    if inner != 4 or lax.axis_size("rep") != 2 or rows % 256:
        return general(acts, value_cots, inner_weights, first_moment, second_moment, anchor, outer_momentum)
    tokens = acts.shape[1]
    half = rows // 2
    o = lax.axis_index("fsdp") // inner
    r = lax.axis_index("rep")
    near = jnp.where(o < PLANES // 2, o, PLANES - 1 - o)
    at_end = near == 0

    def line(x, *pairs):
        return lax.ppermute(x, "fsdp", [(a * inner + i, b * inner + i) for a, b in pairs for i in range(inner)])

    def across(x, k):
        return lax.ppermute(x, "fsdp", [(p * inner + i, p * inner + (i ^ k)) for p in range(PLANES) for i in range(inner)])

    def swap(x):
        return lax.ppermute(x, "rep", [(0, 1), (1, 0)])

    def inward(x):
        return line(x, (0, 1), (3, 2))

    def middle(x):
        return line(x, (1, 2), (2, 1))

    def outward(x):
        return line(x, (1, 0), (2, 3))

    firsts, rests = repack(acts[0], value_cots[0], inner, rows)
    firsts = [firsts[0]] + [across(firsts[k], k) for k in range(1, inner)]
    rests = [rests[0]] + [across(rests[k], k) for k in range(1, inner)]

    f32 = jax.ShapeDtypeStruct((rows, width), jnp.float32)
    bf16 = jax.ShapeDtypeStruct((rows, width), jnp.bfloat16)
    flops = 2 * inner * tokens * rows * width
    total3, sent3 = call(partial(first_partial_kernel, inner, tokens), "partial_first", [f32, bf16], firsts, flops)
    a1 = inward(sent3)
    total2, total1, total0, sent2, sent1 = call(
        partial(rest_partial_kernel, inner, tokens), "partial_rest", [f32, f32, f32, bf16, bf16], firsts + rests, 3 * flops
    )
    a2 = inward(sent2)
    a3 = inward(sent1)

    def add(total, got):
        return (total + got.astype(jnp.float32)).astype(jnp.bfloat16)

    b2 = middle(add(total3, a1))
    b3 = middle(add(total2, a2))
    c3 = outward(add(total0, b2))
    own = jnp.where(at_end, total0 + c3.astype(jnp.float32), total1 + a3.astype(jnp.float32) + b3.astype(jnp.float32))
    first_next, drift = inner_update(own, inner_weights[0], first_moment[0], second_moment[0], anchor)

    def half_of(x, which):
        return lax.dynamic_slice_in_dim(x, which * half, half, 0)

    summed = half_of(drift, r) + swap(half_of(drift, 1 - r))
    mine = outer_update(summed / 2, half_of(anchor, r), half_of(outer_momentum, r))
    beside = line(mine, (0, 1), (1, 0), (2, 3), (3, 2))
    far2 = middle(mine)
    far3 = middle(beside)
    mine2 = jnp.where(at_end, outward(far2), far2)
    mine3 = jnp.where(at_end, outward(far3), far3)
    mine = jnp.stack([mine, beside])
    pieces = [mine, swap(mine), mine2, swap(mine2), mine3, swap(mine3)]
    block = jax.ShapeDtypeStruct((tokens, width), jnp.bfloat16)
    values, *sent = call(
        partial(values_kernel, inner, tokens, rows),
        "values",
        [jax.ShapeDtypeStruct((tokens, width), jnp.float32)] + [block] * (inner - 1),
        firsts + rests + pieces,
        4 * flops,
        [pltpu.VMEM((PLANES * rows, width), jnp.bfloat16)],
    )
    for k in range(1, inner):
        values = values + across(sent[k - 1], k).astype(jnp.float32)
    return (first_next[None], values.astype(jnp.bfloat16)[None])


def solution(mesh):
    placed = (
        P("rep", "fsdp", None),
        P("rep", "fsdp", None),
        P("rep", "fsdp", None),
        P("rep", "fsdp", None),
        P("rep", "fsdp", None),
        P("fsdp", None),
        P("fsdp", None),
    )
    return jax.shard_map(
        on_device,
        mesh=mesh,
        in_specs=placed,
        out_specs=(P("rep", "fsdp", None), P("rep", "fsdp", None)),
        check_vma=False,
    )
```

time: 253 us -> 203 us (0.80)
  waiting for transfers between devices: 208 us -> 74.2 us
  Pallas kernels: 0 us -> 84.2 us
  starting transfers between devices: 8.43 us -> 29.3 us
  between operations: 13.8 us -> 0.95 us
  matrix products: 12 us -> 0 us
  other arithmetic: 2.75 us -> 10.3 us
  local copies, waits for them, and re-layouts: 7.45 us -> 3.28 us
    all_gather x2 -> x0, waiting for transfers between devices: 143 us -> none  [the longest x1 114 us: on_device(): lax.all_gather(weights_next, 'fsdp', axis=0, tiled=True)]
    pallas_call x0 -> x4, Pallas kernels: none -> 84.2 us  [the longest x1 80.7 us: repack(): pl.pallas_call(partial(repack_kernel, inner, rows), out_shape=out, in_spe...]
    ppermute x0 -> x24, waiting for transfers between devices: none -> 74.2 us  [the longest x11 39.1 us: line(): lax.ppermute(x, 'fsdp', [(a * inner + i, b * inner + i) for a, b in pairs...]
    all_to_all x1 -> x0, waiting for transfers between devices: 45.9 us -> none  [on_device(): lax.all_to_all(tokens_local, 'fsdp', split_axis=1, concat_axis=0, tiled=T...]
    ppermute x0 -> x24, starting transfers between devices: none -> 29.3 us  [the longest x11 17.4 us: line(): lax.ppermute(x, 'fsdp', [(a * inner + i, b * inner + i) for a, b in pairs...]
    psum x1 -> x0, waiting for transfers between devices: 18.3 us -> none  [on_device(): summed_drift = lax.psum(drift, 'rep')]
    dot_general x2 -> x0, matrix products: 12 us -> none  [the longest x1 6.22 us: on_device(): lax.dot_general(columns, lax.all_gather(cots_local, 'fsdp', axis=0, tiled...]
    all_to_all x1 -> x0, starting transfers between devices: 8.31 us -> none  [on_device(): lax.all_to_all(tokens_local, 'fsdp', split_axis=1, concat_axis=0, tiled=T...]
  transfers between devices with their start and end apart: 4 -> 24, of which waited for: 4 -> 14; matrix products, arithmetic and copies ran while one was open for 1% -> 2% of each run, Pallas kernels for 0% -> 1%
where the time goes in v1:
time: 203 us; the launch traced here: 202 us
  Pallas kernels  84.2 us (41%)
  waiting for transfers between devices  74.2 us (37%)
  starting transfers between devices  29.3 us (14%)
  other arithmetic  10.3 us (5%)
  local copies, waits for them, and re-layouts  3.28 us (2%)
    pallas_call x1, Pallas kernels, repack(): pl.pallas_call(partial(repack_kernel, inner, rows), out_shape=out, in_spe...  80.7 us
    ppermute x11, waiting for transfers between devices, line(): lax.ppermute(x, 'fsdp', [(a * inner + i, b * inner + i) for a, b in pairs...  39.1 us
    ppermute x9, waiting for transfers between devices, across(): lax.ppermute(x, 'fsdp', [(p * inner + i, p * inner + (i ^ k)) for p in ra...  31.8 us
    ppermute x11, starting transfers between devices, line(): lax.ppermute(x, 'fsdp', [(a * inner + i, b * inner + i) for a, b in pairs...  17.4 us
    ppermute x9, starting transfers between devices, across(): lax.ppermute(x, 'fsdp', [(p * inner + i, p * inner + (i ^ k)) for p in ra...  11.7 us
    sub x1, other arithmetic, inner_update(): return (first_next, anchor - stepped)  4.53 us
  transfers between devices with their start and end apart: 24, of which 14 were waited for; matrix products, arithmetic and copies ran while one was open for 2% of the time, Pallas kernels for 1%

profile of v1, /device:TPU:0, one launch (start us, length us, event | category | flops | bytes accessed | tf_op | source)
XLA Modules:
  0.0 202.2 jit_solution(2786323386496321867)
XLA Ops:
  0.6 80.7 %repack.1 = (bf16[256,512]{1,0:T(8,128)(2,1)}, bf16[256,512]{1,0:T(8,128)(2,1)}, bf16[256,512]{1,0:T(8,128)(2,1)}, bf16[256,512]{1,0:T(8,128)(2,1)}, bf16[384,51...) custom-call(bf16[128,8192]{1,0:T(8,128)(2,1)} %bitcast.18, ...), custom_call_target="tpu_custom_call" | custom-call | tf_op jit(solution)/shard_map/repack/pallas_call | solution.py:71
  81.4 3.0 %collective-permute-start = (bf16[256,512]{1,0:T(8,128)(2,1)}, bf16[256,512]{1,0:T(8,128)(2,1)S(1)}, u32[]{:S(2)}, u32[]{:S(2)}) collective-permute-start(bf16[256,512]{1,0:T(8,128)(2,1)} %get-tuple-element.22), channel_id=1, source_target_pairs={{0,1},{1,0},{2,3},{3,2},{4,5},{5,4},{6,7},{7,6},{8,9},{9,8},{10,11... | collective-permute-start | bytes 786440 | tf_op jit(solution)/shard_map/ppermute | solution.py:164
  84.4 1.5 collective-permute-start.1
  85.9 5.8 %collective-permute-done.refs_1_ = bf16[256,512]{1,0:T(8,128)(2,1)S(1)} collective-permute-done((bf16[256,512]{1,0:T(8,128)(2,1)}, bf16[256,512]{1,0:T(8,128)(2,1)S(1)}, u32[]{:S(2)}, u32[]{:S(2)}) %collective-permute-start) | collective-permute-done | bytes 262176 | tf_op jit(solution)/shard_map/ppermute | solution.py:164
  91.7 6.2 %collective-permute-done.1.refs_2_ = bf16[256,512]{1,0:T(8,128)(2,1)S(1)} collective-permute-done((bf16[256,512]{1,0:T(8,128)(2,1)}, bf16[256,512]{1,0:T(8,128)(2,1)S(1)}, u32[]{:S(2)}, u32[]{:S(2)}) %collective-permute-start.1) | collective-permute-done | bytes 262176 | tf_op jit(solution)/shard_map/ppermute | solution.py:164
  99.4 3.5 %collective-permute-start.6 = (bf16[512,512]{1,0:T(8,128)(2,1)S(1)}, bf16[512,512]{1,0:T(8,128)(2,1)S(1)}, u32[]{:S(2)}, u32[]{:S(2)}) collective-permute-start(bf16[512,512]{1,0:T(8,128)(2,1)S(1)} %get-tuple-element.31), channel_id=1, source_target_pairs={{0,4},{1,5},{2,6},{3,7},{12,8},{13,9},{14,10},{15,11},{16,20},{17,... | collective-permute-start | bytes 1572872 | tf_op jit(solution)/shard_map/ppermute | solution.py:161
  106.5 8.8 %collective-permute-done.3.refs_5_ = bf16[384,512]{1,0:T(8,128)(2,1)S(1)} collective-permute-done((bf16[384,512]{1,0:T(8,128)(2,1)}, bf16[384,512]{1,0:T(8,128)(2,1)S(1)}, u32[]{:S(2)}, u32[]{:S(2)}) %collective-permute-start.3) | collective-permute-done | bytes 393248 | tf_op jit(solution)/shard_map/ppermute | solution.py:164
  115.2 7.0 %collective-permute-done.4.refs_6_ = bf16[384,512]{1,0:T(8,128)(2,1)S(1)} collective-permute-done((bf16[384,512]{1,0:T(8,128)(2,1)}, bf16[384,512]{1,0:T(8,128)(2,1)S(1)}, u32[]{:S(2)}, u32[]{:S(2)}) %collective-permute-start.4) | collective-permute-done | bytes 393248 | tf_op jit(solution)/shard_map/ppermute | solution.py:164
  123.5 1.5 partial_rest.1
  125.1 1.6 collective-permute-start.10
  127.5 4.9 %collective-permute-start.9 = (bf16[512,512]{1,0:T(8,128)(2,1)}, bf16[512,512]{1,0:T(8,128)(2,1)}, u32[]{:S(2)}, u32[]{:S(2)}) collective-permute-start(bf16[512,512]{1,0:T(8,128)(2,1)} %get-tuple-element.33), channel_id=1, source_target_pairs={{0,4},{1,5},{2,6},{3,7},{12,8},{13,9},{14,10},{15,11},{16,20},{17,... | collective-permute-start | bytes 1572872 | tf_op jit(solution)/shard_map/ppermute | solution.py:161
  132.4 6.6 %collective-permute-done.10 = bf16[512,512]{1,0:T(8,128)(2,1)S(1)} collective-permute-done((bf16[512,512]{1,0:T(8,128)(2,1)S(1)}, bf16[512,512]{1,0:T(8,128)(2,1)S(1)}, u32[]{:S(2)}, u32[]{:S(2)}) %collective-permute-start.10) | collective-permute-done | bytes 524320 | tf_op jit(solution)/shard_map/ppermute | solution.py:161
  139.9 1.5 collective-permute-start.11
  145.1 10.6 %collective-permute-done.8 = bf16[512,512]{1,0:T(8,128)(2,1)} collective-permute-done((bf16[512,512]{1,0:T(8,128)(2,1)}, bf16[512,512]{1,0:T(8,128)(2,1)}, u32[]{:S(2)}, u32[]{:S(2)}) %collective-permute-start.8) | collective-permute-done | bytes 524320 | tf_op jit(solution)/shard_map/ppermute | solution.py:161
  155.6 4.5 %fusion.5 = (f32[512,512]{1,0:T(8,128)S(1)}, f32[512,512]{1,0:T(8,128)}) fusion(f32[512,512]{1,0:T(8,128)} %param.12, f32[1,512,512]{2,1,0:T(8,128)} %param.9, f32[1,512,512]{2,1,0:T(8,128)} %param.11, f32[1,512,512]{2,1,0:T(8,128)} %param.10, bf16[512,512]{1,0:T(8,128)(2,1)} %collective-permute-done.11, f32[512,512]{1,0:T(8,128)S(1)} %get-tuple-element.32, ...), kind=kLoop, calls=%fused_computation.6 | loop fusion | flops 4980736 | bytes 9961473 | tf_op jit(solution)/shard_map/sub | solution.py:31
  161.3 1.9 collective-permute-done.12
  163.2 1.6 subtract_convert_fusion
  165.5 7.6 %collective-permute-done.13 = bf16[256,512]{1,0:T(8,128)(2,1)S(1)} collective-permute-done((bf16[256,512]{1,0:T(8,128)(2,1)S(1)}, bf16[256,512]{1,0:T(8,128)(2,1)S(1)}, u32[]{:S(2)}, u32[]{:S(2)}) %collective-permute-start.13) | collective-permute-done | bytes 262176 | tf_op jit(solution)/shard_map/ppermute | solution.py:161
  176.6 6.9 %collective-permute-done.16 = bf16[256,512]{1,0:T(8,128)(2,1)S(1)} collective-permute-done((bf16[256,512]{1,0:T(8,128)(2,1)S(1)}, bf16[256,512]{1,0:T(8,128)(2,1)S(1)}, u32[]{:S(2)}, u32[]{:S(2)}) %collective-permute-start.16) | collective-permute-done | bytes 262176 | tf_op jit(solution)/shard_map/ppermute | solution.py:161
  183.6 6.0 %collective-permute-done.19 = bf16[256,512]{1,0:T(8,128)(2,1)S(1)} collective-permute-done((bf16[256,512]{1,0:T(8,128)(2,1)S(1)}, bf16[256,512]{1,0:T(8,128)(2,1)S(1)}, u32[]{:S(2)}, u32[]{:S(2)}) %collective-permute-start.19) | collective-permute-done | bytes 262176 | tf_op jit(solution)/shard_map/ppermute | solution.py:161
  189.8 1.5 collective-permute-done.20.refs_13_
  194.4 1.9 collective-permute-start.23
  197.6 1.6 collective-permute-done.21
  199.2 2.3 %collective-permute-done.22 = bf16[128,512]{1,0:T(8,128)(2,1)S(1)} collective-permute-done((bf16[128,512]{1,0:T(8,128)(2,1)S(1)}, bf16[128,512]{1,0:T(8,128)(2,1)S(1)}, u32[]{:S(2)}, u32[]{:S(2)}) %collective-permute-start.22) | collective-permute-done | bytes 131104 | tf_op jit(solution)/shard_map/ppermute | solution.py:164
  (61 shorter events, 22.2 us)
Async XLA Ops:
  81.4 10.3 %collective-permute-start = (bf16[256,512]{1,0:T(8,128)(2,1)}, bf16[256,512]{1,0:T(8,128)(2,1)S(1)}, u32[]{:S(2)}, u32[]{:S(2)}) collective-permute-start(bf16[256,512]{1,0:T(8,128)(2,1)} %get-tuple-element.22), channel_id=1, source_target_pairs={{0,1},{1,0},{2,3},{3,2},{4,5},{5,4},{6,7},{7,6},{8,9},{9,8},{10,11... | collective-permute-start | bytes 786440 | tf_op jit(solution)/shard_map/ppermute | solution.py:164
  84.4 13.6 %collective-permute-start.1 = (bf16[256,512]{1,0:T(8,128)(2,1)}, bf16[256,512]{1,0:T(8,128)(2,1)S(1)}, u32[]{:S(2)}, u32[]{:S(2)}) collective-permute-start(bf16[256,512]{1,0:T(8,128)(2,1)} %get-tuple-element.23), channel_id=1, source_target_pairs={{0,2},{1,3},{2,0},{3,1},{4,6},{5,7},{6,4},{7,5},{8,10},{9,11},{10,... | collective-permute-start | bytes 786440 | tf_op jit(solution)/shard_map/ppermute | solution.py:164
  85.9 12.1 %collective-permute-start.2 = (bf16[256,512]{1,0:T(8,128)(2,1)}, bf16[256,512]{1,0:T(8,128)(2,1)S(1)}, u32[]{:S(2)}, u32[]{:S(2)}) collective-permute-start(bf16[256,512]{1,0:T(8,128)(2,1)} %get-tuple-element.24), channel_id=1, source_target_pairs={{0,3},{1,2},{2,1},{3,0},{4,7},{5,6},{6,5},{7,4},{8,11},{9,10},{10,... | collective-permute-start | bytes 786440 | tf_op jit(solution)/shard_map/ppermute | solution.py:164
  99.4 27.3 %collective-permute-start.6 = (bf16[512,512]{1,0:T(8,128)(2,1)S(1)}, bf16[512,512]{1,0:T(8,128)(2,1)S(1)}, u32[]{:S(2)}, u32[]{:S(2)}) collective-permute-start(bf16[512,512]{1,0:T(8,128)(2,1)S(1)} %get-tuple-element.31), channel_id=1, source_target_pairs={{0,4},{1,5},{2,6},{3,7},{12,8},{13,9},{14,10},{15,11},{16,20},{17,... | collective-permute-start | bytes 1572872 | tf_op jit(solution)/shard_map/ppermute | solution.py:161
  102.9 12.3 %collective-permute-start.3 = (bf16[384,512]{1,0:T(8,128)(2,1)}, bf16[384,512]{1,0:T(8,128)(2,1)S(1)}, u32[]{:S(2)}, u32[]{:S(2)}) collective-permute-start(bf16[384,512]{1,0:T(8,128)(2,1)} %get-tuple-element.26), channel_id=1, source_target_pairs={{0,1},{1,0},{2,3},{3,2},{4,5},{5,4},{6,7},{7,6},{8,9},{9,8},{10,11... | collective-permute-start | bytes 1179656 | tf_op jit(solution)/shard_map/ppermute | solution.py:164
  104.2 18.1 %collective-permute-start.4 = (bf16[384,512]{1,0:T(8,128)(2,1)}, bf16[384,512]{1,0:T(8,128)(2,1)S(1)}, u32[]{:S(2)}, u32[]{:S(2)}) collective-permute-start(bf16[384,512]{1,0:T(8,128)(2,1)} %get-tuple-element.27), channel_id=1, source_target_pairs={{0,2},{1,3},{2,0},{3,1},{4,6},{5,7},{6,4},{7,5},{8,10},{9,11},{10,... | collective-permute-start | bytes 1179656 | tf_op jit(solution)/shard_map/ppermute | solution.py:164
  105.0 17.2 %collective-permute-start.5 = (bf16[384,512]{1,0:T(8,128)(2,1)}, bf16[384,512]{1,0:T(8,128)(2,1)S(1)}, u32[]{:S(2)}, u32[]{:S(2)}) collective-permute-start(bf16[384,512]{1,0:T(8,128)(2,1)} %get-tuple-element.28), channel_id=1, source_target_pairs={{0,3},{1,2},{2,1},{3,0},{4,7},{5,6},{6,5},{7,4},{8,11},{9,10},{10,... | collective-permute-start | bytes 1179656 | tf_op jit(solution)/shard_map/ppermute | solution.py:164
  125.1 13.9 %collective-permute-start.10 = (bf16[512,512]{1,0:T(8,128)(2,1)S(1)}, bf16[512,512]{1,0:T(8,128)(2,1)S(1)}, u32[]{:S(2)}, u32[]{:S(2)}) collective-permute-start(bf16[512,512]{1,0:T(8,128)(2,1)S(1)} %get-tuple-element.35), channel_id=1, source_target_pairs={{0,4},{1,5},{2,6},{3,7},{12,8},{13,9},{14,10},{15,11},{16,20},{17,... | collective-permute-start | bytes 1572872 | tf_op jit(solution)/shard_map/ppermute | solution.py:161
  126.8 14.6 %collective-permute-start.7 = (bf16[512,512]{1,0:T(8,128)(2,1)S(1)}, bf16[512,512]{1,0:T(8,128)(2,1)S(1)}, u32[]{:S(2)}, u32[]{:S(2)}) collective-permute-start(bf16[512,512]{1,0:T(8,128)(2,1)S(1)} %add_convert_fusion.2), channel_id=1, source_target_pairs={{4,8},{5,9},{6,10},{7,11},{8,4},{9,5},{10,6},{11,7},{20,24},{21,25... | collective-permute-start | bytes 1572872 | tf_op jit(solution)/shard_map/ppermute | solution.py:161
  127.5 17.5 %collective-permute-start.9 = (bf16[512,512]{1,0:T(8,128)(2,1)}, bf16[512,512]{1,0:T(8,128)(2,1)}, u32[]{:S(2)}, u32[]{:S(2)}) collective-permute-start(bf16[512,512]{1,0:T(8,128)(2,1)} %get-tuple-element.33), channel_id=1, source_target_pairs={{0,4},{1,5},{2,6},{3,7},{12,8},{13,9},{14,10},{15,11},{16,20},{17,... | collective-permute-start | bytes 1572872 | tf_op jit(solution)/shard_map/ppermute | solution.py:161
  139.9 5.1 %collective-permute-start.11 = (bf16[512,512]{1,0:T(8,128)(2,1)}, bf16[512,512]{1,0:T(8,128)(2,1)}, u32[]{:S(2)}, u32[]{:S(2)}) collective-permute-start(bf16[512,512]{1,0:T(8,128)(2,1)} %add_convert_fusion), channel_id=1, source_target_pairs={{4,8},{5,9},{6,10},{7,11},{8,4},{9,5},{10,6},{11,7},{20,24},{21,25... | collective-permute-start | bytes 1572872 | tf_op jit(solution)/shard_map/ppermute | solution.py:161
  142.4 13.3 %collective-permute-start.8 = (bf16[512,512]{1,0:T(8,128)(2,1)}, bf16[512,512]{1,0:T(8,128)(2,1)}, u32[]{:S(2)}, u32[]{:S(2)}) collective-permute-start(bf16[512,512]{1,0:T(8,128)(2,1)} %add_convert_fusion.1), channel_id=1, source_target_pairs={{4,0},{5,1},{6,2},{7,3},{8,12},{9,13},{10,14},{11,15},{20,16},{21,... | collective-permute-start | bytes 1572872 | tf_op jit(solution)/shard_map/ppermute | solution.py:161
  161.2 2.0 collective-permute-start.12
  164.8 8.4 %collective-permute-start.13 = (bf16[256,512]{1,0:T(8,128)(2,1)S(1)}, bf16[256,512]{1,0:T(8,128)(2,1)S(1)}, u32[]{:S(2)}, u32[]{:S(2)}) collective-permute-start(bf16[256,512]{1,0:T(8,128)(2,1)S(1)} %subtract_convert_fusion), channel_id=1, source_target_pairs={{0,4},{1,5},{2,6},{3,7},{4,0},{5,1},{6,2},{7,3},{8,12},{9,13},{10,... | collective-permute-start | bytes 786440 | tf_op jit(solution)/shard_map/ppermute | solution.py:161
  164.8 9.0 %collective-permute-start.15 = (bf16[256,512]{1,0:T(8,128)(2,1)S(1)}, bf16[256,512]{1,0:T(8,128)(2,1)S(1)}, u32[]{:S(2)}, u32[]{:S(2)}) collective-permute-start(bf16[256,512]{1,0:T(8,128)(2,1)S(1)} %subtract_convert_fusion), channel_id=1, source_target_pairs={{4,8},{5,9},{6,10},{7,11},{8,4},{9,5},{10,6},{11,7},{20,24},{21,25... | collective-permute-start | bytes 786440 | tf_op jit(solution)/shard_map/ppermute | solution.py:161
  173.2 2.0 collective-permute-start.18
  173.9 9.7 %collective-permute-start.16 = (bf16[256,512]{1,0:T(8,128)(2,1)S(1)}, bf16[256,512]{1,0:T(8,128)(2,1)S(1)}, u32[]{:S(2)}, u32[]{:S(2)}) collective-permute-start(bf16[256,512]{1,0:T(8,128)(2,1)S(1)} %collective-permute-done.15), channel_id=1, source_target_pairs={{4,0},{5,1},{6,2},{7,3},{8,12},{9,13},{10,14},{11,15},{20,16},{21,... | collective-permute-start | bytes 786440 | tf_op jit(solution)/shard_map/ppermute | solution.py:161
  175.2 14.5 %collective-permute-start.19 = (bf16[256,512]{1,0:T(8,128)(2,1)S(1)}, bf16[256,512]{1,0:T(8,128)(2,1)S(1)}, u32[]{:S(2)}, u32[]{:S(2)}) collective-permute-start(bf16[256,512]{1,0:T(8,128)(2,1)S(1)} %collective-permute-done.18), channel_id=1, source_target_pairs={{4,0},{5,1},{6,2},{7,3},{8,12},{9,13},{10,14},{11,15},{20,16},{21,... | collective-permute-start | bytes 786440 | tf_op jit(solution)/shard_map/ppermute | solution.py:161
  176.5 13.3 %collective-permute-start.14 = (bf16[2,256,512]{2,1,0:T(8,128)(2,1)S(1)}, bf16[2,256,512]{2,1,0:T(8,128)(2,1)S(1)}, u32[]{:S(2)}, u32[]{:S(2)}) collective-permute-start(bf16[2,256,512]{2,1,0:T(8,128)(2,1)S(1)} %pad_maximum_fusion.refs_8_), channel_id=1, source_target_pairs={{0,16},{16,0},{1,17},{17,1},{2,18},{18,2},{3,19},{19,3},{4,20},{20... | collective-permute-start | bytes 1572872 | tf_op jit(solution)/shard_map/ppermute | solution.py:167
  183.6 6.2 %collective-permute-start.17 = (bf16[256,512]{1,0:T(8,128)(2,1)S(1)}, bf16[256,512]{1,0:T(8,128)(2,1)S(1)}, u32[]{:S(2)}, u32[]{:S(2)}) collective-permute-start(bf16[256,512]{1,0:T(8,128)(2,1)S(1)} %broadcast_select_fusion.1.refs_10_), channel_id=1, source_target_pairs={{0,16},{16,0},{1,17},{17,1},{2,18},{18,2},{3,19},{19,3},{4,20},{20... | collective-permute-start | bytes 786440 | tf_op jit(solution)/shard_map/ppermute | solution.py:167
  189.7 1.6 collective-permute-start.20
  192.8 6.4 %collective-permute-start.21 = (bf16[128,512]{1,0:T(8,128)(2,1)S(1)}, bf16[128,512]{1,0:T(8,128)(2,1)S(1)}, u32[]{:S(2)}, u32[]{:S(2)}) collective-permute-start(bf16[128,512]{1,0:T(8,128)(2,1)S(1)} %get-tuple-element.37), channel_id=1, source_target_pairs={{0,1},{1,0},{2,3},{3,2},{4,5},{5,4},{6,7},{7,6},{8,9},{9,8},{10,11... | collective-permute-start | bytes 393224 | tf_op jit(solution)/shard_map/ppermute | solution.py:164
  193.4 8.1 %collective-permute-start.22 = (bf16[128,512]{1,0:T(8,128)(2,1)S(1)}, bf16[128,512]{1,0:T(8,128)(2,1)S(1)}, u32[]{:S(2)}, u32[]{:S(2)}) collective-permute-start(bf16[128,512]{1,0:T(8,128)(2,1)S(1)} %get-tuple-element.38), channel_id=1, source_target_pairs={{0,2},{1,3},{2,0},{3,1},{4,6},{5,7},{6,4},{7,5},{8,10},{9,11},{10,... | collective-permute-start | bytes 393224 | tf_op jit(solution)/shard_map/ppermute | solution.py:164
  194.4 7.1 %collective-permute-start.23 = (bf16[128,512]{1,0:T(8,128)(2,1)S(1)}, bf16[128,512]{1,0:T(8,128)(2,1)S(1)}, u32[]{:S(2)}, u32[]{:S(2)}) collective-permute-start(bf16[128,512]{1,0:T(8,128)(2,1)S(1)} %get-tuple-element.39), channel_id=1, source_target_pairs={{0,3},{1,2},{2,1},{3,0},{4,7},{5,6},{6,5},{7,4},{8,11},{9,10},{10,... | collective-permute-start | bytes 393224 | tf_op jit(solution)/shard_map/ppermute | solution.py:164
  (11 other events, 145.8 us)

commit v2 on v1

v2 whole, which is shorter than its diff:
```python
from functools import partial

import jax
import jax.numpy as jnp
from jax import lax
from jax.experimental import pallas as pl
from jax.experimental.pallas import tpu as pltpu
from jax.sharding import PartitionSpec as P

decay_first = 0.9
decay_second = 0.95
inner_rate = 0.006
epsilon = 1e-08
outer_rate = 0.7
outer_decay = 0.9

PLANES = 4
CONTRACT_ROWS = (((0,), (0,)), ((), ()))
VMEM_BYTES = 16 * 1024 * 1024


def outer_update(average, anchor_rows, momentum_rows):
    velocity = outer_decay * momentum_rows + average
    return (anchor_rows - outer_rate * (average + outer_decay * velocity)).astype(jnp.bfloat16)


def inner_update(gradient, inner_weights, first_moment, second_moment, anchor):
    first_next = decay_first * first_moment + (1.0 - decay_first) * gradient
    second_next = decay_second * second_moment + (1.0 - decay_second) * gradient * gradient
    stepped = inner_weights - inner_rate * first_next / (jnp.sqrt(second_next) + epsilon)
    return first_next, anchor - stepped


def general(acts, value_cots, inner_weights, first_moment, second_moment, anchor, outer_momentum):
    tokens_local = acts[0]
    columns = lax.all_to_all(tokens_local, "fsdp", split_axis=1, concat_axis=0, tiled=True)
    cots = lax.all_gather(value_cots[0], "fsdp", axis=0, tiled=True)
    gradient = lax.dot_general(columns, cots, CONTRACT_ROWS, preferred_element_type=jnp.float32)
    first_next, drift = inner_update(gradient, inner_weights[0], first_moment[0], second_moment[0], anchor)
    average = lax.psum(drift, "rep") / lax.axis_size("rep")
    weights_next = outer_update(average, anchor, outer_momentum)
    gathered = lax.all_gather(weights_next, "fsdp", axis=0, tiled=True)
    values = jnp.dot(tokens_local, gathered, preferred_element_type=jnp.float32)
    return (first_next[None], values.astype(jnp.bfloat16)[None])


def mirrored():
    planes_at = lax.axis_size("fsdp") // PLANES
    f = lax.axis_index("fsdp")
    o = f // planes_at
    return o, lax.rem(f, planes_at), jnp.where(o < PLANES // 2, o, PLANES - 1 - o)


def repack_kernel(inner, targets, *refs):
    acts_ref, cots, outs = refs[0], refs[1 : len(refs) - inner], refs[len(refs) - inner :]
    tokens, rows = acts_ref.shape[0], outs[0].shape[1]
    o, i, _ = mirrored()
    for k in range(inner):
        x, y = lax.rem(i, 2), i // 2
        place = (y + k // 2 - 2 * y * (k // 2)) * 2 + x + k % 2 - 2 * x * (k % 2)
        for slot, t in enumerate(targets):
            plane = jnp.where(o < PLANES // 2, t, PLANES - 1 - t)
            start = pl.multiple_of((plane * inner + place) * rows, rows)
            outs[k][slot * tokens : (slot + 1) * tokens] = acts_ref[:, pl.ds(start, rows)]
        for cots_ref in cots:
            outs[k][len(targets) * tokens :] = cots_ref[...]


def repack(inputs, inner, targets, rows):
    tokens = inputs[0].shape[0]
    out = [jax.ShapeDtypeStruct(((len(targets) + len(inputs) - 1) * tokens, rows), jnp.bfloat16)] * inner
    return call(partial(repack_kernel, inner, targets), "repack", out, inputs, 0)


def partial_kernel(inner, tokens, slots, *refs):
    firsts, blocks, outs = refs[:inner], refs[inner : 2 * inner], refs[2 * inner :]
    cots = jnp.concatenate([ref[tokens:] for ref in firsts], axis=0)
    for slot in range(slots):
        columns = jnp.concatenate([ref[slot * tokens : (slot + 1) * tokens] for ref in blocks], axis=0)
        total = lax.dot_general(columns, cots, CONTRACT_ROWS, preferred_element_type=jnp.float32)
        outs[slot][...] = total
        if slot == 0:
            outs[slots][...] = total.astype(jnp.bfloat16)


def first_partial_kernel(inner, tokens, *refs):
    partial_kernel(inner, tokens, 1, *refs[:inner], *refs)


CHUNK = 32


def own_gradient(near, at, refs):
    total0, total1, a3, b3, c3 = refs
    end = total0[at, :] + c3[at, :].astype(jnp.float32)
    inside = total1[at, :] + a3[at, :].astype(jnp.float32) + b3[at, :].astype(jnp.float32)
    return jnp.where(near == 0, end, inside)


def drift_kernel(*refs):
    gradient_refs, (weights, first, second, anchor), drift_ref = refs[:5], refs[5:9], refs[9]
    half = drift_ref.shape[0]
    _, _, near = mirrored()
    base = (1 - lax.axis_index("rep")) * half

    @pl.loop(0, half // CHUNK)
    def _(step):
        at = pl.ds(pl.multiple_of(base + step * CHUNK, CHUNK), CHUNK)
        gradient = own_gradient(near, at, gradient_refs)
        _, drift = inner_update(gradient, weights[at, :], first[at, :], second[at, :], anchor[at, :])
        drift_ref[pl.ds(pl.multiple_of(step * CHUNK, CHUNK), CHUNK), :] = drift


def update_kernel(*refs):
    gradient_refs, (weights, first, second, anchor), (first_ref, drift_ref) = refs[:5], refs[5:9], refs[9:]
    half = drift_ref.shape[0]
    _, _, near = mirrored()
    r = lax.axis_index("rep")

    @pl.loop(0, half // CHUNK)
    def _(step):
        at = pl.ds(pl.multiple_of(r * half + step * CHUNK, CHUNK), CHUNK)
        gradient = own_gradient(near, at, gradient_refs)
        first_next, drift = inner_update(gradient, weights[at, :], first[at, :], second[at, :], anchor[at, :])
        first_ref[at, :] = first_next
        drift_ref[pl.ds(pl.multiple_of(step * CHUNK, CHUNK), CHUNK), :] = drift

    @pl.loop(0, half // CHUNK)
    def _(step):
        at = pl.ds(pl.multiple_of((1 - r) * half + step * CHUNK, CHUNK), CHUNK)
        gradient = own_gradient(near, at, gradient_refs)
        first_ref[at, :] = decay_first * first[at, :] + (1.0 - decay_first) * gradient


def outer_kernel(drift, other, anchor, momentum, out):
    half = out.shape[0]
    at = pl.ds(pl.multiple_of(lax.axis_index("rep") * half, half), half)
    out[...] = outer_update((drift[...] + other[...]) / 2, anchor[at, :], momentum[at, :])


def values_kernel(inner, tokens, rows, *refs):
    firsts, seconds, lasts = refs[:inner], refs[inner : 2 * inner], refs[2 * inner : 3 * inner]
    mine_ref, other_ref, mine2_ref, other2_ref, mine3_ref, other3_ref = refs[3 * inner : 3 * inner + 6]
    own_ref, sent_refs, weights = refs[3 * inner + 6], refs[3 * inner + 7 : -1], refs[-1]
    half = rows // 2
    r = lax.axis_index("rep")
    _, _, near = mirrored()

    def put(t, which, value):
        weights[pl.ds(pl.multiple_of(t * rows + which * half, half), half), :] = value

    for slot, t in ((0, near), (1, 1 - near)):
        put(t, r, mine_ref[slot])
        put(t, 1 - r, other_ref[slot])
    put(2, r, mine2_ref[...])
    put(2, 1 - r, other2_ref[...])
    put(3, r, mine3_ref[...])
    put(3, 1 - r, other3_ref[...])
    for k in range(inner):
        blocks = (lasts[k][tokens:], lasts[k][:tokens], seconds[k][...], firsts[k][:tokens])
        total = jnp.dot(jnp.concatenate(blocks, axis=1), weights[...], preferred_element_type=jnp.float32)
        if k == 0:
            own_ref[...] = total
        else:
            sent_refs[k - 1][...] = total.astype(jnp.bfloat16)


def call(kernel, name, out, inputs, flops, scratch=()):
    moved = sum(x.size * x.dtype.itemsize for x in list(inputs) + list(out))
    return pl.pallas_call(
        kernel,
        out_shape=out,
        in_specs=[pl.BlockSpec(memory_space=pltpu.VMEM)] * len(inputs),
        out_specs=[pl.BlockSpec(memory_space=pltpu.VMEM)] * len(out),
        scratch_shapes=list(scratch),
        compiler_params=pltpu.CompilerParams(vmem_limit_bytes=VMEM_BYTES),
        cost_estimate=pl.CostEstimate(flops=flops, bytes_accessed=moved, transcendentals=0),
        name=name,
    )(*inputs)


def on_device(acts, value_cots, inner_weights, first_moment, second_moment, anchor, outer_momentum):
    inner = lax.axis_size("fsdp") // PLANES
    rows, width = anchor.shape
    if inner != 4 or lax.axis_size("rep") != 2 or rows % 256:
        return general(acts, value_cots, inner_weights, first_moment, second_moment, anchor, outer_momentum)
    tokens = acts.shape[1]
    half = rows // 2
    at_end = mirrored()[2] == 0

    def line(x, *pairs):
        return lax.ppermute(x, "fsdp", [(a * inner + i, b * inner + i) for a, b in pairs for i in range(inner)])

    def across(x, k):
        return lax.ppermute(x, "fsdp", [(p * inner + i, p * inner + (i ^ k)) for p in range(PLANES) for i in range(inner)])

    def swap(x):
        return lax.ppermute(x, "rep", [(0, 1), (1, 0)])

    def inward(x):
        return line(x, (0, 1), (3, 2))

    def middle(x):
        return line(x, (1, 2), (2, 1))

    def outward(x):
        return line(x, (1, 0), (2, 3))

    def around(blocks):
        return [blocks[0]] + [across(blocks[k], k) for k in range(1, inner)]

    firsts = around(repack([acts[0], value_cots[0]], inner, (3,), rows))
    seconds = around(repack([acts[0]], inner, (2,), rows))
    lasts = around(repack([acts[0]], inner, (1, 0), rows))

    f32 = jax.ShapeDtypeStruct((rows, width), jnp.float32)
    bf16 = jax.ShapeDtypeStruct((rows, width), jnp.bfloat16)
    flops = 2 * inner * tokens * rows * width
    total3, sent3 = call(partial(first_partial_kernel, inner, tokens), "partial_first", [f32, bf16], firsts, flops)
    total2, sent2 = call(partial(partial_kernel, inner, tokens, 1), "partial_second", [f32, bf16], firsts + seconds, flops)
    total1, total0, sent1 = call(
        partial(partial_kernel, inner, tokens, 2), "partial_last", [f32, f32, bf16], firsts + lasts, 2 * flops
    )
    a1 = inward(sent3)
    a2 = inward(sent2)
    a3 = inward(sent1)

    def add(total, got):
        return (total + got.astype(jnp.float32)).astype(jnp.bfloat16)

    b2 = middle(add(total3, a1))
    b3 = middle(add(total2, a2))
    c3 = outward(add(total0, b2))
    state = [total0, total1, a3, b3, c3, inner_weights[0], first_moment[0], second_moment[0], anchor]
    half_block = jax.ShapeDtypeStruct((half, width), jnp.float32)
    (drift_out,) = call(drift_kernel, "drift", [half_block], state, 0)
    drift_in = swap(drift_out)
    first_next, drift = call(update_kernel, "update", [f32, half_block], state, 0)
    (mine,) = call(
        outer_kernel,
        "outer",
        [jax.ShapeDtypeStruct((half, width), jnp.bfloat16)],
        [drift, drift_in, anchor, outer_momentum],
        0,
    )
    beside = line(mine, (0, 1), (1, 0), (2, 3), (3, 2))
    far2 = middle(mine)
    far3 = middle(beside)
    mine2 = jnp.where(at_end, outward(far2), far2)
    mine3 = jnp.where(at_end, outward(far3), far3)
    mine = jnp.stack([mine, beside])
    pieces = [mine, swap(mine), mine2, swap(mine2), mine3, swap(mine3)]
    block = jax.ShapeDtypeStruct((tokens, width), jnp.bfloat16)
    values, *sent = call(
        partial(values_kernel, inner, tokens, rows),
        "values",
        [jax.ShapeDtypeStruct((tokens, width), jnp.float32)] + [block] * (inner - 1),
        firsts + seconds + lasts + pieces,
        4 * flops,
        [pltpu.VMEM((PLANES * rows, width), jnp.bfloat16)],
    )
    for k in range(1, inner):
        values = values + across(sent[k - 1], k).astype(jnp.float32)
    return (first_next[None], values.astype(jnp.bfloat16)[None])


def solution(mesh):
    placed = (
        P("rep", "fsdp", None),
        P("rep", "fsdp", None),
        P("rep", "fsdp", None),
        P("rep", "fsdp", None),
        P("rep", "fsdp", None),
        P("fsdp", None),
        P("fsdp", None),
    )
    return jax.shard_map(
        on_device,
        mesh=mesh,
        in_specs=placed,
        out_specs=(P("rep", "fsdp", None), P("rep", "fsdp", None)),
        check_vma=False,
    )
```

time: 203 us -> 104 us (0.51)
  Pallas kernels: 84.2 us -> 5.92 us
  waiting for transfers between devices: 74.2 us -> 59.3 us
  other arithmetic: 10.3 us -> 3.21 us
  starting transfers between devices: 29.3 us -> 31.6 us
    pallas_call x1 -> x0, Pallas kernels: 80.7 us -> none  [repack(): pl.pallas_call(partial(repack_kernel, inner, rows), out_shape=out, in_spe...]
    ppermute x9 -> x12, waiting for transfers between devices: 31.8 us -> 24.1 us  [across(): lax.ppermute(x, 'fsdp', [(p * inner + i, p * inner + (i ^ k)) for p in ra...]
    ppermute x9 -> x12, starting transfers between devices: 11.7 us -> 17.4 us  [across(): lax.ppermute(x, 'fsdp', [(p * inner + i, p * inner + (i ^ k)) for p in ra...]
    ppermute x11, waiting for transfers between devices: 39.1 us -> 33.6 us  [line(): lax.ppermute(x, 'fsdp', [(a * inner + i, b * inner + i) for a, b in pairs...]
    sub x1 -> x0, other arithmetic: 4.53 us -> none  [inner_update(): return (first_next, anchor - stepped)]
    ppermute x11, starting transfers between devices: 17.4 us -> 13.9 us  [line(): lax.ppermute(x, 'fsdp', [(a * inner + i, b * inner + i) for a, b in pairs...]
    pallas_call x3 -> x10, Pallas kernels: 3.45 us -> 5.92 us  [call(): pl.pallas_call(kernel, out_shape=out, in_specs=[pl.BlockSpec(memory_space...]
  transfers between devices with their start and end apart: 24 -> 27, of which waited for: 14 -> 16; matrix products, arithmetic and copies ran while one was open for 2% -> 2% of each run, Pallas kernels for 1% -> 3%
where the time goes in v2:
time: 104 us
  waiting for transfers between devices  59.3 us (57%)
  starting transfers between devices  31.6 us (30%)
  Pallas kernels  5.92 us (6%)
  other arithmetic  3.21 us (3%)
  local copies, waits for them, and re-layouts  2.51 us (2%)
    ppermute x11, waiting for transfers between devices, line(): lax.ppermute(x, 'fsdp', [(a * inner + i, b * inner + i) for a, b in pairs...  33.6 us
    ppermute x12, waiting for transfers between devices, across(): lax.ppermute(x, 'fsdp', [(p * inner + i, p * inner + (i ^ k)) for p in ra...  24.1 us
    ppermute x12, starting transfers between devices, across(): lax.ppermute(x, 'fsdp', [(p * inner + i, p * inner + (i ^ k)) for p in ra...  17.4 us
    ppermute x11, starting transfers between devices, line(): lax.ppermute(x, 'fsdp', [(a * inner + i, b * inner + i) for a, b in pairs...  13.9 us
    pallas_call x10, Pallas kernels, call(): pl.pallas_call(kernel, out_shape=out, in_specs=[pl.BlockSpec(memory_space...  5.92 us
    unnamed x16, local copies, waits for them, and re-layouts  2.51 us
  transfers between devices with their start and end apart: 27, of which 16 were waited for; matrix products, arithmetic and copies ran while one was open for 2% of the time, Pallas kernels for 3%

profile of v2, /device:TPU:0, one launch (start us, length us, event | category | flops | bytes accessed | tf_op | source)
XLA Modules:
  0.0 103.5 jit_solution(2864483749661442353)
XLA Ops:
  0.6 1.6 %copy-done = bf16[1,128,8192]{2,1,0:T(8,128)(2,1)S(1)} copy-done((bf16[1,128,8192]{2,1,0:T(8,128)(2,1)S(1)}, bf16[1,128,8192]{2,1,0:T(8,128)(2,1)}, u32[]{:S(2)}) %copy-start) | copy-done | bytes 2097176
  3.2 3.0 %collective-permute-start = (bf16[256,512]{1,0:T(8,128)(2,1)S(1)}, bf16[256,512]{1,0:T(8,128)(2,1)S(1)}, u32[]{:S(2)}, u32[]{:S(2)}) collective-permute-start(bf16[256,512]{1,0:T(8,128)(2,1)S(1)} %get-tuple-element.28), channel_id=1, source_target_pairs={{0,1},{1,0},{2,3},{3,2},{4,5},{5,4},{6,7},{7,6},{8,9},{9,8},{10,11... | collective-permute-start | bytes 786440 | tf_op jit(solution)/shard_map/ppermute | solution.py:195
  6.2 1.5 %collective-permute-start.1 = (bf16[256,512]{1,0:T(8,128)(2,1)S(1)}, bf16[256,512]{1,0:T(8,128)(2,1)S(1)}, u32[]{:S(2)}, u32[]{:S(2)}) collective-permute-start(bf16[256,512]{1,0:T(8,128)(2,1)S(1)} %get-tuple-element.29), channel_id=1, source_target_pairs={{0,2},{1,3},{2,0},{3,1},{4,6},{5,7},{6,4},{7,5},{8,10},{9,11},{10,... | collective-permute-start | bytes 786440 | tf_op jit(solution)/shard_map/ppermute | solution.py:195
  7.7 5.6 %collective-permute-done.refs_1_ = bf16[256,512]{1,0:T(8,128)(2,1)S(1)} collective-permute-done((bf16[256,512]{1,0:T(8,128)(2,1)S(1)}, bf16[256,512]{1,0:T(8,128)(2,1)S(1)}, u32[]{:S(2)}, u32[]{:S(2)}) %collective-permute-start) | collective-permute-done | bytes 262176 | tf_op jit(solution)/shard_map/ppermute | solution.py:195
  13.3 6.2 %collective-permute-done.1.refs_2_ = bf16[256,512]{1,0:T(8,128)(2,1)S(1)} collective-permute-done((bf16[256,512]{1,0:T(8,128)(2,1)S(1)}, bf16[256,512]{1,0:T(8,128)(2,1)S(1)}, u32[]{:S(2)}, u32[]{:S(2)}) %collective-permute-start.1) | collective-permute-done | bytes 262176 | tf_op jit(solution)/shard_map/ppermute | solution.py:195
  20.1 3.5 %collective-permute-start.12 = (bf16[512,512]{1,0:T(8,128)(2,1)S(1)}, bf16[512,512]{1,0:T(8,128)(2,1)S(1)}, u32[]{:S(2)}, u32[]{:S(2)}) collective-permute-start(bf16[512,512]{1,0:T(8,128)(2,1)S(1)} %get-tuple-element.45), channel_id=1, source_target_pairs={{0,4},{1,5},{2,6},{3,7},{12,8},{13,9},{14,10},{15,11},{16,20},{17,... | collective-permute-start | bytes 1572872 | tf_op jit(solution)/shard_map/ppermute | solution.py:192
  28.6 1.5 %collective-permute-done.7.refs_5_ = bf16[128,512]{1,0:T(8,128)(2,1)S(1)} collective-permute-done((bf16[128,512]{1,0:T(8,128)(2,1)S(1)}, bf16[128,512]{1,0:T(8,128)(2,1)S(1)}, u32[]{:S(2)}, u32[]{:S(2)}) %collective-permute-start.7) | collective-permute-done | bytes 131104 | tf_op jit(solution)/shard_map/ppermute | solution.py:195
  30.1 1.5 %collective-permute-start.4 = (bf16[256,512]{1,0:T(8,128)(2,1)S(1)}, bf16[256,512]{1,0:T(8,128)(2,1)S(1)}, u32[]{:S(2)}, u32[]{:S(2)}) collective-permute-start(bf16[256,512]{1,0:T(8,128)(2,1)S(1)} %get-tuple-element.33), channel_id=1, source_target_pairs={{0,2},{1,3},{2,0},{3,1},{4,6},{5,7},{6,4},{7,5},{8,10},{9,11},{10,... | collective-permute-start | bytes 786440 | tf_op jit(solution)/shard_map/ppermute | solution.py:195
  32.0 2.4 %collective-permute-start.5 = (bf16[256,512]{1,0:T(8,128)(2,1)S(1)}, bf16[256,512]{1,0:T(8,128)(2,1)S(1)}, u32[]{:S(2)}, u32[]{:S(2)}) collective-permute-start(bf16[256,512]{1,0:T(8,128)(2,1)S(1)} %get-tuple-element.34), channel_id=1, source_target_pairs={{0,3},{1,2},{2,1},{3,0},{4,7},{5,6},{6,5},{7,4},{8,11},{9,10},{10,... | collective-permute-start | bytes 786440 | tf_op jit(solution)/shard_map/ppermute | solution.py:195
  34.8 1.9 %collective-permute-start.10 = (bf16[512,512]{1,0:T(8,128)(2,1)S(1)}, bf16[512,512]{1,0:T(8,128)(2,1)S(1)}, u32[]{:S(2)}, u32[]{:S(2)}) collective-permute-start(bf16[512,512]{1,0:T(8,128)(2,1)S(1)} %get-tuple-element.43), channel_id=1, source_target_pairs={{0,4},{1,5},{2,6},{3,7},{12,8},{13,9},{14,10},{15,11},{16,20},{17,... | collective-permute-start | bytes 1572872 | tf_op jit(solution)/shard_map/ppermute | solution.py:192
  38.5 4.3 %collective-permute-done.4.refs_6_.refs_10_ = bf16[256,512]{1,0:T(8,128)(2,1)S(1)} collective-permute-done((bf16[256,512]{1,0:T(8,128)(2,1)S(1)}, bf16[256,512]{1,0:T(8,128)(2,1)S(1)}, u32[]{:S(2)}, u32[]{:S(2)}) %collective-permute-start.4) | collective-permute-done | bytes 262176 | tf_op jit(solution)/shard_map/ppermute | solution.py:195
  43.6 1.6 %collective-permute-start.6 = (bf16[512,512]{1,0:T(8,128)(2,1)S(1)}, bf16[512,512]{1,0:T(8,128)(2,1)S(1)}, u32[]{:S(2)}, u32[]{:S(2)}) collective-permute-start(bf16[512,512]{1,0:T(8,128)(2,1)S(1)} %get-tuple-element.37), channel_id=1, source_target_pairs={{0,4},{1,5},{2,6},{3,7},{12,8},{13,9},{14,10},{15,11},{16,20},{17,... | collective-permute-start | bytes 1572872 | tf_op jit(solution)/shard_map/ppermute | solution.py:192
  45.1 1.6 %collective-permute-done.10 = bf16[512,512]{1,0:T(8,128)(2,1)S(1)} collective-permute-done((bf16[512,512]{1,0:T(8,128)(2,1)S(1)}, bf16[512,512]{1,0:T(8,128)(2,1)S(1)}, u32[]{:S(2)}, u32[]{:S(2)}) %collective-permute-start.10) | collective-permute-done | bytes 524320 | tf_op jit(solution)/shard_map/ppermute | solution.py:192
  49.4 6.7 %collective-permute-done.6.refs_2_ = bf16[512,512]{1,0:T(8,128)(2,1)S(1)} collective-permute-done((bf16[512,512]{1,0:T(8,128)(2,1)S(1)}, bf16[512,512]{1,0:T(8,128)(2,1)S(1)}, u32[]{:S(2)}, u32[]{:S(2)}) %collective-permute-start.6) | collective-permute-done | bytes 524320 | tf_op jit(solution)/shard_map/ppermute | solution.py:192
  56.1 5.7 %collective-permute-done.14.refs_4_ = bf16[512,512]{1,0:T(8,128)(2,1)S(1)} collective-permute-done((bf16[512,512]{1,0:T(8,128)(2,1)S(1)}, bf16[512,512]{1,0:T(8,128)(2,1)S(1)}, u32[]{:S(2)}, u32[]{:S(2)}) %collective-permute-start.14) | collective-permute-done | bytes 524320 | tf_op jit(solution)/shard_map/ppermute | solution.py:192
  62.5 1.8 %update.1 = (f32[512,512]{1,0:T(8,128)}, f32[256,512]{1,0:T(8,128)S(1)}) custom-call(f32[512,512]{1,0:T(8,128)S(1)} %get-tuple-element.35.refs_0_, f32[512,512]{1,0:T(8,128)S(1)} %get-tuple-element.36.refs_1_, bf16[512,512]{1,0:T(8,128)(2,1)S(1)} %collective-permute-done.6.refs_2_, bf16[512,512]{1,0:T(8,128)(2,1)S(1)} %collective-permute-done.11.refs_3_, ...), custom_call_target="tpu_custom_call" | custom-call | bytes 9437184 | tf_op jit(solution)/shard_map/update/pallas_call | solution.py:170
  65.4 8.0 %collective-permute-done.16 = bf16[256,512]{1,0:T(8,128)(2,1)} collective-permute-done((bf16[256,512]{1,0:T(8,128)(2,1)S(1)}, bf16[256,512]{1,0:T(8,128)(2,1)}, u32[]{:S(2)}, u32[]{:S(2)}) %collective-permute-start.16) | collective-permute-done | bytes 262176 | tf_op jit(solution)/shard_map/ppermute | solution.py:192
  77.7 6.2 %collective-permute-done.19 = bf16[256,512]{1,0:T(8,128)(2,1)} collective-permute-done((bf16[256,512]{1,0:T(8,128)(2,1)S(1)}, bf16[256,512]{1,0:T(8,128)(2,1)}, u32[]{:S(2)}, u32[]{:S(2)}) %collective-permute-start.19) | collective-permute-done | bytes 262176 | tf_op jit(solution)/shard_map/ppermute | solution.py:192
  85.0 5.3 %collective-permute-done.22 = bf16[256,512]{1,0:T(8,128)(2,1)S(1)} collective-permute-done((bf16[256,512]{1,0:T(8,128)(2,1)S(1)}, bf16[256,512]{1,0:T(8,128)(2,1)S(1)}, u32[]{:S(2)}, u32[]{:S(2)}) %collective-permute-start.22) | collective-permute-done | bytes 262176 | tf_op jit(solution)/shard_map/ppermute | solution.py:192
  90.5 1.5 %collective-permute-done.23.refs_17_ = bf16[256,512]{1,0:T(8,128)(2,1)S(1)} collective-permute-done((bf16[256,512]{1,0:T(8,128)(2,1)S(1)}, bf16[256,512]{1,0:T(8,128)(2,1)S(1)}, u32[]{:S(2)}, u32[]{:S(2)}) %collective-permute-start.23) | collective-permute-done | bytes 262176 | tf_op jit(solution)/shard_map/ppermute | solution.py:198
  92.0 1.5 %values.1 = (f32[128,512]{1,0:T(8,128)S(1)}, bf16[128,512]{1,0:T(8,128)(2,1)S(1)}, bf16[128,512]{1,0:T(8,128)(2,1)S(1)}, bf16[128,512]{1,0:T(8,128)(2,1)S(1)}) custom-call(bf16[256,512]{1,0:T(8,128)(2,1)S(1)} %get-tuple-element.27.refs_0_, bf16[256,512]{1,0:T(8,128)(2,1)S(1)} %collective-permute-done.refs_1_, ...), custom_call_target="tpu_custom_call" | custom-call | flops 1073741824 | bytes 5373952 | tf_op jit(solution)/shard_map/values/pallas_call | solution.py:170
  94.8 2.8 %collective-permute-start.25 = (bf16[128,512]{1,0:T(8,128)(2,1)S(1)}, bf16[128,512]{1,0:T(8,128)(2,1)S(1)}, u32[]{:S(2)}, u32[]{:S(2)}) collective-permute-start(bf16[128,512]{1,0:T(8,128)(2,1)S(1)} %get-tuple-element.50), channel_id=1, source_target_pairs={{0,2},{1,3},{2,0},{3,1},{4,6},{5,7},{6,4},{7,5},{8,10},{9,11},{10,... | collective-permute-start | bytes 393224 | tf_op jit(solution)/shard_map/ppermute | solution.py:195
  97.6 2.8 %collective-permute-done.26 = bf16[128,512]{1,0:T(8,128)(2,1)S(1)} collective-permute-done((bf16[128,512]{1,0:T(8,128)(2,1)S(1)}, bf16[128,512]{1,0:T(8,128)(2,1)S(1)}, u32[]{:S(2)}, u32[]{:S(2)}) %collective-permute-start.26) | collective-permute-done | bytes 131104 | tf_op jit(solution)/shard_map/ppermute | solution.py:195
  100.4 2.4 %collective-permute-done.25 = bf16[128,512]{1,0:T(8,128)(2,1)S(1)} collective-permute-done((bf16[128,512]{1,0:T(8,128)(2,1)S(1)}, bf16[128,512]{1,0:T(8,128)(2,1)S(1)}, u32[]{:S(2)}, u32[]{:S(2)}) %collective-permute-start.25) | collective-permute-done | bytes 131104 | tf_op jit(solution)/shard_map/ppermute | solution.py:195
  (63 shorter events, 21.6 us)
Async XLA Ops:
  3.2 10.1 %collective-permute-start = (bf16[256,512]{1,0:T(8,128)(2,1)S(1)}, bf16[256,512]{1,0:T(8,128)(2,1)S(1)}, u32[]{:S(2)}, u32[]{:S(2)}) collective-permute-start(bf16[256,512]{1,0:T(8,128)(2,1)S(1)} %get-tuple-element.28), channel_id=1, source_target_pairs={{0,1},{1,0},{2,3},{3,2},{4,5},{5,4},{6,7},{7,6},{8,9},{9,8},{10,11... | collective-permute-start | bytes 786440 | tf_op jit(solution)/shard_map/ppermute | solution.py:195
  6.2 13.4 %collective-permute-start.1 = (bf16[256,512]{1,0:T(8,128)(2,1)S(1)}, bf16[256,512]{1,0:T(8,128)(2,1)S(1)}, u32[]{:S(2)}, u32[]{:S(2)}) collective-permute-start(bf16[256,512]{1,0:T(8,128)(2,1)S(1)} %get-tuple-element.29), channel_id=1, source_target_pairs={{0,2},{1,3},{2,0},{3,1},{4,6},{5,7},{6,4},{7,5},{8,10},{9,11},{10,... | collective-permute-start | bytes 786440 | tf_op jit(solution)/shard_map/ppermute | solution.py:195
  7.7 11.9 %collective-permute-start.2 = (bf16[256,512]{1,0:T(8,128)(2,1)S(1)}, bf16[256,512]{1,0:T(8,128)(2,1)S(1)}, u32[]{:S(2)}, u32[]{:S(2)}) collective-permute-start(bf16[256,512]{1,0:T(8,128)(2,1)S(1)} %get-tuple-element.30), channel_id=1, source_target_pairs={{0,3},{1,2},{2,1},{3,0},{4,7},{5,6},{6,5},{7,4},{8,11},{9,10},{10,... | collective-permute-start | bytes 786440 | tf_op jit(solution)/shard_map/ppermute | solution.py:195
  20.1 16.6 %collective-permute-start.12 = (bf16[512,512]{1,0:T(8,128)(2,1)S(1)}, bf16[512,512]{1,0:T(8,128)(2,1)S(1)}, u32[]{:S(2)}, u32[]{:S(2)}) collective-permute-start(bf16[512,512]{1,0:T(8,128)(2,1)S(1)} %get-tuple-element.45), channel_id=1, source_target_pairs={{0,4},{1,5},{2,6},{3,7},{12,8},{13,9},{14,10},{15,11},{16,20},{17,... | collective-permute-start | bytes 1572872 | tf_op jit(solution)/shard_map/ppermute | solution.py:192
  23.7 6.4 %collective-permute-start.7 = (bf16[128,512]{1,0:T(8,128)(2,1)S(1)}, bf16[128,512]{1,0:T(8,128)(2,1)S(1)}, u32[]{:S(2)}, u32[]{:S(2)}) collective-permute-start(bf16[128,512]{1,0:T(8,128)(2,1)S(1)} %get-tuple-element.39), channel_id=1, source_target_pairs={{0,1},{1,0},{2,3},{3,2},{4,5},{5,4},{6,7},{7,6},{8,9},{9,8},{10,11... | collective-permute-start | bytes 393224 | tf_op jit(solution)/shard_map/ppermute | solution.py:195
  25.0 7.0 %collective-permute-start.8 = (bf16[128,512]{1,0:T(8,128)(2,1)S(1)}, bf16[128,512]{1,0:T(8,128)(2,1)S(1)}, u32[]{:S(2)}, u32[]{:S(2)}) collective-permute-start(bf16[128,512]{1,0:T(8,128)(2,1)S(1)} %get-tuple-element.40), channel_id=1, source_target_pairs={{0,2},{1,3},{2,0},{3,1},{4,6},{5,7},{6,4},{7,5},{8,10},{9,11},{10,... | collective-permute-start | bytes 393224 | tf_op jit(solution)/shard_map/ppermute | solution.py:195
  25.8 8.5 %collective-permute-start.9 = (bf16[128,512]{1,0:T(8,128)(2,1)S(1)}, bf16[128,512]{1,0:T(8,128)(2,1)S(1)}, u32[]{:S(2)}, u32[]{:S(2)}) collective-permute-start(bf16[128,512]{1,0:T(8,128)(2,1)S(1)} %get-tuple-element.41), channel_id=1, source_target_pairs={{0,3},{1,2},{2,1},{3,0},{4,7},{5,6},{6,5},{7,4},{8,11},{9,10},{10,... | collective-permute-start | bytes 393224 | tf_op jit(solution)/shard_map/ppermute | solution.py:195
  27.3 11.2 %collective-permute-start.3 = (bf16[256,512]{1,0:T(8,128)(2,1)S(1)}, bf16[256,512]{1,0:T(8,128)(2,1)S(1)}, u32[]{:S(2)}, u32[]{:S(2)}) collective-permute-start(bf16[256,512]{1,0:T(8,128)(2,1)S(1)} %get-tuple-element.32), channel_id=1, source_target_pairs={{0,1},{1,0},{2,3},{3,2},{4,5},{5,4},{6,7},{7,6},{8,9},{9,8},{10,11... | collective-permute-start | bytes 786440 | tf_op jit(solution)/shard_map/ppermute | solution.py:195
  30.1 12.7 %collective-permute-start.4 = (bf16[256,512]{1,0:T(8,128)(2,1)S(1)}, bf16[256,512]{1,0:T(8,128)(2,1)S(1)}, u32[]{:S(2)}, u32[]{:S(2)}) collective-permute-start(bf16[256,512]{1,0:T(8,128)(2,1)S(1)} %get-tuple-element.33), channel_id=1, source_target_pairs={{0,2},{1,3},{2,0},{3,1},{4,6},{5,7},{6,4},{7,5},{8,10},{9,11},{10,... | collective-permute-start | bytes 786440 | tf_op jit(solution)/shard_map/ppermute | solution.py:195
  32.0 10.8 %collective-permute-start.5 = (bf16[256,512]{1,0:T(8,128)(2,1)S(1)}, bf16[256,512]{1,0:T(8,128)(2,1)S(1)}, u32[]{:S(2)}, u32[]{:S(2)}) collective-permute-start(bf16[256,512]{1,0:T(8,128)(2,1)S(1)} %get-tuple-element.34), channel_id=1, source_target_pairs={{0,3},{1,2},{2,1},{3,0},{4,7},{5,6},{6,5},{7,4},{8,11},{9,10},{10,... | collective-permute-start | bytes 786440 | tf_op jit(solution)/shard_map/ppermute | solution.py:195
  34.8 12.0 %collective-permute-start.10 = (bf16[512,512]{1,0:T(8,128)(2,1)S(1)}, bf16[512,512]{1,0:T(8,128)(2,1)S(1)}, u32[]{:S(2)}, u32[]{:S(2)}) collective-permute-start(bf16[512,512]{1,0:T(8,128)(2,1)S(1)} %get-tuple-element.43), channel_id=1, source_target_pairs={{0,4},{1,5},{2,6},{3,7},{12,8},{13,9},{14,10},{15,11},{16,20},{17,... | collective-permute-start | bytes 1572872 | tf_op jit(solution)/shard_map/ppermute | solution.py:192
  36.9 10.9 %collective-permute-start.13 = (bf16[512,512]{1,0:T(8,128)(2,1)S(1)}, bf16[512,512]{1,0:T(8,128)(2,1)S(1)}, u32[]{:S(2)}, u32[]{:S(2)}) collective-permute-start(bf16[512,512]{1,0:T(8,128)(2,1)S(1)} %add_convert_fusion.1), channel_id=1, source_target_pairs={{4,8},{5,9},{6,10},{7,11},{8,4},{9,5},{10,6},{11,7},{20,24},{21,25... | collective-permute-start | bytes 1572872 | tf_op jit(solution)/shard_map/ppermute | solution.py:192
  43.6 12.5 %collective-permute-start.6 = (bf16[512,512]{1,0:T(8,128)(2,1)S(1)}, bf16[512,512]{1,0:T(8,128)(2,1)S(1)}, u32[]{:S(2)}, u32[]{:S(2)}) collective-permute-start(bf16[512,512]{1,0:T(8,128)(2,1)S(1)} %get-tuple-element.37), channel_id=1, source_target_pairs={{0,4},{1,5},{2,6},{3,7},{12,8},{13,9},{14,10},{15,11},{16,20},{17,... | collective-permute-start | bytes 1572872 | tf_op jit(solution)/shard_map/ppermute | solution.py:192
  46.9 9.2 %collective-permute-start.11 = (bf16[512,512]{1,0:T(8,128)(2,1)S(1)}, bf16[512,512]{1,0:T(8,128)(2,1)S(1)}, u32[]{:S(2)}, u32[]{:S(2)}) collective-permute-start(bf16[512,512]{1,0:T(8,128)(2,1)S(1)} %add_convert_fusion.2), channel_id=1, source_target_pairs={{4,8},{5,9},{6,10},{7,11},{8,4},{9,5},{10,6},{11,7},{20,24},{21,25... | collective-permute-start | bytes 1572872 | tf_op jit(solution)/shard_map/ppermute | solution.py:192
  48.0 13.9 %collective-permute-start.14 = (bf16[512,512]{1,0:T(8,128)(2,1)S(1)}, bf16[512,512]{1,0:T(8,128)(2,1)S(1)}, u32[]{:S(2)}, u32[]{:S(2)}) collective-permute-start(bf16[512,512]{1,0:T(8,128)(2,1)S(1)} %add_convert_fusion), channel_id=1, source_target_pairs={{4,0},{5,1},{6,2},{7,3},{8,12},{9,13},{10,14},{11,15},{20,16},{21,... | collective-permute-start | bytes 1572872 | tf_op jit(solution)/shard_map/ppermute | solution.py:192
  64.6 8.7 %collective-permute-start.16 = (bf16[256,512]{1,0:T(8,128)(2,1)S(1)}, bf16[256,512]{1,0:T(8,128)(2,1)}, u32[]{:S(2)}, u32[]{:S(2)}) collective-permute-start(bf16[256,512]{1,0:T(8,128)(2,1)S(1)} %outer.1), channel_id=1, source_target_pairs={{0,4},{1,5},{2,6},{3,7},{4,0},{5,1},{6,2},{7,3},{8,12},{9,13},{10,... | collective-permute-start | bytes 786440 | tf_op jit(solution)/shard_map/ppermute | solution.py:192
  64.7 9.3 %collective-permute-start.18 = (bf16[256,512]{1,0:T(8,128)(2,1)S(1)}, bf16[256,512]{1,0:T(8,128)(2,1)S(1)}, u32[]{:S(2)}, u32[]{:S(2)}) collective-permute-start(bf16[256,512]{1,0:T(8,128)(2,1)S(1)} %outer.1), channel_id=1, source_target_pairs={{4,8},{5,9},{6,10},{7,11},{8,4},{9,5},{10,6},{11,7},{20,24},{21,25... | collective-permute-start | bytes 786440 | tf_op jit(solution)/shard_map/ppermute | solution.py:192
  74.0 9.9 %collective-permute-start.19 = (bf16[256,512]{1,0:T(8,128)(2,1)S(1)}, bf16[256,512]{1,0:T(8,128)(2,1)}, u32[]{:S(2)}, u32[]{:S(2)}) collective-permute-start(bf16[256,512]{1,0:T(8,128)(2,1)S(1)} %collective-permute-done.18), channel_id=1, source_target_pairs={{4,0},{5,1},{6,2},{7,3},{8,12},{9,13},{10,14},{11,15},{20,16},{21,... | collective-permute-start | bytes 786440 | tf_op jit(solution)/shard_map/ppermute | solution.py:192
  75.4 15.0 %collective-permute-start.22 = (bf16[256,512]{1,0:T(8,128)(2,1)S(1)}, bf16[256,512]{1,0:T(8,128)(2,1)S(1)}, u32[]{:S(2)}, u32[]{:S(2)}) collective-permute-start(bf16[256,512]{1,0:T(8,128)(2,1)S(1)} %collective-permute-done.21), channel_id=1, source_target_pairs={{4,0},{5,1},{6,2},{7,3},{8,12},{9,13},{10,14},{11,15},{20,16},{21,... | collective-permute-start | bytes 786440 | tf_op jit(solution)/shard_map/ppermute | solution.py:192
  77.7 12.8 %collective-permute-start.17 = (bf16[2,256,512]{2,1,0:T(8,128)(2,1)S(1)}, bf16[2,256,512]{2,1,0:T(8,128)(2,1)S(1)}, u32[]{:S(2)}, u32[]{:S(2)}) collective-permute-start(bf16[2,256,512]{2,1,0:T(8,128)(2,1)S(1)} %pad_maximum_fusion.refs_12_), channel_id=1, source_target_pairs={{0,16},{16,0},{1,17},{17,1},{2,18},{18,2},{3,19},{19,3},{4,20},{20... | collective-permute-start | bytes 1572872 | tf_op jit(solution)/shard_map/ppermute | solution.py:198
  84.9 5.5 %collective-permute-start.20 = (bf16[256,512]{1,0:T(8,128)(2,1)S(1)}, bf16[256,512]{1,0:T(8,128)(2,1)S(1)}, u32[]{:S(2)}, u32[]{:S(2)}) collective-permute-start(bf16[256,512]{1,0:T(8,128)(2,1)S(1)} %broadcast_select_fusion.1.refs_14_), channel_id=1, source_target_pairs={{0,16},{16,0},{1,17},{17,1},{2,18},{18,2},{3,19},{19,3},{4,20},{20... | collective-permute-start | bytes 786440 | tf_op jit(solution)/shard_map/ppermute | solution.py:198
  93.5 6.9 %collective-permute-start.26 = (bf16[128,512]{1,0:T(8,128)(2,1)S(1)}, bf16[128,512]{1,0:T(8,128)(2,1)S(1)}, u32[]{:S(2)}, u32[]{:S(2)}) collective-permute-start(bf16[128,512]{1,0:T(8,128)(2,1)S(1)} %get-tuple-element.51), channel_id=1, source_target_pairs={{0,3},{1,2},{2,1},{3,0},{4,7},{5,6},{6,5},{7,4},{8,11},{9,10},{10,... | collective-permute-start | bytes 393224 | tf_op jit(solution)/shard_map/ppermute | solution.py:195
  94.8 8.0 %collective-permute-start.25 = (bf16[128,512]{1,0:T(8,128)(2,1)S(1)}, bf16[128,512]{1,0:T(8,128)(2,1)S(1)}, u32[]{:S(2)}, u32[]{:S(2)}) collective-permute-start(bf16[128,512]{1,0:T(8,128)(2,1)S(1)} %get-tuple-element.50), channel_id=1, source_target_pairs={{0,2},{1,3},{2,0},{3,1},{4,6},{5,7},{6,4},{7,5},{8,10},{9,11},{10,... | collective-permute-start | bytes 393224 | tf_op jit(solution)/shard_map/ppermute | solution.py:195
  97.6 5.2 %collective-permute-start.24 = (bf16[128,512]{1,0:T(8,128)(2,1)S(1)}, bf16[128,512]{1,0:T(8,128)(2,1)S(1)}, u32[]{:S(2)}, u32[]{:S(2)}) collective-permute-start(bf16[128,512]{1,0:T(8,128)(2,1)S(1)} %get-tuple-element.49), channel_id=1, source_target_pairs={{0,1},{1,0},{2,3},{3,2},{4,5},{5,4},{6,7},{7,6},{8,9},{9,8},{10,11... | collective-permute-start | bytes 393224 | tf_op jit(solution)/shard_map/ppermute | solution.py:195
  (11 other events, 90.7 us)

commit v3 on v2

--- a/solution.py
+++ b/solution.py
@@ -52,39 +52,38 @@
 
 
 def repack_kernel(inner, targets, *refs):
-    acts_ref, cots, outs = refs[0], refs[1 : len(refs) - inner], refs[len(refs) - inner :]
-    tokens, rows = acts_ref.shape[0], outs[0].shape[1]
-    o, i, _ = mirrored()
-    for k in range(inner):
-        x, y = lax.rem(i, 2), i // 2
-        place = (y + k // 2 - 2 * y * (k // 2)) * 2 + x + k % 2 - 2 * x * (k % 2)
+    acts_ref, cots, out = refs[0], refs[1:-1], refs[-1]
+    tokens, rows = acts_ref.shape[0], out.shape[2]
+    o, _, _ = mirrored()
+    for place in range(inner):
         for slot, t in enumerate(targets):
             plane = jnp.where(o < PLANES // 2, t, PLANES - 1 - t)
             start = pl.multiple_of((plane * inner + place) * rows, rows)
-            outs[k][slot * tokens : (slot + 1) * tokens] = acts_ref[:, pl.ds(start, rows)]
+            out[place, slot * tokens : (slot + 1) * tokens] = acts_ref[:, pl.ds(start, rows)]
         for cots_ref in cots:
-            outs[k][len(targets) * tokens :] = cots_ref[...]
+            out[place, len(targets) * tokens :] = cots_ref[...]
 
 
 def repack(inputs, inner, targets, rows):
     tokens = inputs[0].shape[0]
-    out = [jax.ShapeDtypeStruct(((len(targets) + len(inputs) - 1) * tokens, rows), jnp.bfloat16)] * inner
-    return call(partial(repack_kernel, inner, targets), "repack", out, inputs, 0)
-
-
-def partial_kernel(inner, tokens, slots, *refs):
-    firsts, blocks, outs = refs[:inner], refs[inner : 2 * inner], refs[2 * inner :]
-    cots = jnp.concatenate([ref[tokens:] for ref in firsts], axis=0)
+    out = jax.ShapeDtypeStruct((inner, (len(targets) + len(inputs) - 1) * tokens, rows), jnp.bfloat16)
+    return call(partial(repack_kernel, inner, targets), "repack", [out], inputs, 0)[0]
+
+
+def partial_kernel(slots, first, block, *outs):
+    inner, tokens, _ = first.shape
+    tokens = tokens // 2
+    cots = jnp.concatenate([first[k, tokens:] for k in range(inner)], axis=0)
     for slot in range(slots):
-        columns = jnp.concatenate([ref[slot * tokens : (slot + 1) * tokens] for ref in blocks], axis=0)
+        columns = jnp.concatenate([block[k, slot * tokens : (slot + 1) * tokens] for k in range(inner)], axis=0)
         total = lax.dot_general(columns, cots, CONTRACT_ROWS, preferred_element_type=jnp.float32)
         outs[slot][...] = total
         if slot == 0:
             outs[slots][...] = total.astype(jnp.bfloat16)
 
 
-def first_partial_kernel(inner, tokens, *refs):
-    partial_kernel(inner, tokens, 1, *refs[:inner], *refs)
+def first_partial_kernel(first, *outs):
+    partial_kernel(1, first, first, *outs)
 
 
 CHUNK = 32
@@ -138,10 +137,8 @@
     out[...] = outer_update((drift[...] + other[...]) / 2, anchor[at, :], momentum[at, :])
 
 
-def values_kernel(inner, tokens, rows, *refs):
-    firsts, seconds, lasts = refs[:inner], refs[inner : 2 * inner], refs[2 * inner : 3 * inner]
-    mine_ref, other_ref, mine2_ref, other2_ref, mine3_ref, other3_ref = refs[3 * inner : 3 * inner + 6]
-    own_ref, sent_refs, weights = refs[3 * inner + 6], refs[3 * inner + 7 : -1], refs[-1]
+def values_kernel(first, second, last, mine_ref, other_ref, mine2_ref, other2_ref, mine3_ref, other3_ref, out, weights):
+    inner, tokens, rows = second.shape
     half = rows // 2
     r = lax.axis_index("rep")
     _, _, near = mirrored()
@@ -157,12 +154,9 @@
     put(3, r, mine3_ref[...])
     put(3, 1 - r, other3_ref[...])
     for k in range(inner):
-        blocks = (lasts[k][tokens:], lasts[k][:tokens], seconds[k][...], firsts[k][:tokens])
+        blocks = (last[k, tokens:], last[k, :tokens], second[k], first[k, :tokens])
         total = jnp.dot(jnp.concatenate(blocks, axis=1), weights[...], preferred_element_type=jnp.float32)
-        if k == 0:
-            own_ref[...] = total
-        else:
-            sent_refs[k - 1][...] = total.astype(jnp.bfloat16)
+        out[k] = total.astype(jnp.bfloat16)
 
 
 def call(kernel, name, out, inputs, flops, scratch=()):
@@ -191,8 +185,9 @@
     def line(x, *pairs):
         return lax.ppermute(x, "fsdp", [(a * inner + i, b * inner + i) for a, b in pairs for i in range(inner)])
 
-    def across(x, k):
-        return lax.ppermute(x, "fsdp", [(p * inner + i, p * inner + (i ^ k)) for p in range(PLANES) for i in range(inner)])
+    def around(x):
+        groups = [[p * inner + i for i in range(inner)] for p in range(PLANES)]
+        return lax.all_to_all(x, "fsdp", split_axis=0, concat_axis=0, axis_index_groups=groups)
 
     def swap(x):
         return lax.ppermute(x, "rep", [(0, 1), (1, 0)])
@@ -206,21 +201,16 @@
     def outward(x):
         return line(x, (1, 0), (2, 3))
 
-    def around(blocks):
-        return [blocks[0]] + [across(blocks[k], k) for k in range(1, inner)]
-
-    firsts = around(repack([acts[0], value_cots[0]], inner, (3,), rows))
-    seconds = around(repack([acts[0]], inner, (2,), rows))
-    lasts = around(repack([acts[0]], inner, (1, 0), rows))
+    first = around(repack([acts[0], value_cots[0]], inner, (3,), rows))
+    second = around(repack([acts[0]], inner, (2,), rows))
+    last = around(repack([acts[0]], inner, (1, 0), rows))
 
     f32 = jax.ShapeDtypeStruct((rows, width), jnp.float32)
     bf16 = jax.ShapeDtypeStruct((rows, width), jnp.bfloat16)
     flops = 2 * inner * tokens * rows * width
-    total3, sent3 = call(partial(first_partial_kernel, inner, tokens), "partial_first", [f32, bf16], firsts, flops)
-    total2, sent2 = call(partial(partial_kernel, inner, tokens, 1), "partial_second", [f32, bf16], firsts + seconds, flops)
-    total1, total0, sent1 = call(
-        partial(partial_kernel, inner, tokens, 2), "partial_last", [f32, f32, bf16], firsts + lasts, 2 * flops
-    )
+    total3, sent3 = call(first_partial_kernel, "partial_first", [f32, bf16], [first], flops)
+    total2, sent2 = call(partial(partial_kernel, 1), "partial_second", [f32, bf16], [first, second], flops)
+    total1, total0, sent1 = call(partial(partial_kernel, 2), "partial_last", [f32, f32, bf16], [first, last], 2 * flops)
     a1 = inward(sent3)
     a2 = inward(sent2)
     a3 = inward(sent1)
@@ -250,17 +240,15 @@
     mine3 = jnp.where(at_end, outward(far3), far3)
     mine = jnp.stack([mine, beside])
     pieces = [mine, swap(mine), mine2, swap(mine2), mine3, swap(mine3)]
-    block = jax.ShapeDtypeStruct((tokens, width), jnp.bfloat16)
-    values, *sent = call(
-        partial(values_kernel, inner, tokens, rows),
+    (sent,) = call(
+        values_kernel,
         "values",
-        [jax.ShapeDtypeStruct((tokens, width), jnp.float32)] + [block] * (inner - 1),
-        firsts + seconds + lasts + pieces,
+        [jax.ShapeDtypeStruct((inner, tokens, width), jnp.bfloat16)],
+        [first, second, last] + pieces,
         4 * flops,
         [pltpu.VMEM((PLANES * rows, width), jnp.bfloat16)],
     )
-    for k in range(1, inner):
-        values = values + across(sent[k - 1], k).astype(jnp.float32)
+    values = jnp.sum(around(sent).astype(jnp.float32), axis=0)
     return (first_next[None], values.astype(jnp.bfloat16)[None])
 
 

time: 104 us -> 121 us (1.16)
  blocking collectives: 0 us -> 12.2 us
  waiting for transfers between devices: 59.3 us -> 52.7 us
  local copies, waits for them, and re-layouts: 2.51 us -> 6.21 us
  Pallas kernels: 5.92 us -> 9.57 us
  other arithmetic: 3.21 us -> 5.72 us
    ppermute x12 -> x0, waiting for transfers between devices: 24.1 us -> none  [across(): lax.ppermute(x, 'fsdp', [(p * inner + i, p * inner + (i ^ k)) for p in ra...]
    ppermute x12 -> x0, starting transfers between devices: 17.4 us -> none  [across(): lax.ppermute(x, 'fsdp', [(p * inner + i, p * inner + (i ^ k)) for p in ra...]
    all_to_all x0 -> x3, waiting for transfers between devices: none -> 15.4 us  [around(): lax.all_to_all(x, 'fsdp', split_axis=0, concat_axis=0, axis_index_groups=...]
    all_to_all x0 -> x3, starting transfers between devices: none -> 13.5 us  [around(): lax.all_to_all(x, 'fsdp', split_axis=0, concat_axis=0, axis_index_groups=...]
    all_to_all x0 -> x1, blocking collectives: none -> 12.2 us  [around(): lax.all_to_all(x, 'fsdp', split_axis=0, concat_axis=0, axis_index_groups=...]
    ppermute x11, starting transfers between devices: 13.9 us -> 19.1 us  [line(): lax.ppermute(x, 'fsdp', [(a * inner + i, b * inner + i) for a, b in pairs...]
    convert_element_type x3, other arithmetic: 0.48 us -> 4.87 us  [add(): return (total + got.astype(jnp.float32)).astype(jnp.bfloat16)]
    unnamed x16 -> x24, local copies, waits for them, and re-layouts: 2.51 us -> 6.21 us
  transfers between devices with their start and end apart: 27 -> 18, of which waited for: 16 -> 10; matrix products, arithmetic and copies ran while one was open for 2% -> 4% of each run, Pallas kernels for 3% -> 5%
where the time goes in v3:
time: 121 us; the launch traced here: 120 us
  waiting for transfers between devices  52.7 us (44%)
  starting transfers between devices  32.8 us (27%)
  blocking collectives  12.2 us (10%)
  Pallas kernels  9.57 us (8%)
  local copies, waits for them, and re-layouts  6.21 us (5%)
  other arithmetic  5.72 us (5%)
    ppermute x11, waiting for transfers between devices, line(): lax.ppermute(x, 'fsdp', [(a * inner + i, b * inner + i) for a, b in pairs...  35.7 us
    ppermute x11, starting transfers between devices, line(): lax.ppermute(x, 'fsdp', [(a * inner + i, b * inner + i) for a, b in pairs...  19.1 us
    all_to_all x3, waiting for transfers between devices, around(): lax.all_to_all(x, 'fsdp', split_axis=0, concat_axis=0, axis_index_groups=...  15.4 us
    all_to_all x3, starting transfers between devices, around(): lax.all_to_all(x, 'fsdp', split_axis=0, concat_axis=0, axis_index_groups=...  13.5 us
    all_to_all x1, blocking collectives, around(): lax.all_to_all(x, 'fsdp', split_axis=0, concat_axis=0, axis_index_groups=...  12.2 us
    pallas_call x10, Pallas kernels, call(): pl.pallas_call(kernel, out_shape=out, in_specs=[pl.BlockSpec(memory_space...  9.57 us
    unnamed x24, local copies, waits for them, and re-layouts  6.21 us
    convert_element_type x3, other arithmetic, add(): return (total + got.astype(jnp.float32)).astype(jnp.bfloat16)  4.87 us
  transfers between devices with their start and end apart: 18, of which 10 were waited for; matrix products, arithmetic and copies ran while one was open for 4% of the time, Pallas kernels for 5%

profile of v3, /device:TPU:0, one launch (start us, length us, event | category | flops | bytes accessed | tf_op | source)
XLA Modules:
  0.0 120.2 jit_solution(499610357927852791)
XLA Ops:
  0.6 1.6 %copy-done = bf16[1,128,8192]{2,1,0:T(8,128)(2,1)S(1)} copy-done((bf16[1,128,8192]{2,1,0:T(8,128)(2,1)S(1)}, bf16[1,128,8192]{2,1,0:T(8,128)(2,1)}, u32[]{:S(2)}) %copy-start) | copy-done | bytes 2097176
  4.2 5.2 %all-to-all-start = ((bf16[4,256,512]{2,1,0:T(8,128)(2,1)}), bf16[4,256,512]{2,1,0:T(8,128)(2,1)S(1)}, u32[]{:S(2)}, u32[]{:S(2)}) async-start(bf16[4,256,512]{2,1,0:T(8,128)(2,1)} %copy-done.4), calls=%async_computation | async-start | bytes 2097152 | tf_op jit(solution)/shard_map/all_to_all | solution.py:190
  10.2 12.8 %all-to-all-done.first = bf16[4,256,512]{2,1,0:T(8,128)(2,1)S(1)} async-done(((bf16[4,256,512]{2,1,0:T(8,128)(2,1)}), bf16[4,256,512]{2,1,0:T(8,128)(2,1)S(1)}, u32[]{:S(2)}, u32[]{:S(2)}) %all-to-all-start) | async-done | bytes 1048608 | tf_op jit(solution)/shard_map/all_to_all | solution.py:190
  23.0 4.1 %all-to-all-start.2 = ((bf16[4,128,512]{2,1,0:T(8,128)(2,1)}), bf16[4,128,512]{2,1,0:T(8,128)(2,1)}, u32[]{:S(2)}, u32[]{:S(2)}) async-start(bf16[4,128,512]{2,1,0:T(8,128)(2,1)} %copy-done.8), calls=%async_computation.2 | async-start | bytes 1048576 | tf_op jit(solution)/shard_map/all_to_all | solution.py:190
  29.4 4.3 %collective-permute-start.3 = (bf16[512,512]{1,0:T(8,128)(2,1)}, bf16[512,512]{1,0:T(8,128)(2,1)}, u32[]{:S(2)}, u32[]{:S(2)}) collective-permute-start(bf16[512,512]{1,0:T(8,128)(2,1)} %get-tuple-element.17), channel_id=1, source_target_pairs={{0,4},{1,5},{2,6},{3,7},{12,8},{13,9},{14,10},{15,11},{16,20},{17,... | collective-permute-start | bytes 1572872 | tf_op jit(solution)/shard_map/ppermute | solution.py:186
  34.8 4.1 %all-to-all-start.1 = ((bf16[4,256,512]{2,1,0:T(8,128)(2,1)}), bf16[4,256,512]{2,1,0:T(8,128)(2,1)S(1)}, u32[]{:S(2)}, u32[]{:S(2)}) async-start(bf16[4,256,512]{2,1,0:T(8,128)(2,1)} %copy-done.3), calls=%async_computation.1 | async-start | bytes 2097152 | tf_op jit(solution)/shard_map/all_to_all | solution.py:190
  38.9 2.3 %partial_second.1 = (f32[512,512]{1,0:T(8,128)S(1)}, bf16[512,512]{1,0:T(8,128)(2,1)}) custom-call(bf16[4,256,512]{2,1,0:T(8,128)(2,1)S(1)} %all-to-all-done.first, bf16[4,128,512]{2,1,0:T(8,128)(2,1)} %all-to-all-done.2.block.second), custom_call_target="tpu_custom_call" | custom-call | flops 268435456 | bytes 3145728 | tf_op jit(solution)/shard_map/partial_second/pallas_call | solution.py:164
  41.2 3.6 %collective-permute-start.1 = (bf16[512,512]{1,0:T(8,128)(2,1)}, bf16[512,512]{1,0:T(8,128)(2,1)}, u32[]{:S(2)}, u32[]{:S(2)}) collective-permute-start(bf16[512,512]{1,0:T(8,128)(2,1)} %get-tuple-element.15), channel_id=1, source_target_pairs={{0,4},{1,5},{2,6},{3,7},{12,8},{13,9},{14,10},{15,11},{16,20},{17,... | collective-permute-start | bytes 1572872 | tf_op jit(solution)/shard_map/ppermute | solution.py:186
  44.8 2.3 %add_convert_fusion.1 = bf16[512,512]{1,0:T(8,128)(2,1)} fusion(f32[512,512]{1,0:T(8,128)} %copy-done.10, bf16[512,512]{1,0:T(8,128)(2,1)} %collective-permute-done.3), kind=kLoop, calls=%fused_computation.1 | loop fusion | flops 786432 | bytes 2097152 | tf_op jit(solution)/shard_map/convert_element_type | solution.py:219
  47.1 1.4 %collective-permute-start.4 = (bf16[512,512]{1,0:T(8,128)(2,1)}, bf16[512,512]{1,0:T(8,128)(2,1)}, u32[]{:S(2)}, u32[]{:S(2)}) collective-permute-start(bf16[512,512]{1,0:T(8,128)(2,1)} %add_convert_fusion.1), channel_id=1, source_target_pairs={{4,8},{5,9},{6,10},{7,11},{8,4},{9,5},{10,6},{11,7},{20,24},{21,25... | collective-permute-start | bytes 1572872 | tf_op jit(solution)/shard_map/ppermute | solution.py:186
  48.6 2.6 %all-to-all-done.1.block.last = bf16[4,256,512]{2,1,0:T(8,128)(2,1)S(1)} async-done(((bf16[4,256,512]{2,1,0:T(8,128)(2,1)}), bf16[4,256,512]{2,1,0:T(8,128)(2,1)S(1)}, u32[]{:S(2)}, u32[]{:S(2)}) %all-to-all-start.1) | async-done | bytes 1048608 | tf_op jit(solution)/shard_map/all_to_all | solution.py:190
  51.9 3.6 %collective-permute-start = (bf16[512,512]{1,0:T(8,128)(2,1)S(1)}, bf16[512,512]{1,0:T(8,128)(2,1)S(1)}, u32[]{:S(2)}, u32[]{:S(2)}) collective-permute-start(bf16[512,512]{1,0:T(8,128)(2,1)S(1)} %get-tuple-element.13), channel_id=1, source_target_pairs={{0,4},{1,5},{2,6},{3,7},{12,8},{13,9},{14,10},{15,11},{16,20},{17,... | collective-permute-start | bytes 1572872 | tf_op jit(solution)/shard_map/ppermute | solution.py:186
  55.6 1.4 %add_convert_fusion.2 = bf16[512,512]{1,0:T(8,128)(2,1)S(1)} fusion(f32[512,512]{1,0:T(8,128)S(1)} %get-tuple-element.14, bf16[512,512]{1,0:T(8,128)(2,1)} %collective-permute-done.1), kind=kLoop, calls=%fused_computation.2 | loop fusion | flops 786432 | bytes 2097152 | tf_op jit(solution)/shard_map/convert_element_type | solution.py:219
  59.0 1.3 %collective-permute-start.5 = (bf16[512,512]{1,0:T(8,128)(2,1)S(1)}, bf16[512,512]{1,0:T(8,128)(2,1)S(1)}, u32[]{:S(2)}, u32[]{:S(2)}) collective-permute-start(bf16[512,512]{1,0:T(8,128)(2,1)S(1)} %add_convert_fusion), channel_id=1, source_target_pairs={{4,0},{5,1},{6,2},{7,3},{8,12},{9,13},{10,14},{11,15},{20,16},{21,... | collective-permute-start | bytes 1572872 | tf_op jit(solution)/shard_map/ppermute | solution.py:186
  60.3 5.6 %collective-permute-done.refs_2_ = bf16[512,512]{1,0:T(8,128)(2,1)S(1)} collective-permute-done((bf16[512,512]{1,0:T(8,128)(2,1)S(1)}, bf16[512,512]{1,0:T(8,128)(2,1)S(1)}, u32[]{:S(2)}, u32[]{:S(2)}) %collective-permute-start) | collective-permute-done | bytes 524320 | tf_op jit(solution)/shard_map/ppermute | solution.py:186
  65.9 8.9 %collective-permute-done.5.refs_4_ = bf16[512,512]{1,0:T(8,128)(2,1)S(1)} collective-permute-done((bf16[512,512]{1,0:T(8,128)(2,1)S(1)}, bf16[512,512]{1,0:T(8,128)(2,1)S(1)}, u32[]{:S(2)}, u32[]{:S(2)}) %collective-permute-start.5) | collective-permute-done | bytes 524320 | tf_op jit(solution)/shard_map/ppermute | solution.py:186
  75.5 1.8 %update.1 = (f32[512,512]{1,0:T(8,128)}, f32[256,512]{1,0:T(8,128)S(1)}) custom-call(f32[512,512]{1,0:T(8,128)S(1)} %get-tuple-element.11.refs_0_, f32[512,512]{1,0:T(8,128)S(1)} %get-tuple-element.12.refs_1_, bf16[512,512]{1,0:T(8,128)(2,1)S(1)} %collective-permute-done.refs_2_, bf16[512,512]{1,0:T(8,128)(2,1)S(1)} %collective-permute-done.2.refs_3_, ...), custom_call_target="tpu_custom_call" | custom-call | bytes 9437184 | tf_op jit(solution)/shard_map/update/pallas_call | solution.py:164
  78.4 7.9 %collective-permute-done.7 = bf16[256,512]{1,0:T(8,128)(2,1)S(1)} collective-permute-done((bf16[256,512]{1,0:T(8,128)(2,1)S(1)}, bf16[256,512]{1,0:T(8,128)(2,1)S(1)}, u32[]{:S(2)}, u32[]{:S(2)}) %collective-permute-start.7) | collective-permute-done | bytes 262176 | tf_op jit(solution)/shard_map/ppermute | solution.py:186
  86.9 1.3 %collective-permute-start.10 = (bf16[256,512]{1,0:T(8,128)(2,1)S(1)}, bf16[256,512]{1,0:T(8,128)(2,1)S(1)}, u32[]{:S(2)}, u32[]{:S(2)}) collective-permute-start(bf16[256,512]{1,0:T(8,128)(2,1)S(1)} %collective-permute-done.9), channel_id=1, source_target_pairs={{4,0},{5,1},{6,2},{7,3},{8,12},{9,13},{10,14},{11,15},{20,16},{21,... | collective-permute-start | bytes 786440 | tf_op jit(solution)/shard_map/ppermute | solution.py:186
  89.7 7.1 %collective-permute-done.10 = bf16[256,512]{1,0:T(8,128)(2,1)S(1)} collective-permute-done((bf16[256,512]{1,0:T(8,128)(2,1)S(1)}, bf16[256,512]{1,0:T(8,128)(2,1)S(1)}, u32[]{:S(2)}, u32[]{:S(2)}) %collective-permute-start.10) | collective-permute-done | bytes 262176 | tf_op jit(solution)/shard_map/ppermute | solution.py:186
  96.9 6.1 %collective-permute-done.13 = bf16[256,512]{1,0:T(8,128)(2,1)S(1)} collective-permute-done((bf16[256,512]{1,0:T(8,128)(2,1)S(1)}, bf16[256,512]{1,0:T(8,128)(2,1)S(1)}, u32[]{:S(2)}, u32[]{:S(2)}) %collective-permute-start.13) | collective-permute-done | bytes 262176 | tf_op jit(solution)/shard_map/ppermute | solution.py:186
  103.1 1.5 %collective-permute-done.14.other3_ref = bf16[256,512]{1,0:T(8,128)(2,1)S(1)} collective-permute-done((bf16[256,512]{1,0:T(8,128)(2,1)S(1)}, bf16[256,512]{1,0:T(8,128)(2,1)S(1)}, u32[]{:S(2)}, u32[]{:S(2)}) %collective-permute-start.14) | collective-permute-done | bytes 262176 | tf_op jit(solution)/shard_map/ppermute | solution.py:193
  104.6 2.5 %values.1 = bf16[4,128,512]{2,1,0:T(8,128)(2,1)S(1)} custom-call(bf16[4,256,512]{2,1,0:T(8,128)(2,1)S(1)} %all-to-all-done.first, bf16[4,128,512]{2,1,0:T(8,128)(2,1)} %all-to-all-done.2.block.second, bf16[4,256,512]{2,1,0:T(8,128)(2,1)S(1)} %all-to-all-done.1.block.last, bf16[2,256,512]{2,1,0:T(8,128)(2,1)S(1)} %pad_maximum_fusion.mine_ref, ...), custom_call_target="tpu_custom_call" | custom-call | flops 1073741824 | bytes 5242880 | tf_op jit(solution)/shard_map/values/pallas_call | solution.py:164
  107.2 12.2 %all_to_all.20 = bf16[4,128,512]{2,1,0:T(8,128)(2,1)S(1)} all-to-all(bf16[4,128,512]{2,1,0:T(8,128)(2,1)S(1)} %values.1), channel_id=1, replica_groups={{0,1,2,3},{4,5,6,7},{8,9,10,11},{12,13,14,15},{16,17,18,19},{20,21,22,2..., dimensions={0} | all-to-all | bytes 1048576 | tf_op jit(solution)/shard_map/all_to_all | solution.py:190
  (54 shorter events, 13.7 us)
Async XLA Ops:
  3.1 6.2 %copy-start.1 = (bf16[1,128,8192]{2,1,0:T(8,128)(2,1)S(1)}, bf16[1,128,8192]{2,1,0:T(8,128)(2,1)}, u32[]{:S(2)}) copy-start(bf16[1,128,8192]{2,1,0:T(8,128)(2,1)} %param.7) | copy-start | bytes 6291460
  4.2 18.8 %all-to-all-start = ((bf16[4,256,512]{2,1,0:T(8,128)(2,1)}), bf16[4,256,512]{2,1,0:T(8,128)(2,1)S(1)}, u32[]{:S(2)}, u32[]{:S(2)}) async-start(bf16[4,256,512]{2,1,0:T(8,128)(2,1)} %copy-done.4), calls=%async_computation | async-start | bytes 2097152 | tf_op jit(solution)/shard_map/all_to_all | solution.py:190
  23.0 11.8 %all-to-all-start.2 = ((bf16[4,128,512]{2,1,0:T(8,128)(2,1)}), bf16[4,128,512]{2,1,0:T(8,128)(2,1)}, u32[]{:S(2)}, u32[]{:S(2)}) async-start(bf16[4,128,512]{2,1,0:T(8,128)(2,1)} %copy-done.8), calls=%async_computation.2 | async-start | bytes 1048576 | tf_op jit(solution)/shard_map/all_to_all | solution.py:190
  29.4 15.4 %collective-permute-start.3 = (bf16[512,512]{1,0:T(8,128)(2,1)}, bf16[512,512]{1,0:T(8,128)(2,1)}, u32[]{:S(2)}, u32[]{:S(2)}) collective-permute-start(bf16[512,512]{1,0:T(8,128)(2,1)} %get-tuple-element.17), channel_id=1, source_target_pairs={{0,4},{1,5},{2,6},{3,7},{12,8},{13,9},{14,10},{15,11},{16,20},{17,... | collective-permute-start | bytes 1572872 | tf_op jit(solution)/shard_map/ppermute | solution.py:186
  34.8 16.4 %all-to-all-start.1 = ((bf16[4,256,512]{2,1,0:T(8,128)(2,1)}), bf16[4,256,512]{2,1,0:T(8,128)(2,1)S(1)}, u32[]{:S(2)}, u32[]{:S(2)}) async-start(bf16[4,256,512]{2,1,0:T(8,128)(2,1)} %copy-done.3), calls=%async_computation.1 | async-start | bytes 2097152 | tf_op jit(solution)/shard_map/all_to_all | solution.py:190
  41.2 14.4 %collective-permute-start.1 = (bf16[512,512]{1,0:T(8,128)(2,1)}, bf16[512,512]{1,0:T(8,128)(2,1)}, u32[]{:S(2)}, u32[]{:S(2)}) collective-permute-start(bf16[512,512]{1,0:T(8,128)(2,1)} %get-tuple-element.15), channel_id=1, source_target_pairs={{0,4},{1,5},{2,6},{3,7},{12,8},{13,9},{14,10},{15,11},{16,20},{17,... | collective-permute-start | bytes 1572872 | tf_op jit(solution)/shard_map/ppermute | solution.py:186
  47.1 10.6 %collective-permute-start.4 = (bf16[512,512]{1,0:T(8,128)(2,1)}, bf16[512,512]{1,0:T(8,128)(2,1)}, u32[]{:S(2)}, u32[]{:S(2)}) collective-permute-start(bf16[512,512]{1,0:T(8,128)(2,1)} %add_convert_fusion.1), channel_id=1, source_target_pairs={{4,8},{5,9},{6,10},{7,11},{8,4},{9,5},{10,6},{11,7},{20,24},{21,25... | collective-permute-start | bytes 1572872 | tf_op jit(solution)/shard_map/ppermute | solution.py:186
  51.9 14.0 %collective-permute-start = (bf16[512,512]{1,0:T(8,128)(2,1)S(1)}, bf16[512,512]{1,0:T(8,128)(2,1)S(1)}, u32[]{:S(2)}, u32[]{:S(2)}) collective-permute-start(bf16[512,512]{1,0:T(8,128)(2,1)S(1)} %get-tuple-element.13), channel_id=1, source_target_pairs={{0,4},{1,5},{2,6},{3,7},{12,8},{13,9},{14,10},{15,11},{16,20},{17,... | collective-permute-start | bytes 1572872 | tf_op jit(solution)/shard_map/ppermute | solution.py:186
  55.6 19.2 %copy-start.2 = (f32[512,512]{1,0:T(8,128)S(1)}, f32[512,512]{1,0:T(8,128)}, u32[]{:S(2)}) copy-start(f32[512,512]{1,0:T(8,128)} %anchor.1) | copy-start | bytes 3145732
  55.6 19.2 %copy-start.5 = (f32[1,512,512]{2,1,0:T(8,128)S(1)}, f32[1,512,512]{2,1,0:T(8,128)}, u32[]{:S(2)}) copy-start(f32[1,512,512]{2,1,0:T(8,128)} %param.9) | copy-start | bytes 3145732
  55.6 19.2 %copy-start.6 = (f32[1,512,512]{2,1,0:T(8,128)S(1)}, f32[1,512,512]{2,1,0:T(8,128)}, u32[]{:S(2)}) copy-start(f32[1,512,512]{2,1,0:T(8,128)} %param.10) | copy-start | bytes 3145732
  55.6 19.2 %copy-start.7 = (f32[1,512,512]{2,1,0:T(8,128)S(1)}, f32[1,512,512]{2,1,0:T(8,128)}, u32[]{:S(2)}) copy-start(f32[1,512,512]{2,1,0:T(8,128)} %param.11) | copy-start | bytes 3145732
  56.9 9.0 %collective-permute-start.2 = (bf16[512,512]{1,0:T(8,128)(2,1)S(1)}, bf16[512,512]{1,0:T(8,128)(2,1)S(1)}, u32[]{:S(2)}, u32[]{:S(2)}) collective-permute-start(bf16[512,512]{1,0:T(8,128)(2,1)S(1)} %add_convert_fusion.2), channel_id=1, source_target_pairs={{4,8},{5,9},{6,10},{7,11},{8,4},{9,5},{10,6},{11,7},{20,24},{21,25... | collective-permute-start | bytes 1572872 | tf_op jit(solution)/shard_map/ppermute | solution.py:186
  59.0 15.8 %collective-permute-start.5 = (bf16[512,512]{1,0:T(8,128)(2,1)S(1)}, bf16[512,512]{1,0:T(8,128)(2,1)S(1)}, u32[]{:S(2)}, u32[]{:S(2)}) collective-permute-start(bf16[512,512]{1,0:T(8,128)(2,1)S(1)} %add_convert_fusion), channel_id=1, source_target_pairs={{4,0},{5,1},{6,2},{7,3},{8,12},{9,13},{10,14},{11,15},{20,16},{21,... | collective-permute-start | bytes 1572872 | tf_op jit(solution)/shard_map/ppermute | solution.py:186
  75.4 2.0 %copy-start.9 = (f32[512,512]{1,0:T(8,128)S(1)}, f32[512,512]{1,0:T(8,128)}, u32[]{:S(2)}) copy-start(f32[512,512]{1,0:T(8,128)} %momentum.1) | copy-start | bytes 3145732
  75.5 2.0 %collective-permute-start.6 = (f32[256,512]{1,0:T(8,128)S(1)}, f32[256,512]{1,0:T(8,128)S(1)}, u32[]{:S(2)}, u32[]{:S(2)}) collective-permute-start(f32[256,512]{1,0:T(8,128)S(1)} %drift.1), channel_id=1, source_target_pairs={{0,16},{16,0},{1,17},{17,1},{2,18},{18,2},{3,19},{19,3},{4,20},{20... | collective-permute-start | bytes 1572872 | tf_op jit(solution)/shard_map/ppermute | solution.py:193
  77.6 8.6 %collective-permute-start.7 = (bf16[256,512]{1,0:T(8,128)(2,1)S(1)}, bf16[256,512]{1,0:T(8,128)(2,1)S(1)}, u32[]{:S(2)}, u32[]{:S(2)}) collective-permute-start(bf16[256,512]{1,0:T(8,128)(2,1)S(1)} %outer.1), channel_id=1, source_target_pairs={{0,4},{1,5},{2,6},{3,7},{4,0},{5,1},{6,2},{7,3},{8,12},{9,13},{10,... | collective-permute-start | bytes 786440 | tf_op jit(solution)/shard_map/ppermute | solution.py:186
  77.7 9.2 %collective-permute-start.9 = (bf16[256,512]{1,0:T(8,128)(2,1)S(1)}, bf16[256,512]{1,0:T(8,128)(2,1)S(1)}, u32[]{:S(2)}, u32[]{:S(2)}) collective-permute-start(bf16[256,512]{1,0:T(8,128)(2,1)S(1)} %outer.1), channel_id=1, source_target_pairs={{4,8},{5,9},{6,10},{7,11},{8,4},{9,5},{10,6},{11,7},{20,24},{21,25... | collective-permute-start | bytes 786440 | tf_op jit(solution)/shard_map/ppermute | solution.py:186
  86.2 2.0 %collective-permute-start.12 = (bf16[256,512]{1,0:T(8,128)(2,1)S(1)}, bf16[256,512]{1,0:T(8,128)(2,1)S(1)}, u32[]{:S(2)}, u32[]{:S(2)}) collective-permute-start(bf16[256,512]{1,0:T(8,128)(2,1)S(1)} %collective-permute-done.7), channel_id=1, source_target_pairs={{4,8},{5,9},{6,10},{7,11},{8,4},{9,5},{10,6},{11,7},{20,24},{21,25... | collective-permute-start | bytes 786440 | tf_op jit(solution)/shard_map/ppermute | solution.py:186
  86.9 9.9 %collective-permute-start.10 = (bf16[256,512]{1,0:T(8,128)(2,1)S(1)}, bf16[256,512]{1,0:T(8,128)(2,1)S(1)}, u32[]{:S(2)}, u32[]{:S(2)}) collective-permute-start(bf16[256,512]{1,0:T(8,128)(2,1)S(1)} %collective-permute-done.9), channel_id=1, source_target_pairs={{4,0},{5,1},{6,2},{7,3},{8,12},{9,13},{10,14},{11,15},{20,16},{21,... | collective-permute-start | bytes 786440 | tf_op jit(solution)/shard_map/ppermute | solution.py:186
  88.2 14.8 %collective-permute-start.13 = (bf16[256,512]{1,0:T(8,128)(2,1)S(1)}, bf16[256,512]{1,0:T(8,128)(2,1)S(1)}, u32[]{:S(2)}, u32[]{:S(2)}) collective-permute-start(bf16[256,512]{1,0:T(8,128)(2,1)S(1)} %collective-permute-done.12), channel_id=1, source_target_pairs={{4,0},{5,1},{6,2},{7,3},{8,12},{9,13},{10,14},{11,15},{20,16},{21,... | collective-permute-start | bytes 786440 | tf_op jit(solution)/shard_map/ppermute | solution.py:186
  89.6 13.5 %collective-permute-start.8 = (bf16[2,256,512]{2,1,0:T(8,128)(2,1)S(1)}, bf16[2,256,512]{2,1,0:T(8,128)(2,1)S(1)}, u32[]{:S(2)}, u32[]{:S(2)}) collective-permute-start(bf16[2,256,512]{2,1,0:T(8,128)(2,1)S(1)} %pad_maximum_fusion.mine_ref), channel_id=1, source_target_pairs={{0,16},{16,0},{1,17},{17,1},{2,18},{18,2},{3,19},{19,3},{4,20},{20... | collective-permute-start | bytes 1572872 | tf_op jit(solution)/shard_map/ppermute | solution.py:193
  96.9 6.3 %collective-permute-start.11 = (bf16[256,512]{1,0:T(8,128)(2,1)S(1)}, bf16[256,512]{1,0:T(8,128)(2,1)S(1)}, u32[]{:S(2)}, u32[]{:S(2)}) collective-permute-start(bf16[256,512]{1,0:T(8,128)(2,1)S(1)} %broadcast_select_fusion.1.mine2_ref), channel_id=1, source_target_pairs={{0,16},{16,0},{1,17},{17,1},{2,18},{18,2},{3,19},{19,3},{4,20},{20... | collective-permute-start | bytes 786440 | tf_op jit(solution)/shard_map/ppermute | solution.py:193
  103.0 1.6 %collective-permute-start.14 = (bf16[256,512]{1,0:T(8,128)(2,1)S(1)}, bf16[256,512]{1,0:T(8,128)(2,1)S(1)}, u32[]{:S(2)}, u32[]{:S(2)}) collective-permute-start(bf16[256,512]{1,0:T(8,128)(2,1)S(1)} %broadcast_select_fusion.mine3_ref), channel_id=1, source_target_pairs={{0,16},{16,0},{1,17},{17,1},{2,18},{18,2},{3,19},{19,3},{4,20},{20... | collective-permute-start | bytes 786440 | tf_op jit(solution)/shard_map/ppermute | solution.py:193
  (6 other events, 6.2 us)

commit v4 on v0

v4 whole, which is shorter than its diff:
```python
from functools import partial

import jax
import jax.numpy as jnp
from jax import lax
from jax.experimental import pallas as pl
from jax.experimental.pallas import tpu as pltpu
from jax.sharding import PartitionSpec as P

decay_first = 0.9
decay_second = 0.95
inner_rate = 0.006
epsilon = 1e-08
outer_rate = 0.7
outer_decay = 0.9

PLANES = 4
PARTS = 1
CHUNK = 32
CONTRACT_ROWS = (((0,), (0,)), ((), ()))
VMEM_BYTES = 16 * 1024 * 1024


def outer_update(average, anchor_rows, momentum_rows):
    velocity = outer_decay * momentum_rows + average
    return (anchor_rows - outer_rate * (average + outer_decay * velocity)).astype(jnp.bfloat16)


def inner_update(gradient, inner_weights, first_moment, second_moment, anchor):
    first_next = decay_first * first_moment + (1.0 - decay_first) * gradient
    second_next = decay_second * second_moment + (1.0 - decay_second) * gradient * gradient
    stepped = inner_weights - inner_rate * first_next / (jnp.sqrt(second_next) + epsilon)
    return first_next, anchor - stepped


def general(acts, value_cots, inner_weights, first_moment, second_moment, anchor, outer_momentum):
    tokens_local = acts[0]
    columns = lax.all_to_all(tokens_local, "fsdp", split_axis=1, concat_axis=0, tiled=True)
    cots = lax.all_gather(value_cots[0], "fsdp", axis=0, tiled=True)
    gradient = lax.dot_general(columns, cots, CONTRACT_ROWS, preferred_element_type=jnp.float32)
    first_next, drift = inner_update(gradient, inner_weights[0], first_moment[0], second_moment[0], anchor)
    average = lax.psum(drift, "rep") / lax.axis_size("rep")
    weights_next = outer_update(average, anchor, outer_momentum)
    gathered = lax.all_gather(weights_next, "fsdp", axis=0, tiled=True)
    values = jnp.dot(tokens_local, gathered, preferred_element_type=jnp.float32)
    return (first_next[None], values.astype(jnp.bfloat16)[None])


def flip(at, bits):
    low = lax.rem(at, 2)
    return (at // 2 + bits // 2 - 2 * (at // 2) * (bits // 2)) * 2 + low + bits % 2 - 2 * low * (bits % 2)


def call(kernel, name, out, inputs, flops, scratch=()):
    moved = sum(x.size * x.dtype.itemsize for x in list(inputs) + list(out))
    return pl.pallas_call(
        kernel,
        out_shape=out,
        in_specs=[pl.BlockSpec(memory_space=pltpu.VMEM)] * len(inputs),
        out_specs=[pl.BlockSpec(memory_space=pltpu.VMEM)] * len(out),
        scratch_shapes=list(scratch),
        compiler_params=pltpu.CompilerParams(vmem_limit_bytes=VMEM_BYTES),
        cost_estimate=pl.CostEstimate(flops=flops, bytes_accessed=moved, transcendentals=0),
        name=name,
    )(*inputs)


def repack_kernel(inner, rows, messages, acts_ref, cots_ref, *outs):
    f = lax.axis_index("fsdp")
    o, i = f // inner, lax.rem(f, inner)
    for number, (planes, columns) in enumerate(messages):
        for k in range(inner):
            out = outs[number * inner + k]
            for slot, bits in enumerate(planes):
                start = pl.multiple_of((flip(o, bits) * inner + flip(i, k)) * rows, rows)
                out[:, slot * rows : (slot + 1) * rows] = acts_ref[:, pl.ds(start, rows)]
            if columns:
                out[:, len(planes) * rows :] = cots_ref[:, columns[0] : columns[1]]


def repack(acts, cots, inner, rows, messages):
    tokens = acts.shape[0]
    out = []
    for planes, columns in messages:
        wide = len(planes) * rows + (columns[1] - columns[0] if columns else 0)
        out += [jax.ShapeDtypeStruct((tokens, wide), jnp.bfloat16)] * inner
    got = call(partial(repack_kernel, inner, rows, messages), "repack", out, [acts, cots], 0)
    return [got[n * inner : (n + 1) * inner] for n in range(len(messages))]


def gradient_kernel(inner, rows, acts_at, cots_at, *refs):
    acts_refs, cots_refs, added, out = refs[:inner], refs[inner : 2 * inner], refs[2 * inner : -1], refs[-1]
    columns = jnp.concatenate([ref[:, acts_at : acts_at + rows] for ref in acts_refs], axis=0)
    cots = jnp.concatenate([ref[:, cots_at : cots_at + out.shape[1]] for ref in cots_refs], axis=0)
    total = lax.dot_general(columns, cots, CONTRACT_ROWS, preferred_element_type=jnp.float32)
    for ref in added:
        total += ref[...].astype(jnp.float32)
    out[...] = total.astype(out.dtype)


def gradient_at(at, refs):
    total, beside, far = refs
    return total[at, :] + beside[at, :].astype(jnp.float32) + far[at, :].astype(jnp.float32)


def steps(half, which, body):
    @pl.loop(0, half // CHUNK)
    def _(step):
        start = pl.multiple_of(step * CHUNK, CHUNK)
        body(pl.ds(start, CHUNK), pl.ds(pl.multiple_of(which * half + start, CHUNK), CHUNK))


def drift_kernel(columns, *refs):
    gradient_refs, (weights, first, second, anchor), drift_ref = refs[:3], refs[3:7], refs[7]
    cols = slice(*columns)

    def body(here, at):
        gradient = gradient_at(at, gradient_refs)
        state = (weights[at, cols], first[at, cols], second[at, cols], anchor[at, cols])
        drift_ref[here, :] = inner_update(gradient, *state)[1]

    steps(drift_ref.shape[0], 1 - lax.axis_index("rep"), body)


def update_kernel(columns, *refs):
    gradient_refs, (weights, first, second, anchor), earlier = refs[:3], refs[3:7], refs[7:-2]
    first_ref, drift_ref = refs[-2:]
    cols = slice(*columns)
    half = drift_ref.shape[0]
    r = lax.axis_index("rep")

    def body(here, at):
        gradient = gradient_at(at, gradient_refs)
        state = (weights[at, cols], first[at, cols], second[at, cols], anchor[at, cols])
        first_ref[at, cols], drift_ref[here, :] = inner_update(gradient, *state)

    def others(here, at):
        first_ref[at, cols] = decay_first * first[at, cols] + (1.0 - decay_first) * gradient_at(at, gradient_refs)

    steps(half, r, body)
    steps(half, 1 - r, others)
    for ref in earlier:
        first_ref[:, : columns[0]] = ref[:, : columns[0]]


def outer_kernel(columns, drift, other, anchor, momentum, out):
    half = out.shape[0]
    at = pl.ds(pl.multiple_of(lax.axis_index("rep") * half, half), half)
    cols = slice(*columns)
    out[...] = outer_update((drift[...] + other[...]) / 2, anchor[at, cols], momentum[at, cols])


def values_kernel(inner, rows, places, *refs):
    messages = [refs[n * inner : (n + 1) * inner] for n in range(3)]
    pieces, own_ref, sent_refs, weights = refs[3 * inner : 3 * inner + 8], refs[3 * inner + 8], refs[3 * inner + 9 : -1], refs[-1]
    half = rows // 2
    r = lax.axis_index("rep")
    for bits in range(PLANES):
        for which, piece in ((r, pieces[2 * bits]), (1 - r, pieces[2 * bits + 1])):
            weights[pl.ds(pl.multiple_of(bits * rows + which * half, half), half), :] = piece[...]
    for k in range(inner):
        blocks = [messages[number][k][:, at : at + rows] for number, at in places]
        total = jnp.dot(jnp.concatenate(blocks, axis=1), weights[...], preferred_element_type=jnp.float32)
        if k == 0:
            own_ref[...] = total
        else:
            sent_refs[k - 1][...] = total.astype(jnp.bfloat16)


def on_device(acts, value_cots, inner_weights, first_moment, second_moment, anchor, outer_momentum):
    inner = lax.axis_size("fsdp") // PLANES
    rows, width = anchor.shape
    if inner != 4 or lax.axis_size("rep") != 2 or rows % 256 or width % (128 * PARTS):
        return general(acts, value_cots, inner_weights, first_moment, second_moment, anchor, outer_momentum)
    tokens = acts.shape[1]
    half = rows // 2
    part_width = width // PARTS

    def planes(x, bits):
        return lax.ppermute(x, "fsdp", [(p * inner + i, (p ^ bits) * inner + i) for p in range(PLANES) for i in range(inner)])

    def across(x, k):
        return lax.ppermute(x, "fsdp", [(p * inner + i, p * inner + (i ^ k)) for p in range(PLANES) for i in range(inner)])

    def around(blocks):
        return [blocks[0]] + [across(blocks[k], k) for k in range(1, inner)]

    def swap(x):
        return lax.ppermute(x, "rep", [(0, 1), (1, 0)])

    later = (part_width, width) if PARTS > 1 else None
    (first,) = repack(acts[0], value_cots[0], inner, rows, [((3,), (0, part_width))])
    second, last = repack(acts[0], value_cots[0], inner, rows, [((2, 1), later), ((0,), None)])
    messages = [around(first), around(second), around(last)]
    places = [(2, 0), (1, rows), (1, 0), (0, 0)]

    def gradient(bits, part, dtype, *added):
        number, at = places[bits]
        cots, cots_at = (messages[0], rows) if part == 0 else (messages[1], 2 * rows + (part - 1) * part_width)
        out = jax.ShapeDtypeStruct((rows, part_width), dtype)
        kernel = partial(gradient_kernel, inner, rows, at, cots_at)
        flops = 2 * inner * tokens * rows * part_width
        return call(kernel, "gradient", [out], messages[number] + cots + list(added), flops)[0]

    state = [inner_weights[0], first_moment[0], second_moment[0], anchor]
    half_block = jax.ShapeDtypeStruct((half, part_width), jnp.float32)
    first_next, values = [], []
    for part in range(PARTS):
        columns = (part * part_width, (part + 1) * part_width)
        beside_far = planes(gradient(3, part, jnp.bfloat16), 1)
        beside = planes(gradient(1, part, jnp.bfloat16), 1)
        far = planes(gradient(2, part, jnp.bfloat16, beside_far), 2)
        known = [gradient(0, part, jnp.float32), beside, far] + state
        (drift_out,) = call(partial(drift_kernel, columns), "drift", [half_block], known, 0)
        drift_in = swap(drift_out)
        full = jax.ShapeDtypeStruct((rows, width), jnp.float32)
        *first_next, drift = call(partial(update_kernel, columns), "update", [full, half_block], known + first_next, 0)
        new_half = jax.ShapeDtypeStruct((half, part_width), jnp.bfloat16)
        (mine,) = call(partial(outer_kernel, columns), "outer", [new_half], [drift, drift_in, anchor, outer_momentum], 0)
        mine2 = planes(mine, 2)
        mine1 = planes(mine, 1)
        mine3 = planes(mine2, 1)
        pieces = [y for x in (mine, mine1, mine2, mine3) for y in (x, swap(x))]
        block = jax.ShapeDtypeStruct((tokens, part_width), jnp.bfloat16)
        own, *sent = call(
            partial(values_kernel, inner, rows, places),
            "values",
            [jax.ShapeDtypeStruct((tokens, part_width), jnp.float32)] + [block] * (inner - 1),
            messages[0] + messages[1] + messages[2] + pieces,
            2 * inner * tokens * PLANES * rows * part_width,
            [pltpu.VMEM((PLANES * rows, part_width), jnp.bfloat16)],
        )
        for k in range(1, inner):
            own = own + across(sent[k - 1], k).astype(jnp.float32)
        values.append(own.astype(jnp.bfloat16))
    values = values[0] if PARTS == 1 else jnp.concatenate(values, axis=1)
    return (first_next[0][None], values[None])


def solution(mesh):
    placed = (
        P("rep", "fsdp", None),
        P("rep", "fsdp", None),
        P("rep", "fsdp", None),
        P("rep", "fsdp", None),
        P("rep", "fsdp", None),
        P("fsdp", None),
        P("fsdp", None),
    )
    return jax.shard_map(
        on_device,
        mesh=mesh,
        in_specs=placed,
        out_specs=(P("rep", "fsdp", None), P("rep", "fsdp", None)),
        check_vma=False,
    )
```

time: 253 us -> 96.1 us (0.38)
  waiting for transfers between devices: 208 us -> 59 us
  starting transfers between devices: 8.43 us -> 27 us
  between operations: 13.8 us -> 0.78 us
  matrix products: 12 us -> 0 us
  Pallas kernels: 0 us -> 5.92 us
  local copies, waits for them, and re-layouts: 7.45 us -> 2.52 us
    all_gather x2 -> x0, waiting for transfers between devices: 143 us -> none  [the longest x1 114 us: on_device(): lax.all_gather(weights_next, 'fsdp', axis=0, tiled=True)]
    ppermute x0 -> x23, waiting for transfers between devices: none -> 59 us  [the longest x12 32.3 us: across(): lax.ppermute(x, 'fsdp', [(p * inner + i, p * inner + (i ^ k)) for p in ra...]
    all_to_all x1 -> x0, waiting for transfers between devices: 45.9 us -> none  [on_device(): lax.all_to_all(tokens_local, 'fsdp', split_axis=1, concat_axis=0, tiled=T...]
    ppermute x0 -> x23, starting transfers between devices: none -> 27 us  [the longest x12 15.7 us: across(): lax.ppermute(x, 'fsdp', [(p * inner + i, p * inner + (i ^ k)) for p in ra...]
    psum x1 -> x0, waiting for transfers between devices: 18.3 us -> none  [on_device(): summed_drift = lax.psum(drift, 'rep')]
    dot_general x2 -> x0, matrix products: 12 us -> none  [the longest x1 6.22 us: on_device(): lax.dot_general(columns, lax.all_gather(cots_local, 'fsdp', axis=0, tiled...]
    all_to_all x1 -> x0, starting transfers between devices: 8.31 us -> none  [on_device(): lax.all_to_all(tokens_local, 'fsdp', split_axis=1, concat_axis=0, tiled=T...]
    pallas_call x0 -> x10, Pallas kernels: none -> 5.92 us  [call(): pl.pallas_call(kernel, out_shape=out, in_specs=[pl.BlockSpec(memory_space...]
  transfers between devices with their start and end apart: 4 -> 23, of which waited for: 4 -> 15; matrix products, arithmetic and copies ran while one was open for 1% -> 0% of each run, Pallas kernels for 0% -> 3%
where the time goes in v4:
time: 96.1 us; the launch traced here: 95.9 us
  waiting for transfers between devices  59 us (61%)
  starting transfers between devices  27 us (28%)
  Pallas kernels  5.92 us (6%)
  local copies, waits for them, and re-layouts  2.52 us (3%)
    ppermute x12, waiting for transfers between devices, across(): lax.ppermute(x, 'fsdp', [(p * inner + i, p * inner + (i ^ k)) for p in ra...  32.3 us
    ppermute x6, waiting for transfers between devices, planes(): lax.ppermute(x, 'fsdp', [(p * inner + i, (p ^ bits) * inner + i) for p in...  24.8 us
    ppermute x12, starting transfers between devices, across(): lax.ppermute(x, 'fsdp', [(p * inner + i, p * inner + (i ^ k)) for p in ra...  15.7 us
    ppermute x6, starting transfers between devices, planes(): lax.ppermute(x, 'fsdp', [(p * inner + i, (p ^ bits) * inner + i) for p in...  10.7 us
    pallas_call x10, Pallas kernels, call(): pl.pallas_call(kernel, out_shape=out, in_specs=[pl.BlockSpec(memory_space...  5.92 us
    unnamed x16, local copies, waits for them, and re-layouts  2.52 us
  transfers between devices with their start and end apart: 23, of which 15 were waited for; matrix products, arithmetic and copies ran while one was open for 0% of the time, Pallas kernels for 3%

profile of v4, /device:TPU:0, one launch (start us, length us, event | category | flops | bytes accessed | tf_op | source)
XLA Modules:
  0.0 95.9 jit_solution(6027376293566340318)
XLA Ops:
  0.6 1.6 %copy-done.1 = bf16[1,128,8192]{2,1,0:T(8,128)(2,1)S(1)} copy-done((bf16[1,128,8192]{2,1,0:T(8,128)(2,1)S(1)}, bf16[1,128,8192]{2,1,0:T(8,128)(2,1)}, u32[]{:S(2)}) %copy-start.1) | copy-done | bytes 2097176
  3.2 3.0 %collective-permute-start.3 = (bf16[128,1024]{1,0:T(8,128)(2,1)S(1)}, bf16[128,1024]{1,0:T(8,128)(2,1)S(1)}, u32[]{:S(2)}, u32[]{:S(2)}) collective-permute-start(bf16[128,1024]{1,0:T(8,128)(2,1)S(1)} %get-tuple-element.25), channel_id=1, source_target_pairs={{0,1},{1,0},{2,3},{3,2},{4,5},{5,4},{6,7},{7,6},{8,9},{9,8},{10,11... | collective-permute-start | bytes 786440 | tf_op jit(solution)/shard_map/ppermute | solution.py:183
  6.2 1.5 %collective-permute-start.4 = (bf16[128,1024]{1,0:T(8,128)(2,1)S(1)}, bf16[128,1024]{1,0:T(8,128)(2,1)S(1)}, u32[]{:S(2)}, u32[]{:S(2)}) collective-permute-start(bf16[128,1024]{1,0:T(8,128)(2,1)S(1)} %get-tuple-element.26), channel_id=1, source_target_pairs={{0,2},{1,3},{2,0},{3,1},{4,6},{5,7},{6,4},{7,5},{8,10},{9,11},{10,... | collective-permute-start | bytes 786440 | tf_op jit(solution)/shard_map/ppermute | solution.py:183
  7.8 5.6 %collective-permute-done.3.refs_5_.refs_1_ = bf16[128,1024]{1,0:T(8,128)(2,1)S(1)} collective-permute-done((bf16[128,1024]{1,0:T(8,128)(2,1)S(1)}, bf16[128,1024]{1,0:T(8,128)(2,1)S(1)}, u32[]{:S(2)}, u32[]{:S(2)}) %collective-permute-start.3) | collective-permute-done | bytes 262176 | tf_op jit(solution)/shard_map/ppermute | solution.py:183
  13.4 6.2 %collective-permute-done.4.refs_6_.refs_2_ = bf16[128,1024]{1,0:T(8,128)(2,1)S(1)} collective-permute-done((bf16[128,1024]{1,0:T(8,128)(2,1)S(1)}, bf16[128,1024]{1,0:T(8,128)(2,1)S(1)}, u32[]{:S(2)}, u32[]{:S(2)}) %collective-permute-start.4) | collective-permute-done | bytes 262176 | tf_op jit(solution)/shard_map/ppermute | solution.py:183
  20.1 1.6 %collective-permute-start.10 = (bf16[512,512]{1,0:T(8,128)(2,1)S(1)}, bf16[512,512]{1,0:T(8,128)(2,1)S(1)}, u32[]{:S(2)}, u32[]{:S(2)}) collective-permute-start(bf16[512,512]{1,0:T(8,128)(2,1)S(1)} %gradient.6), channel_id=1, source_target_pairs={{0,4},{1,5},{2,6},{3,7},{4,0},{5,1},{6,2},{7,3},{8,12},{9,13},{10,... | collective-permute-start | bytes 1572872 | tf_op jit(solution)/shard_map/ppermute | solution.py:180
  24.0 1.4 %collective-permute-start.8 = (bf16[128,1024]{1,0:T(8,128)(2,1)S(1)}, bf16[128,1024]{1,0:T(8,128)(2,1)S(1)}, u32[]{:S(2)}, u32[]{:S(2)}) collective-permute-start(bf16[128,1024]{1,0:T(8,128)(2,1)S(1)} %get-tuple-element.31), channel_id=1, source_target_pairs={{0,3},{1,2},{2,1},{3,0},{4,7},{5,6},{6,5},{7,4},{8,11},{9,10},{10,... | collective-permute-start | bytes 786440 | tf_op jit(solution)/shard_map/ppermute | solution.py:183
  25.4 5.8 %collective-permute-done.6.refs_1_.refs_5_ = bf16[128,1024]{1,0:T(8,128)(2,1)S(1)} collective-permute-done((bf16[128,1024]{1,0:T(8,128)(2,1)S(1)}, bf16[128,1024]{1,0:T(8,128)(2,1)S(1)}, u32[]{:S(2)}, u32[]{:S(2)}) %collective-permute-start.6) | collective-permute-done | bytes 262176 | tf_op jit(solution)/shard_map/ppermute | solution.py:183
  31.2 4.2 %collective-permute-done.7.refs_2_.refs_6_ = bf16[128,1024]{1,0:T(8,128)(2,1)S(1)} collective-permute-done((bf16[128,1024]{1,0:T(8,128)(2,1)S(1)}, bf16[128,1024]{1,0:T(8,128)(2,1)S(1)}, u32[]{:S(2)}, u32[]{:S(2)}) %collective-permute-start.7) | collective-permute-done | bytes 262176 | tf_op jit(solution)/shard_map/ppermute | solution.py:183
  36.9 2.7 %collective-permute-start.11 = (bf16[512,512]{1,0:T(8,128)(2,1)S(1)}, bf16[512,512]{1,0:T(8,128)(2,1)S(1)}, u32[]{:S(2)}, u32[]{:S(2)}) collective-permute-start(bf16[512,512]{1,0:T(8,128)(2,1)S(1)} %gradient.7), channel_id=1, source_target_pairs={{0,8},{1,9},{2,10},{3,11},{4,12},{5,13},{6,14},{7,15},{8,0},{9,1},... | collective-permute-start | bytes 1572872 | tf_op jit(solution)/shard_map/ppermute | solution.py:180
  40.1 1.5 %collective-permute-start.1 = (bf16[128,512]{1,0:T(8,128)(2,1)S(1)}, bf16[128,512]{1,0:T(8,128)(2,1)S(1)}, u32[]{:S(2)}, u32[]{:S(2)}) collective-permute-start(bf16[128,512]{1,0:T(8,128)(2,1)S(1)} %get-tuple-element.22), channel_id=1, source_target_pairs={{0,2},{1,3},{2,0},{3,1},{4,6},{5,7},{6,4},{7,5},{8,10},{9,11},{10,... | collective-permute-start | bytes 393224 | tf_op jit(solution)/shard_map/ppermute | solution.py:183
  43.0 1.5 %collective-permute-done.refs_1_.refs_9_ = bf16[128,512]{1,0:T(8,128)(2,1)S(1)} collective-permute-done((bf16[128,512]{1,0:T(8,128)(2,1)S(1)}, bf16[128,512]{1,0:T(8,128)(2,1)S(1)}, u32[]{:S(2)}, u32[]{:S(2)}) %collective-permute-start) | collective-permute-done | bytes 131104 | tf_op jit(solution)/shard_map/ppermute | solution.py:183
  45.1 2.4 %collective-permute-done.2.refs_3_.refs_11_ = bf16[128,512]{1,0:T(8,128)(2,1)S(1)} collective-permute-done((bf16[128,512]{1,0:T(8,128)(2,1)S(1)}, bf16[128,512]{1,0:T(8,128)(2,1)S(1)}, u32[]{:S(2)}, u32[]{:S(2)}) %collective-permute-start.2) | collective-permute-done | bytes 131104 | tf_op jit(solution)/shard_map/ppermute | solution.py:183
  48.0 8.6 %collective-permute-done.9.refs_1_ = bf16[512,512]{1,0:T(8,128)(2,1)S(1)} collective-permute-done((bf16[512,512]{1,0:T(8,128)(2,1)S(1)}, bf16[512,512]{1,0:T(8,128)(2,1)S(1)}, u32[]{:S(2)}, u32[]{:S(2)}) %collective-permute-start.9) | collective-permute-done | bytes 524320 | tf_op jit(solution)/shard_map/ppermute | solution.py:180
  57.2 1.7 %update.1 = (f32[512,512]{1,0:T(8,128)}, f32[256,512]{1,0:T(8,128)S(1)}) custom-call(f32[512,512]{1,0:T(8,128)S(1)} %gradient.4.refs_0_, bf16[512,512]{1,0:T(8,128)(2,1)S(1)} %collective-permute-done.9.refs_1_, bf16[512,512]{1,0:T(8,128)(2,1)S(1)} %collective-permute-done.11.refs_2_, f32[512,512]{1,0:T(8,128)S(1)} %bitcast.11, f32[512,512]{1,0:T(8,128)S(1)} %bitcast.13, ...), custom_call_target="tpu_custom_call" | custom-call | bytes 7864320 | tf_op jit(solution)/shard_map/update/pallas_call | solution.py:56
  59.3 1.5 %collective-permute-start.16 = (bf16[256,512]{1,0:T(8,128)(2,1)S(1)}, bf16[256,512]{1,0:T(8,128)(2,1)S(1)}, u32[]{:S(2)}, u32[]{:S(2)}) collective-permute-start(bf16[256,512]{1,0:T(8,128)(2,1)S(1)} %outer.1.refs_12_), channel_id=1, source_target_pairs={{0,8},{1,9},{2,10},{3,11},{4,12},{5,13},{6,14},{7,15},{8,0},{9,1},... | collective-permute-start | bytes 786440 | tf_op jit(solution)/shard_map/ppermute | solution.py:180
  60.8 4.4 %collective-permute-start.14 = (bf16[256,512]{1,0:T(8,128)(2,1)S(1)}, bf16[256,512]{1,0:T(8,128)(2,1)S(1)}, u32[]{:S(2)}, u32[]{:S(2)}) collective-permute-start(bf16[256,512]{1,0:T(8,128)(2,1)S(1)} %outer.1.refs_12_), channel_id=1, source_target_pairs={{0,4},{1,5},{2,6},{3,7},{4,0},{5,1},{6,2},{7,3},{8,12},{9,13},{10,... | collective-permute-start | bytes 786440 | tf_op jit(solution)/shard_map/ppermute | solution.py:180
  65.2 9.2 %collective-permute-done.16.refs_16_ = bf16[256,512]{1,0:T(8,128)(2,1)S(1)} collective-permute-done((bf16[256,512]{1,0:T(8,128)(2,1)S(1)}, bf16[256,512]{1,0:T(8,128)(2,1)S(1)}, u32[]{:S(2)}, u32[]{:S(2)}) %collective-permute-start.16) | collective-permute-done | bytes 262176 | tf_op jit(solution)/shard_map/ppermute | solution.py:180
  74.9 7.0 %collective-permute-done.18.refs_18_ = bf16[256,512]{1,0:T(8,128)(2,1)S(1)} collective-permute-done((bf16[256,512]{1,0:T(8,128)(2,1)S(1)}, bf16[256,512]{1,0:T(8,128)(2,1)S(1)}, u32[]{:S(2)}, u32[]{:S(2)}) %collective-permute-start.18) | collective-permute-done | bytes 262176 | tf_op jit(solution)/shard_map/ppermute | solution.py:180
  82.0 1.5 %collective-permute-done.19.refs_19_ = bf16[256,512]{1,0:T(8,128)(2,1)S(1)} collective-permute-done((bf16[256,512]{1,0:T(8,128)(2,1)S(1)}, bf16[256,512]{1,0:T(8,128)(2,1)S(1)}, u32[]{:S(2)}, u32[]{:S(2)}) %collective-permute-start.19) | collective-permute-done | bytes 262176 | tf_op jit(solution)/shard_map/ppermute | solution.py:189
  83.5 1.5 %values.1 = (f32[128,512]{1,0:T(8,128)S(1)}, bf16[128,512]{1,0:T(8,128)(2,1)S(1)}, bf16[128,512]{1,0:T(8,128)(2,1)S(1)}, bf16[128,512]{1,0:T(8,128)(2,1)S(1)}) custom-call(bf16[128,1024]{1,0:T(8,128)(2,1)S(1)} %get-tuple-element.24.refs_4_.refs_0_, bf16[128,1024]{1,0:T(8,128)(2,1)S(1)} %collective-permute-done.3.refs_5_.refs_1_, ...), custom_call_target="tpu_custom_call" | custom-call | flops 1073741824 | bytes 5373952 | tf_op jit(solution)/shard_map/values/pallas_call | solution.py:56
  85.0 3.4 %collective-permute-start.22 = (bf16[128,512]{1,0:T(8,128)(2,1)S(1)}, bf16[128,512]{1,0:T(8,128)(2,1)S(1)}, u32[]{:S(2)}, u32[]{:S(2)}) collective-permute-start(bf16[128,512]{1,0:T(8,128)(2,1)S(1)} %get-tuple-element.37), channel_id=1, source_target_pairs={{0,3},{1,2},{2,1},{3,0},{4,7},{5,6},{6,5},{7,4},{8,11},{9,10},{10,... | collective-permute-start | bytes 393224 | tf_op jit(solution)/shard_map/ppermute | solution.py:183
  89.1 3.3 %collective-permute-done.22 = bf16[128,512]{1,0:T(8,128)(2,1)S(1)} collective-permute-done((bf16[128,512]{1,0:T(8,128)(2,1)S(1)}, bf16[128,512]{1,0:T(8,128)(2,1)S(1)}, u32[]{:S(2)}, u32[]{:S(2)}) %collective-permute-start.22) | collective-permute-done | bytes 131104 | tf_op jit(solution)/shard_map/ppermute | solution.py:183
  92.4 2.7 %collective-permute-done.21 = bf16[128,512]{1,0:T(8,128)(2,1)S(1)} collective-permute-done((bf16[128,512]{1,0:T(8,128)(2,1)S(1)}, bf16[128,512]{1,0:T(8,128)(2,1)S(1)}, u32[]{:S(2)}, u32[]{:S(2)}) %collective-permute-start.21) | collective-permute-done | bytes 131104 | tf_op jit(solution)/shard_map/ppermute | solution.py:183
  (49 shorter events, 11.2 us)
Async XLA Ops:
  3.2 10.1 %collective-permute-start.3 = (bf16[128,1024]{1,0:T(8,128)(2,1)S(1)}, bf16[128,1024]{1,0:T(8,128)(2,1)S(1)}, u32[]{:S(2)}, u32[]{:S(2)}) collective-permute-start(bf16[128,1024]{1,0:T(8,128)(2,1)S(1)} %get-tuple-element.25), channel_id=1, source_target_pairs={{0,1},{1,0},{2,3},{3,2},{4,5},{5,4},{6,7},{7,6},{8,9},{9,8},{10,11... | collective-permute-start | bytes 786440 | tf_op jit(solution)/shard_map/ppermute | solution.py:183
  6.2 13.4 %collective-permute-start.4 = (bf16[128,1024]{1,0:T(8,128)(2,1)S(1)}, bf16[128,1024]{1,0:T(8,128)(2,1)S(1)}, u32[]{:S(2)}, u32[]{:S(2)}) collective-permute-start(bf16[128,1024]{1,0:T(8,128)(2,1)S(1)} %get-tuple-element.26), channel_id=1, source_target_pairs={{0,2},{1,3},{2,0},{3,1},{4,6},{5,7},{6,4},{7,5},{8,10},{9,11},{10,... | collective-permute-start | bytes 786440 | tf_op jit(solution)/shard_map/ppermute | solution.py:183
  7.7 11.9 %collective-permute-start.5 = (bf16[128,1024]{1,0:T(8,128)(2,1)S(1)}, bf16[128,1024]{1,0:T(8,128)(2,1)S(1)}, u32[]{:S(2)}, u32[]{:S(2)}) collective-permute-start(bf16[128,1024]{1,0:T(8,128)(2,1)S(1)} %get-tuple-element.27), channel_id=1, source_target_pairs={{0,3},{1,2},{2,1},{3,0},{4,7},{5,6},{6,5},{7,4},{8,11},{9,10},{10,... | collective-permute-start | bytes 786440 | tf_op jit(solution)/shard_map/ppermute | solution.py:183
  20.1 16.3 %collective-permute-start.10 = (bf16[512,512]{1,0:T(8,128)(2,1)S(1)}, bf16[512,512]{1,0:T(8,128)(2,1)S(1)}, u32[]{:S(2)}, u32[]{:S(2)}) collective-permute-start(bf16[512,512]{1,0:T(8,128)(2,1)S(1)} %gradient.6), channel_id=1, source_target_pairs={{0,4},{1,5},{2,6},{3,7},{4,0},{5,1},{6,2},{7,3},{8,12},{9,13},{10,... | collective-permute-start | bytes 1572872 | tf_op jit(solution)/shard_map/ppermute | solution.py:180
  21.9 9.3 %collective-permute-start.6 = (bf16[128,1024]{1,0:T(8,128)(2,1)S(1)}, bf16[128,1024]{1,0:T(8,128)(2,1)S(1)}, u32[]{:S(2)}, u32[]{:S(2)}) collective-permute-start(bf16[128,1024]{1,0:T(8,128)(2,1)S(1)} %get-tuple-element.29), channel_id=1, source_target_pairs={{0,1},{1,0},{2,3},{3,2},{4,5},{5,4},{6,7},{7,6},{8,9},{9,8},{10,11... | collective-permute-start | bytes 786440 | tf_op jit(solution)/shard_map/ppermute | solution.py:183
  23.1 12.2 %collective-permute-start.7 = (bf16[128,1024]{1,0:T(8,128)(2,1)S(1)}, bf16[128,1024]{1,0:T(8,128)(2,1)S(1)}, u32[]{:S(2)}, u32[]{:S(2)}) collective-permute-start(bf16[128,1024]{1,0:T(8,128)(2,1)S(1)} %get-tuple-element.30), channel_id=1, source_target_pairs={{0,2},{1,3},{2,0},{3,1},{4,6},{5,7},{6,4},{7,5},{8,10},{9,11},{10,... | collective-permute-start | bytes 786440 | tf_op jit(solution)/shard_map/ppermute | solution.py:183
  24.0 11.4 %collective-permute-start.8 = (bf16[128,1024]{1,0:T(8,128)(2,1)S(1)}, bf16[128,1024]{1,0:T(8,128)(2,1)S(1)}, u32[]{:S(2)}, u32[]{:S(2)}) collective-permute-start(bf16[128,1024]{1,0:T(8,128)(2,1)S(1)} %get-tuple-element.31), channel_id=1, source_target_pairs={{0,3},{1,2},{2,1},{3,0},{4,7},{5,6},{6,5},{7,4},{8,11},{9,10},{10,... | collective-permute-start | bytes 786440 | tf_op jit(solution)/shard_map/ppermute | solution.py:183
  35.9 20.7 %collective-permute-start.9 = (bf16[512,512]{1,0:T(8,128)(2,1)S(1)}, bf16[512,512]{1,0:T(8,128)(2,1)S(1)}, u32[]{:S(2)}, u32[]{:S(2)}) collective-permute-start(bf16[512,512]{1,0:T(8,128)(2,1)S(1)} %gradient.5), channel_id=1, source_target_pairs={{0,4},{1,5},{2,6},{3,7},{4,0},{5,1},{6,2},{7,3},{8,12},{9,13},{10,... | collective-permute-start | bytes 1572872 | tf_op jit(solution)/shard_map/ppermute | solution.py:180
  36.4 20.2 %copy-start.5 = (f32[1,512,512]{2,1,0:T(8,128)S(1)}, f32[1,512,512]{2,1,0:T(8,128)}, u32[]{:S(2)}) copy-start(f32[1,512,512]{2,1,0:T(8,128)} %param.11) | copy-start | bytes 3145732
  36.9 19.6 %collective-permute-start.11 = (bf16[512,512]{1,0:T(8,128)(2,1)S(1)}, bf16[512,512]{1,0:T(8,128)(2,1)S(1)}, u32[]{:S(2)}, u32[]{:S(2)}) collective-permute-start(bf16[512,512]{1,0:T(8,128)(2,1)S(1)} %gradient.7), channel_id=1, source_target_pairs={{0,8},{1,9},{2,10},{3,11},{4,12},{5,13},{6,14},{7,15},{8,0},{9,1},... | collective-permute-start | bytes 1572872 | tf_op jit(solution)/shard_map/ppermute | solution.py:180
  39.5 5.0 %collective-permute-start = (bf16[128,512]{1,0:T(8,128)(2,1)S(1)}, bf16[128,512]{1,0:T(8,128)(2,1)S(1)}, u32[]{:S(2)}, u32[]{:S(2)}) collective-permute-start(bf16[128,512]{1,0:T(8,128)(2,1)S(1)} %get-tuple-element.21), channel_id=1, source_target_pairs={{0,1},{1,0},{2,3},{3,2},{4,5},{5,4},{6,7},{7,6},{8,9},{9,8},{10,11... | collective-permute-start | bytes 393224 | tf_op jit(solution)/shard_map/ppermute | solution.py:183
  40.1 5.0 %collective-permute-start.1 = (bf16[128,512]{1,0:T(8,128)(2,1)S(1)}, bf16[128,512]{1,0:T(8,128)(2,1)S(1)}, u32[]{:S(2)}, u32[]{:S(2)}) collective-permute-start(bf16[128,512]{1,0:T(8,128)(2,1)S(1)} %get-tuple-element.22), channel_id=1, source_target_pairs={{0,2},{1,3},{2,0},{3,1},{4,6},{5,7},{6,4},{7,5},{8,10},{9,11},{10,... | collective-permute-start | bytes 393224 | tf_op jit(solution)/shard_map/ppermute | solution.py:183
  41.6 5.9 %collective-permute-start.2 = (bf16[128,512]{1,0:T(8,128)(2,1)S(1)}, bf16[128,512]{1,0:T(8,128)(2,1)S(1)}, u32[]{:S(2)}, u32[]{:S(2)}) collective-permute-start(bf16[128,512]{1,0:T(8,128)(2,1)S(1)} %get-tuple-element.23), channel_id=1, source_target_pairs={{0,3},{1,2},{2,1},{3,0},{4,7},{5,6},{6,5},{7,4},{8,11},{9,10},{10,... | collective-permute-start | bytes 393224 | tf_op jit(solution)/shard_map/ppermute | solution.py:183
  57.1 2.0 %collective-permute-start.12 = (f32[256,512]{1,0:T(8,128)S(1)}, f32[256,512]{1,0:T(8,128)S(1)}, u32[]{:S(2)}, u32[]{:S(2)}) collective-permute-start(f32[256,512]{1,0:T(8,128)S(1)} %drift.1), channel_id=1, source_target_pairs={{0,16},{16,0},{1,17},{17,1},{2,18},{18,2},{3,19},{19,3},{4,20},{20... | collective-permute-start | bytes 1572872 | tf_op jit(solution)/shard_map/ppermute | solution.py:189
  59.3 15.1 %collective-permute-start.16 = (bf16[256,512]{1,0:T(8,128)(2,1)S(1)}, bf16[256,512]{1,0:T(8,128)(2,1)S(1)}, u32[]{:S(2)}, u32[]{:S(2)}) collective-permute-start(bf16[256,512]{1,0:T(8,128)(2,1)S(1)} %outer.1.refs_12_), channel_id=1, source_target_pairs={{0,8},{1,9},{2,10},{3,11},{4,12},{5,13},{6,14},{7,15},{8,0},{9,1},... | collective-permute-start | bytes 786440 | tf_op jit(solution)/shard_map/ppermute | solution.py:180
  60.8 14.1 %collective-permute-start.14 = (bf16[256,512]{1,0:T(8,128)(2,1)S(1)}, bf16[256,512]{1,0:T(8,128)(2,1)S(1)}, u32[]{:S(2)}, u32[]{:S(2)}) collective-permute-start(bf16[256,512]{1,0:T(8,128)(2,1)S(1)} %outer.1.refs_12_), channel_id=1, source_target_pairs={{0,4},{1,5},{2,6},{3,7},{4,0},{5,1},{6,2},{7,3},{8,12},{9,13},{10,... | collective-permute-start | bytes 786440 | tf_op jit(solution)/shard_map/ppermute | solution.py:180
  74.4 7.6 %collective-permute-start.18 = (bf16[256,512]{1,0:T(8,128)(2,1)S(1)}, bf16[256,512]{1,0:T(8,128)(2,1)S(1)}, u32[]{:S(2)}, u32[]{:S(2)}) collective-permute-start(bf16[256,512]{1,0:T(8,128)(2,1)S(1)} %collective-permute-done.16.refs_16_), channel_id=1, source_target_pairs={{0,4},{1,5},{2,6},{3,7},{4,0},{5,1},{6,2},{7,3},{8,12},{9,13},{10,... | collective-permute-start | bytes 786440 | tf_op jit(solution)/shard_map/ppermute | solution.py:180
  74.4 7.6 %collective-permute-start.13 = (bf16[256,512]{1,0:T(8,128)(2,1)S(1)}, bf16[256,512]{1,0:T(8,128)(2,1)S(1)}, u32[]{:S(2)}, u32[]{:S(2)}) collective-permute-start(bf16[256,512]{1,0:T(8,128)(2,1)S(1)} %outer.1.refs_12_), channel_id=1, source_target_pairs={{0,16},{16,0},{1,17},{17,1},{2,18},{18,2},{3,19},{19,3},{4,20},{20... | collective-permute-start | bytes 786440 | tf_op jit(solution)/shard_map/ppermute | solution.py:189
  74.4 7.6 %collective-permute-start.17 = (bf16[256,512]{1,0:T(8,128)(2,1)S(1)}, bf16[256,512]{1,0:T(8,128)(2,1)S(1)}, u32[]{:S(2)}, u32[]{:S(2)}) collective-permute-start(bf16[256,512]{1,0:T(8,128)(2,1)S(1)} %collective-permute-done.16.refs_16_), channel_id=1, source_target_pairs={{0,16},{16,0},{1,17},{17,1},{2,18},{18,2},{3,19},{19,3},{4,20},{20... | collective-permute-start | bytes 786440 | tf_op jit(solution)/shard_map/ppermute | solution.py:189
  74.9 7.1 %collective-permute-start.15 = (bf16[256,512]{1,0:T(8,128)(2,1)S(1)}, bf16[256,512]{1,0:T(8,128)(2,1)S(1)}, u32[]{:S(2)}, u32[]{:S(2)}) collective-permute-start(bf16[256,512]{1,0:T(8,128)(2,1)S(1)} %collective-permute-done.14.refs_14_), channel_id=1, source_target_pairs={{0,16},{16,0},{1,17},{17,1},{2,18},{18,2},{3,19},{19,3},{4,20},{20... | collective-permute-start | bytes 786440 | tf_op jit(solution)/shard_map/ppermute | solution.py:189
  82.0 1.5 %collective-permute-start.19 = (bf16[256,512]{1,0:T(8,128)(2,1)S(1)}, bf16[256,512]{1,0:T(8,128)(2,1)S(1)}, u32[]{:S(2)}, u32[]{:S(2)}) collective-permute-start(bf16[256,512]{1,0:T(8,128)(2,1)S(1)} %collective-permute-done.18.refs_18_), channel_id=1, source_target_pairs={{0,16},{16,0},{1,17},{17,1},{2,18},{18,2},{3,19},{19,3},{4,20},{20... | collective-permute-start | bytes 786440 | tf_op jit(solution)/shard_map/ppermute | solution.py:189
  85.0 7.4 %collective-permute-start.22 = (bf16[128,512]{1,0:T(8,128)(2,1)S(1)}, bf16[128,512]{1,0:T(8,128)(2,1)S(1)}, u32[]{:S(2)}, u32[]{:S(2)}) collective-permute-start(bf16[128,512]{1,0:T(8,128)(2,1)S(1)} %get-tuple-element.37), channel_id=1, source_target_pairs={{0,3},{1,2},{2,1},{3,0},{4,7},{5,6},{6,5},{7,4},{8,11},{9,10},{10,... | collective-permute-start | bytes 393224 | tf_op jit(solution)/shard_map/ppermute | solution.py:183
  88.5 6.6 %collective-permute-start.21 = (bf16[128,512]{1,0:T(8,128)(2,1)S(1)}, bf16[128,512]{1,0:T(8,128)(2,1)S(1)}, u32[]{:S(2)}, u32[]{:S(2)}) collective-permute-start(bf16[128,512]{1,0:T(8,128)(2,1)S(1)} %get-tuple-element.36), channel_id=1, source_target_pairs={{0,2},{1,3},{2,0},{3,1},{4,6},{5,7},{6,4},{7,5},{8,10},{9,11},{10,... | collective-permute-start | bytes 393224 | tf_op jit(solution)/shard_map/ppermute | solution.py:183
  88.7 6.4 %collective-permute-start.20 = (bf16[128,512]{1,0:T(8,128)(2,1)S(1)}, bf16[128,512]{1,0:T(8,128)(2,1)S(1)}, u32[]{:S(2)}, u32[]{:S(2)}) collective-permute-start(bf16[128,512]{1,0:T(8,128)(2,1)S(1)} %get-tuple-element.35), channel_id=1, source_target_pairs={{0,1},{1,0},{2,3},{3,2},{4,5},{5,4},{6,7},{7,6},{8,9},{9,8},{10,11... | collective-permute-start | bytes 393224 | tf_op jit(solution)/shard_map/ppermute | solution.py:183
  (7 other events, 82.6 us)

commit v5 on v4

v5 whole, which is shorter than its diff:
```python
from functools import partial

import jax
import jax.numpy as jnp
from jax import lax
from jax.experimental import pallas as pl
from jax.experimental.pallas import tpu as pltpu
from jax.sharding import PartitionSpec as P

decay_first = 0.9
decay_second = 0.95
inner_rate = 0.006
epsilon = 1e-08
outer_rate = 0.7
outer_decay = 0.9

PLANES = 4
PARTS = 2
CHUNK = 32
CONTRACT_ROWS = (((0,), (0,)), ((), ()))
VMEM_BYTES = 16 * 1024 * 1024


def outer_update(average, anchor_rows, momentum_rows):
    velocity = outer_decay * momentum_rows + average
    return (anchor_rows - outer_rate * (average + outer_decay * velocity)).astype(jnp.bfloat16)


def inner_update(gradient, inner_weights, first_moment, second_moment, anchor):
    first_next = decay_first * first_moment + (1.0 - decay_first) * gradient
    second_next = decay_second * second_moment + (1.0 - decay_second) * gradient * gradient
    stepped = inner_weights - inner_rate * first_next / (jnp.sqrt(second_next) + epsilon)
    return first_next, anchor - stepped


def general(acts, value_cots, inner_weights, first_moment, second_moment, anchor, outer_momentum):
    tokens_local = acts[0]
    columns = lax.all_to_all(tokens_local, "fsdp", split_axis=1, concat_axis=0, tiled=True)
    cots = lax.all_gather(value_cots[0], "fsdp", axis=0, tiled=True)
    gradient = lax.dot_general(columns, cots, CONTRACT_ROWS, preferred_element_type=jnp.float32)
    first_next, drift = inner_update(gradient, inner_weights[0], first_moment[0], second_moment[0], anchor)
    average = lax.psum(drift, "rep") / lax.axis_size("rep")
    weights_next = outer_update(average, anchor, outer_momentum)
    gathered = lax.all_gather(weights_next, "fsdp", axis=0, tiled=True)
    values = jnp.dot(tokens_local, gathered, preferred_element_type=jnp.float32)
    return (first_next[None], values.astype(jnp.bfloat16)[None])


def flip(at, bits):
    low = lax.rem(at, 2)
    return (at // 2 + bits // 2 - 2 * (at // 2) * (bits // 2)) * 2 + low + bits % 2 - 2 * low * (bits % 2)


def call(kernel, name, out, inputs, flops, scratch=(), after=()):
    moved = sum(x.size * x.dtype.itemsize for x in list(inputs) + list(out))
    count = len(inputs)

    def without_after(*refs):
        kernel(*refs[:count], *refs[count + len(after) :])

    return pl.pallas_call(
        without_after,
        out_shape=out,
        in_specs=[pl.BlockSpec(memory_space=pltpu.VMEM)] * count + [pl.BlockSpec(memory_space=pl.ANY)] * len(after),
        out_specs=[pl.BlockSpec(memory_space=pltpu.VMEM)] * len(out),
        scratch_shapes=list(scratch),
        compiler_params=pltpu.CompilerParams(vmem_limit_bytes=VMEM_BYTES),
        cost_estimate=pl.CostEstimate(flops=flops, bytes_accessed=moved, transcendentals=0),
        name=name,
    )(*inputs, *after)


def repack_kernel(inner, rows, messages, acts_ref, cots_ref, *outs):
    f = lax.axis_index("fsdp")
    o, i = f // inner, lax.rem(f, inner)
    for number, (planes, columns) in enumerate(messages):
        for k in range(inner):
            out = outs[number * inner + k]
            for slot, bits in enumerate(planes):
                start = pl.multiple_of((flip(o, bits) * inner + flip(i, k)) * rows, rows)
                out[:, slot * rows : (slot + 1) * rows] = acts_ref[:, pl.ds(start, rows)]
            if columns:
                out[:, len(planes) * rows :] = cots_ref[:, columns[0] : columns[1]]


def repack(acts, cots, inner, rows, messages, after=()):
    tokens = acts.shape[0]
    out = []
    for planes, columns in messages:
        wide = len(planes) * rows + (columns[1] - columns[0] if columns else 0)
        out += [jax.ShapeDtypeStruct((tokens, wide), jnp.bfloat16)] * inner
    got = call(partial(repack_kernel, inner, rows, messages), "repack", out, [acts, cots], 0, after=after)
    return [got[n * inner : (n + 1) * inner] for n in range(len(messages))]


def gradient_kernel(inner, rows, acts_at, cots_at, *refs):
    acts_refs, cots_refs, added, out = refs[:inner], refs[inner : 2 * inner], refs[2 * inner : -1], refs[-1]
    columns = jnp.concatenate([ref[:, acts_at : acts_at + rows] for ref in acts_refs], axis=0)
    cots = jnp.concatenate([ref[:, cots_at : cots_at + out.shape[1]] for ref in cots_refs], axis=0)
    total = lax.dot_general(columns, cots, CONTRACT_ROWS, preferred_element_type=jnp.float32)
    for ref in added:
        total += ref[...].astype(jnp.float32)
    out[...] = total.astype(out.dtype)


def gradient_at(at, refs):
    total, beside, far = refs
    return total[at, :] + beside[at, :].astype(jnp.float32) + far[at, :].astype(jnp.float32)


def drift_kernel(columns, *refs):
    gradient_refs, (weights, first, second, anchor), drift_ref = refs[:3], refs[3:7], refs[7]
    cols = slice(*columns)

    @pl.loop(0, drift_ref.shape[0] // CHUNK)
    def _(step):
        at = pl.ds(pl.multiple_of(step * CHUNK, CHUNK), CHUNK)
        state = (weights[at, cols], first[at, cols], second[at, cols], anchor[at, cols])
        drift_ref[at, :] = inner_update(gradient_at(at, gradient_refs), *state)[1]


def moment_kernel(parts, *refs):
    first, out = refs[-2:]
    width = out.shape[1] // parts

    @pl.loop(0, out.shape[0] // CHUNK)
    def _(step):
        at = pl.ds(pl.multiple_of(step * CHUNK, CHUNK), CHUNK)
        for part in range(parts):
            gradient = gradient_at(at, refs[3 * part : 3 * part + 3])
            cols = slice(part * width, (part + 1) * width)
            out[at, cols] = decay_first * first[at, cols] + (1.0 - decay_first) * gradient


def outer_kernel(columns, drift, other, anchor, momentum, out, mine):
    half = mine.shape[0]
    cols = slice(*columns)

    @pl.loop(0, out.shape[0] // CHUNK)
    def _(step):
        at = pl.ds(pl.multiple_of(step * CHUNK, CHUNK), CHUNK)
        out[at, :] = outer_update((drift[at, :] + other[at, :]) / 2, anchor[at, cols], momentum[at, cols])

    mine[...] = out[pl.ds(pl.multiple_of(lax.axis_index("rep") * half, half), half), :]


def values_kernel(inner, rows, places, *refs):
    messages = [refs[n * inner : (n + 1) * inner] for n in range(PLANES)]
    refs = refs[PLANES * inner :]
    pieces, own_ref, sent_refs, weights = refs[:7], refs[7], refs[8:-1], refs[-1]
    half = rows // 2
    r = lax.axis_index("rep")
    weights[:rows] = pieces[0][...]
    for bits in range(1, PLANES):
        for which, piece in ((r, pieces[2 * bits - 1]), (1 - r, pieces[2 * bits])):
            weights[pl.ds(pl.multiple_of(bits * rows + which * half, half), half), :] = piece[...]
    for k in range(inner):
        blocks = [messages[number][k][:, at : at + rows] for number, at in places]
        total = jnp.dot(jnp.concatenate(blocks, axis=1), weights[...], preferred_element_type=jnp.float32)
        if k == 0:
            own_ref[...] = total
        else:
            sent_refs[k - 1][...] = total.astype(jnp.bfloat16)


def sum_kernel(parts, *refs):
    terms, out = refs[:-1], refs[-1]
    each, width = len(terms) // parts, out.shape[1] // parts
    for part in range(parts):
        total = terms[part * each][...]
        for ref in terms[part * each + 1 : (part + 1) * each]:
            total += ref[...].astype(jnp.float32)
        out[:, part * width : (part + 1) * width] = total.astype(out.dtype)


def on_device(acts, value_cots, inner_weights, first_moment, second_moment, anchor, outer_momentum):
    inner = lax.axis_size("fsdp") // PLANES
    rows, width = anchor.shape
    if inner != 4 or lax.axis_size("rep") != 2 or rows % 256 or width % (128 * PARTS):
        return general(acts, value_cots, inner_weights, first_moment, second_moment, anchor, outer_momentum)
    tokens = acts.shape[1]
    half = rows // 2
    part_width = width // PARTS

    def planes(x, bits):
        return lax.ppermute(x, "fsdp", [(p * inner + i, (p ^ bits) * inner + i) for p in range(PLANES) for i in range(inner)])

    def across(x, k):
        return lax.ppermute(x, "fsdp", [(p * inner + i, p * inner + (i ^ k)) for p in range(PLANES) for i in range(inner)])

    def around(blocks):
        return [blocks[0]] + [across(blocks[k], k) for k in range(1, inner)]

    def swap(x):
        return lax.ppermute(x, "rep", [(0, 1), (1, 0)])

    wanted = [((3,), (0, part_width)), ((1,), None), ((2,), None), ((0,), (part_width, width) if PARTS > 1 else None)]
    places = [(3, 0), (1, 0), (2, 0), (0, 0)]
    messages, arrived = [], []
    for message in wanted:
        (packed,) = repack(acts[0], value_cots[0], inner, rows, [message], arrived)
        messages.append(around(packed))
        arrived = messages[-1][1:2]

    def gradient(bits, part, dtype, *added):
        number, at = places[bits]
        cots, cots_at = (messages[0], rows) if part == 0 else (messages[3], rows + (part - 1) * part_width)
        out = jax.ShapeDtypeStruct((rows, part_width), dtype)
        kernel = partial(gradient_kernel, inner, rows, at, cots_at)
        flops = 2 * inner * tokens * rows * part_width
        return call(kernel, "gradient", [out], messages[number] + cots + list(added), flops)[0]

    state = [inner_weights[0], first_moment[0], second_moment[0], anchor]
    block = jax.ShapeDtypeStruct((rows, part_width), jnp.float32)
    new_block = jax.ShapeDtypeStruct((rows, part_width), jnp.bfloat16)
    new_half = jax.ShapeDtypeStruct((half, part_width), jnp.bfloat16)
    full = jax.ShapeDtypeStruct((rows, width), jnp.float32)
    gradients, terms, earlier = [], [], []
    for part in range(PARTS):
        columns = (part * part_width, (part + 1) * part_width)
        beside_far = planes(gradient(3, part, jnp.bfloat16), 1)
        beside = planes(gradient(1, part, jnp.bfloat16), 1)
        far = planes(gradient(2, part, jnp.bfloat16, beside_far), 2)
        known = [gradient(0, part, jnp.float32), beside, far]
        gradients += known
        (drift,) = call(partial(drift_kernel, columns), "drift", [block], known + state, 0, after=earlier)
        first_next = []
        if part == PARTS - 1:
            first_next = call(partial(moment_kernel, PARTS), "moment", [full], gradients + [first_moment[0]], 0)
        new, mine = call(
            partial(outer_kernel, columns),
            "outer",
            [new_block, new_half],
            [drift, swap(drift), anchor, outer_momentum],
            0,
            after=first_next,
        )
        mine2 = planes(mine, 2)
        mine1 = planes(mine, 1)
        mine3 = planes(mine2, 1)
        earlier = [mine1, mine2]
        pieces = [new] + [y for x in (mine1, mine2, mine3) for y in (x, swap(x))]
        sums = jax.ShapeDtypeStruct((tokens, part_width), jnp.bfloat16)
        own, *sent = call(
            partial(values_kernel, inner, rows, places),
            "values",
            [jax.ShapeDtypeStruct((tokens, part_width), jnp.float32)] + [sums] * (inner - 1),
            sum(messages, []) + pieces,
            2 * inner * tokens * PLANES * rows * part_width,
            [pltpu.VMEM((PLANES * rows, part_width), jnp.bfloat16)],
        )
        terms += [own] + [across(sent[k - 1], k) for k in range(1, inner)]
    whole = jax.ShapeDtypeStruct((tokens, width), jnp.bfloat16)
    (values,) = call(partial(sum_kernel, PARTS), "sum", [whole], terms, 0)
    return (first_next[0][None], values[None])


def solution(mesh):
    placed = (
        P("rep", "fsdp", None),
        P("rep", "fsdp", None),
        P("rep", "fsdp", None),
        P("rep", "fsdp", None),
        P("rep", "fsdp", None),
        P("fsdp", None),
        P("fsdp", None),
    )
    return jax.shard_map(
        on_device,
        mesh=mesh,
        in_specs=placed,
        out_specs=(P("rep", "fsdp", None), P("rep", "fsdp", None)),
        check_vma=False,
    )
```

time: 96.1 us -> 110 us (1.14)
  starting transfers between devices: 27 us -> 39 us
  Pallas kernels: 5.92 us -> 8.58 us
  local copies, waits for them, and re-layouts: 2.52 us -> 3.75 us
  waiting for transfers between devices: 59 us -> 57.8 us
    ppermute x12 -> x18, starting transfers between devices: 15.7 us -> 24.6 us  [across(): lax.ppermute(x, 'fsdp', [(p * inner + i, p * inner + (i ^ k)) for p in ra...]
    ppermute x12 -> x18, waiting for transfers between devices: 32.3 us -> 23.5 us  [across(): lax.ppermute(x, 'fsdp', [(p * inner + i, p * inner + (i ^ k)) for p in ra...]
    ppermute x6 -> x12, waiting for transfers between devices: 24.8 us -> 33.7 us  [planes(): lax.ppermute(x, 'fsdp', [(p * inner + i, (p ^ bits) * inner + i) for p in...]
    ppermute x6 -> x12, starting transfers between devices: 10.7 us -> 13.8 us  [planes(): lax.ppermute(x, 'fsdp', [(p * inner + i, (p ^ bits) * inner + i) for p in...]
    pallas_call x10 -> x20, Pallas kernels: 5.92 us -> 8.58 us  [call(): pl.pallas_call(without_after, out_shape=out, in_specs=[pl.BlockSpec(memor...]
    unnamed x16 -> x18, local copies, waits for them, and re-layouts: 2.52 us -> 3.75 us
    ppermute x5 -> x8, waiting for transfers between devices: 1.77 us -> 0.63 us  [swap(): return lax.ppermute(x, 'rep', [(0, 1), (1, 0)])]
  transfers between devices with their start and end apart: 23 -> 38, of which waited for: 15 -> 20; matrix products, arithmetic and copies ran while one was open for 0% -> 0% of each run, Pallas kernels for 3% -> 6%
where the time goes in v5:
time: 110 us
  waiting for transfers between devices  57.8 us (53%)
  starting transfers between devices  39 us (35%)
  Pallas kernels  8.58 us (8%)
  local copies, waits for them, and re-layouts  3.75 us (3%)
    ppermute x12, waiting for transfers between devices, planes(): lax.ppermute(x, 'fsdp', [(p * inner + i, (p ^ bits) * inner + i) for p in...  33.7 us
    ppermute x18, starting transfers between devices, across(): lax.ppermute(x, 'fsdp', [(p * inner + i, p * inner + (i ^ k)) for p in ra...  24.6 us
    ppermute x18, waiting for transfers between devices, across(): lax.ppermute(x, 'fsdp', [(p * inner + i, p * inner + (i ^ k)) for p in ra...  23.5 us
    ppermute x12, starting transfers between devices, planes(): lax.ppermute(x, 'fsdp', [(p * inner + i, (p ^ bits) * inner + i) for p in...  13.8 us
    pallas_call x20, Pallas kernels, call(): pl.pallas_call(without_after, out_shape=out, in_specs=[pl.BlockSpec(memor...  8.58 us
    unnamed x18, local copies, waits for them, and re-layouts  3.75 us
  transfers between devices with their start and end apart: 38, of which 20 were waited for; matrix products, arithmetic and copies ran while one was open for 0% of the time, Pallas kernels for 6%

profile of v5, /device:TPU:0, one launch (start us, length us, event | category | flops | bytes accessed | tf_op | source)
XLA Modules:
  0.0 110.0 jit_solution(13777433792062729014)
XLA Ops:
  3.2 3.0 %collective-permute-start = (bf16[128,768]{1,0:T(8,128)(2,1)S(1)}, bf16[128,768]{1,0:T(8,128)(2,1)S(1)}, u32[]{:S(2)}, u32[]{:S(2)}) collective-permute-start(bf16[128,768]{1,0:T(8,128)(2,1)S(1)} %get-tuple-element.30), channel_id=1, source_target_pairs={{0,1},{1,0},{2,3},{3,2},{4,5},{5,4},{6,7},{7,6},{8,9},{9,8},{10,11... | collective-permute-start | bytes 589832 | tf_op jit(solution)/shard_map/ppermute | solution.py:189
  7.7 4.2 %collective-permute-done.refs_2_.refs_5_.refs_1_ = bf16[128,768]{1,0:T(8,128)(2,1)S(1)} collective-permute-done((bf16[128,768]{1,0:T(8,128)(2,1)S(1)}, bf16[128,768]{1,0:T(8,128)(2,1)S(1)}, u32[]{:S(2)}, u32[]{:S(2)}) %collective-permute-start) | collective-permute-done | bytes 196640 | tf_op jit(solution)/shard_map/ppermute | solution.py:189
  12.0 2.1 %collective-permute-start.1 = (bf16[128,512]{1,0:T(8,128)(2,1)S(1)}, bf16[128,512]{1,0:T(8,128)(2,1)S(1)}, u32[]{:S(2)}, u32[]{:S(2)}) collective-permute-start(bf16[128,512]{1,0:T(8,128)(2,1)S(1)} %get-tuple-element.31), channel_id=1, source_target_pairs={{0,1},{1,0},{2,3},{3,2},{4,5},{5,4},{6,7},{7,6},{8,9},{9,8},{10,11... | collective-permute-start | bytes 393224 | tf_op jit(solution)/shard_map/ppermute | solution.py:189
  14.1 1.7 %collective-permute-done.6.refs_6_.refs_2_ = bf16[128,768]{1,0:T(8,128)(2,1)S(1)} collective-permute-done((bf16[128,768]{1,0:T(8,128)(2,1)S(1)}, bf16[128,768]{1,0:T(8,128)(2,1)S(1)}, u32[]{:S(2)}, u32[]{:S(2)}) %collective-permute-start.6) | collective-permute-done | bytes 196640 | tf_op jit(solution)/shard_map/ppermute | solution.py:189
  15.8 1.9 %collective-permute-done.7.refs_7_.refs_3_ = bf16[128,768]{1,0:T(8,128)(2,1)S(1)} collective-permute-done((bf16[128,768]{1,0:T(8,128)(2,1)S(1)}, bf16[128,768]{1,0:T(8,128)(2,1)S(1)}, u32[]{:S(2)}, u32[]{:S(2)}) %collective-permute-start.7) | collective-permute-done | bytes 196640 | tf_op jit(solution)/shard_map/ppermute | solution.py:189
  18.1 1.6 %collective-permute-start.13 = (bf16[512,256]{1,0:T(8,128)(2,1)S(1)}, bf16[512,256]{1,0:T(8,128)(2,1)S(1)}, u32[]{:S(2)}, u32[]{:S(2)}) collective-permute-start(bf16[512,256]{1,0:T(8,128)(2,1)S(1)} %gradient.10), channel_id=1, source_target_pairs={{0,4},{1,5},{2,6},{3,7},{4,0},{5,1},{6,2},{7,3},{8,12},{9,13},{10,... | collective-permute-start | bytes 786440 | tf_op jit(solution)/shard_map/ppermute | solution.py:186
  20.3 2.3 %collective-permute-start.9 = (bf16[128,512]{1,0:T(8,128)(2,1)S(1)}, bf16[128,512]{1,0:T(8,128)(2,1)S(1)}, u32[]{:S(2)}, u32[]{:S(2)}) collective-permute-start(bf16[128,512]{1,0:T(8,128)(2,1)S(1)} %get-tuple-element.42), channel_id=1, source_target_pairs={{0,3},{1,2},{2,1},{3,0},{4,7},{5,6},{6,5},{7,4},{8,11},{9,10},{10,... | collective-permute-start | bytes 393224 | tf_op jit(solution)/shard_map/ppermute | solution.py:189
  23.9 3.6 %collective-permute-done.8.refs_2_.refs_6_ = bf16[128,512]{1,0:T(8,128)(2,1)S(1)} collective-permute-done((bf16[128,512]{1,0:T(8,128)(2,1)S(1)}, bf16[128,512]{1,0:T(8,128)(2,1)S(1)}, u32[]{:S(2)}, u32[]{:S(2)}) %collective-permute-start.8) | collective-permute-done | bytes 131104 | tf_op jit(solution)/shard_map/ppermute | solution.py:189
  27.5 2.9 %collective-permute-start.12 = (bf16[128,512]{1,0:T(8,128)(2,1)S(1)}, bf16[128,512]{1,0:T(8,128)(2,1)S(1)}, u32[]{:S(2)}, u32[]{:S(2)}) collective-permute-start(bf16[128,512]{1,0:T(8,128)(2,1)S(1)} %get-tuple-element.45), channel_id=1, source_target_pairs={{0,3},{1,2},{2,1},{3,0},{4,7},{5,6},{6,5},{7,4},{8,11},{9,10},{10,... | collective-permute-start | bytes 393224 | tf_op jit(solution)/shard_map/ppermute | solution.py:189
  31.3 2.1 %collective-permute-done.12.refs_3_.refs_11_ = bf16[128,512]{1,0:T(8,128)(2,1)S(1)} collective-permute-done((bf16[128,512]{1,0:T(8,128)(2,1)S(1)}, bf16[128,512]{1,0:T(8,128)(2,1)S(1)}, u32[]{:S(2)}, u32[]{:S(2)}) %collective-permute-start.12) | collective-permute-done | bytes 131104 | tf_op jit(solution)/shard_map/ppermute | solution.py:189
  33.7 3.8 %collective-permute-start.14 = (bf16[512,256]{1,0:T(8,128)(2,1)S(1)}, bf16[512,256]{1,0:T(8,128)(2,1)S(1)}, u32[]{:S(2)}, u32[]{:S(2)}) collective-permute-start(bf16[512,256]{1,0:T(8,128)(2,1)S(1)} %gradient.11), channel_id=1, source_target_pairs={{0,8},{1,9},{2,10},{3,11},{4,12},{5,13},{6,14},{7,15},{8,0},{9,1},... | collective-permute-start | bytes 786440 | tf_op jit(solution)/shard_map/ppermute | solution.py:186
  39.0 2.3 %collective-permute-start.4 = (bf16[128,768]{1,0:T(8,128)(2,1)S(1)}, bf16[128,768]{1,0:T(8,128)(2,1)S(1)}, u32[]{:S(2)}, u32[]{:S(2)}) collective-permute-start(bf16[128,768]{1,0:T(8,128)(2,1)S(1)} %get-tuple-element.35), channel_id=1, source_target_pairs={{0,2},{1,3},{2,0},{3,1},{4,6},{5,7},{6,4},{7,5},{8,10},{9,11},{10,... | collective-permute-start | bytes 589832 | tf_op jit(solution)/shard_map/ppermute | solution.py:189
  41.3 2.0 %collective-permute-done.3.refs_1_.refs_5_.refs_13_ = bf16[128,768]{1,0:T(8,128)(2,1)S(1)} collective-permute-done((bf16[128,768]{1,0:T(8,128)(2,1)S(1)}, bf16[128,768]{1,0:T(8,128)(2,1)S(1)}, u32[]{:S(2)}, u32[]{:S(2)}) %collective-permute-start.3) | collective-permute-done | bytes 196640 | tf_op jit(solution)/shard_map/ppermute | solution.py:189
  43.3 3.3 %collective-permute-done.4.refs_2_.refs_6_.refs_14_ = bf16[128,768]{1,0:T(8,128)(2,1)S(1)} collective-permute-done((bf16[128,768]{1,0:T(8,128)(2,1)S(1)}, bf16[128,768]{1,0:T(8,128)(2,1)S(1)}, u32[]{:S(2)}, u32[]{:S(2)}) %collective-permute-start.4) | collective-permute-done | bytes 196640 | tf_op jit(solution)/shard_map/ppermute | solution.py:189
  51.9 6.7 %collective-permute-done.16.refs_8_ = bf16[512,256]{1,0:T(8,128)(2,1)S(1)} collective-permute-done((bf16[512,256]{1,0:T(8,128)(2,1)S(1)}, bf16[512,256]{1,0:T(8,128)(2,1)S(1)}, u32[]{:S(2)}, u32[]{:S(2)}) %collective-permute-start.16) | collective-permute-done | bytes 262176 | tf_op jit(solution)/shard_map/ppermute | solution.py:186
  59.3 3.0 %collective-permute-start.21 = (bf16[256,256]{1,0:T(8,128)(2,1)S(1)}, bf16[256,256]{1,0:T(8,128)(2,1)S(1)}, u32[]{:S(2)}, u32[]{:S(2)}) collective-permute-start(bf16[256,256]{1,0:T(8,128)(2,1)S(1)} %get-tuple-element.47), channel_id=1, source_target_pairs={{0,8},{1,9},{2,10},{3,11},{4,12},{5,13},{6,14},{7,15},{8,0},{9,1},... | collective-permute-start | bytes 393224 | tf_op jit(solution)/shard_map/ppermute | solution.py:186
  63.1 2.6 %collective-permute-done.15.refs_4_.refs_1_ = bf16[512,256]{1,0:T(8,128)(2,1)S(1)} collective-permute-done((bf16[512,256]{1,0:T(8,128)(2,1)S(1)}, bf16[512,256]{1,0:T(8,128)(2,1)S(1)}, u32[]{:S(2)}, u32[]{:S(2)}) %collective-permute-start.15) | collective-permute-done | bytes 262176 | tf_op jit(solution)/shard_map/ppermute | solution.py:186
  65.7 11.5 %collective-permute-done.17.refs_5_.refs_2_ = bf16[512,256]{1,0:T(8,128)(2,1)S(1)} collective-permute-done((bf16[512,256]{1,0:T(8,128)(2,1)S(1)}, bf16[512,256]{1,0:T(8,128)(2,1)S(1)}, u32[]{:S(2)}, u32[]{:S(2)}) %collective-permute-start.17) | collective-permute-done | bytes 262176 | tf_op jit(solution)/shard_map/ppermute | solution.py:186
  85.0 4.8 %collective-permute-done.31.refs_19_ = bf16[256,256]{1,0:T(8,128)(2,1)S(1)} collective-permute-done((bf16[256,256]{1,0:T(8,128)(2,1)S(1)}, bf16[256,256]{1,0:T(8,128)(2,1)S(1)}, u32[]{:S(2)}, u32[]{:S(2)}) %collective-permute-start.31) | collective-permute-done | bytes 131104 | tf_op jit(solution)/shard_map/ppermute | solution.py:186
  89.8 2.3 %collective-permute-done.23.refs_21_ = bf16[256,256]{1,0:T(8,128)(2,1)S(1)} collective-permute-done((bf16[256,256]{1,0:T(8,128)(2,1)S(1)}, bf16[256,256]{1,0:T(8,128)(2,1)S(1)}, u32[]{:S(2)}, u32[]{:S(2)}) %collective-permute-start.23) | collective-permute-done | bytes 131104 | tf_op jit(solution)/shard_map/ppermute | solution.py:186
  92.6 2.3 %collective-permute-done.29.refs_17_ = bf16[256,256]{1,0:T(8,128)(2,1)S(1)} collective-permute-done((bf16[256,256]{1,0:T(8,128)(2,1)S(1)}, bf16[256,256]{1,0:T(8,128)(2,1)S(1)}, u32[]{:S(2)}, u32[]{:S(2)}) %collective-permute-start.29) | collective-permute-done | bytes 131104 | tf_op jit(solution)/shard_map/ppermute | solution.py:186
  94.9 2.0 %collective-permute-done.33.refs_21_ = bf16[256,256]{1,0:T(8,128)(2,1)S(1)} collective-permute-done((bf16[256,256]{1,0:T(8,128)(2,1)S(1)}, bf16[256,256]{1,0:T(8,128)(2,1)S(1)}, u32[]{:S(2)}, u32[]{:S(2)}) %collective-permute-start.33) | collective-permute-done | bytes 131104 | tf_op jit(solution)/shard_map/ppermute | solution.py:186
  99.7 1.7 %collective-permute-start.27 = (bf16[128,256]{1,0:T(8,128)(2,1)S(1)}, bf16[128,256]{1,0:T(8,128)(2,1)S(1)}, u32[]{:S(2)}, u32[]{:S(2)}) collective-permute-start(bf16[128,256]{1,0:T(8,128)(2,1)S(1)} %get-tuple-element.51), channel_id=1, source_target_pairs={{0,3},{1,2},{2,1},{3,0},{4,7},{5,6},{6,5},{7,4},{8,11},{9,10},{10,... | collective-permute-start | bytes 196616 | tf_op jit(solution)/shard_map/ppermute | solution.py:189
  104.2 1.7 %collective-permute-start.37 = (bf16[128,256]{1,0:T(8,128)(2,1)S(1)}, bf16[128,256]{1,0:T(8,128)(2,1)S(1)}, u32[]{:S(2)}, u32[]{:S(2)}) collective-permute-start(bf16[128,256]{1,0:T(8,128)(2,1)S(1)} %get-tuple-element.57), channel_id=1, source_target_pairs={{0,3},{1,2},{2,1},{3,0},{4,7},{5,6},{6,5},{7,4},{8,11},{9,10},{10,... | collective-permute-start | bytes 196616 | tf_op jit(solution)/shard_map/ppermute | solution.py:189
  (90 shorter events, 33.7 us)
Async XLA Ops:
  3.2 8.7 %collective-permute-start = (bf16[128,768]{1,0:T(8,128)(2,1)S(1)}, bf16[128,768]{1,0:T(8,128)(2,1)S(1)}, u32[]{:S(2)}, u32[]{:S(2)}) collective-permute-start(bf16[128,768]{1,0:T(8,128)(2,1)S(1)} %get-tuple-element.30), channel_id=1, source_target_pairs={{0,1},{1,0},{2,3},{3,2},{4,5},{5,4},{6,7},{7,6},{8,9},{9,8},{10,11... | collective-permute-start | bytes 589832 | tf_op jit(solution)/shard_map/ppermute | solution.py:189
  6.2 9.6 %collective-permute-start.6 = (bf16[128,768]{1,0:T(8,128)(2,1)S(1)}, bf16[128,768]{1,0:T(8,128)(2,1)S(1)}, u32[]{:S(2)}, u32[]{:S(2)}) collective-permute-start(bf16[128,768]{1,0:T(8,128)(2,1)S(1)} %get-tuple-element.38), channel_id=1, source_target_pairs={{0,2},{1,3},{2,0},{3,1},{4,6},{5,7},{6,4},{7,5},{8,10},{9,11},{10,... | collective-permute-start | bytes 589832 | tf_op jit(solution)/shard_map/ppermute | solution.py:189
  7.7 10.0 %collective-permute-start.7 = (bf16[128,768]{1,0:T(8,128)(2,1)S(1)}, bf16[128,768]{1,0:T(8,128)(2,1)S(1)}, u32[]{:S(2)}, u32[]{:S(2)}) collective-permute-start(bf16[128,768]{1,0:T(8,128)(2,1)S(1)} %get-tuple-element.39), channel_id=1, source_target_pairs={{0,3},{1,2},{2,1},{3,0},{4,7},{5,6},{6,5},{7,4},{8,11},{9,10},{10,... | collective-permute-start | bytes 589832 | tf_op jit(solution)/shard_map/ppermute | solution.py:189
  12.0 10.6 %collective-permute-start.1 = (bf16[128,512]{1,0:T(8,128)(2,1)S(1)}, bf16[128,512]{1,0:T(8,128)(2,1)S(1)}, u32[]{:S(2)}, u32[]{:S(2)}) collective-permute-start(bf16[128,512]{1,0:T(8,128)(2,1)S(1)} %get-tuple-element.31), channel_id=1, source_target_pairs={{0,1},{1,0},{2,3},{3,2},{4,5},{5,4},{6,7},{7,6},{8,9},{9,8},{10,11... | collective-permute-start | bytes 393224 | tf_op jit(solution)/shard_map/ppermute | solution.py:189
  18.1 13.2 %collective-permute-start.13 = (bf16[512,256]{1,0:T(8,128)(2,1)S(1)}, bf16[512,256]{1,0:T(8,128)(2,1)S(1)}, u32[]{:S(2)}, u32[]{:S(2)}) collective-permute-start(bf16[512,256]{1,0:T(8,128)(2,1)S(1)} %gradient.10), channel_id=1, source_target_pairs={{0,4},{1,5},{2,6},{3,7},{4,0},{5,1},{6,2},{7,3},{8,12},{9,13},{10,... | collective-permute-start | bytes 786440 | tf_op jit(solution)/shard_map/ppermute | solution.py:186
  19.7 7.8 %collective-permute-start.8 = (bf16[128,512]{1,0:T(8,128)(2,1)S(1)}, bf16[128,512]{1,0:T(8,128)(2,1)S(1)}, u32[]{:S(2)}, u32[]{:S(2)}) collective-permute-start(bf16[128,512]{1,0:T(8,128)(2,1)S(1)} %get-tuple-element.41), channel_id=1, source_target_pairs={{0,2},{1,3},{2,0},{3,1},{4,6},{5,7},{6,4},{7,5},{8,10},{9,11},{10,... | collective-permute-start | bytes 393224 | tf_op jit(solution)/shard_map/ppermute | solution.py:189
  20.3 10.1 %collective-permute-start.9 = (bf16[128,512]{1,0:T(8,128)(2,1)S(1)}, bf16[128,512]{1,0:T(8,128)(2,1)S(1)}, u32[]{:S(2)}, u32[]{:S(2)}) collective-permute-start(bf16[128,512]{1,0:T(8,128)(2,1)S(1)} %get-tuple-element.42), channel_id=1, source_target_pairs={{0,3},{1,2},{2,1},{3,0},{4,7},{5,6},{6,5},{7,4},{8,11},{9,10},{10,... | collective-permute-start | bytes 393224 | tf_op jit(solution)/shard_map/ppermute | solution.py:189
  22.7 8.6 %collective-permute-start.2 = (bf16[128,512]{1,0:T(8,128)(2,1)S(1)}, bf16[128,512]{1,0:T(8,128)(2,1)S(1)}, u32[]{:S(2)}, u32[]{:S(2)}) collective-permute-start(bf16[128,512]{1,0:T(8,128)(2,1)S(1)} %get-tuple-element.32), channel_id=1, source_target_pairs={{0,1},{1,0},{2,3},{3,2},{4,5},{5,4},{6,7},{7,6},{8,9},{9,8},{10,11... | collective-permute-start | bytes 393224 | tf_op jit(solution)/shard_map/ppermute | solution.py:189
  23.3 8.0 %collective-permute-start.11 = (bf16[128,512]{1,0:T(8,128)(2,1)S(1)}, bf16[128,512]{1,0:T(8,128)(2,1)S(1)}, u32[]{:S(2)}, u32[]{:S(2)}) collective-permute-start(bf16[128,512]{1,0:T(8,128)(2,1)S(1)} %get-tuple-element.44), channel_id=1, source_target_pairs={{0,2},{1,3},{2,0},{3,1},{4,6},{5,7},{6,4},{7,5},{8,10},{9,11},{10,... | collective-permute-start | bytes 393224 | tf_op jit(solution)/shard_map/ppermute | solution.py:189
  30.7 17.5 %collective-permute-start.10 = (bf16[512,256]{1,0:T(8,128)(2,1)S(1)}, bf16[512,256]{1,0:T(8,128)(2,1)S(1)}, u32[]{:S(2)}, u32[]{:S(2)}) collective-permute-start(bf16[512,256]{1,0:T(8,128)(2,1)S(1)} %gradient.9), channel_id=1, source_target_pairs={{0,4},{1,5},{2,6},{3,7},{4,0},{5,1},{6,2},{7,3},{8,12},{9,13},{10,... | collective-permute-start | bytes 786440 | tf_op jit(solution)/shard_map/ppermute | solution.py:186
  33.7 14.5 %collective-permute-start.14 = (bf16[512,256]{1,0:T(8,128)(2,1)S(1)}, bf16[512,256]{1,0:T(8,128)(2,1)S(1)}, u32[]{:S(2)}, u32[]{:S(2)}) collective-permute-start(bf16[512,256]{1,0:T(8,128)(2,1)S(1)} %gradient.11), channel_id=1, source_target_pairs={{0,8},{1,9},{2,10},{3,11},{4,12},{5,13},{6,14},{7,15},{8,0},{9,1},... | collective-permute-start | bytes 786440 | tf_op jit(solution)/shard_map/ppermute | solution.py:186
  39.0 7.6 %collective-permute-start.4 = (bf16[128,768]{1,0:T(8,128)(2,1)S(1)}, bf16[128,768]{1,0:T(8,128)(2,1)S(1)}, u32[]{:S(2)}, u32[]{:S(2)}) collective-permute-start(bf16[128,768]{1,0:T(8,128)(2,1)S(1)} %get-tuple-element.35), channel_id=1, source_target_pairs={{0,2},{1,3},{2,0},{3,1},{4,6},{5,7},{6,4},{7,5},{8,10},{9,11},{10,... | collective-permute-start | bytes 589832 | tf_op jit(solution)/shard_map/ppermute | solution.py:189
  48.9 10.0 %collective-permute-start.18 = (f32[512,256]{1,0:T(8,128)S(1)}, f32[512,256]{1,0:T(8,128)S(1)}, u32[]{:S(2)}, u32[]{:S(2)}) collective-permute-start(f32[512,256]{1,0:T(8,128)S(1)} %drift.2.refs_0_), channel_id=1, source_target_pairs={{0,16},{16,0},{1,17},{17,1},{2,18},{18,2},{3,19},{19,3},{4,20},{20... | collective-permute-start | bytes 1572872 | tf_op jit(solution)/shard_map/ppermute | solution.py:195
  49.4 9.2 %collective-permute-start.16 = (bf16[512,256]{1,0:T(8,128)(2,1)S(1)}, bf16[512,256]{1,0:T(8,128)(2,1)S(1)}, u32[]{:S(2)}, u32[]{:S(2)}) collective-permute-start(bf16[512,256]{1,0:T(8,128)(2,1)S(1)} %gradient.14), channel_id=1, source_target_pairs={{0,4},{1,5},{2,6},{3,7},{4,0},{5,1},{6,2},{7,3},{8,12},{9,13},{10,... | collective-permute-start | bytes 786440 | tf_op jit(solution)/shard_map/ppermute | solution.py:186
  50.3 15.4 %collective-permute-start.15 = (bf16[512,256]{1,0:T(8,128)(2,1)S(1)}, bf16[512,256]{1,0:T(8,128)(2,1)S(1)}, u32[]{:S(2)}, u32[]{:S(2)}) collective-permute-start(bf16[512,256]{1,0:T(8,128)(2,1)S(1)} %gradient.13), channel_id=1, source_target_pairs={{0,4},{1,5},{2,6},{3,7},{4,0},{5,1},{6,2},{7,3},{8,12},{9,13},{10,... | collective-permute-start | bytes 786440 | tf_op jit(solution)/shard_map/ppermute | solution.py:186
  58.9 18.3 %collective-permute-start.17 = (bf16[512,256]{1,0:T(8,128)(2,1)S(1)}, bf16[512,256]{1,0:T(8,128)(2,1)S(1)}, u32[]{:S(2)}, u32[]{:S(2)}) collective-permute-start(bf16[512,256]{1,0:T(8,128)(2,1)S(1)} %gradient.15), channel_id=1, source_target_pairs={{0,8},{1,9},{2,10},{3,11},{4,12},{5,13},{6,14},{7,15},{8,0},{9,1},... | collective-permute-start | bytes 786440 | tf_op jit(solution)/shard_map/ppermute | solution.py:186
  59.3 19.4 %collective-permute-start.21 = (bf16[256,256]{1,0:T(8,128)(2,1)S(1)}, bf16[256,256]{1,0:T(8,128)(2,1)S(1)}, u32[]{:S(2)}, u32[]{:S(2)}) collective-permute-start(bf16[256,256]{1,0:T(8,128)(2,1)S(1)} %get-tuple-element.47), channel_id=1, source_target_pairs={{0,8},{1,9},{2,10},{3,11},{4,12},{5,13},{6,14},{7,15},{8,0},{9,1},... | collective-permute-start | bytes 393224 | tf_op jit(solution)/shard_map/ppermute | solution.py:186
  62.2 16.4 %collective-permute-start.19 = (bf16[256,256]{1,0:T(8,128)(2,1)S(1)}, bf16[256,256]{1,0:T(8,128)(2,1)S(1)}, u32[]{:S(2)}, u32[]{:S(2)}) collective-permute-start(bf16[256,256]{1,0:T(8,128)(2,1)S(1)} %get-tuple-element.47), channel_id=1, source_target_pairs={{0,4},{1,5},{2,6},{3,7},{4,0},{5,1},{6,2},{7,3},{8,12},{9,13},{10,... | collective-permute-start | bytes 393224 | tf_op jit(solution)/shard_map/ppermute | solution.py:186
  82.9 9.2 %collective-permute-start.23 = (bf16[256,256]{1,0:T(8,128)(2,1)S(1)}, bf16[256,256]{1,0:T(8,128)(2,1)S(1)}, u32[]{:S(2)}, u32[]{:S(2)}) collective-permute-start(bf16[256,256]{1,0:T(8,128)(2,1)S(1)} %collective-permute-done.21.refs_19_.refs_8_), channel_id=1, source_target_pairs={{0,4},{1,5},{2,6},{3,7},{4,0},{5,1},{6,2},{7,3},{8,12},{9,13},{10,... | collective-permute-start | bytes 393224 | tf_op jit(solution)/shard_map/ppermute | solution.py:186
  83.6 8.5 %collective-permute-start.22 = (bf16[256,256]{1,0:T(8,128)(2,1)S(1)}, bf16[256,256]{1,0:T(8,128)(2,1)S(1)}, u32[]{:S(2)}, u32[]{:S(2)}) collective-permute-start(bf16[256,256]{1,0:T(8,128)(2,1)S(1)} %collective-permute-done.21.refs_19_.refs_8_), channel_id=1, source_target_pairs={{0,16},{16,0},{1,17},{17,1},{2,18},{18,2},{3,19},{19,3},{4,20},{20... | collective-permute-start | bytes 393224 | tf_op jit(solution)/shard_map/ppermute | solution.py:195
  83.6 11.3 %collective-permute-start.29 = (bf16[256,256]{1,0:T(8,128)(2,1)S(1)}, bf16[256,256]{1,0:T(8,128)(2,1)S(1)}, u32[]{:S(2)}, u32[]{:S(2)}) collective-permute-start(bf16[256,256]{1,0:T(8,128)(2,1)S(1)} %get-tuple-element.53), channel_id=1, source_target_pairs={{0,4},{1,5},{2,6},{3,7},{4,0},{5,1},{6,2},{7,3},{8,12},{9,13},{10,... | collective-permute-start | bytes 393224 | tf_op jit(solution)/shard_map/ppermute | solution.py:186
  89.8 7.1 %collective-permute-start.20 = (bf16[256,256]{1,0:T(8,128)(2,1)S(1)}, bf16[256,256]{1,0:T(8,128)(2,1)S(1)}, u32[]{:S(2)}, u32[]{:S(2)}) collective-permute-start(bf16[256,256]{1,0:T(8,128)(2,1)S(1)} %collective-permute-done.19.refs_17_.refs_7_), channel_id=1, source_target_pairs={{0,16},{16,0},{1,17},{17,1},{2,18},{18,2},{3,19},{19,3},{4,20},{20... | collective-permute-start | bytes 393224 | tf_op jit(solution)/shard_map/ppermute | solution.py:195
  92.1 7.6 %collective-permute-start.32 = (bf16[256,256]{1,0:T(8,128)(2,1)S(1)}, bf16[256,256]{1,0:T(8,128)(2,1)S(1)}, u32[]{:S(2)}, u32[]{:S(2)}) collective-permute-start(bf16[256,256]{1,0:T(8,128)(2,1)S(1)} %collective-permute-done.31.refs_19_), channel_id=1, source_target_pairs={{0,16},{16,0},{1,17},{17,1},{2,18},{18,2},{3,19},{19,3},{4,20},{20... | collective-permute-start | bytes 393224 | tf_op jit(solution)/shard_map/ppermute | solution.py:195
  98.5 7.3 %collective-permute-start.26 = (bf16[128,256]{1,0:T(8,128)(2,1)S(1)}, bf16[128,256]{1,0:T(8,128)(2,1)S(1)}, u32[]{:S(2)}, u32[]{:S(2)}) collective-permute-start(bf16[128,256]{1,0:T(8,128)(2,1)S(1)} %get-tuple-element.50), channel_id=1, source_target_pairs={{0,2},{1,3},{2,0},{3,1},{4,6},{5,7},{6,4},{7,5},{8,10},{9,11},{10,... | collective-permute-start | bytes 196616 | tf_op jit(solution)/shard_map/ppermute | solution.py:189
  (23 other events, 163.8 us)

commit v6 on v0

v6 whole, which is shorter than its diff:
```python
from functools import partial

import jax
import jax.numpy as jnp
from jax import lax
from jax.experimental import pallas as pl
from jax.experimental.pallas import tpu as pltpu
from jax.sharding import PartitionSpec as P

decay_first = 0.9
decay_second = 0.95
inner_rate = 0.006
epsilon = 1e-08
outer_rate = 0.7
outer_decay = 0.9

PLANES = 4
CHUNK = 32
CONTRACT_ROWS = (((0,), (0,)), ((), ()))
AHEAD_FLOPS = 30 * 10**12
VMEM_BYTES = 16 * 1024 * 1024


def outer_update(average, anchor_rows, momentum_rows):
    velocity = outer_decay * momentum_rows + average
    return (anchor_rows - outer_rate * (average + outer_decay * velocity)).astype(jnp.bfloat16)


def inner_update(gradient, inner_weights, first_moment, second_moment, anchor):
    first_next = decay_first * first_moment + (1.0 - decay_first) * gradient
    second_next = decay_second * second_moment + (1.0 - decay_second) * gradient * gradient
    stepped = inner_weights - inner_rate * first_next / (jnp.sqrt(second_next) + epsilon)
    return first_next, anchor - stepped


def general(acts, value_cots, inner_weights, first_moment, second_moment, anchor, outer_momentum):
    tokens_local = acts[0]
    columns = lax.all_to_all(tokens_local, "fsdp", split_axis=1, concat_axis=0, tiled=True)
    cots = lax.all_gather(value_cots[0], "fsdp", axis=0, tiled=True)
    gradient = lax.dot_general(columns, cots, CONTRACT_ROWS, preferred_element_type=jnp.float32)
    first_next, drift = inner_update(gradient, inner_weights[0], first_moment[0], second_moment[0], anchor)
    average = lax.psum(drift, "rep") / lax.axis_size("rep")
    weights_next = outer_update(average, anchor, outer_momentum)
    gathered = lax.all_gather(weights_next, "fsdp", axis=0, tiled=True)
    values = jnp.dot(tokens_local, gathered, preferred_element_type=jnp.float32)
    return (first_next[None], values.astype(jnp.bfloat16)[None])


def flip(at, bits):
    low = lax.rem(at, 2)
    return (at // 2 + bits // 2 - 2 * (at // 2) * (bits // 2)) * 2 + low + bits % 2 - 2 * low * (bits % 2)


def call(kernel, name, out, inputs, flops, scratch=(), after=(), space=pltpu.VMEM):
    moved = sum(x.size * x.dtype.itemsize for x in list(inputs) + list(out))
    count = len(inputs)

    def without_after(*refs):
        kernel(*refs[:count], *refs[count + len(after) :])

    return pl.pallas_call(
        without_after,
        out_shape=out,
        in_specs=[pl.BlockSpec(memory_space=space)] * count + [pl.BlockSpec(memory_space=pl.ANY)] * len(after),
        out_specs=[pl.BlockSpec(memory_space=pltpu.VMEM)] * len(out),
        scratch_shapes=list(scratch),
        compiler_params=pltpu.CompilerParams(vmem_limit_bytes=VMEM_BYTES),
        cost_estimate=pl.CostEstimate(flops=flops, bytes_accessed=moved, transcendentals=0),
        name=name,
    )(*inputs, *after)


def block_start(inner, rows, bits, k):
    f = lax.axis_index("fsdp")
    return pl.multiple_of((flip(f // inner, bits) * inner + flip(lax.rem(f, inner), k)) * rows, rows)


def pack_first_kernel(inner, rows, acts_ref, cots_ref, *refs):
    outs, sems = refs[:inner], refs[inner]
    copies = []
    for k in range(inner):
        block = acts_ref.at[:, pl.ds(block_start(inner, rows, 3, k), rows)]
        copies.append(pltpu.make_async_copy(block, outs[k].at[:, :rows], sems.at[2 * k]))
        copies.append(pltpu.make_async_copy(cots_ref, outs[k].at[:, rows:], sems.at[2 * k + 1]))
    for copy in copies:
        copy.start()
    for copy in copies:
        copy.wait()


def pack_kernel(inner, rows, blocks, acts_ref, *outs):
    for k in range(inner):
        for slot, bits in enumerate(blocks):
            outs[k][:, slot * rows : (slot + 1) * rows] = acts_ref[:, pl.ds(block_start(inner, rows, bits, k), rows)]


def gradient_kernel(inner, rows, acts_at, *refs):
    acts_refs, cots_refs, out = refs[:inner], refs[inner : 2 * inner], refs[-1]
    columns = jnp.concatenate([ref[:, acts_at : acts_at + rows] for ref in acts_refs], axis=0)
    cots = jnp.concatenate([ref[:, rows:] for ref in cots_refs], axis=0)
    out[...] = lax.dot_general(columns, cots, CONTRACT_ROWS, preferred_element_type=jnp.float32).astype(out.dtype)


def add_kernel(total, arrived, out):
    @pl.loop(0, out.shape[0] // CHUNK)
    def _(step):
        at = pl.ds(pl.multiple_of(step * CHUNK, CHUNK), CHUNK)
        out[at, :] = (total[at, :] + arrived[at, :].astype(jnp.float32)).astype(out.dtype)


def gradient_at(at, refs):
    total, beside, far = refs
    return total[at, :] + beside[at, :].astype(jnp.float32) + far[at, :].astype(jnp.float32)


def steps(half, which, body):
    @pl.loop(0, half // CHUNK)
    def _(step):
        start = pl.multiple_of(step * CHUNK, CHUNK)
        body(pl.ds(start, CHUNK), pl.ds(pl.multiple_of(which * half + start, CHUNK), CHUNK))


def drift_kernel(*refs):
    gradient_refs, (weights, first, second, anchor), drift_ref = refs[:3], refs[3:7], refs[7]

    def body(here, at):
        gradient = gradient_at(at, gradient_refs)
        state = (weights[at, :], first[at, :], second[at, :], anchor[at, :])
        drift_ref[here, :] = inner_update(gradient, *state)[1]

    steps(drift_ref.shape[0], 1 - lax.axis_index("rep"), body)


def update_kernel(*refs):
    gradient_refs, (weights, first, second, anchor), (first_ref, drift_ref) = refs[:3], refs[3:7], refs[7:]
    half = drift_ref.shape[0]
    r = lax.axis_index("rep")

    def body(here, at):
        gradient = gradient_at(at, gradient_refs)
        state = (weights[at, :], first[at, :], second[at, :], anchor[at, :])
        first_ref[at, :], drift_ref[here, :] = inner_update(gradient, *state)

    def others(here, at):
        first_ref[at, :] = decay_first * first[at, :] + (1.0 - decay_first) * gradient_at(at, gradient_refs)

    steps(half, r, body)
    steps(half, 1 - r, others)


def outer_kernel(drift, other, anchor, momentum, out):
    half = out.shape[0]
    at = pl.ds(pl.multiple_of(lax.axis_index("rep") * half, half), half)
    out[...] = outer_update((drift[...] + other[...]) / 2, anchor[at, :], momentum[at, :])


def product(messages, rows, pieces):
    r = lax.axis_index("rep")
    half = rows // 2
    total = 0.0
    for (blocks, start), (mine, other) in zip(messages, pieces):
        for which, piece in ((r, mine), (1 - r, other)):
            at = pl.ds(pl.multiple_of(start + which * half, half), half)
            columns = jnp.concatenate([block[:, at] for block in blocks], axis=0)
            total += jnp.dot(columns, piece[...], preferred_element_type=jnp.float32)
    return total


def paired(refs):
    return [(refs[2 * n], refs[2 * n + 1]) for n in range(len(refs) // 2)]


def early_values_kernel(inner, rows, *refs):
    own, both = refs[:inner], refs[inner : 2 * inner]
    refs[-1][...] = product([(own, 0), (both, rows), (both, 0)], rows, paired(refs[2 * inner : -1]))


def late_values_kernel(inner, rows, early, *refs):
    tokens = early.shape[0] // inner
    total = early[...] + product([(refs[:inner], 0)], rows, [refs[inner : inner + 2]])
    for k, out in enumerate(refs[inner + 2 :]):
        out[...] = total[k * tokens : (k + 1) * tokens].astype(out.dtype)


def sum_kernel(*refs):
    total = refs[0][...]
    for ref in refs[1:-1]:
        total += ref[...].astype(jnp.float32)
    refs[-1][...] = total.astype(refs[-1].dtype)


def on_device(acts, value_cots, inner_weights, first_moment, second_moment, anchor, outer_momentum):
    inner = lax.axis_size("fsdp") // PLANES
    rows, width = anchor.shape
    if inner != 4 or lax.axis_size("rep") != 2 or rows % 256 or width % 128:
        return general(acts, value_cots, inner_weights, first_moment, second_moment, anchor, outer_momentum)
    tokens = acts.shape[1]
    half = rows // 2

    def planes(x, bits):
        return lax.ppermute(x, "fsdp", [(p * inner + i, (p ^ bits) * inner + i) for p in range(PLANES) for i in range(inner)])

    def across(x, k):
        return lax.ppermute(x, "fsdp", [(p * inner + i, p * inner + (i ^ k)) for p in range(PLANES) for i in range(inner)])

    def around(blocks):
        return [blocks[0]] + [across(blocks[k], k) for k in range(1, inner)]

    def swap(x):
        return lax.ppermute(x, "rep", [(0, 1), (1, 0)])

    out = [jax.ShapeDtypeStruct((tokens, rows + width), jnp.bfloat16)] * inner
    sems = [pltpu.SemaphoreType.DMA((2 * inner,))]
    kernel = partial(pack_first_kernel, inner, rows)
    first = around(call(kernel, "pack", out, [acts[0], value_cots[0]], 0, sems, space=pltpu.HBM))

    def pack(blocks, after):
        out = [jax.ShapeDtypeStruct((tokens, len(blocks) * rows), jnp.bfloat16)] * inner
        return call(partial(pack_kernel, inner, rows, blocks), "pack", out, [acts[0]], 0, after=after)

    second = around(pack((2, 1), first[1:2]))
    last = around(pack((0,), second[1:]))
    full = jax.ShapeDtypeStruct((rows, width), jnp.float32)
    sent = jax.ShapeDtypeStruct((rows, width), jnp.bfloat16)

    def gradient(message, at, out, flops=2 * inner * tokens * rows * width, after=()):
        return call(partial(gradient_kernel, inner, rows, at), "gradient", [out], message + first, flops, after=after)[0]

    beside_far = planes(gradient(first, 0, sent), 1)
    for_far = gradient(second, 0, full, AHEAD_FLOPS)
    (for_far,) = call(add_kernel, "add", [sent], [for_far, beside_far], 0)
    far = planes(for_far, 2)
    beside = planes(gradient(second, rows, sent, AHEAD_FLOPS // 6, [for_far]), 1)
    known = [gradient(last, 0, full), beside, far, inner_weights[0], first_moment[0], second_moment[0], anchor]
    half_block = jax.ShapeDtypeStruct((half, width), jnp.float32)
    (drift_out,) = call(drift_kernel, "drift", [half_block], known, 0)
    drift_in = swap(drift_out)
    first_next, drift = call(update_kernel, "update", [full, half_block], known, 0)
    new_half = jax.ShapeDtypeStruct((half, width), jnp.bfloat16)
    (mine,) = call(outer_kernel, "outer", [new_half], [drift, drift_in, anchor, outer_momentum], 0)
    mine2 = planes(mine, 2)
    mine1 = planes(mine, 1)
    mine3 = planes(mine2, 1)
    pieces = [y for x in (mine, mine1, mine2) for y in (x, swap(x))]
    flops = 2 * inner * tokens * rows * width
    (early,) = call(
        partial(early_values_kernel, inner, rows),
        "early_values",
        [jax.ShapeDtypeStruct((inner * tokens, width), jnp.float32)],
        last + second + pieces,
        3 * flops,
    )
    block = jax.ShapeDtypeStruct((tokens, width), jnp.bfloat16)
    own, *sums = call(
        partial(late_values_kernel, inner, rows),
        "late_values",
        [jax.ShapeDtypeStruct((tokens, width), jnp.float32)] + [block] * (inner - 1),
        [early] + first + [mine3, swap(mine3)],
        flops,
    )
    terms = [own] + [across(sums[k - 1], k) for k in range(1, inner)]
    (values,) = call(sum_kernel, "sum", [block], terms, 0)
    return (first_next[None], values[None])


def solution(mesh):
    placed = (
        P("rep", "fsdp", None),
        P("rep", "fsdp", None),
        P("rep", "fsdp", None),
        P("rep", "fsdp", None),
        P("rep", "fsdp", None),
        P("fsdp", None),
        P("fsdp", None),
    )
    return jax.shard_map(
        on_device,
        mesh=mesh,
        in_specs=placed,
        out_specs=(P("rep", "fsdp", None), P("rep", "fsdp", None)),
        check_vma=False,
    )
```

time: 253 us -> 98.4 us (0.39)
  waiting for transfers between devices: 208 us -> 61.4 us
  starting transfers between devices: 8.43 us -> 24.8 us
  between operations: 13.8 us -> 0.8 us
  matrix products: 12 us -> 0 us
  Pallas kernels: 0 us -> 8.71 us
  local copies, waits for them, and re-layouts: 7.45 us -> 2.53 us
  other arithmetic: 2.75 us -> 0 us
    all_gather x2 -> x0, waiting for transfers between devices: 143 us -> none  [the longest x1 114 us: on_device(): lax.all_gather(weights_next, 'fsdp', axis=0, tiled=True)]
    ppermute x0 -> x23, waiting for transfers between devices: none -> 61.4 us  [the longest x6 33.7 us: planes(): lax.ppermute(x, 'fsdp', [(p * inner + i, (p ^ bits) * inner + i) for p in...]
    all_to_all x1 -> x0, waiting for transfers between devices: 45.9 us -> none  [on_device(): lax.all_to_all(tokens_local, 'fsdp', split_axis=1, concat_axis=0, tiled=T...]
    ppermute x0 -> x23, starting transfers between devices: none -> 24.8 us  [the longest x12 15.3 us: across(): lax.ppermute(x, 'fsdp', [(p * inner + i, p * inner + (i ^ k)) for p in ra...]
    psum x1 -> x0, waiting for transfers between devices: 18.3 us -> none  [on_device(): summed_drift = lax.psum(drift, 'rep')]
    dot_general x2 -> x0, matrix products: 12 us -> none  [the longest x1 6.22 us: on_device(): lax.dot_general(columns, lax.all_gather(cots_local, 'fsdp', axis=0, tiled...]
    pallas_call x0 -> x14, Pallas kernels: none -> 8.71 us  [call(): pl.pallas_call(without_after, out_shape=out, in_specs=[pl.BlockSpec(memor...]
    all_to_all x1 -> x0, starting transfers between devices: 8.31 us -> none  [on_device(): lax.all_to_all(tokens_local, 'fsdp', split_axis=1, concat_axis=0, tiled=T...]
  transfers between devices with their start and end apart: 4 -> 23, of which waited for: 4 -> 18; matrix products, arithmetic and copies ran while one was open for 1% -> 0% of each run, Pallas kernels for 0% -> 5%
where the time goes in v6:
time: 98.4 us; the launch traced here: 98.2 us
  waiting for transfers between devices  61.4 us (62%)
  starting transfers between devices  24.8 us (25%)
  Pallas kernels  8.71 us (9%)
  local copies, waits for them, and re-layouts  2.53 us (3%)
    ppermute x6, waiting for transfers between devices, planes(): lax.ppermute(x, 'fsdp', [(p * inner + i, (p ^ bits) * inner + i) for p in...  33.7 us
    ppermute x12, waiting for transfers between devices, across(): lax.ppermute(x, 'fsdp', [(p * inner + i, p * inner + (i ^ k)) for p in ra...  26.9 us
    ppermute x12, starting transfers between devices, across(): lax.ppermute(x, 'fsdp', [(p * inner + i, p * inner + (i ^ k)) for p in ra...  15.3 us
    ppermute x6, starting transfers between devices, planes(): lax.ppermute(x, 'fsdp', [(p * inner + i, (p ^ bits) * inner + i) for p in...  8.89 us
    pallas_call x14, Pallas kernels, call(): pl.pallas_call(without_after, out_shape=out, in_specs=[pl.BlockSpec(memor...  8.71 us
    unnamed x16, local copies, waits for them, and re-layouts  2.53 us
  transfers between devices with their start and end apart: 23, of which 18 were waited for; matrix products, arithmetic and copies ran while one was open for 0% of the time, Pallas kernels for 5%

profile of v6, /device:TPU:0, one launch (start us, length us, event | category | flops | bytes accessed | tf_op | source)
XLA Modules:
  0.0 98.2 jit_solution(6779414987636503426)
XLA Ops:
  0.6 1.6 %copy-done = bf16[1,128,8192]{2,1,0:T(8,128)(2,1)S(1)} copy-done((bf16[1,128,8192]{2,1,0:T(8,128)(2,1)S(1)}, bf16[1,128,8192]{2,1,0:T(8,128)(2,1)}, u32[]{:S(2)}) %copy-start) | copy-done | bytes 2097176
  3.4 3.0 %collective-permute-start = (bf16[128,1024]{1,0:T(8,128)(2,1)S(1)}, bf16[128,1024]{1,0:T(8,128)(2,1)S(1)}, u32[]{:S(2)}, u32[]{:S(2)}) collective-permute-start(bf16[128,1024]{1,0:T(8,128)(2,1)S(1)} %get-tuple-element.20), channel_id=1, source_target_pairs={{0,1},{1,0},{2,3},{3,2},{4,5},{5,4},{6,7},{7,6},{8,9},{9,8},{10,11... | collective-permute-start | bytes 786440 | tf_op jit(solution)/shard_map/ppermute | solution.py:204
  6.4 1.5 %collective-permute-start.7 = (bf16[128,1024]{1,0:T(8,128)(2,1)S(1)}, bf16[128,1024]{1,0:T(8,128)(2,1)S(1)}, u32[]{:S(2)}, u32[]{:S(2)}) collective-permute-start(bf16[128,1024]{1,0:T(8,128)(2,1)S(1)} %get-tuple-element.29), channel_id=1, source_target_pairs={{0,2},{1,3},{2,0},{3,1},{4,6},{5,7},{6,4},{7,5},{8,10},{9,11},{10,... | collective-permute-start | bytes 786440 | tf_op jit(solution)/shard_map/ppermute | solution.py:204
  7.9 5.6 %collective-permute-done.refs_1_.refs_5_.refs_2_ = bf16[128,1024]{1,0:T(8,128)(2,1)S(1)} collective-permute-done((bf16[128,1024]{1,0:T(8,128)(2,1)S(1)}, bf16[128,1024]{1,0:T(8,128)(2,1)S(1)}, u32[]{:S(2)}, u32[]{:S(2)}) %collective-permute-start) | collective-permute-done | bytes 262176 | tf_op jit(solution)/shard_map/ppermute | solution.py:204
  13.6 2.1 %collective-permute-start.1 = (bf16[128,1024]{1,0:T(8,128)(2,1)S(1)}, bf16[128,1024]{1,0:T(8,128)(2,1)S(1)}, u32[]{:S(2)}, u32[]{:S(2)}) collective-permute-start(bf16[128,1024]{1,0:T(8,128)(2,1)S(1)} %get-tuple-element.21), channel_id=1, source_target_pairs={{0,1},{1,0},{2,3},{3,2},{4,5},{5,4},{6,7},{7,6},{8,9},{9,8},{10,11... | collective-permute-start | bytes 786440 | tf_op jit(solution)/shard_map/ppermute | solution.py:204
  15.7 1.5 %collective-permute-start.2 = (bf16[128,1024]{1,0:T(8,128)(2,1)S(1)}, bf16[128,1024]{1,0:T(8,128)(2,1)S(1)}, u32[]{:S(2)}, u32[]{:S(2)}) collective-permute-start(bf16[128,1024]{1,0:T(8,128)(2,1)S(1)} %get-tuple-element.22), channel_id=1, source_target_pairs={{0,2},{1,3},{2,0},{3,1},{4,6},{5,7},{6,4},{7,5},{8,10},{9,11},{10,... | collective-permute-start | bytes 786440 | tf_op jit(solution)/shard_map/ppermute | solution.py:204
  17.2 2.9 %collective-permute-done.7.refs_6_.refs_2_.refs_3_ = bf16[128,1024]{1,0:T(8,128)(2,1)S(1)} collective-permute-done((bf16[128,1024]{1,0:T(8,128)(2,1)S(1)}, bf16[128,1024]{1,0:T(8,128)(2,1)S(1)}, u32[]{:S(2)}, u32[]{:S(2)}) %collective-permute-start.7) | collective-permute-done | bytes 262176 | tf_op jit(solution)/shard_map/ppermute | solution.py:204
  22.0 1.6 %collective-permute-start.9 = (bf16[512,512]{1,0:T(8,128)(2,1)}, bf16[512,512]{1,0:T(8,128)(2,1)}, u32[]{:S(2)}, u32[]{:S(2)}) collective-permute-start(bf16[512,512]{1,0:T(8,128)(2,1)} %gradient.6), channel_id=1, source_target_pairs={{0,4},{1,5},{2,6},{3,7},{4,0},{5,1},{6,2},{7,3},{8,12},{9,13},{10,... | collective-permute-start | bytes 1572872 | tf_op jit(solution)/shard_map/ppermute | solution.py:201
  24.8 6.2 %collective-permute-done.2.refs_2_.refs_6_ = bf16[128,1024]{1,0:T(8,128)(2,1)S(1)} collective-permute-done((bf16[128,1024]{1,0:T(8,128)(2,1)S(1)}, bf16[128,1024]{1,0:T(8,128)(2,1)S(1)}, u32[]{:S(2)}, u32[]{:S(2)}) %collective-permute-start.2) | collective-permute-done | bytes 262176 | tf_op jit(solution)/shard_map/ppermute | solution.py:204
  31.5 2.5 %collective-permute-done.9.refs_1_ = bf16[512,512]{1,0:T(8,128)(2,1)} collective-permute-done((bf16[512,512]{1,0:T(8,128)(2,1)}, bf16[512,512]{1,0:T(8,128)(2,1)}, u32[]{:S(2)}, u32[]{:S(2)}) %collective-permute-start.9) | collective-permute-done | bytes 524320 | tf_op jit(solution)/shard_map/ppermute | solution.py:201
  35.7 1.6 %collective-permute-start.10 = (bf16[512,512]{1,0:T(8,128)(2,1)S(1)}, bf16[512,512]{1,0:T(8,128)(2,1)S(1)}, u32[]{:S(2)}, u32[]{:S(2)}) collective-permute-start(bf16[512,512]{1,0:T(8,128)(2,1)S(1)} %gradient.7), channel_id=1, source_target_pairs={{0,4},{1,5},{2,6},{3,7},{4,0},{5,1},{6,2},{7,3},{8,12},{9,13},{10,... | collective-permute-start | bytes 1572872 | tf_op jit(solution)/shard_map/ppermute | solution.py:201
  37.3 2.6 %collective-permute-start.11 = (bf16[512,512]{1,0:T(8,128)(2,1)S(1)}, bf16[512,512]{1,0:T(8,128)(2,1)S(1)}, u32[]{:S(2)}, u32[]{:S(2)}) collective-permute-start(bf16[512,512]{1,0:T(8,128)(2,1)S(1)} %add.1.refs_8_), channel_id=1, source_target_pairs={{0,8},{1,9},{2,10},{3,11},{4,12},{5,13},{6,14},{7,15},{8,0},{9,1},... | collective-permute-start | bytes 1572872 | tf_op jit(solution)/shard_map/ppermute | solution.py:201
  40.0 1.6 %collective-permute-start.4 = (bf16[128,512]{1,0:T(8,128)(2,1)S(1)}, bf16[128,512]{1,0:T(8,128)(2,1)S(1)}, u32[]{:S(2)}, u32[]{:S(2)}) collective-permute-start(bf16[128,512]{1,0:T(8,128)(2,1)S(1)} %get-tuple-element.25), channel_id=1, source_target_pairs={{0,1},{1,0},{2,3},{3,2},{4,5},{5,4},{6,7},{7,6},{8,9},{9,8},{10,11... | collective-permute-start | bytes 393224 | tf_op jit(solution)/shard_map/ppermute | solution.py:204
  42.0 1.5 %collective-permute-start.6 = (bf16[128,512]{1,0:T(8,128)(2,1)S(1)}, bf16[128,512]{1,0:T(8,128)(2,1)S(1)}, u32[]{:S(2)}, u32[]{:S(2)}) collective-permute-start(bf16[128,512]{1,0:T(8,128)(2,1)S(1)} %get-tuple-element.27), channel_id=1, source_target_pairs={{0,3},{1,2},{2,1},{3,0},{4,7},{5,6},{6,5},{7,4},{8,11},{9,10},{10,... | collective-permute-start | bytes 393224 | tf_op jit(solution)/shard_map/ppermute | solution.py:204
  45.0 1.5 %collective-permute-done.5.refs_2_ = bf16[128,512]{1,0:T(8,128)(2,1)S(1)} collective-permute-done((bf16[128,512]{1,0:T(8,128)(2,1)S(1)}, bf16[128,512]{1,0:T(8,128)(2,1)S(1)}, u32[]{:S(2)}, u32[]{:S(2)}) %collective-permute-start.5) | collective-permute-done | bytes 131104 | tf_op jit(solution)/shard_map/ppermute | solution.py:204
  48.4 9.2 %collective-permute-done.10.refs_1_ = bf16[512,512]{1,0:T(8,128)(2,1)S(1)} collective-permute-done((bf16[512,512]{1,0:T(8,128)(2,1)S(1)}, bf16[512,512]{1,0:T(8,128)(2,1)S(1)}, u32[]{:S(2)}, u32[]{:S(2)}) %collective-permute-start.10) | collective-permute-done | bytes 524320 | tf_op jit(solution)/shard_map/ppermute | solution.py:201
  57.6 2.4 %collective-permute-done.11.refs_2_ = bf16[512,512]{1,0:T(8,128)(2,1)S(1)} collective-permute-done((bf16[512,512]{1,0:T(8,128)(2,1)S(1)}, bf16[512,512]{1,0:T(8,128)(2,1)S(1)}, u32[]{:S(2)}, u32[]{:S(2)}) %collective-permute-start.11) | collective-permute-done | bytes 524320 | tf_op jit(solution)/shard_map/ppermute | solution.py:201
  60.6 1.7 %update.1 = (f32[512,512]{1,0:T(8,128)}, f32[256,512]{1,0:T(8,128)S(1)}) custom-call(f32[512,512]{1,0:T(8,128)S(1)} %gradient.4.refs_0_, bf16[512,512]{1,0:T(8,128)(2,1)S(1)} %collective-permute-done.10.refs_1_, bf16[512,512]{1,0:T(8,128)(2,1)S(1)} %collective-permute-done.11.refs_2_, f32[512,512]{1,0:T(8,128)S(1)} %bitcast.11, f32[512,512]{1,0:T(8,128)S(1)} %bitcast.13, ...), custom_call_target="tpu_custom_call" | custom-call | bytes 7864320 | tf_op jit(solution)/shard_map/update/pallas_call | solution.py:61
  63.1 2.7 %collective-permute-start.14 = (bf16[256,512]{1,0:T(8,128)(2,1)S(1)}, bf16[256,512]{1,0:T(8,128)(2,1)S(1)}, u32[]{:S(2)}, u32[]{:S(2)}) collective-permute-start(bf16[256,512]{1,0:T(8,128)(2,1)S(1)} %outer.1.refs_8_), channel_id=1, source_target_pairs={{0,4},{1,5},{2,6},{3,7},{4,0},{5,1},{6,2},{7,3},{8,12},{9,13},{10,... | collective-permute-start | bytes 786440 | tf_op jit(solution)/shard_map/ppermute | solution.py:201
  65.8 11.9 %collective-permute-done.16.refs_12_ = bf16[256,512]{1,0:T(8,128)(2,1)S(1)} collective-permute-done((bf16[256,512]{1,0:T(8,128)(2,1)S(1)}, bf16[256,512]{1,0:T(8,128)(2,1)S(1)}, u32[]{:S(2)}, u32[]{:S(2)}) %collective-permute-start.16) | collective-permute-done | bytes 262176 | tf_op jit(solution)/shard_map/ppermute | solution.py:201
  78.3 7.6 %collective-permute-done.18.refs_5_ = bf16[256,512]{1,0:T(8,128)(2,1)S(1)} collective-permute-done((bf16[256,512]{1,0:T(8,128)(2,1)S(1)}, bf16[256,512]{1,0:T(8,128)(2,1)S(1)}, u32[]{:S(2)}, u32[]{:S(2)}) %collective-permute-start.18) | collective-permute-done | bytes 262176 | tf_op jit(solution)/shard_map/ppermute | solution.py:201
  87.9 1.6 %collective-permute-start.20 = (bf16[128,512]{1,0:T(8,128)(2,1)S(1)}, bf16[128,512]{1,0:T(8,128)(2,1)S(1)}, u32[]{:S(2)}, u32[]{:S(2)}) collective-permute-start(bf16[128,512]{1,0:T(8,128)(2,1)S(1)} %get-tuple-element.35), channel_id=1, source_target_pairs={{0,1},{1,0},{2,3},{3,2},{4,5},{5,4},{6,7},{7,6},{8,9},{9,8},{10,11... | collective-permute-start | bytes 393224 | tf_op jit(solution)/shard_map/ppermute | solution.py:204
  91.4 2.4 %collective-permute-done.20.refs_1_ = bf16[128,512]{1,0:T(8,128)(2,1)S(1)} collective-permute-done((bf16[128,512]{1,0:T(8,128)(2,1)S(1)}, bf16[128,512]{1,0:T(8,128)(2,1)S(1)}, u32[]{:S(2)}, u32[]{:S(2)}) %collective-permute-start.20) | collective-permute-done | bytes 131104 | tf_op jit(solution)/shard_map/ppermute | solution.py:204
  93.8 3.7 %collective-permute-done.21.refs_2_ = bf16[128,512]{1,0:T(8,128)(2,1)S(1)} collective-permute-done((bf16[128,512]{1,0:T(8,128)(2,1)S(1)}, bf16[128,512]{1,0:T(8,128)(2,1)S(1)}, u32[]{:S(2)}, u32[]{:S(2)}) %collective-permute-start.21) | collective-permute-done | bytes 131104 | tf_op jit(solution)/shard_map/ppermute | solution.py:204
  (52 shorter events, 17.1 us)
Async XLA Ops:
  3.4 10.1 %collective-permute-start = (bf16[128,1024]{1,0:T(8,128)(2,1)S(1)}, bf16[128,1024]{1,0:T(8,128)(2,1)S(1)}, u32[]{:S(2)}, u32[]{:S(2)}) collective-permute-start(bf16[128,1024]{1,0:T(8,128)(2,1)S(1)} %get-tuple-element.20), channel_id=1, source_target_pairs={{0,1},{1,0},{2,3},{3,2},{4,5},{5,4},{6,7},{7,6},{8,9},{9,8},{10,11... | collective-permute-start | bytes 786440 | tf_op jit(solution)/shard_map/ppermute | solution.py:204
  6.4 13.8 %collective-permute-start.7 = (bf16[128,1024]{1,0:T(8,128)(2,1)S(1)}, bf16[128,1024]{1,0:T(8,128)(2,1)S(1)}, u32[]{:S(2)}, u32[]{:S(2)}) collective-permute-start(bf16[128,1024]{1,0:T(8,128)(2,1)S(1)} %get-tuple-element.29), channel_id=1, source_target_pairs={{0,2},{1,3},{2,0},{3,1},{4,6},{5,7},{6,4},{7,5},{8,10},{9,11},{10,... | collective-permute-start | bytes 786440 | tf_op jit(solution)/shard_map/ppermute | solution.py:204
  7.9 12.8 %collective-permute-start.8 = (bf16[128,1024]{1,0:T(8,128)(2,1)S(1)}, bf16[128,1024]{1,0:T(8,128)(2,1)S(1)}, u32[]{:S(2)}, u32[]{:S(2)}) collective-permute-start(bf16[128,1024]{1,0:T(8,128)(2,1)S(1)} %get-tuple-element.30), channel_id=1, source_target_pairs={{0,3},{1,2},{2,1},{3,0},{4,7},{5,6},{6,5},{7,4},{8,11},{9,10},{10,... | collective-permute-start | bytes 786440 | tf_op jit(solution)/shard_map/ppermute | solution.py:204
  13.6 11.2 %collective-permute-start.1 = (bf16[128,1024]{1,0:T(8,128)(2,1)S(1)}, bf16[128,1024]{1,0:T(8,128)(2,1)S(1)}, u32[]{:S(2)}, u32[]{:S(2)}) collective-permute-start(bf16[128,1024]{1,0:T(8,128)(2,1)S(1)} %get-tuple-element.21), channel_id=1, source_target_pairs={{0,1},{1,0},{2,3},{3,2},{4,5},{5,4},{6,7},{7,6},{8,9},{9,8},{10,11... | collective-permute-start | bytes 786440 | tf_op jit(solution)/shard_map/ppermute | solution.py:204
  15.7 15.3 %collective-permute-start.2 = (bf16[128,1024]{1,0:T(8,128)(2,1)S(1)}, bf16[128,1024]{1,0:T(8,128)(2,1)S(1)}, u32[]{:S(2)}, u32[]{:S(2)}) collective-permute-start(bf16[128,1024]{1,0:T(8,128)(2,1)S(1)} %get-tuple-element.22), channel_id=1, source_target_pairs={{0,2},{1,3},{2,0},{3,1},{4,6},{5,7},{6,4},{7,5},{8,10},{9,11},{10,... | collective-permute-start | bytes 786440 | tf_op jit(solution)/shard_map/ppermute | solution.py:204
  17.2 13.8 %collective-permute-start.3 = (bf16[128,1024]{1,0:T(8,128)(2,1)S(1)}, bf16[128,1024]{1,0:T(8,128)(2,1)S(1)}, u32[]{:S(2)}, u32[]{:S(2)}) collective-permute-start(bf16[128,1024]{1,0:T(8,128)(2,1)S(1)} %get-tuple-element.23), channel_id=1, source_target_pairs={{0,3},{1,2},{2,1},{3,0},{4,7},{5,6},{6,5},{7,4},{8,11},{9,10},{10,... | collective-permute-start | bytes 786440 | tf_op jit(solution)/shard_map/ppermute | solution.py:204
  22.0 12.0 %collective-permute-start.9 = (bf16[512,512]{1,0:T(8,128)(2,1)}, bf16[512,512]{1,0:T(8,128)(2,1)}, u32[]{:S(2)}, u32[]{:S(2)}) collective-permute-start(bf16[512,512]{1,0:T(8,128)(2,1)} %gradient.6), channel_id=1, source_target_pairs={{0,4},{1,5},{2,6},{3,7},{4,0},{5,1},{6,2},{7,3},{8,12},{9,13},{10,... | collective-permute-start | bytes 1572872 | tf_op jit(solution)/shard_map/ppermute | solution.py:201
  35.6 24.3 %copy-start.2 = (f32[512,512]{1,0:T(8,128)S(1)}, f32[512,512]{1,0:T(8,128)}, u32[]{:S(2)}) copy-start(f32[512,512]{1,0:T(8,128)} %refs_2_.1) | copy-start | bytes 3145732
  35.7 21.9 %collective-permute-start.10 = (bf16[512,512]{1,0:T(8,128)(2,1)S(1)}, bf16[512,512]{1,0:T(8,128)(2,1)S(1)}, u32[]{:S(2)}, u32[]{:S(2)}) collective-permute-start(bf16[512,512]{1,0:T(8,128)(2,1)S(1)} %gradient.7), channel_id=1, source_target_pairs={{0,4},{1,5},{2,6},{3,7},{4,0},{5,1},{6,2},{7,3},{8,12},{9,13},{10,... | collective-permute-start | bytes 1572872 | tf_op jit(solution)/shard_map/ppermute | solution.py:201
  37.3 22.6 %collective-permute-start.11 = (bf16[512,512]{1,0:T(8,128)(2,1)S(1)}, bf16[512,512]{1,0:T(8,128)(2,1)S(1)}, u32[]{:S(2)}, u32[]{:S(2)}) collective-permute-start(bf16[512,512]{1,0:T(8,128)(2,1)S(1)} %add.1.refs_8_), channel_id=1, source_target_pairs={{0,8},{1,9},{2,10},{3,11},{4,12},{5,13},{6,14},{7,15},{8,0},{9,1},... | collective-permute-start | bytes 1572872 | tf_op jit(solution)/shard_map/ppermute | solution.py:201
  40.0 5.0 %collective-permute-start.4 = (bf16[128,512]{1,0:T(8,128)(2,1)S(1)}, bf16[128,512]{1,0:T(8,128)(2,1)S(1)}, u32[]{:S(2)}, u32[]{:S(2)}) collective-permute-start(bf16[128,512]{1,0:T(8,128)(2,1)S(1)} %get-tuple-element.25), channel_id=1, source_target_pairs={{0,1},{1,0},{2,3},{3,2},{4,5},{5,4},{6,7},{7,6},{8,9},{9,8},{10,11... | collective-permute-start | bytes 393224 | tf_op jit(solution)/shard_map/ppermute | solution.py:204
  41.5 5.0 %collective-permute-start.5 = (bf16[128,512]{1,0:T(8,128)(2,1)S(1)}, bf16[128,512]{1,0:T(8,128)(2,1)S(1)}, u32[]{:S(2)}, u32[]{:S(2)}) collective-permute-start(bf16[128,512]{1,0:T(8,128)(2,1)S(1)} %get-tuple-element.26), channel_id=1, source_target_pairs={{0,2},{1,3},{2,0},{3,1},{4,6},{5,7},{6,4},{7,5},{8,10},{9,11},{10,... | collective-permute-start | bytes 393224 | tf_op jit(solution)/shard_map/ppermute | solution.py:204
  42.0 5.9 %collective-permute-start.6 = (bf16[128,512]{1,0:T(8,128)(2,1)S(1)}, bf16[128,512]{1,0:T(8,128)(2,1)S(1)}, u32[]{:S(2)}, u32[]{:S(2)}) collective-permute-start(bf16[128,512]{1,0:T(8,128)(2,1)S(1)} %get-tuple-element.27), channel_id=1, source_target_pairs={{0,3},{1,2},{2,1},{3,0},{4,7},{5,6},{6,5},{7,4},{8,11},{9,10},{10,... | collective-permute-start | bytes 393224 | tf_op jit(solution)/shard_map/ppermute | solution.py:204
  60.5 2.0 %collective-permute-start.12 = (f32[256,512]{1,0:T(8,128)S(1)}, f32[256,512]{1,0:T(8,128)S(1)}, u32[]{:S(2)}, u32[]{:S(2)}) collective-permute-start(f32[256,512]{1,0:T(8,128)S(1)} %drift.1), channel_id=1, source_target_pairs={{0,16},{16,0},{1,17},{17,1},{2,18},{18,2},{3,19},{19,3},{4,20},{20... | collective-permute-start | bytes 1572872 | tf_op jit(solution)/shard_map/ppermute | solution.py:210
  62.7 15.0 %collective-permute-start.16 = (bf16[256,512]{1,0:T(8,128)(2,1)S(1)}, bf16[256,512]{1,0:T(8,128)(2,1)S(1)}, u32[]{:S(2)}, u32[]{:S(2)}) collective-permute-start(bf16[256,512]{1,0:T(8,128)(2,1)S(1)} %outer.1.refs_8_), channel_id=1, source_target_pairs={{0,8},{1,9},{2,10},{3,11},{4,12},{5,13},{6,14},{7,15},{8,0},{9,1},... | collective-permute-start | bytes 786440 | tf_op jit(solution)/shard_map/ppermute | solution.py:201
  63.1 14.7 %collective-permute-start.14 = (bf16[256,512]{1,0:T(8,128)(2,1)S(1)}, bf16[256,512]{1,0:T(8,128)(2,1)S(1)}, u32[]{:S(2)}, u32[]{:S(2)}) collective-permute-start(bf16[256,512]{1,0:T(8,128)(2,1)S(1)} %outer.1.refs_8_), channel_id=1, source_target_pairs={{0,4},{1,5},{2,6},{3,7},{4,0},{5,1},{6,2},{7,3},{8,12},{9,13},{10,... | collective-permute-start | bytes 786440 | tf_op jit(solution)/shard_map/ppermute | solution.py:201
  77.7 8.2 %collective-permute-start.18 = (bf16[256,512]{1,0:T(8,128)(2,1)S(1)}, bf16[256,512]{1,0:T(8,128)(2,1)S(1)}, u32[]{:S(2)}, u32[]{:S(2)}) collective-permute-start(bf16[256,512]{1,0:T(8,128)(2,1)S(1)} %collective-permute-done.16.refs_12_), channel_id=1, source_target_pairs={{0,4},{1,5},{2,6},{3,7},{4,0},{5,1},{6,2},{7,3},{8,12},{9,13},{10,... | collective-permute-start | bytes 786440 | tf_op jit(solution)/shard_map/ppermute | solution.py:201
  77.7 8.2 %collective-permute-start.13 = (bf16[256,512]{1,0:T(8,128)(2,1)S(1)}, bf16[256,512]{1,0:T(8,128)(2,1)S(1)}, u32[]{:S(2)}, u32[]{:S(2)}) collective-permute-start(bf16[256,512]{1,0:T(8,128)(2,1)S(1)} %outer.1.refs_8_), channel_id=1, source_target_pairs={{0,16},{16,0},{1,17},{17,1},{2,18},{18,2},{3,19},{19,3},{4,20},{20... | collective-permute-start | bytes 786440 | tf_op jit(solution)/shard_map/ppermute | solution.py:210
  77.8 8.1 %collective-permute-start.15 = (bf16[256,512]{1,0:T(8,128)(2,1)S(1)}, bf16[256,512]{1,0:T(8,128)(2,1)S(1)}, u32[]{:S(2)}, u32[]{:S(2)}) collective-permute-start(bf16[256,512]{1,0:T(8,128)(2,1)S(1)} %collective-permute-done.14.refs_10_), channel_id=1, source_target_pairs={{0,16},{16,0},{1,17},{17,1},{2,18},{18,2},{3,19},{19,3},{4,20},{20... | collective-permute-start | bytes 786440 | tf_op jit(solution)/shard_map/ppermute | solution.py:210
  78.2 7.7 %collective-permute-start.17 = (bf16[256,512]{1,0:T(8,128)(2,1)S(1)}, bf16[256,512]{1,0:T(8,128)(2,1)S(1)}, u32[]{:S(2)}, u32[]{:S(2)}) collective-permute-start(bf16[256,512]{1,0:T(8,128)(2,1)S(1)} %collective-permute-done.16.refs_12_), channel_id=1, source_target_pairs={{0,16},{16,0},{1,17},{17,1},{2,18},{18,2},{3,19},{19,3},{4,20},{20... | collective-permute-start | bytes 786440 | tf_op jit(solution)/shard_map/ppermute | solution.py:210
  85.9 1.5 %collective-permute-start.19 = (bf16[256,512]{1,0:T(8,128)(2,1)S(1)}, bf16[256,512]{1,0:T(8,128)(2,1)S(1)}, u32[]{:S(2)}, u32[]{:S(2)}) collective-permute-start(bf16[256,512]{1,0:T(8,128)(2,1)S(1)} %collective-permute-done.18.refs_5_), channel_id=1, source_target_pairs={{0,16},{16,0},{1,17},{17,1},{2,18},{18,2},{3,19},{19,3},{4,20},{20... | collective-permute-start | bytes 786440 | tf_op jit(solution)/shard_map/ppermute | solution.py:210
  87.9 5.9 %collective-permute-start.20 = (bf16[128,512]{1,0:T(8,128)(2,1)S(1)}, bf16[128,512]{1,0:T(8,128)(2,1)S(1)}, u32[]{:S(2)}, u32[]{:S(2)}) collective-permute-start(bf16[128,512]{1,0:T(8,128)(2,1)S(1)} %get-tuple-element.35), channel_id=1, source_target_pairs={{0,1},{1,0},{2,3},{3,2},{4,5},{5,4},{6,7},{7,6},{8,9},{9,8},{10,11... | collective-permute-start | bytes 393224 | tf_op jit(solution)/shard_map/ppermute | solution.py:204
  89.4 8.1 %collective-permute-start.21 = (bf16[128,512]{1,0:T(8,128)(2,1)S(1)}, bf16[128,512]{1,0:T(8,128)(2,1)S(1)}, u32[]{:S(2)}, u32[]{:S(2)}) collective-permute-start(bf16[128,512]{1,0:T(8,128)(2,1)S(1)} %get-tuple-element.36), channel_id=1, source_target_pairs={{0,2},{1,3},{2,0},{3,1},{4,6},{5,7},{6,4},{7,5},{8,10},{9,11},{10,... | collective-permute-start | bytes 393224 | tf_op jit(solution)/shard_map/ppermute | solution.py:204
  89.9 7.6 %collective-permute-start.22 = (bf16[128,512]{1,0:T(8,128)(2,1)S(1)}, bf16[128,512]{1,0:T(8,128)(2,1)S(1)}, u32[]{:S(2)}, u32[]{:S(2)}) collective-permute-start(bf16[128,512]{1,0:T(8,128)(2,1)S(1)} %get-tuple-element.37), channel_id=1, source_target_pairs={{0,3},{1,2},{2,1},{3,0},{4,7},{5,6},{6,5},{7,4},{8,11},{9,10},{10,... | collective-permute-start | bytes 393224 | tf_op jit(solution)/shard_map/ppermute | solution.py:204
  (7 other events, 82.2 us)

commit v7 on v6

--- a/solution.py
+++ b/solution.py
@@ -17,7 +17,7 @@
 PLANES = 4
 CHUNK = 32
 CONTRACT_ROWS = (((0,), (0,)), ((), ()))
-AHEAD_FLOPS = 30 * 10**12
+AHEAD_FLOPS = 12 * 10**12
 VMEM_BYTES = 16 * 1024 * 1024
 
 
@@ -94,23 +94,34 @@
             outs[k][:, slot * rows : (slot + 1) * rows] = acts_ref[:, pl.ds(block_start(inner, rows, bits, k), rows)]
 
 
-def gradient_kernel(inner, rows, acts_at, *refs):
-    acts_refs, cots_refs, out = refs[:inner], refs[inner : 2 * inner], refs[-1]
+def partial_gradient(inner, rows, acts_at, acts_refs, cots_refs):
     columns = jnp.concatenate([ref[:, acts_at : acts_at + rows] for ref in acts_refs], axis=0)
     cots = jnp.concatenate([ref[:, rows:] for ref in cots_refs], axis=0)
-    out[...] = lax.dot_general(columns, cots, CONTRACT_ROWS, preferred_element_type=jnp.float32).astype(out.dtype)
-
-
-def add_kernel(total, arrived, out):
+    return lax.dot_general(columns, cots, CONTRACT_ROWS, preferred_element_type=jnp.float32)
+
+
+def gradient_kernel(inner, rows, acts_at, *refs):
+    total = partial_gradient(inner, rows, acts_at, refs[:inner], refs[inner : 2 * inner])
+    at = 0
+    for out in refs[2 * inner :]:
+        out[...] = total[:, at : at + out.shape[1]].astype(out.dtype)
+        at += out.shape[1]
+
+
+def add_kernel(start, total, arrived, out):
     @pl.loop(0, out.shape[0] // CHUNK)
     def _(step):
         at = pl.ds(pl.multiple_of(step * CHUNK, CHUNK), CHUNK)
-        out[at, :] = (total[at, :] + arrived[at, :].astype(jnp.float32)).astype(out.dtype)
+        here = total[at, start : start + out.shape[1]]
+        out[at, :] = (here + arrived[at, :].astype(jnp.float32)).astype(out.dtype)
 
 
 def gradient_at(at, refs):
-    total, beside, far = refs
-    return total[at, :] + beside[at, :].astype(jnp.float32) + far[at, :].astype(jnp.float32)
+    total, *arrived = refs
+    beside, far = (
+        jnp.concatenate([ref[at, :].astype(jnp.float32) for ref in pair], axis=1) for pair in (arrived[:2], arrived[2:])
+    )
+    return total[at, :] + beside + far
 
 
 def steps(half, which, body):
@@ -121,7 +132,7 @@
 
 
 def drift_kernel(*refs):
-    gradient_refs, (weights, first, second, anchor), drift_ref = refs[:3], refs[3:7], refs[7]
+    gradient_refs, (weights, first, second, anchor), drift_ref = refs[:-5], refs[-5:-1], refs[-1]
 
     def body(here, at):
         gradient = gradient_at(at, gradient_refs)
@@ -132,7 +143,7 @@
 
 
 def update_kernel(*refs):
-    gradient_refs, (weights, first, second, anchor), (first_ref, drift_ref) = refs[:3], refs[3:7], refs[7:]
+    gradient_refs, (weights, first, second, anchor), (first_ref, drift_ref) = refs[:-6], refs[-6:-2], refs[-2:]
     half = drift_ref.shape[0]
     r = lax.axis_index("rep")
 
@@ -148,10 +159,14 @@
     steps(half, 1 - r, others)
 
 
-def outer_kernel(drift, other, anchor, momentum, out):
+def outer_kernel(drift, other, anchor, momentum, out, *cut):
     half = out.shape[0]
     at = pl.ds(pl.multiple_of(lax.axis_index("rep") * half, half), half)
     out[...] = outer_update((drift[...] + other[...]) / 2, anchor[at, :], momentum[at, :])
+    start = 0
+    for ref in cut:
+        ref[...] = out[:, start : start + ref.shape[1]]
+        start += ref.shape[1]
 
 
 def product(messages, rows, pieces):
@@ -171,15 +186,21 @@
 
 
 def early_values_kernel(inner, rows, *refs):
-    own, both = refs[:inner], refs[inner : 2 * inner]
-    refs[-1][...] = product([(own, 0), (both, rows), (both, 0)], rows, paired(refs[2 * inner : -1]))
+    own, both, pieces, out = refs[:inner], refs[inner : 2 * inner], paired(refs[2 * inner : -1]), refs[-1]
+    far = [product([(both, 0)], rows, [piece]) for piece in pieces[2:]]
+    out[...] = product([(own, 0), (both, rows)], rows, pieces[:2]) + jnp.concatenate(far, axis=1)
 
 
 def late_values_kernel(inner, rows, early, *refs):
+    blocks, pieces, outs = refs[:inner], paired(refs[inner : inner + 4]), refs[inner + 4 :]
     tokens = early.shape[0] // inner
-    total = early[...] + product([(refs[:inner], 0)], rows, [refs[inner : inner + 2]])
-    for k, out in enumerate(refs[inner + 2 :]):
-        out[...] = total[k * tokens : (k + 1) * tokens].astype(out.dtype)
+    start = 0
+    for piece in pieces:
+        cols = slice(start, start + piece[0].shape[1])
+        total = early[:, cols] + product([(blocks, 0)], rows, [piece])
+        for k, out in enumerate(outs):
+            out[:, cols] = total[k * tokens : (k + 1) * tokens].astype(out.dtype)
+        start = cols.stop
 
 
 def sum_kernel(*refs):
@@ -192,7 +213,7 @@
 def on_device(acts, value_cots, inner_weights, first_moment, second_moment, anchor, outer_momentum):
     inner = lax.axis_size("fsdp") // PLANES
     rows, width = anchor.shape
-    if inner != 4 or lax.axis_size("rep") != 2 or rows % 256 or width % 128:
+    if inner != 4 or lax.axis_size("rep") != 2 or rows % 256 or width % 512:
         return general(acts, value_cots, inner_weights, first_moment, second_moment, anchor, outer_momentum)
     tokens = acts.shape[1]
     half = rows // 2
@@ -219,29 +240,37 @@
         return call(partial(pack_kernel, inner, rows, blocks), "pack", out, [acts[0]], 0, after=after)
 
     second = around(pack((2, 1), first[1:2]))
-    last = around(pack((0,), second[1:]))
     full = jax.ShapeDtypeStruct((rows, width), jnp.float32)
     sent = jax.ShapeDtypeStruct((rows, width), jnp.bfloat16)
+    cut = [jax.ShapeDtypeStruct((rows, columns), jnp.bfloat16) for columns in (3 * width // 4, width // 4)]
+    equal = [jax.ShapeDtypeStruct((rows, width // 2), jnp.bfloat16)] * 2
 
     def gradient(message, at, out, flops=2 * inner * tokens * rows * width, after=()):
-        return call(partial(gradient_kernel, inner, rows, at), "gradient", [out], message + first, flops, after=after)[0]
-
-    beside_far = planes(gradient(first, 0, sent), 1)
-    for_far = gradient(second, 0, full, AHEAD_FLOPS)
-    (for_far,) = call(add_kernel, "add", [sent], [for_far, beside_far], 0)
-    far = planes(for_far, 2)
-    beside = planes(gradient(second, rows, sent, AHEAD_FLOPS // 6, [for_far]), 1)
-    known = [gradient(last, 0, full), beside, far, inner_weights[0], first_moment[0], second_moment[0], anchor]
+        return call(partial(gradient_kernel, inner, rows, at), "gradient", out, message + first, flops, after=after)
+
+    beside_far = [planes(x, 1) for x in gradient(first, 0, cut)]
+    (for_far,) = gradient(second, 0, [full], AHEAD_FLOPS)
+    far, start = [], 0
+    for out, arrived in zip(cut, beside_far):
+        (added,) = call(partial(add_kernel, start), "add", [out], [for_far, arrived], 0)
+        far.append(planes(added, 2))
+        if start == 0:
+            for_beside = gradient(second, rows, equal, after=[added])
+            beside = [planes(x, 1) for x in for_beside]
+        start += out.shape[1]
+    last = around(pack((0,), [added, *for_beside]))
+    known = [gradient(last, 0, [full])[0], *beside, *far, inner_weights[0], first_moment[0], second_moment[0], anchor]
     half_block = jax.ShapeDtypeStruct((half, width), jnp.float32)
     (drift_out,) = call(drift_kernel, "drift", [half_block], known, 0)
     drift_in = swap(drift_out)
     first_next, drift = call(update_kernel, "update", [full, half_block], known, 0)
     new_half = jax.ShapeDtypeStruct((half, width), jnp.bfloat16)
-    (mine,) = call(outer_kernel, "outer", [new_half], [drift, drift_in, anchor, outer_momentum], 0)
-    mine2 = planes(mine, 2)
+    new_cut = [jax.ShapeDtypeStruct((half, width // 2), jnp.bfloat16)] * 2
+    mine, *mine_cut = call(outer_kernel, "outer", [new_half] + new_cut, [drift, drift_in, anchor, outer_momentum], 0)
+    mine2 = [planes(x, 2) for x in mine_cut]
     mine1 = planes(mine, 1)
-    mine3 = planes(mine2, 1)
-    pieces = [y for x in (mine, mine1, mine2) for y in (x, swap(x))]
+    mine3 = [planes(x, 1) for x in mine2]
+    pieces = [y for x in (mine, mine1, *mine2) for y in (x, swap(x))]
     flops = 2 * inner * tokens * rows * width
     (early,) = call(
         partial(early_values_kernel, inner, rows),
@@ -255,7 +284,7 @@
         partial(late_values_kernel, inner, rows),
         "late_values",
         [jax.ShapeDtypeStruct((tokens, width), jnp.float32)] + [block] * (inner - 1),
-        [early] + first + [mine3, swap(mine3)],
+        [early] + first + [y for x in mine3 for y in (x, swap(x))],
         flops,
     )
     terms = [own] + [across(sums[k - 1], k) for k in range(1, inner)]

time: 98.4 us -> 98.7 us (level)
  waiting for transfers between devices: 61.4 us -> 58.9 us
  starting transfers between devices: 24.8 us -> 26.3 us
  Pallas kernels: 8.71 us -> 9.84 us
    ppermute x6 -> x11, waiting for transfers between devices: 33.7 us -> 30.2 us  [planes(): lax.ppermute(x, 'fsdp', [(p * inner + i, (p ^ bits) * inner + i) for p in...]
    ppermute x6 -> x11, starting transfers between devices: 8.89 us -> 10.3 us  [planes(): lax.ppermute(x, 'fsdp', [(p * inner + i, (p ^ bits) * inner + i) for p in...]
    ppermute x12, waiting for transfers between devices: 26.9 us -> 28.2 us  [across(): lax.ppermute(x, 'fsdp', [(p * inner + i, p * inner + (i ^ k)) for p in ra...]
    pallas_call x14 -> x15, Pallas kernels: 8.71 us -> 9.84 us  [call(): pl.pallas_call(without_after, out_shape=out, in_specs=[pl.BlockSpec(memor...]
  transfers between devices with their start and end apart: 23 -> 30, of which waited for: 18 -> 19; matrix products, arithmetic and copies ran while one was open for 0% -> 0% of each run, Pallas kernels for 5% -> 8%
where the time goes in v7:
time: 98.7 us; the launch traced here: 98.4 us
  waiting for transfers between devices  58.9 us (60%)
  starting transfers between devices  26.3 us (27%)
  Pallas kernels  9.84 us (10%)
  local copies, waits for them, and re-layouts  2.53 us (3%)
    ppermute x11, waiting for transfers between devices, planes(): lax.ppermute(x, 'fsdp', [(p * inner + i, (p ^ bits) * inner + i) for p in...  30.2 us
    ppermute x12, waiting for transfers between devices, across(): lax.ppermute(x, 'fsdp', [(p * inner + i, p * inner + (i ^ k)) for p in ra...  28.2 us
    ppermute x12, starting transfers between devices, across(): lax.ppermute(x, 'fsdp', [(p * inner + i, p * inner + (i ^ k)) for p in ra...  15.1 us
    ppermute x11, starting transfers between devices, planes(): lax.ppermute(x, 'fsdp', [(p * inner + i, (p ^ bits) * inner + i) for p in...  10.3 us
    pallas_call x15, Pallas kernels, call(): pl.pallas_call(without_after, out_shape=out, in_specs=[pl.BlockSpec(memor...  9.84 us
    unnamed x16, local copies, waits for them, and re-layouts  2.53 us
  transfers between devices with their start and end apart: 30, of which 19 were waited for; matrix products, arithmetic and copies ran while one was open for 0% of the time, Pallas kernels for 8%

profile of v7, /device:TPU:0, one launch (start us, length us, event | category | flops | bytes accessed | tf_op | source)
XLA Modules:
  0.0 98.4 jit_solution(276195449308869574)
XLA Ops:
  0.6 1.6 %copy-done = bf16[1,128,8192]{2,1,0:T(8,128)(2,1)S(1)} copy-done((bf16[1,128,8192]{2,1,0:T(8,128)(2,1)S(1)}, bf16[1,128,8192]{2,1,0:T(8,128)(2,1)}, u32[]{:S(2)}) %copy-start) | copy-done | bytes 2097176
  3.4 3.0 %collective-permute-start = (bf16[128,1024]{1,0:T(8,128)(2,1)S(1)}, bf16[128,1024]{1,0:T(8,128)(2,1)S(1)}, u32[]{:S(2)}, u32[]{:S(2)}) collective-permute-start(bf16[128,1024]{1,0:T(8,128)(2,1)S(1)} %get-tuple-element.27), channel_id=1, source_target_pairs={{0,1},{1,0},{2,3},{3,2},{4,5},{5,4},{6,7},{7,6},{8,9},{9,8},{10,11... | collective-permute-start | bytes 786440 | tf_op jit(solution)/shard_map/ppermute | solution.py:225
  6.4 1.5 %collective-permute-start.4 = (bf16[128,1024]{1,0:T(8,128)(2,1)S(1)}, bf16[128,1024]{1,0:T(8,128)(2,1)S(1)}, u32[]{:S(2)}, u32[]{:S(2)}) collective-permute-start(bf16[128,1024]{1,0:T(8,128)(2,1)S(1)} %get-tuple-element.33), channel_id=1, source_target_pairs={{0,2},{1,3},{2,0},{3,1},{4,6},{5,7},{6,4},{7,5},{8,10},{9,11},{10,... | collective-permute-start | bytes 786440 | tf_op jit(solution)/shard_map/ppermute | solution.py:225
  7.9 5.6 %collective-permute-done.refs_1_.refs_5_.refs_2_ = bf16[128,1024]{1,0:T(8,128)(2,1)S(1)} collective-permute-done((bf16[128,1024]{1,0:T(8,128)(2,1)S(1)}, bf16[128,1024]{1,0:T(8,128)(2,1)S(1)}, u32[]{:S(2)}, u32[]{:S(2)}) %collective-permute-start) | collective-permute-done | bytes 262176 | tf_op jit(solution)/shard_map/ppermute | solution.py:225
  13.6 2.1 %collective-permute-start.1 = (bf16[128,1024]{1,0:T(8,128)(2,1)S(1)}, bf16[128,1024]{1,0:T(8,128)(2,1)S(1)}, u32[]{:S(2)}, u32[]{:S(2)}) collective-permute-start(bf16[128,1024]{1,0:T(8,128)(2,1)S(1)} %get-tuple-element.29), channel_id=1, source_target_pairs={{0,1},{1,0},{2,3},{3,2},{4,5},{5,4},{6,7},{7,6},{8,9},{9,8},{10,11... | collective-permute-start | bytes 786440 | tf_op jit(solution)/shard_map/ppermute | solution.py:225
  17.2 2.9 %collective-permute-done.4.refs_6_.refs_2_.refs_3_ = bf16[128,1024]{1,0:T(8,128)(2,1)S(1)} collective-permute-done((bf16[128,1024]{1,0:T(8,128)(2,1)S(1)}, bf16[128,1024]{1,0:T(8,128)(2,1)S(1)}, u32[]{:S(2)}, u32[]{:S(2)}) %collective-permute-start.4) | collective-permute-done | bytes 262176 | tf_op jit(solution)/shard_map/ppermute | solution.py:225
  22.0 1.6 %collective-permute-start.6 = (bf16[512,128]{1,0:T(8,128)(2,1)}, bf16[512,128]{1,0:T(8,128)(2,1)}, u32[]{:S(2)}, u32[]{:S(2)}) collective-permute-start(bf16[512,128]{1,0:T(8,128)(2,1)} %get-tuple-element.35), channel_id=1, source_target_pairs={{0,4},{1,5},{2,6},{3,7},{4,0},{5,1},{6,2},{7,3},{8,12},{9,13},{10,... | collective-permute-start | bytes 393224 | tf_op jit(solution)/shard_map/ppermute | solution.py:222
  24.8 6.2 %collective-permute-done.2.refs_2_.refs_6_ = bf16[128,1024]{1,0:T(8,128)(2,1)S(1)} collective-permute-done((bf16[128,1024]{1,0:T(8,128)(2,1)S(1)}, bf16[128,1024]{1,0:T(8,128)(2,1)S(1)}, u32[]{:S(2)}, u32[]{:S(2)}) %collective-permute-start.2) | collective-permute-done | bytes 262176 | tf_op jit(solution)/shard_map/ppermute | solution.py:225
  31.5 2.5 %collective-permute-done.7.refs_1_ = bf16[512,384]{1,0:T(8,128)(2,1)} collective-permute-done((bf16[512,384]{1,0:T(8,128)(2,1)}, bf16[512,384]{1,0:T(8,128)(2,1)}, u32[]{:S(2)}, u32[]{:S(2)}) %collective-permute-start.7) | collective-permute-done | bytes 393248 | tf_op jit(solution)/shard_map/ppermute | solution.py:222
  35.1 2.6 %collective-permute-start.13 = (bf16[512,384]{1,0:T(8,128)(2,1)S(1)}, bf16[512,384]{1,0:T(8,128)(2,1)S(1)}, u32[]{:S(2)}, u32[]{:S(2)}) collective-permute-start(bf16[512,384]{1,0:T(8,128)(2,1)S(1)} %add.3.refs_8_), channel_id=1, source_target_pairs={{0,8},{1,9},{2,10},{3,11},{4,12},{5,13},{6,14},{7,15},{8,0},{9,1},... | collective-permute-start | bytes 1179656 | tf_op jit(solution)/shard_map/ppermute | solution.py:222
  39.4 1.6 %collective-permute-start.8 = (bf16[128,512]{1,0:T(8,128)(2,1)S(1)}, bf16[128,512]{1,0:T(8,128)(2,1)S(1)}, u32[]{:S(2)}, u32[]{:S(2)}) collective-permute-start(bf16[128,512]{1,0:T(8,128)(2,1)S(1)} %get-tuple-element.40), channel_id=1, source_target_pairs={{0,1},{1,0},{2,3},{3,2},{4,5},{5,4},{6,7},{7,6},{8,9},{9,8},{10,11... | collective-permute-start | bytes 393224 | tf_op jit(solution)/shard_map/ppermute | solution.py:225
  41.4 1.6 %collective-permute-start.11 = (bf16[512,256]{1,0:T(8,128)(2,1)S(1)}, bf16[512,256]{1,0:T(8,128)(2,1)S(1)}, u32[]{:S(2)}, u32[]{:S(2)}) collective-permute-start(bf16[512,256]{1,0:T(8,128)(2,1)S(1)} %get-tuple-element.37.refs_2_), channel_id=1, source_target_pairs={{0,4},{1,5},{2,6},{3,7},{4,0},{5,1},{6,2},{7,3},{8,12},{9,13},{10,... | collective-permute-start | bytes 786440 | tf_op jit(solution)/shard_map/ppermute | solution.py:222
  43.5 2.1 %collective-permute-done.8.refs_1_ = bf16[128,512]{1,0:T(8,128)(2,1)S(1)} collective-permute-done((bf16[128,512]{1,0:T(8,128)(2,1)S(1)}, bf16[128,512]{1,0:T(8,128)(2,1)S(1)}, u32[]{:S(2)}, u32[]{:S(2)}) %collective-permute-start.8) | collective-permute-done | bytes 131104 | tf_op jit(solution)/shard_map/ppermute | solution.py:225
  47.4 4.0 %collective-permute-done.10.refs_3_ = bf16[128,512]{1,0:T(8,128)(2,1)S(1)} collective-permute-done((bf16[128,512]{1,0:T(8,128)(2,1)S(1)}, bf16[128,512]{1,0:T(8,128)(2,1)S(1)}, u32[]{:S(2)}, u32[]{:S(2)}) %collective-permute-start.10) | collective-permute-done | bytes 131104 | tf_op jit(solution)/shard_map/ppermute | solution.py:225
  51.9 5.3 %collective-permute-done.14.refs_4_ = bf16[512,128]{1,0:T(8,128)(2,1)S(1)} collective-permute-done((bf16[512,128]{1,0:T(8,128)(2,1)S(1)}, bf16[512,128]{1,0:T(8,128)(2,1)S(1)}, u32[]{:S(2)}, u32[]{:S(2)}) %collective-permute-start.14) | collective-permute-done | bytes 131104 | tf_op jit(solution)/shard_map/ppermute | solution.py:222
  58.6 2.8 %collective-permute-done.12.refs_2_ = bf16[512,256]{1,0:T(8,128)(2,1)S(1)} collective-permute-done((bf16[512,256]{1,0:T(8,128)(2,1)S(1)}, bf16[512,256]{1,0:T(8,128)(2,1)S(1)}, u32[]{:S(2)}, u32[]{:S(2)}) %collective-permute-start.12) | collective-permute-done | bytes 262176 | tf_op jit(solution)/shard_map/ppermute | solution.py:222
  62.1 1.7 %update.1 = (f32[512,512]{1,0:T(8,128)}, f32[256,512]{1,0:T(8,128)S(1)}) custom-call(f32[512,512]{1,0:T(8,128)S(1)} %gradient.7.refs_0_, bf16[512,256]{1,0:T(8,128)(2,1)S(1)} %collective-permute-done.11.refs_1_, bf16[512,256]{1,0:T(8,128)(2,1)S(1)} %collective-permute-done.12.refs_2_, bf16[512,384]{1,0:T(8,128)(2,1)S(1)} %collective-permute-done.13.refs_3_, ...), custom_call_target="tpu_custom_call" | custom-call | bytes 7864320 | tf_op jit(solution)/shard_map/update/pallas_call | solution.py:61
  64.7 2.7 %collective-permute-start.19 = (bf16[256,256]{1,0:T(8,128)(2,1)S(1)}, bf16[256,256]{1,0:T(8,128)(2,1)S(1)}, u32[]{:S(2)}, u32[]{:S(2)}) collective-permute-start(bf16[256,256]{1,0:T(8,128)(2,1)S(1)} %get-tuple-element.46), channel_id=1, source_target_pairs={{0,8},{1,9},{2,10},{3,11},{4,12},{5,13},{6,14},{7,15},{8,0},{9,1},... | collective-permute-start | bytes 393224 | tf_op jit(solution)/shard_map/ppermute | solution.py:222
  67.6 10.1 %collective-permute-done.17.refs_10_ = bf16[256,512]{1,0:T(8,128)(2,1)S(1)} collective-permute-done((bf16[256,512]{1,0:T(8,128)(2,1)S(1)}, bf16[256,512]{1,0:T(8,128)(2,1)S(1)}, u32[]{:S(2)}, u32[]{:S(2)}) %collective-permute-start.17) | collective-permute-done | bytes 262176 | tf_op jit(solution)/shard_map/ppermute | solution.py:222
  77.7 2.4 %collective-permute-done.21.refs_14_ = bf16[256,256]{1,0:T(8,128)(2,1)S(1)} collective-permute-done((bf16[256,256]{1,0:T(8,128)(2,1)S(1)}, bf16[256,256]{1,0:T(8,128)(2,1)S(1)}, u32[]{:S(2)}, u32[]{:S(2)}) %collective-permute-start.21) | collective-permute-done | bytes 131104 | tf_op jit(solution)/shard_map/ppermute | solution.py:222
  80.6 3.4 %collective-permute-done.23.refs_5_ = bf16[256,256]{1,0:T(8,128)(2,1)S(1)} collective-permute-done((bf16[256,256]{1,0:T(8,128)(2,1)S(1)}, bf16[256,256]{1,0:T(8,128)(2,1)S(1)}, u32[]{:S(2)}, u32[]{:S(2)}) %collective-permute-start.23) | collective-permute-done | bytes 131104 | tf_op jit(solution)/shard_map/ppermute | solution.py:222
  84.0 2.4 %collective-permute-done.25.refs_7_ = bf16[256,256]{1,0:T(8,128)(2,1)S(1)} collective-permute-done((bf16[256,256]{1,0:T(8,128)(2,1)S(1)}, bf16[256,256]{1,0:T(8,128)(2,1)S(1)}, u32[]{:S(2)}, u32[]{:S(2)}) %collective-permute-start.25) | collective-permute-done | bytes 131104 | tf_op jit(solution)/shard_map/ppermute | solution.py:222
  91.7 2.6 %collective-permute-done.27.refs_1_ = bf16[128,512]{1,0:T(8,128)(2,1)S(1)} collective-permute-done((bf16[128,512]{1,0:T(8,128)(2,1)S(1)}, bf16[128,512]{1,0:T(8,128)(2,1)S(1)}, u32[]{:S(2)}, u32[]{:S(2)}) %collective-permute-start.27) | collective-permute-done | bytes 131104 | tf_op jit(solution)/shard_map/ppermute | solution.py:225
  94.3 3.4 %collective-permute-done.28.refs_2_ = bf16[128,512]{1,0:T(8,128)(2,1)S(1)} collective-permute-done((bf16[128,512]{1,0:T(8,128)(2,1)S(1)}, bf16[128,512]{1,0:T(8,128)(2,1)S(1)}, u32[]{:S(2)}, u32[]{:S(2)}) %collective-permute-start.28) | collective-permute-done | bytes 131104 | tf_op jit(solution)/shard_map/ppermute | solution.py:225
  (67 shorter events, 21.9 us)
Async XLA Ops:
  3.4 10.1 %collective-permute-start = (bf16[128,1024]{1,0:T(8,128)(2,1)S(1)}, bf16[128,1024]{1,0:T(8,128)(2,1)S(1)}, u32[]{:S(2)}, u32[]{:S(2)}) collective-permute-start(bf16[128,1024]{1,0:T(8,128)(2,1)S(1)} %get-tuple-element.27), channel_id=1, source_target_pairs={{0,1},{1,0},{2,3},{3,2},{4,5},{5,4},{6,7},{7,6},{8,9},{9,8},{10,11... | collective-permute-start | bytes 786440 | tf_op jit(solution)/shard_map/ppermute | solution.py:225
  6.4 13.8 %collective-permute-start.4 = (bf16[128,1024]{1,0:T(8,128)(2,1)S(1)}, bf16[128,1024]{1,0:T(8,128)(2,1)S(1)}, u32[]{:S(2)}, u32[]{:S(2)}) collective-permute-start(bf16[128,1024]{1,0:T(8,128)(2,1)S(1)} %get-tuple-element.33), channel_id=1, source_target_pairs={{0,2},{1,3},{2,0},{3,1},{4,6},{5,7},{6,4},{7,5},{8,10},{9,11},{10,... | collective-permute-start | bytes 786440 | tf_op jit(solution)/shard_map/ppermute | solution.py:225
  7.9 12.8 %collective-permute-start.5 = (bf16[128,1024]{1,0:T(8,128)(2,1)S(1)}, bf16[128,1024]{1,0:T(8,128)(2,1)S(1)}, u32[]{:S(2)}, u32[]{:S(2)}) collective-permute-start(bf16[128,1024]{1,0:T(8,128)(2,1)S(1)} %get-tuple-element.34), channel_id=1, source_target_pairs={{0,3},{1,2},{2,1},{3,0},{4,7},{5,6},{6,5},{7,4},{8,11},{9,10},{10,... | collective-permute-start | bytes 786440 | tf_op jit(solution)/shard_map/ppermute | solution.py:225
  13.6 11.2 %collective-permute-start.1 = (bf16[128,1024]{1,0:T(8,128)(2,1)S(1)}, bf16[128,1024]{1,0:T(8,128)(2,1)S(1)}, u32[]{:S(2)}, u32[]{:S(2)}) collective-permute-start(bf16[128,1024]{1,0:T(8,128)(2,1)S(1)} %get-tuple-element.29), channel_id=1, source_target_pairs={{0,1},{1,0},{2,3},{3,2},{4,5},{5,4},{6,7},{7,6},{8,9},{9,8},{10,11... | collective-permute-start | bytes 786440 | tf_op jit(solution)/shard_map/ppermute | solution.py:225
  15.7 15.3 %collective-permute-start.2 = (bf16[128,1024]{1,0:T(8,128)(2,1)S(1)}, bf16[128,1024]{1,0:T(8,128)(2,1)S(1)}, u32[]{:S(2)}, u32[]{:S(2)}) collective-permute-start(bf16[128,1024]{1,0:T(8,128)(2,1)S(1)} %get-tuple-element.30), channel_id=1, source_target_pairs={{0,2},{1,3},{2,0},{3,1},{4,6},{5,7},{6,4},{7,5},{8,10},{9,11},{10,... | collective-permute-start | bytes 786440 | tf_op jit(solution)/shard_map/ppermute | solution.py:225
  17.2 13.8 %collective-permute-start.3 = (bf16[128,1024]{1,0:T(8,128)(2,1)S(1)}, bf16[128,1024]{1,0:T(8,128)(2,1)S(1)}, u32[]{:S(2)}, u32[]{:S(2)}) collective-permute-start(bf16[128,1024]{1,0:T(8,128)(2,1)S(1)} %get-tuple-element.31), channel_id=1, source_target_pairs={{0,3},{1,2},{2,1},{3,0},{4,7},{5,6},{6,5},{7,4},{8,11},{9,10},{10,... | collective-permute-start | bytes 786440 | tf_op jit(solution)/shard_map/ppermute | solution.py:225
  22.0 15.8 %collective-permute-start.6 = (bf16[512,128]{1,0:T(8,128)(2,1)}, bf16[512,128]{1,0:T(8,128)(2,1)}, u32[]{:S(2)}, u32[]{:S(2)}) collective-permute-start(bf16[512,128]{1,0:T(8,128)(2,1)} %get-tuple-element.35), channel_id=1, source_target_pairs={{0,4},{1,5},{2,6},{3,7},{4,0},{5,1},{6,2},{7,3},{8,12},{9,13},{10,... | collective-permute-start | bytes 393224 | tf_op jit(solution)/shard_map/ppermute | solution.py:222
  23.5 10.4 %collective-permute-start.7 = (bf16[512,384]{1,0:T(8,128)(2,1)}, bf16[512,384]{1,0:T(8,128)(2,1)}, u32[]{:S(2)}, u32[]{:S(2)}) collective-permute-start(bf16[512,384]{1,0:T(8,128)(2,1)} %get-tuple-element.36), channel_id=1, source_target_pairs={{0,4},{1,5},{2,6},{3,7},{4,0},{5,1},{6,2},{7,3},{8,12},{9,13},{10,... | collective-permute-start | bytes 1179656 | tf_op jit(solution)/shard_map/ppermute | solution.py:222
  35.1 26.3 %collective-permute-start.13 = (bf16[512,384]{1,0:T(8,128)(2,1)S(1)}, bf16[512,384]{1,0:T(8,128)(2,1)S(1)}, u32[]{:S(2)}, u32[]{:S(2)}) collective-permute-start(bf16[512,384]{1,0:T(8,128)(2,1)S(1)} %add.3.refs_8_), channel_id=1, source_target_pairs={{0,8},{1,9},{2,10},{3,11},{4,12},{5,13},{6,14},{7,15},{8,0},{9,1},... | collective-permute-start | bytes 1179656 | tf_op jit(solution)/shard_map/ppermute | solution.py:222
  39.4 6.2 %collective-permute-start.8 = (bf16[128,512]{1,0:T(8,128)(2,1)S(1)}, bf16[128,512]{1,0:T(8,128)(2,1)S(1)}, u32[]{:S(2)}, u32[]{:S(2)}) collective-permute-start(bf16[128,512]{1,0:T(8,128)(2,1)S(1)} %get-tuple-element.40), channel_id=1, source_target_pairs={{0,1},{1,0},{2,3},{3,2},{4,5},{5,4},{6,7},{7,6},{8,9},{9,8},{10,11... | collective-permute-start | bytes 393224 | tf_op jit(solution)/shard_map/ppermute | solution.py:225
  41.4 17.2 %collective-permute-start.11 = (bf16[512,256]{1,0:T(8,128)(2,1)S(1)}, bf16[512,256]{1,0:T(8,128)(2,1)S(1)}, u32[]{:S(2)}, u32[]{:S(2)}) collective-permute-start(bf16[512,256]{1,0:T(8,128)(2,1)S(1)} %get-tuple-element.37.refs_2_), channel_id=1, source_target_pairs={{0,4},{1,5},{2,6},{3,7},{4,0},{5,1},{6,2},{7,3},{8,12},{9,13},{10,... | collective-permute-start | bytes 786440 | tf_op jit(solution)/shard_map/ppermute | solution.py:222
  43.0 18.4 %collective-permute-start.12 = (bf16[512,256]{1,0:T(8,128)(2,1)S(1)}, bf16[512,256]{1,0:T(8,128)(2,1)S(1)}, u32[]{:S(2)}, u32[]{:S(2)}) collective-permute-start(bf16[512,256]{1,0:T(8,128)(2,1)S(1)} %get-tuple-element.38.refs_3_), channel_id=1, source_target_pairs={{0,4},{1,5},{2,6},{3,7},{4,0},{5,1},{6,2},{7,3},{8,12},{9,13},{10,... | collective-permute-start | bytes 786440 | tf_op jit(solution)/shard_map/ppermute | solution.py:222
  46.9 10.4 %collective-permute-start.14 = (bf16[512,128]{1,0:T(8,128)(2,1)S(1)}, bf16[512,128]{1,0:T(8,128)(2,1)S(1)}, u32[]{:S(2)}, u32[]{:S(2)}) collective-permute-start(bf16[512,128]{1,0:T(8,128)(2,1)S(1)} %add.2.refs_1_), channel_id=1, source_target_pairs={{0,8},{1,9},{2,10},{3,11},{4,12},{5,13},{6,14},{7,15},{8,0},{9,1},... | collective-permute-start | bytes 393224 | tf_op jit(solution)/shard_map/ppermute | solution.py:222
  64.3 13.4 %collective-permute-start.17 = (bf16[256,512]{1,0:T(8,128)(2,1)S(1)}, bf16[256,512]{1,0:T(8,128)(2,1)S(1)}, u32[]{:S(2)}, u32[]{:S(2)}) collective-permute-start(bf16[256,512]{1,0:T(8,128)(2,1)S(1)} %get-tuple-element.45.refs_8_), channel_id=1, source_target_pairs={{0,4},{1,5},{2,6},{3,7},{4,0},{5,1},{6,2},{7,3},{8,12},{9,13},{10,... | collective-permute-start | bytes 786440 | tf_op jit(solution)/shard_map/ppermute | solution.py:222
  64.4 15.7 %collective-permute-start.16 = (bf16[256,512]{1,0:T(8,128)(2,1)S(1)}, bf16[256,512]{1,0:T(8,128)(2,1)S(1)}, u32[]{:S(2)}, u32[]{:S(2)}) collective-permute-start(bf16[256,512]{1,0:T(8,128)(2,1)S(1)} %get-tuple-element.45.refs_8_), channel_id=1, source_target_pairs={{0,16},{16,0},{1,17},{17,1},{2,18},{18,2},{3,19},{19,3},{4,20},{20... | collective-permute-start | bytes 786440 | tf_op jit(solution)/shard_map/ppermute | solution.py:231
  64.7 13.0 %collective-permute-start.19 = (bf16[256,256]{1,0:T(8,128)(2,1)S(1)}, bf16[256,256]{1,0:T(8,128)(2,1)S(1)}, u32[]{:S(2)}, u32[]{:S(2)}) collective-permute-start(bf16[256,256]{1,0:T(8,128)(2,1)S(1)} %get-tuple-element.46), channel_id=1, source_target_pairs={{0,8},{1,9},{2,10},{3,11},{4,12},{5,13},{6,14},{7,15},{8,0},{9,1},... | collective-permute-start | bytes 393224 | tf_op jit(solution)/shard_map/ppermute | solution.py:222
  67.4 12.6 %collective-permute-start.21 = (bf16[256,256]{1,0:T(8,128)(2,1)S(1)}, bf16[256,256]{1,0:T(8,128)(2,1)S(1)}, u32[]{:S(2)}, u32[]{:S(2)}) collective-permute-start(bf16[256,256]{1,0:T(8,128)(2,1)S(1)} %get-tuple-element.47), channel_id=1, source_target_pairs={{0,8},{1,9},{2,10},{3,11},{4,12},{5,13},{6,14},{7,15},{8,0},{9,1},... | collective-permute-start | bytes 393224 | tf_op jit(solution)/shard_map/ppermute | solution.py:222
  77.7 8.7 %collective-permute-start.18 = (bf16[256,512]{1,0:T(8,128)(2,1)S(1)}, bf16[256,512]{1,0:T(8,128)(2,1)S(1)}, u32[]{:S(2)}, u32[]{:S(2)}) collective-permute-start(bf16[256,512]{1,0:T(8,128)(2,1)S(1)} %collective-permute-done.17.refs_10_), channel_id=1, source_target_pairs={{0,16},{16,0},{1,17},{17,1},{2,18},{18,2},{3,19},{19,3},{4,20},{20... | collective-permute-start | bytes 786440 | tf_op jit(solution)/shard_map/ppermute | solution.py:231
  77.7 6.3 %collective-permute-start.23 = (bf16[256,256]{1,0:T(8,128)(2,1)S(1)}, bf16[256,256]{1,0:T(8,128)(2,1)S(1)}, u32[]{:S(2)}, u32[]{:S(2)}) collective-permute-start(bf16[256,256]{1,0:T(8,128)(2,1)S(1)} %collective-permute-done.19.refs_12_), channel_id=1, source_target_pairs={{0,4},{1,5},{2,6},{3,7},{4,0},{5,1},{6,2},{7,3},{8,12},{9,13},{10,... | collective-permute-start | bytes 393224 | tf_op jit(solution)/shard_map/ppermute | solution.py:222
  80.1 6.3 %collective-permute-start.25 = (bf16[256,256]{1,0:T(8,128)(2,1)S(1)}, bf16[256,256]{1,0:T(8,128)(2,1)S(1)}, u32[]{:S(2)}, u32[]{:S(2)}) collective-permute-start(bf16[256,256]{1,0:T(8,128)(2,1)S(1)} %collective-permute-done.21.refs_14_), channel_id=1, source_target_pairs={{0,4},{1,5},{2,6},{3,7},{4,0},{5,1},{6,2},{7,3},{8,12},{9,13},{10,... | collective-permute-start | bytes 393224 | tf_op jit(solution)/shard_map/ppermute | solution.py:222
  80.1 6.3 %collective-permute-start.20 = (bf16[256,256]{1,0:T(8,128)(2,1)S(1)}, bf16[256,256]{1,0:T(8,128)(2,1)S(1)}, u32[]{:S(2)}, u32[]{:S(2)}) collective-permute-start(bf16[256,256]{1,0:T(8,128)(2,1)S(1)} %collective-permute-done.19.refs_12_), channel_id=1, source_target_pairs={{0,16},{16,0},{1,17},{17,1},{2,18},{18,2},{3,19},{19,3},{4,20},{20... | collective-permute-start | bytes 393224 | tf_op jit(solution)/shard_map/ppermute | solution.py:231
  80.1 6.3 %collective-permute-start.22 = (bf16[256,256]{1,0:T(8,128)(2,1)S(1)}, bf16[256,256]{1,0:T(8,128)(2,1)S(1)}, u32[]{:S(2)}, u32[]{:S(2)}) collective-permute-start(bf16[256,256]{1,0:T(8,128)(2,1)S(1)} %collective-permute-done.21.refs_14_), channel_id=1, source_target_pairs={{0,16},{16,0},{1,17},{17,1},{2,18},{18,2},{3,19},{19,3},{4,20},{20... | collective-permute-start | bytes 393224 | tf_op jit(solution)/shard_map/ppermute | solution.py:231
  89.6 8.1 %collective-permute-start.28 = (bf16[128,512]{1,0:T(8,128)(2,1)S(1)}, bf16[128,512]{1,0:T(8,128)(2,1)S(1)}, u32[]{:S(2)}, u32[]{:S(2)}) collective-permute-start(bf16[128,512]{1,0:T(8,128)(2,1)S(1)} %get-tuple-element.50), channel_id=1, source_target_pairs={{0,2},{1,3},{2,0},{3,1},{4,6},{5,7},{6,4},{7,5},{8,10},{9,11},{10,... | collective-permute-start | bytes 393224 | tf_op jit(solution)/shard_map/ppermute | solution.py:225
  90.3 7.4 %collective-permute-start.29 = (bf16[128,512]{1,0:T(8,128)(2,1)S(1)}, bf16[128,512]{1,0:T(8,128)(2,1)S(1)}, u32[]{:S(2)}, u32[]{:S(2)}) collective-permute-start(bf16[128,512]{1,0:T(8,128)(2,1)S(1)} %get-tuple-element.51), channel_id=1, source_target_pairs={{0,3},{1,2},{2,1},{3,0},{4,7},{5,6},{6,5},{7,4},{8,11},{9,10},{10,... | collective-permute-start | bytes 393224 | tf_op jit(solution)/shard_map/ppermute | solution.py:225
  (14 other events, 122.1 us)

commit v8 on v6

--- a/solution.py
+++ b/solution.py
@@ -17,7 +17,8 @@
 PLANES = 4
 CHUNK = 32
 CONTRACT_ROWS = (((0,), (0,)), ((), ()))
-AHEAD_FLOPS = 30 * 10**12
+AHEAD_FLOPS = 2 * 10**12
+LAST_FLOPS = 5 * 10**11
 VMEM_BYTES = 16 * 1024 * 1024
 
 
@@ -94,11 +95,18 @@
             outs[k][:, slot * rows : (slot + 1) * rows] = acts_ref[:, pl.ds(block_start(inner, rows, bits, k), rows)]
 
 
-def gradient_kernel(inner, rows, acts_at, *refs):
-    acts_refs, cots_refs, out = refs[:inner], refs[inner : 2 * inner], refs[-1]
+def partial_gradient(inner, rows, acts_at, acts_refs, cots_refs):
     columns = jnp.concatenate([ref[:, acts_at : acts_at + rows] for ref in acts_refs], axis=0)
     cots = jnp.concatenate([ref[:, rows:] for ref in cots_refs], axis=0)
-    out[...] = lax.dot_general(columns, cots, CONTRACT_ROWS, preferred_element_type=jnp.float32).astype(out.dtype)
+    return lax.dot_general(columns, cots, CONTRACT_ROWS, preferred_element_type=jnp.float32)
+
+
+def gradient_kernel(inner, rows, acts_at, *refs):
+    total = partial_gradient(inner, rows, acts_at, refs[:inner], refs[inner : 2 * inner])
+    at = 0
+    for out in refs[2 * inner :]:
+        out[...] = total[:, at : at + out.shape[1]].astype(out.dtype)
+        at += out.shape[1]
 
 
 def add_kernel(total, arrived, out):
@@ -109,8 +117,9 @@
 
 
 def gradient_at(at, refs):
-    total, beside, far = refs
-    return total[at, :] + beside[at, :].astype(jnp.float32) + far[at, :].astype(jnp.float32)
+    total = refs[0][at, :]
+    beside, far_left, far_right, straight = (ref[at, :].astype(jnp.float32) for ref in refs[1:])
+    return total + beside + jnp.concatenate([far_left + straight, far_right], axis=1)
 
 
 def steps(half, which, body):
@@ -121,7 +130,7 @@
 
 
 def drift_kernel(*refs):
-    gradient_refs, (weights, first, second, anchor), drift_ref = refs[:3], refs[3:7], refs[7]
+    gradient_refs, (weights, first, second, anchor), drift_ref = refs[:-5], refs[-5:-1], refs[-1]
 
     def body(here, at):
         gradient = gradient_at(at, gradient_refs)
@@ -132,7 +141,7 @@
 
 
 def update_kernel(*refs):
-    gradient_refs, (weights, first, second, anchor), (first_ref, drift_ref) = refs[:3], refs[3:7], refs[7:]
+    gradient_refs, (weights, first, second, anchor), (first_ref, drift_ref) = refs[:-6], refs[-6:-2], refs[-2:]
     half = drift_ref.shape[0]
     r = lax.axis_index("rep")
 
@@ -192,7 +201,7 @@
 def on_device(acts, value_cots, inner_weights, first_moment, second_moment, anchor, outer_momentum):
     inner = lax.axis_size("fsdp") // PLANES
     rows, width = anchor.shape
-    if inner != 4 or lax.axis_size("rep") != 2 or rows % 256 or width % 128:
+    if inner != 4 or lax.axis_size("rep") != 2 or rows % 256 or width % 512:
         return general(acts, value_cots, inner_weights, first_moment, second_moment, anchor, outer_momentum)
     tokens = acts.shape[1]
     half = rows // 2
@@ -214,24 +223,28 @@
     kernel = partial(pack_first_kernel, inner, rows)
     first = around(call(kernel, "pack", out, [acts[0], value_cots[0]], 0, sems, space=pltpu.HBM))
 
-    def pack(blocks, after):
+    def pack(blocks, after, flops=0):
         out = [jax.ShapeDtypeStruct((tokens, len(blocks) * rows), jnp.bfloat16)] * inner
-        return call(partial(pack_kernel, inner, rows, blocks), "pack", out, [acts[0]], 0, after=after)
+        return call(partial(pack_kernel, inner, rows, blocks), "pack", out, [acts[0]], flops, after=after)
 
     second = around(pack((2, 1), first[1:2]))
-    last = around(pack((0,), second[1:]))
     full = jax.ShapeDtypeStruct((rows, width), jnp.float32)
     sent = jax.ShapeDtypeStruct((rows, width), jnp.bfloat16)
+    piece = jax.ShapeDtypeStruct((rows, width // 2), jnp.bfloat16)
+    kept = jax.ShapeDtypeStruct((rows, width // 2), jnp.float32)
 
     def gradient(message, at, out, flops=2 * inner * tokens * rows * width, after=()):
-        return call(partial(gradient_kernel, inner, rows, at), "gradient", [out], message + first, flops, after=after)[0]
-
-    beside_far = planes(gradient(first, 0, sent), 1)
-    for_far = gradient(second, 0, full, AHEAD_FLOPS)
-    (for_far,) = call(add_kernel, "add", [sent], [for_far, beside_far], 0)
-    far = planes(for_far, 2)
-    beside = planes(gradient(second, rows, sent, AHEAD_FLOPS // 6, [for_far]), 1)
-    known = [gradient(last, 0, full), beside, far, inner_weights[0], first_moment[0], second_moment[0], anchor]
+        return call(partial(gradient_kernel, inner, rows, at), "gradient", out, message + first, flops, after=after)
+
+    straight, beside_far = gradient(first, 0, [piece] * 2)
+    straight, beside_far = planes(straight, 3), planes(beside_far, 1)
+    for_far, to_add = gradient(second, 0, [piece, kept])
+    (added,) = call(add_kernel, "add", [piece], [to_add, beside_far], AHEAD_FLOPS, after=[straight])
+    far = [planes(for_far, 2), planes(added, 2)]
+    (for_beside,) = gradient(second, rows, [sent], after=[added])
+    last = around(pack((0,), [far[0], for_beside], LAST_FLOPS))
+    known = [gradient(last, 0, [full])[0], planes(for_beside, 1), *far, straight]
+    known += [inner_weights[0], first_moment[0], second_moment[0], anchor]
     half_block = jax.ShapeDtypeStruct((half, width), jnp.float32)
     (drift_out,) = call(drift_kernel, "drift", [half_block], known, 0)
     drift_in = swap(drift_out)

time: 98.4 us -> 105 us (1.067)
  starting transfers between devices: 24.8 us -> 29.3 us
  waiting for transfers between devices: 61.4 us -> 58.2 us
  Pallas kernels: 8.71 us -> 11.5 us
  local copies, waits for them, and re-layouts: 2.53 us -> 5.04 us
    ppermute x6 -> x8, starting transfers between devices: 8.89 us -> 13.2 us  [planes(): lax.ppermute(x, 'fsdp', [(p * inner + i, (p ^ bits) * inner + i) for p in...]
    pallas_call x14, Pallas kernels: 8.71 us -> 11.5 us  [call(): pl.pallas_call(without_after, out_shape=out, in_specs=[pl.BlockSpec(memor...]
    unnamed x16 -> x60, local copies, waits for them, and re-layouts: 2.53 us -> 5.04 us
    ppermute x6 -> x8, waiting for transfers between devices: 33.7 us -> 32.1 us  [planes(): lax.ppermute(x, 'fsdp', [(p * inner + i, (p ^ bits) * inner + i) for p in...]
    ppermute x12, waiting for transfers between devices: 26.9 us -> 25.6 us  [across(): lax.ppermute(x, 'fsdp', [(p * inner + i, p * inner + (i ^ k)) for p in ra...]
  transfers between devices with their start and end apart: 23 -> 25, of which waited for: 18 -> 15; matrix products, arithmetic and copies ran while one was open for 0% -> 0% of each run, Pallas kernels for 5% -> 8%
where the time goes in v8:
time: 105 us
  waiting for transfers between devices  58.2 us (55%)
  starting transfers between devices  29.3 us (28%)
  Pallas kernels  11.5 us (11%)
  local copies, waits for them, and re-layouts  5.04 us (5%)
    ppermute x8, waiting for transfers between devices, planes(): lax.ppermute(x, 'fsdp', [(p * inner + i, (p ^ bits) * inner + i) for p in...  32.1 us
    ppermute x12, waiting for transfers between devices, across(): lax.ppermute(x, 'fsdp', [(p * inner + i, p * inner + (i ^ k)) for p in ra...  25.6 us
    ppermute x12, starting transfers between devices, across(): lax.ppermute(x, 'fsdp', [(p * inner + i, p * inner + (i ^ k)) for p in ra...  15.5 us
    ppermute x8, starting transfers between devices, planes(): lax.ppermute(x, 'fsdp', [(p * inner + i, (p ^ bits) * inner + i) for p in...  13.2 us
    pallas_call x14, Pallas kernels, call(): pl.pallas_call(without_after, out_shape=out, in_specs=[pl.BlockSpec(memor...  11.5 us
    unnamed x60, local copies, waits for them, and re-layouts  5.04 us
  transfers between devices with their start and end apart: 25, of which 15 were waited for; matrix products, arithmetic and copies ran while one was open for 0% of the time, Pallas kernels for 8%

profile of v8, /device:TPU:0, one launch (start us, length us, event | category | flops | bytes accessed | tf_op | source)
XLA Modules:
  0.0 105.1 jit_solution(13764845168794263077)
XLA Ops:
  0.6 1.6 %copy-done.9 = bf16[1,128,8192]{2,1,0:T(8,128)(2,1)S(1)} copy-done((bf16[1,128,8192]{2,1,0:T(8,128)(2,1)S(1)}, bf16[1,128,8192]{2,1,0:T(8,128)(2,1)}, u32[]{:S(2)}) %copy-start.9) | copy-done | bytes 2097176
  3.4 3.0 %collective-permute-start = (bf16[128,1024]{1,0:T(8,128)(2,1)S(1)}, bf16[128,1024]{1,0:T(8,128)(2,1)S(1)}, u32[]{:S(2)}, u32[]{:S(2)}) collective-permute-start(bf16[128,1024]{1,0:T(8,128)(2,1)S(1)} %get-tuple-element.24), channel_id=1, source_target_pairs={{0,1},{1,0},{2,3},{3,2},{4,5},{5,4},{6,7},{7,6},{8,9},{9,8},{10,11... | collective-permute-start | bytes 786440 | tf_op jit(solution)/shard_map/ppermute | solution.py:213
  6.4 1.5 %collective-permute-start.4 = (bf16[128,1024]{1,0:T(8,128)(2,1)S(1)}, bf16[128,1024]{1,0:T(8,128)(2,1)S(1)}, u32[]{:S(2)}, u32[]{:S(2)}) collective-permute-start(bf16[128,1024]{1,0:T(8,128)(2,1)S(1)} %get-tuple-element.30), channel_id=1, source_target_pairs={{0,2},{1,3},{2,0},{3,1},{4,6},{5,7},{6,4},{7,5},{8,10},{9,11},{10,... | collective-permute-start | bytes 786440 | tf_op jit(solution)/shard_map/ppermute | solution.py:213
  7.9 5.6 %collective-permute-done.refs_1_.refs_5_.refs_2_ = bf16[128,1024]{1,0:T(8,128)(2,1)S(1)} collective-permute-done((bf16[128,1024]{1,0:T(8,128)(2,1)S(1)}, bf16[128,1024]{1,0:T(8,128)(2,1)S(1)}, u32[]{:S(2)}, u32[]{:S(2)}) %collective-permute-start) | collective-permute-done | bytes 262176 | tf_op jit(solution)/shard_map/ppermute | solution.py:213
  13.6 2.1 %collective-permute-start.1 = (bf16[128,1024]{1,0:T(8,128)(2,1)S(1)}, bf16[128,1024]{1,0:T(8,128)(2,1)S(1)}, u32[]{:S(2)}, u32[]{:S(2)}) collective-permute-start(bf16[128,1024]{1,0:T(8,128)(2,1)S(1)} %get-tuple-element.26), channel_id=1, source_target_pairs={{0,1},{1,0},{2,3},{3,2},{4,5},{5,4},{6,7},{7,6},{8,9},{9,8},{10,11... | collective-permute-start | bytes 786440 | tf_op jit(solution)/shard_map/ppermute | solution.py:213
  15.7 1.5 %collective-permute-start.2 = (bf16[128,1024]{1,0:T(8,128)(2,1)S(1)}, bf16[128,1024]{1,0:T(8,128)(2,1)S(1)}, u32[]{:S(2)}, u32[]{:S(2)}) collective-permute-start(bf16[128,1024]{1,0:T(8,128)(2,1)S(1)} %get-tuple-element.27), channel_id=1, source_target_pairs={{0,2},{1,3},{2,0},{3,1},{4,6},{5,7},{6,4},{7,5},{8,10},{9,11},{10,... | collective-permute-start | bytes 786440 | tf_op jit(solution)/shard_map/ppermute | solution.py:213
  17.3 2.9 %collective-permute-done.4.refs_6_.refs_2_.refs_3_ = bf16[128,1024]{1,0:T(8,128)(2,1)S(1)} collective-permute-done((bf16[128,1024]{1,0:T(8,128)(2,1)S(1)}, bf16[128,1024]{1,0:T(8,128)(2,1)S(1)}, u32[]{:S(2)}, u32[]{:S(2)}) %collective-permute-start.4) | collective-permute-done | bytes 262176 | tf_op jit(solution)/shard_map/ppermute | solution.py:213
  21.2 1.6 %collective-permute-start.7 = (bf16[512,256]{1,0:T(8,128)(2,1)S(1)}, bf16[512,256]{1,0:T(8,128)(2,1)S(1)}, u32[]{:S(2)}, u32[]{:S(2)}) collective-permute-start(bf16[512,256]{1,0:T(8,128)(2,1)S(1)} %get-tuple-element.34), channel_id=1, source_target_pairs={{0,4},{1,5},{2,6},{3,7},{4,0},{5,1},{6,2},{7,3},{8,12},{9,13},{10,... | collective-permute-start | bytes 786440 | tf_op jit(solution)/shard_map/ppermute | solution.py:210
  22.8 2.5 %collective-permute-start.8 = (bf16[512,256]{1,0:T(8,128)(2,1)S(1)}, bf16[512,256]{1,0:T(8,128)(2,1)S(1)}, u32[]{:S(2)}, u32[]{:S(2)}) collective-permute-start(bf16[512,256]{1,0:T(8,128)(2,1)S(1)} %get-tuple-element.35), channel_id=1, source_target_pairs={{0,12},{1,13},{2,14},{3,15},{4,8},{5,9},{6,10},{7,11},{8,4},{9,5},... | collective-permute-start | bytes 786440 | tf_op jit(solution)/shard_map/ppermute | solution.py:210
  25.3 5.7 %collective-permute-done.2.refs_2_.refs_6_ = bf16[128,1024]{1,0:T(8,128)(2,1)S(1)} collective-permute-done((bf16[128,1024]{1,0:T(8,128)(2,1)S(1)}, bf16[128,1024]{1,0:T(8,128)(2,1)S(1)}, u32[]{:S(2)}, u32[]{:S(2)}) %collective-permute-start.2) | collective-permute-done | bytes 262176 | tf_op jit(solution)/shard_map/ppermute | solution.py:213
  32.2 2.6 %collective-permute-start.6 = (bf16[512,256]{1,0:T(8,128)(2,1)}, bf16[512,256]{1,0:T(8,128)(2,1)}, u32[]{:S(2)}, u32[]{:S(2)}) collective-permute-start(bf16[512,256]{1,0:T(8,128)(2,1)} %get-tuple-element.32), channel_id=1, source_target_pairs={{0,8},{1,9},{2,10},{3,11},{4,12},{5,13},{6,14},{7,15},{8,0},{9,1},... | collective-permute-start | bytes 786440 | tf_op jit(solution)/shard_map/ppermute | solution.py:210
  35.8 1.8 %collective-permute-start.13 = (bf16[512,256]{1,0:T(8,128)(2,1)}, bf16[512,256]{1,0:T(8,128)(2,1)}, u32[]{:S(2)}, u32[]{:S(2)}) collective-permute-start(bf16[512,256]{1,0:T(8,128)(2,1)} %add.1.refs_8_), channel_id=1, source_target_pairs={{0,8},{1,9},{2,10},{3,11},{4,12},{5,13},{6,14},{7,15},{8,0},{9,1},... | collective-permute-start | bytes 786440 | tf_op jit(solution)/shard_map/ppermute | solution.py:210
  39.2 13.7 %collective-permute-done.6.refs_1_.refs_2_ = bf16[512,256]{1,0:T(8,128)(2,1)} collective-permute-done((bf16[512,256]{1,0:T(8,128)(2,1)}, bf16[512,256]{1,0:T(8,128)(2,1)}, u32[]{:S(2)}, u32[]{:S(2)}) %collective-permute-start.6) | collective-permute-done | bytes 262176 | tf_op jit(solution)/shard_map/ppermute | solution.py:210
  53.0 1.5 %collective-permute-start.9 = (bf16[128,512]{1,0:T(8,128)(2,1)S(1)}, bf16[128,512]{1,0:T(8,128)(2,1)S(1)}, u32[]{:S(2)}, u32[]{:S(2)}) collective-permute-start(bf16[128,512]{1,0:T(8,128)(2,1)S(1)} %get-tuple-element.37), channel_id=1, source_target_pairs={{0,1},{1,0},{2,3},{3,2},{4,5},{5,4},{6,7},{7,6},{8,9},{9,8},{10,11... | collective-permute-start | bytes 393224 | tf_op jit(solution)/shard_map/ppermute | solution.py:213
  55.1 1.5 %collective-permute-start.11 = (bf16[128,512]{1,0:T(8,128)(2,1)S(1)}, bf16[128,512]{1,0:T(8,128)(2,1)S(1)}, u32[]{:S(2)}, u32[]{:S(2)}) collective-permute-start(bf16[128,512]{1,0:T(8,128)(2,1)S(1)} %get-tuple-element.39), channel_id=1, source_target_pairs={{0,3},{1,2},{2,1},{3,0},{4,7},{5,6},{6,5},{7,4},{8,11},{9,10},{10,... | collective-permute-start | bytes 393224 | tf_op jit(solution)/shard_map/ppermute | solution.py:213
  56.6 2.7 %collective-permute-done.9.refs_1_ = bf16[128,512]{1,0:T(8,128)(2,1)S(1)} collective-permute-done((bf16[128,512]{1,0:T(8,128)(2,1)S(1)}, bf16[128,512]{1,0:T(8,128)(2,1)S(1)}, u32[]{:S(2)}, u32[]{:S(2)}) %collective-permute-start.9) | collective-permute-done | bytes 131104 | tf_op jit(solution)/shard_map/ppermute | solution.py:213
  63.9 1.7 %drift.1 = f32[256,512]{1,0:T(8,128)S(1)} custom-call(f32[512,512]{1,0:T(8,128)S(1)} %gradient.7.refs_0_, bf16[512,512]{1,0:T(8,128)(2,1)} %collective-permute-done.12.refs_1_, bf16[512,256]{1,0:T(8,128)(2,1)} %collective-permute-done.6.refs_1_.refs_2_, bf16[512,256]{1,0:T(8,128)(2,1)} %collective-permute-done.13.refs_3_, bf16[512,256]{1,0:T(8,128)(2,1)S(1)} %copy-done.27, ...), custom_call_target="tpu_custom_call" | custom-call | bytes 7077888 | tf_op jit(solution)/shard_map/drift/pallas_call | solution.py:62
  65.8 2.9 %update.1 = (f32[512,512]{1,0:T(8,128)}, f32[256,512]{1,0:T(8,128)S(1)}) custom-call(f32[512,512]{1,0:T(8,128)S(1)} %gradient.7.refs_0_, bf16[512,512]{1,0:T(8,128)(2,1)} %collective-permute-done.12.refs_1_, bf16[512,256]{1,0:T(8,128)(2,1)} %collective-permute-done.6.refs_1_.refs_2_, bf16[512,256]{1,0:T(8,128)(2,1)} %collective-permute-done.13.refs_3_, ...), custom_call_target="tpu_custom_call" | custom-call | bytes 8126464 | tf_op jit(solution)/shard_map/update/pallas_call | solution.py:62
  70.0 3.3 %collective-permute-start.16 = (bf16[256,512]{1,0:T(8,128)(2,1)S(1)}, bf16[256,512]{1,0:T(8,128)(2,1)S(1)}, u32[]{:S(2)}, u32[]{:S(2)}) collective-permute-start(bf16[256,512]{1,0:T(8,128)(2,1)S(1)} %outer.1.refs_8_), channel_id=1, source_target_pairs={{0,4},{1,5},{2,6},{3,7},{4,0},{5,1},{6,2},{7,3},{8,12},{9,13},{10,... | collective-permute-start | bytes 786440 | tf_op jit(solution)/shard_map/ppermute | solution.py:210
  73.3 10.9 %collective-permute-done.18.refs_12_ = bf16[256,512]{1,0:T(8,128)(2,1)S(1)} collective-permute-done((bf16[256,512]{1,0:T(8,128)(2,1)S(1)}, bf16[256,512]{1,0:T(8,128)(2,1)S(1)}, u32[]{:S(2)}, u32[]{:S(2)}) %collective-permute-start.18) | collective-permute-done | bytes 262176 | tf_op jit(solution)/shard_map/ppermute | solution.py:210
  84.9 7.2 %collective-permute-done.20.refs_5_ = bf16[256,512]{1,0:T(8,128)(2,1)S(1)} collective-permute-done((bf16[256,512]{1,0:T(8,128)(2,1)S(1)}, bf16[256,512]{1,0:T(8,128)(2,1)S(1)}, u32[]{:S(2)}, u32[]{:S(2)}) %collective-permute-start.20) | collective-permute-done | bytes 262176 | tf_op jit(solution)/shard_map/ppermute | solution.py:210
  94.1 2.2 %collective-permute-start.22 = (bf16[128,512]{1,0:T(8,128)(2,1)S(1)}, bf16[128,512]{1,0:T(8,128)(2,1)S(1)}, u32[]{:S(2)}, u32[]{:S(2)}) collective-permute-start(bf16[128,512]{1,0:T(8,128)(2,1)S(1)} %get-tuple-element.43), channel_id=1, source_target_pairs={{0,1},{1,0},{2,3},{3,2},{4,5},{5,4},{6,7},{7,6},{8,9},{9,8},{10,11... | collective-permute-start | bytes 393224 | tf_op jit(solution)/shard_map/ppermute | solution.py:213
  97.8 2.3 %collective-permute-done.22.refs_1_ = bf16[128,512]{1,0:T(8,128)(2,1)S(1)} collective-permute-done((bf16[128,512]{1,0:T(8,128)(2,1)S(1)}, bf16[128,512]{1,0:T(8,128)(2,1)S(1)}, u32[]{:S(2)}, u32[]{:S(2)}) %collective-permute-start.22) | collective-permute-done | bytes 131104 | tf_op jit(solution)/shard_map/ppermute | solution.py:213
  100.2 4.2 %collective-permute-done.23.refs_2_ = bf16[128,512]{1,0:T(8,128)(2,1)S(1)} collective-permute-done((bf16[128,512]{1,0:T(8,128)(2,1)S(1)}, bf16[128,512]{1,0:T(8,128)(2,1)S(1)}, u32[]{:S(2)}, u32[]{:S(2)}) %collective-permute-start.23) | collective-permute-done | bytes 131104 | tf_op jit(solution)/shard_map/ppermute | solution.py:213
  (100 shorter events, 17.4 us)
Async XLA Ops:
  3.4 10.1 %collective-permute-start = (bf16[128,1024]{1,0:T(8,128)(2,1)S(1)}, bf16[128,1024]{1,0:T(8,128)(2,1)S(1)}, u32[]{:S(2)}, u32[]{:S(2)}) collective-permute-start(bf16[128,1024]{1,0:T(8,128)(2,1)S(1)} %get-tuple-element.24), channel_id=1, source_target_pairs={{0,1},{1,0},{2,3},{3,2},{4,5},{5,4},{6,7},{7,6},{8,9},{9,8},{10,11... | collective-permute-start | bytes 786440 | tf_op jit(solution)/shard_map/ppermute | solution.py:213
  6.4 13.8 %collective-permute-start.4 = (bf16[128,1024]{1,0:T(8,128)(2,1)S(1)}, bf16[128,1024]{1,0:T(8,128)(2,1)S(1)}, u32[]{:S(2)}, u32[]{:S(2)}) collective-permute-start(bf16[128,1024]{1,0:T(8,128)(2,1)S(1)} %get-tuple-element.30), channel_id=1, source_target_pairs={{0,2},{1,3},{2,0},{3,1},{4,6},{5,7},{6,4},{7,5},{8,10},{9,11},{10,... | collective-permute-start | bytes 786440 | tf_op jit(solution)/shard_map/ppermute | solution.py:213
  7.9 12.8 %collective-permute-start.5 = (bf16[128,1024]{1,0:T(8,128)(2,1)S(1)}, bf16[128,1024]{1,0:T(8,128)(2,1)S(1)}, u32[]{:S(2)}, u32[]{:S(2)}) collective-permute-start(bf16[128,1024]{1,0:T(8,128)(2,1)S(1)} %get-tuple-element.31), channel_id=1, source_target_pairs={{0,3},{1,2},{2,1},{3,0},{4,7},{5,6},{6,5},{7,4},{8,11},{9,10},{10,... | collective-permute-start | bytes 786440 | tf_op jit(solution)/shard_map/ppermute | solution.py:213
  13.6 11.7 %collective-permute-start.1 = (bf16[128,1024]{1,0:T(8,128)(2,1)S(1)}, bf16[128,1024]{1,0:T(8,128)(2,1)S(1)}, u32[]{:S(2)}, u32[]{:S(2)}) collective-permute-start(bf16[128,1024]{1,0:T(8,128)(2,1)S(1)} %get-tuple-element.26), channel_id=1, source_target_pairs={{0,1},{1,0},{2,3},{3,2},{4,5},{5,4},{6,7},{7,6},{8,9},{9,8},{10,11... | collective-permute-start | bytes 786440 | tf_op jit(solution)/shard_map/ppermute | solution.py:213
  15.7 15.3 %collective-permute-start.2 = (bf16[128,1024]{1,0:T(8,128)(2,1)S(1)}, bf16[128,1024]{1,0:T(8,128)(2,1)S(1)}, u32[]{:S(2)}, u32[]{:S(2)}) collective-permute-start(bf16[128,1024]{1,0:T(8,128)(2,1)S(1)} %get-tuple-element.27), channel_id=1, source_target_pairs={{0,2},{1,3},{2,0},{3,1},{4,6},{5,7},{6,4},{7,5},{8,10},{9,11},{10,... | collective-permute-start | bytes 786440 | tf_op jit(solution)/shard_map/ppermute | solution.py:213
  17.2 13.8 %collective-permute-start.3 = (bf16[128,1024]{1,0:T(8,128)(2,1)S(1)}, bf16[128,1024]{1,0:T(8,128)(2,1)S(1)}, u32[]{:S(2)}, u32[]{:S(2)}) collective-permute-start(bf16[128,1024]{1,0:T(8,128)(2,1)S(1)} %get-tuple-element.28), channel_id=1, source_target_pairs={{0,3},{1,2},{2,1},{3,0},{4,7},{5,6},{6,5},{7,4},{8,11},{9,10},{10,... | collective-permute-start | bytes 786440 | tf_op jit(solution)/shard_map/ppermute | solution.py:213
  21.2 13.6 %collective-permute-start.7 = (bf16[512,256]{1,0:T(8,128)(2,1)S(1)}, bf16[512,256]{1,0:T(8,128)(2,1)S(1)}, u32[]{:S(2)}, u32[]{:S(2)}) collective-permute-start(bf16[512,256]{1,0:T(8,128)(2,1)S(1)} %get-tuple-element.34), channel_id=1, source_target_pairs={{0,4},{1,5},{2,6},{3,7},{4,0},{5,1},{6,2},{7,3},{8,12},{9,13},{10,... | collective-permute-start | bytes 786440 | tf_op jit(solution)/shard_map/ppermute | solution.py:210
  22.8 12.1 %collective-permute-start.8 = (bf16[512,256]{1,0:T(8,128)(2,1)S(1)}, bf16[512,256]{1,0:T(8,128)(2,1)S(1)}, u32[]{:S(2)}, u32[]{:S(2)}) collective-permute-start(bf16[512,256]{1,0:T(8,128)(2,1)S(1)} %get-tuple-element.35), channel_id=1, source_target_pairs={{0,12},{1,13},{2,14},{3,15},{4,8},{5,9},{6,10},{7,11},{8,4},{9,5},... | collective-permute-start | bytes 786440 | tf_op jit(solution)/shard_map/ppermute | solution.py:210
  32.2 20.7 %collective-permute-start.6 = (bf16[512,256]{1,0:T(8,128)(2,1)}, bf16[512,256]{1,0:T(8,128)(2,1)}, u32[]{:S(2)}, u32[]{:S(2)}) collective-permute-start(bf16[512,256]{1,0:T(8,128)(2,1)} %get-tuple-element.32), channel_id=1, source_target_pairs={{0,8},{1,9},{2,10},{3,11},{4,12},{5,13},{6,14},{7,15},{8,0},{9,1},... | collective-permute-start | bytes 786440 | tf_op jit(solution)/shard_map/ppermute | solution.py:210
  35.8 25.6 %collective-permute-start.13 = (bf16[512,256]{1,0:T(8,128)(2,1)}, bf16[512,256]{1,0:T(8,128)(2,1)}, u32[]{:S(2)}, u32[]{:S(2)}) collective-permute-start(bf16[512,256]{1,0:T(8,128)(2,1)} %add.1.refs_8_), channel_id=1, source_target_pairs={{0,8},{1,9},{2,10},{3,11},{4,12},{5,13},{6,14},{7,15},{8,0},{9,1},... | collective-permute-start | bytes 786440 | tf_op jit(solution)/shard_map/ppermute | solution.py:210
  38.9 22.5 %collective-permute-start.12 = (bf16[512,512]{1,0:T(8,128)(2,1)}, bf16[512,512]{1,0:T(8,128)(2,1)}, u32[]{:S(2)}, u32[]{:S(2)}) collective-permute-start(bf16[512,512]{1,0:T(8,128)(2,1)} %gradient.6.refs_2_), channel_id=1, source_target_pairs={{0,4},{1,5},{2,6},{3,7},{4,0},{5,1},{6,2},{7,3},{8,12},{9,13},{10,... | collective-permute-start | bytes 1572872 | tf_op jit(solution)/shard_map/ppermute | solution.py:210
  53.0 6.3 %collective-permute-start.9 = (bf16[128,512]{1,0:T(8,128)(2,1)S(1)}, bf16[128,512]{1,0:T(8,128)(2,1)S(1)}, u32[]{:S(2)}, u32[]{:S(2)}) collective-permute-start(bf16[128,512]{1,0:T(8,128)(2,1)S(1)} %get-tuple-element.37), channel_id=1, source_target_pairs={{0,1},{1,0},{2,3},{3,2},{4,5},{5,4},{6,7},{7,6},{8,9},{9,8},{10,11... | collective-permute-start | bytes 393224 | tf_op jit(solution)/shard_map/ppermute | solution.py:213
  54.5 5.0 %collective-permute-start.10 = (bf16[128,512]{1,0:T(8,128)(2,1)S(1)}, bf16[128,512]{1,0:T(8,128)(2,1)S(1)}, u32[]{:S(2)}, u32[]{:S(2)}) collective-permute-start(bf16[128,512]{1,0:T(8,128)(2,1)S(1)} %get-tuple-element.38), channel_id=1, source_target_pairs={{0,2},{1,3},{2,0},{3,1},{4,6},{5,7},{6,4},{7,5},{8,10},{9,11},{10,... | collective-permute-start | bytes 393224 | tf_op jit(solution)/shard_map/ppermute | solution.py:213
  55.1 5.9 %collective-permute-start.11 = (bf16[128,512]{1,0:T(8,128)(2,1)S(1)}, bf16[128,512]{1,0:T(8,128)(2,1)S(1)}, u32[]{:S(2)}, u32[]{:S(2)}) collective-permute-start(bf16[128,512]{1,0:T(8,128)(2,1)S(1)} %get-tuple-element.39), channel_id=1, source_target_pairs={{0,3},{1,2},{2,1},{3,0},{4,7},{5,6},{6,5},{7,4},{8,11},{9,10},{10,... | collective-permute-start | bytes 393224 | tf_op jit(solution)/shard_map/ppermute | solution.py:213
  65.7 3.0 %collective-permute-start.14 = (f32[256,512]{1,0:T(8,128)S(1)}, f32[256,512]{1,0:T(8,128)S(1)}, u32[]{:S(2)}, u32[]{:S(2)}) collective-permute-start(f32[256,512]{1,0:T(8,128)S(1)} %drift.1), channel_id=1, source_target_pairs={{0,16},{16,0},{1,17},{17,1},{2,18},{18,2},{3,19},{19,3},{4,20},{20... | collective-permute-start | bytes 1572872 | tf_op jit(solution)/shard_map/ppermute | solution.py:219
  68.9 15.3 %collective-permute-start.18 = (bf16[256,512]{1,0:T(8,128)(2,1)S(1)}, bf16[256,512]{1,0:T(8,128)(2,1)S(1)}, u32[]{:S(2)}, u32[]{:S(2)}) collective-permute-start(bf16[256,512]{1,0:T(8,128)(2,1)S(1)} %outer.1.refs_8_), channel_id=1, source_target_pairs={{0,8},{1,9},{2,10},{3,11},{4,12},{5,13},{6,14},{7,15},{8,0},{9,1},... | collective-permute-start | bytes 786440 | tf_op jit(solution)/shard_map/ppermute | solution.py:210
  70.0 14.3 %collective-permute-start.16 = (bf16[256,512]{1,0:T(8,128)(2,1)S(1)}, bf16[256,512]{1,0:T(8,128)(2,1)S(1)}, u32[]{:S(2)}, u32[]{:S(2)}) collective-permute-start(bf16[256,512]{1,0:T(8,128)(2,1)S(1)} %outer.1.refs_8_), channel_id=1, source_target_pairs={{0,4},{1,5},{2,6},{3,7},{4,0},{5,1},{6,2},{7,3},{8,12},{9,13},{10,... | collective-permute-start | bytes 786440 | tf_op jit(solution)/shard_map/ppermute | solution.py:210
  84.3 7.8 %collective-permute-start.20 = (bf16[256,512]{1,0:T(8,128)(2,1)S(1)}, bf16[256,512]{1,0:T(8,128)(2,1)S(1)}, u32[]{:S(2)}, u32[]{:S(2)}) collective-permute-start(bf16[256,512]{1,0:T(8,128)(2,1)S(1)} %collective-permute-done.18.refs_12_), channel_id=1, source_target_pairs={{0,4},{1,5},{2,6},{3,7},{4,0},{5,1},{6,2},{7,3},{8,12},{9,13},{10,... | collective-permute-start | bytes 786440 | tf_op jit(solution)/shard_map/ppermute | solution.py:210
  84.3 7.8 %collective-permute-start.15 = (bf16[256,512]{1,0:T(8,128)(2,1)S(1)}, bf16[256,512]{1,0:T(8,128)(2,1)S(1)}, u32[]{:S(2)}, u32[]{:S(2)}) collective-permute-start(bf16[256,512]{1,0:T(8,128)(2,1)S(1)} %outer.1.refs_8_), channel_id=1, source_target_pairs={{0,16},{16,0},{1,17},{17,1},{2,18},{18,2},{3,19},{19,3},{4,20},{20... | collective-permute-start | bytes 786440 | tf_op jit(solution)/shard_map/ppermute | solution.py:219
  84.4 7.7 %collective-permute-start.17 = (bf16[256,512]{1,0:T(8,128)(2,1)S(1)}, bf16[256,512]{1,0:T(8,128)(2,1)S(1)}, u32[]{:S(2)}, u32[]{:S(2)}) collective-permute-start(bf16[256,512]{1,0:T(8,128)(2,1)S(1)} %collective-permute-done.16.refs_10_), channel_id=1, source_target_pairs={{0,16},{16,0},{1,17},{17,1},{2,18},{18,2},{3,19},{19,3},{4,20},{20... | collective-permute-start | bytes 786440 | tf_op jit(solution)/shard_map/ppermute | solution.py:219
  84.8 7.3 %collective-permute-start.19 = (bf16[256,512]{1,0:T(8,128)(2,1)S(1)}, bf16[256,512]{1,0:T(8,128)(2,1)S(1)}, u32[]{:S(2)}, u32[]{:S(2)}) collective-permute-start(bf16[256,512]{1,0:T(8,128)(2,1)S(1)} %collective-permute-done.18.refs_12_), channel_id=1, source_target_pairs={{0,16},{16,0},{1,17},{17,1},{2,18},{18,2},{3,19},{19,3},{4,20},{20... | collective-permute-start | bytes 786440 | tf_op jit(solution)/shard_map/ppermute | solution.py:219
  94.1 6.1 %collective-permute-start.22 = (bf16[128,512]{1,0:T(8,128)(2,1)S(1)}, bf16[128,512]{1,0:T(8,128)(2,1)S(1)}, u32[]{:S(2)}, u32[]{:S(2)}) collective-permute-start(bf16[128,512]{1,0:T(8,128)(2,1)S(1)} %get-tuple-element.43), channel_id=1, source_target_pairs={{0,1},{1,0},{2,3},{3,2},{4,5},{5,4},{6,7},{7,6},{8,9},{9,8},{10,11... | collective-permute-start | bytes 393224 | tf_op jit(solution)/shard_map/ppermute | solution.py:213
  96.3 8.1 %collective-permute-start.23 = (bf16[128,512]{1,0:T(8,128)(2,1)S(1)}, bf16[128,512]{1,0:T(8,128)(2,1)S(1)}, u32[]{:S(2)}, u32[]{:S(2)}) collective-permute-start(bf16[128,512]{1,0:T(8,128)(2,1)S(1)} %get-tuple-element.44), channel_id=1, source_target_pairs={{0,2},{1,3},{2,0},{3,1},{4,6},{5,7},{6,4},{7,5},{8,10},{9,11},{10,... | collective-permute-start | bytes 393224 | tf_op jit(solution)/shard_map/ppermute | solution.py:213
  96.4 7.9 %collective-permute-start.24 = (bf16[128,512]{1,0:T(8,128)(2,1)S(1)}, bf16[128,512]{1,0:T(8,128)(2,1)S(1)}, u32[]{:S(2)}, u32[]{:S(2)}) collective-permute-start(bf16[128,512]{1,0:T(8,128)(2,1)S(1)} %get-tuple-element.45), channel_id=1, source_target_pairs={{0,3},{1,2},{2,1},{3,0},{4,7},{5,6},{6,5},{7,4},{8,11},{9,10},{10,... | collective-permute-start | bytes 393224 | tf_op jit(solution)/shard_map/ppermute | solution.py:213
  (31 other events, 478.3 us)

commit v9 on v6

--- a/solution.py
+++ b/solution.py
@@ -17,7 +17,7 @@
 PLANES = 4
 CHUNK = 32
 CONTRACT_ROWS = (((0,), (0,)), ((), ()))
-AHEAD_FLOPS = 30 * 10**12
+AHEAD_FLOPS = 10**12
 VMEM_BYTES = 16 * 1024 * 1024
 
 
@@ -95,17 +95,13 @@
 
 
 def gradient_kernel(inner, rows, acts_at, *refs):
-    acts_refs, cots_refs, out = refs[:inner], refs[inner : 2 * inner], refs[-1]
+    acts_refs, cots_refs, arrived, out = refs[:inner], refs[inner : 2 * inner], refs[2 * inner : -1], refs[-1]
     columns = jnp.concatenate([ref[:, acts_at : acts_at + rows] for ref in acts_refs], axis=0)
     cots = jnp.concatenate([ref[:, rows:] for ref in cots_refs], axis=0)
-    out[...] = lax.dot_general(columns, cots, CONTRACT_ROWS, preferred_element_type=jnp.float32).astype(out.dtype)
-
-
-def add_kernel(total, arrived, out):
-    @pl.loop(0, out.shape[0] // CHUNK)
-    def _(step):
-        at = pl.ds(pl.multiple_of(step * CHUNK, CHUNK), CHUNK)
-        out[at, :] = (total[at, :] + arrived[at, :].astype(jnp.float32)).astype(out.dtype)
+    total = lax.dot_general(columns, cots, CONTRACT_ROWS, preferred_element_type=jnp.float32)
+    for ref in arrived:
+        total += ref[...].astype(jnp.float32)
+    out[...] = total.astype(out.dtype)
 
 
 def gradient_at(at, refs):
@@ -219,18 +215,18 @@
         return call(partial(pack_kernel, inner, rows, blocks), "pack", out, [acts[0]], 0, after=after)
 
     second = around(pack((2, 1), first[1:2]))
-    last = around(pack((0,), second[1:]))
     full = jax.ShapeDtypeStruct((rows, width), jnp.float32)
     sent = jax.ShapeDtypeStruct((rows, width), jnp.bfloat16)
 
-    def gradient(message, at, out, flops=2 * inner * tokens * rows * width, after=()):
-        return call(partial(gradient_kernel, inner, rows, at), "gradient", [out], message + first, flops, after=after)[0]
+    def gradient(message, at, out, arrived=(), flops=2 * inner * tokens * rows * width):
+        kernel = partial(gradient_kernel, inner, rows, at)
+        return call(kernel, "gradient", [out], message + first + list(arrived), flops)[0]
 
     beside_far = planes(gradient(first, 0, sent), 1)
-    for_far = gradient(second, 0, full, AHEAD_FLOPS)
-    (for_far,) = call(add_kernel, "add", [sent], [for_far, beside_far], 0)
+    beside = planes(gradient(second, rows, sent, flops=AHEAD_FLOPS), 1)
+    for_far = gradient(second, 0, sent, [beside_far])
     far = planes(for_far, 2)
-    beside = planes(gradient(second, rows, sent, AHEAD_FLOPS // 6, [for_far]), 1)
+    last = around(pack((0,), [for_far]))
     known = [gradient(last, 0, full), beside, far, inner_weights[0], first_moment[0], second_moment[0], anchor]
     half_block = jax.ShapeDtypeStruct((half, width), jnp.float32)
     (drift_out,) = call(drift_kernel, "drift", [half_block], known, 0)

time: 98.4 us -> 97.9 us (level)
    ppermute x6, waiting for transfers between devices: 33.7 us -> 32.6 us  [planes(): lax.ppermute(x, 'fsdp', [(p * inner + i, (p ^ bits) * inner + i) for p in...]
    pallas_call x14 -> x13, Pallas kernels: 8.71 us -> 8.55 us  [call(): pl.pallas_call(without_after, out_shape=out, in_specs=[pl.BlockSpec(memor...]
  transfers between devices with their start and end apart: 23 -> 23, of which waited for: 18 -> 19; matrix products, arithmetic and copies ran while one was open for 0% -> 0% of each run, Pallas kernels for 5% -> 7%
where the time goes in v9:
time: 97.9 us; the launch traced here: 97.7 us
  waiting for transfers between devices  60.6 us (62%)
  starting transfers between devices  25.2 us (26%)
  Pallas kernels  8.55 us (9%)
  local copies, waits for them, and re-layouts  2.53 us (3%)
    ppermute x6, waiting for transfers between devices, planes(): lax.ppermute(x, 'fsdp', [(p * inner + i, (p ^ bits) * inner + i) for p in...  32.6 us
    ppermute x12, waiting for transfers between devices, across(): lax.ppermute(x, 'fsdp', [(p * inner + i, p * inner + (i ^ k)) for p in ra...  27.2 us
    ppermute x12, starting transfers between devices, across(): lax.ppermute(x, 'fsdp', [(p * inner + i, p * inner + (i ^ k)) for p in ra...  15.3 us
    ppermute x6, starting transfers between devices, planes(): lax.ppermute(x, 'fsdp', [(p * inner + i, (p ^ bits) * inner + i) for p in...  9.32 us
    pallas_call x13, Pallas kernels, call(): pl.pallas_call(without_after, out_shape=out, in_specs=[pl.BlockSpec(memor...  8.55 us
    unnamed x16, local copies, waits for them, and re-layouts  2.53 us
  transfers between devices with their start and end apart: 23, of which 19 were waited for; matrix products, arithmetic and copies ran while one was open for 0% of the time, Pallas kernels for 7%

profile of v9, /device:TPU:0, one launch (start us, length us, event | category | flops | bytes accessed | tf_op | source)
XLA Modules:
  0.0 97.7 jit_solution(5383454974560733479)
XLA Ops:
  0.6 1.6 %copy-done = bf16[1,128,8192]{2,1,0:T(8,128)(2,1)S(1)} copy-done((bf16[1,128,8192]{2,1,0:T(8,128)(2,1)S(1)}, bf16[1,128,8192]{2,1,0:T(8,128)(2,1)}, u32[]{:S(2)}) %copy-start) | copy-done | bytes 2097176
  3.4 3.0 %collective-permute-start = (bf16[128,1024]{1,0:T(8,128)(2,1)S(1)}, bf16[128,1024]{1,0:T(8,128)(2,1)S(1)}, u32[]{:S(2)}, u32[]{:S(2)}) collective-permute-start(bf16[128,1024]{1,0:T(8,128)(2,1)S(1)} %get-tuple-element.20), channel_id=1, source_target_pairs={{0,1},{1,0},{2,3},{3,2},{4,5},{5,4},{6,7},{7,6},{8,9},{9,8},{10,11... | collective-permute-start | bytes 786440 | tf_op jit(solution)/shard_map/ppermute | solution.py:200
  6.4 1.5 %collective-permute-start.4 = (bf16[128,1024]{1,0:T(8,128)(2,1)S(1)}, bf16[128,1024]{1,0:T(8,128)(2,1)S(1)}, u32[]{:S(2)}, u32[]{:S(2)}) collective-permute-start(bf16[128,1024]{1,0:T(8,128)(2,1)S(1)} %get-tuple-element.26), channel_id=1, source_target_pairs={{0,2},{1,3},{2,0},{3,1},{4,6},{5,7},{6,4},{7,5},{8,10},{9,11},{10,... | collective-permute-start | bytes 786440 | tf_op jit(solution)/shard_map/ppermute | solution.py:200
  7.9 5.6 %collective-permute-done.refs_1_.refs_5_.refs_2_ = bf16[128,1024]{1,0:T(8,128)(2,1)S(1)} collective-permute-done((bf16[128,1024]{1,0:T(8,128)(2,1)S(1)}, bf16[128,1024]{1,0:T(8,128)(2,1)S(1)}, u32[]{:S(2)}, u32[]{:S(2)}) %collective-permute-start) | collective-permute-done | bytes 262176 | tf_op jit(solution)/shard_map/ppermute | solution.py:200
  13.6 2.1 %collective-permute-start.1 = (bf16[128,1024]{1,0:T(8,128)(2,1)S(1)}, bf16[128,1024]{1,0:T(8,128)(2,1)S(1)}, u32[]{:S(2)}, u32[]{:S(2)}) collective-permute-start(bf16[128,1024]{1,0:T(8,128)(2,1)S(1)} %get-tuple-element.22), channel_id=1, source_target_pairs={{0,1},{1,0},{2,3},{3,2},{4,5},{5,4},{6,7},{7,6},{8,9},{9,8},{10,11... | collective-permute-start | bytes 786440 | tf_op jit(solution)/shard_map/ppermute | solution.py:200
  15.7 1.5 %collective-permute-start.2 = (bf16[128,1024]{1,0:T(8,128)(2,1)S(1)}, bf16[128,1024]{1,0:T(8,128)(2,1)S(1)}, u32[]{:S(2)}, u32[]{:S(2)}) collective-permute-start(bf16[128,1024]{1,0:T(8,128)(2,1)S(1)} %get-tuple-element.23), channel_id=1, source_target_pairs={{0,2},{1,3},{2,0},{3,1},{4,6},{5,7},{6,4},{7,5},{8,10},{9,11},{10,... | collective-permute-start | bytes 786440 | tf_op jit(solution)/shard_map/ppermute | solution.py:200
  17.2 2.9 %collective-permute-done.4.refs_2_.refs_6_.refs_3_ = bf16[128,1024]{1,0:T(8,128)(2,1)S(1)} collective-permute-done((bf16[128,1024]{1,0:T(8,128)(2,1)S(1)}, bf16[128,1024]{1,0:T(8,128)(2,1)S(1)}, u32[]{:S(2)}, u32[]{:S(2)}) %collective-permute-start.4) | collective-permute-done | bytes 262176 | tf_op jit(solution)/shard_map/ppermute | solution.py:200
  22.0 1.6 %collective-permute-start.6 = (bf16[512,512]{1,0:T(8,128)(2,1)}, bf16[512,512]{1,0:T(8,128)(2,1)}, u32[]{:S(2)}, u32[]{:S(2)}) collective-permute-start(bf16[512,512]{1,0:T(8,128)(2,1)} %gradient.4), channel_id=1, source_target_pairs={{0,4},{1,5},{2,6},{3,7},{4,0},{5,1},{6,2},{7,3},{8,12},{9,13},{10,... | collective-permute-start | bytes 1572872 | tf_op jit(solution)/shard_map/ppermute | solution.py:197
  24.8 6.2 %collective-permute-done.2.refs_2_.refs_6_ = bf16[128,1024]{1,0:T(8,128)(2,1)S(1)} collective-permute-done((bf16[128,1024]{1,0:T(8,128)(2,1)S(1)}, bf16[128,1024]{1,0:T(8,128)(2,1)S(1)}, u32[]{:S(2)}, u32[]{:S(2)}) %collective-permute-start.2) | collective-permute-done | bytes 262176 | tf_op jit(solution)/shard_map/ppermute | solution.py:200
  31.5 1.6 %collective-permute-start.10 = (bf16[512,512]{1,0:T(8,128)(2,1)S(1)}, bf16[512,512]{1,0:T(8,128)(2,1)S(1)}, u32[]{:S(2)}, u32[]{:S(2)}) collective-permute-start(bf16[512,512]{1,0:T(8,128)(2,1)S(1)} %gradient.7), channel_id=1, source_target_pairs={{0,4},{1,5},{2,6},{3,7},{4,0},{5,1},{6,2},{7,3},{8,12},{9,13},{10,... | collective-permute-start | bytes 1572872 | tf_op jit(solution)/shard_map/ppermute | solution.py:197
  33.1 1.6 %collective-permute-done.6.refs_8_ = bf16[512,512]{1,0:T(8,128)(2,1)} collective-permute-done((bf16[512,512]{1,0:T(8,128)(2,1)}, bf16[512,512]{1,0:T(8,128)(2,1)}, u32[]{:S(2)}, u32[]{:S(2)}) %collective-permute-start.6) | collective-permute-done | bytes 524320 | tf_op jit(solution)/shard_map/ppermute | solution.py:197
  34.7 1.5 %gradient.5.refs_1_ = bf16[512,512]{1,0:T(8,128)(2,1)S(1)} custom-call(bf16[128,1024]{1,0:T(8,128)(2,1)S(1)} %get-tuple-element.21.refs_0_.refs_4_, bf16[128,1024]{1,0:T(8,128)(2,1)S(1)} %collective-permute-done.1.refs_1_.refs_5_, bf16[128,1024]{1,0:T(8,128)(2,1)S(1)} %collective-permute-done.2.refs_2_.refs_6_, ...), custom_call_target="tpu_custom_call" | custom-call | flops 268435456 | bytes 3145728 | tf_op jit(solution)/shard_map/gradient/pallas_call | solution.py:61
  36.3 2.6 %collective-permute-start.11 = (bf16[512,512]{1,0:T(8,128)(2,1)S(1)}, bf16[512,512]{1,0:T(8,128)(2,1)S(1)}, u32[]{:S(2)}, u32[]{:S(2)}) collective-permute-start(bf16[512,512]{1,0:T(8,128)(2,1)S(1)} %gradient.5.refs_1_), channel_id=1, source_target_pairs={{0,8},{1,9},{2,10},{3,11},{4,12},{5,13},{6,14},{7,15},{8,0},{9,1},... | collective-permute-start | bytes 1572872 | tf_op jit(solution)/shard_map/ppermute | solution.py:197
  39.0 1.6 %collective-permute-start.7 = (bf16[128,512]{1,0:T(8,128)(2,1)S(1)}, bf16[128,512]{1,0:T(8,128)(2,1)S(1)}, u32[]{:S(2)}, u32[]{:S(2)}) collective-permute-start(bf16[128,512]{1,0:T(8,128)(2,1)S(1)} %get-tuple-element.29), channel_id=1, source_target_pairs={{0,1},{1,0},{2,3},{3,2},{4,5},{5,4},{6,7},{7,6},{8,9},{9,8},{10,11... | collective-permute-start | bytes 393224 | tf_op jit(solution)/shard_map/ppermute | solution.py:200
  44.0 1.5 %collective-permute-done.8.refs_2_ = bf16[128,512]{1,0:T(8,128)(2,1)S(1)} collective-permute-done((bf16[128,512]{1,0:T(8,128)(2,1)S(1)}, bf16[128,512]{1,0:T(8,128)(2,1)S(1)}, u32[]{:S(2)}, u32[]{:S(2)}) %collective-permute-start.8) | collective-permute-done | bytes 131104 | tf_op jit(solution)/shard_map/ppermute | solution.py:200
  47.4 8.0 %collective-permute-done.10.refs_1_ = bf16[512,512]{1,0:T(8,128)(2,1)S(1)} collective-permute-done((bf16[512,512]{1,0:T(8,128)(2,1)S(1)}, bf16[512,512]{1,0:T(8,128)(2,1)S(1)}, u32[]{:S(2)}, u32[]{:S(2)}) %collective-permute-start.10) | collective-permute-done | bytes 524320 | tf_op jit(solution)/shard_map/ppermute | solution.py:197
  55.4 3.9 %collective-permute-done.11.refs_2_ = bf16[512,512]{1,0:T(8,128)(2,1)S(1)} collective-permute-done((bf16[512,512]{1,0:T(8,128)(2,1)S(1)}, bf16[512,512]{1,0:T(8,128)(2,1)S(1)}, u32[]{:S(2)}, u32[]{:S(2)}) %collective-permute-start.11) | collective-permute-done | bytes 524320 | tf_op jit(solution)/shard_map/ppermute | solution.py:197
  60.0 1.7 %update.1 = (f32[512,512]{1,0:T(8,128)}, f32[256,512]{1,0:T(8,128)S(1)}) custom-call(f32[512,512]{1,0:T(8,128)S(1)} %gradient.6.refs_0_, bf16[512,512]{1,0:T(8,128)(2,1)S(1)} %collective-permute-done.10.refs_1_, bf16[512,512]{1,0:T(8,128)(2,1)S(1)} %collective-permute-done.11.refs_2_, f32[512,512]{1,0:T(8,128)S(1)} %bitcast.11, f32[512,512]{1,0:T(8,128)S(1)} %bitcast.13, ...), custom_call_target="tpu_custom_call" | custom-call | bytes 7864320 | tf_op jit(solution)/shard_map/update/pallas_call | solution.py:61
  62.1 3.4 %collective-permute-start.14 = (bf16[256,512]{1,0:T(8,128)(2,1)S(1)}, bf16[256,512]{1,0:T(8,128)(2,1)S(1)}, u32[]{:S(2)}, u32[]{:S(2)}) collective-permute-start(bf16[256,512]{1,0:T(8,128)(2,1)S(1)} %outer.1.refs_8_), channel_id=1, source_target_pairs={{0,4},{1,5},{2,6},{3,7},{4,0},{5,1},{6,2},{7,3},{8,12},{9,13},{10,... | collective-permute-start | bytes 786440 | tf_op jit(solution)/shard_map/ppermute | solution.py:197
  65.5 11.7 %collective-permute-done.16.refs_12_ = bf16[256,512]{1,0:T(8,128)(2,1)S(1)} collective-permute-done((bf16[256,512]{1,0:T(8,128)(2,1)S(1)}, bf16[256,512]{1,0:T(8,128)(2,1)S(1)}, u32[]{:S(2)}, u32[]{:S(2)}) %collective-permute-start.16) | collective-permute-done | bytes 262176 | tf_op jit(solution)/shard_map/ppermute | solution.py:197
  77.7 7.4 %collective-permute-done.18.refs_5_ = bf16[256,512]{1,0:T(8,128)(2,1)S(1)} collective-permute-done((bf16[256,512]{1,0:T(8,128)(2,1)S(1)}, bf16[256,512]{1,0:T(8,128)(2,1)S(1)}, u32[]{:S(2)}, u32[]{:S(2)}) %collective-permute-start.18) | collective-permute-done | bytes 262176 | tf_op jit(solution)/shard_map/ppermute | solution.py:197
  90.6 2.5 %collective-permute-done.20.refs_1_ = bf16[128,512]{1,0:T(8,128)(2,1)S(1)} collective-permute-done((bf16[128,512]{1,0:T(8,128)(2,1)S(1)}, bf16[128,512]{1,0:T(8,128)(2,1)S(1)}, u32[]{:S(2)}, u32[]{:S(2)}) %collective-permute-start.20) | collective-permute-done | bytes 131104 | tf_op jit(solution)/shard_map/ppermute | solution.py:200
  93.1 2.0 %collective-permute-done.21.refs_2_ = bf16[128,512]{1,0:T(8,128)(2,1)S(1)} collective-permute-done((bf16[128,512]{1,0:T(8,128)(2,1)S(1)}, bf16[128,512]{1,0:T(8,128)(2,1)S(1)}, u32[]{:S(2)}, u32[]{:S(2)}) %collective-permute-start.21) | collective-permute-done | bytes 131104 | tf_op jit(solution)/shard_map/ppermute | solution.py:200
  95.1 1.8 %collective-permute-done.22.refs_3_ = bf16[128,512]{1,0:T(8,128)(2,1)S(1)} collective-permute-done((bf16[128,512]{1,0:T(8,128)(2,1)S(1)}, bf16[128,512]{1,0:T(8,128)(2,1)S(1)}, u32[]{:S(2)}, u32[]{:S(2)}) %collective-permute-start.22) | collective-permute-done | bytes 131104 | tf_op jit(solution)/shard_map/ppermute | solution.py:200
  (51 shorter events, 18.1 us)
Async XLA Ops:
  3.4 10.1 %collective-permute-start = (bf16[128,1024]{1,0:T(8,128)(2,1)S(1)}, bf16[128,1024]{1,0:T(8,128)(2,1)S(1)}, u32[]{:S(2)}, u32[]{:S(2)}) collective-permute-start(bf16[128,1024]{1,0:T(8,128)(2,1)S(1)} %get-tuple-element.20), channel_id=1, source_target_pairs={{0,1},{1,0},{2,3},{3,2},{4,5},{5,4},{6,7},{7,6},{8,9},{9,8},{10,11... | collective-permute-start | bytes 786440 | tf_op jit(solution)/shard_map/ppermute | solution.py:200
  6.4 13.8 %collective-permute-start.4 = (bf16[128,1024]{1,0:T(8,128)(2,1)S(1)}, bf16[128,1024]{1,0:T(8,128)(2,1)S(1)}, u32[]{:S(2)}, u32[]{:S(2)}) collective-permute-start(bf16[128,1024]{1,0:T(8,128)(2,1)S(1)} %get-tuple-element.26), channel_id=1, source_target_pairs={{0,2},{1,3},{2,0},{3,1},{4,6},{5,7},{6,4},{7,5},{8,10},{9,11},{10,... | collective-permute-start | bytes 786440 | tf_op jit(solution)/shard_map/ppermute | solution.py:200
  7.9 12.8 %collective-permute-start.5 = (bf16[128,1024]{1,0:T(8,128)(2,1)S(1)}, bf16[128,1024]{1,0:T(8,128)(2,1)S(1)}, u32[]{:S(2)}, u32[]{:S(2)}) collective-permute-start(bf16[128,1024]{1,0:T(8,128)(2,1)S(1)} %get-tuple-element.27), channel_id=1, source_target_pairs={{0,3},{1,2},{2,1},{3,0},{4,7},{5,6},{6,5},{7,4},{8,11},{9,10},{10,... | collective-permute-start | bytes 786440 | tf_op jit(solution)/shard_map/ppermute | solution.py:200
  13.6 11.2 %collective-permute-start.1 = (bf16[128,1024]{1,0:T(8,128)(2,1)S(1)}, bf16[128,1024]{1,0:T(8,128)(2,1)S(1)}, u32[]{:S(2)}, u32[]{:S(2)}) collective-permute-start(bf16[128,1024]{1,0:T(8,128)(2,1)S(1)} %get-tuple-element.22), channel_id=1, source_target_pairs={{0,1},{1,0},{2,3},{3,2},{4,5},{5,4},{6,7},{7,6},{8,9},{9,8},{10,11... | collective-permute-start | bytes 786440 | tf_op jit(solution)/shard_map/ppermute | solution.py:200
  15.7 15.3 %collective-permute-start.2 = (bf16[128,1024]{1,0:T(8,128)(2,1)S(1)}, bf16[128,1024]{1,0:T(8,128)(2,1)S(1)}, u32[]{:S(2)}, u32[]{:S(2)}) collective-permute-start(bf16[128,1024]{1,0:T(8,128)(2,1)S(1)} %get-tuple-element.23), channel_id=1, source_target_pairs={{0,2},{1,3},{2,0},{3,1},{4,6},{5,7},{6,4},{7,5},{8,10},{9,11},{10,... | collective-permute-start | bytes 786440 | tf_op jit(solution)/shard_map/ppermute | solution.py:200
  17.2 13.8 %collective-permute-start.3 = (bf16[128,1024]{1,0:T(8,128)(2,1)S(1)}, bf16[128,1024]{1,0:T(8,128)(2,1)S(1)}, u32[]{:S(2)}, u32[]{:S(2)}) collective-permute-start(bf16[128,1024]{1,0:T(8,128)(2,1)S(1)} %get-tuple-element.24), channel_id=1, source_target_pairs={{0,3},{1,2},{2,1},{3,0},{4,7},{5,6},{6,5},{7,4},{8,11},{9,10},{10,... | collective-permute-start | bytes 786440 | tf_op jit(solution)/shard_map/ppermute | solution.py:200
  22.0 12.8 %collective-permute-start.6 = (bf16[512,512]{1,0:T(8,128)(2,1)}, bf16[512,512]{1,0:T(8,128)(2,1)}, u32[]{:S(2)}, u32[]{:S(2)}) collective-permute-start(bf16[512,512]{1,0:T(8,128)(2,1)} %gradient.4), channel_id=1, source_target_pairs={{0,4},{1,5},{2,6},{3,7},{4,0},{5,1},{6,2},{7,3},{8,12},{9,13},{10,... | collective-permute-start | bytes 1572872 | tf_op jit(solution)/shard_map/ppermute | solution.py:197
  31.5 23.9 %collective-permute-start.10 = (bf16[512,512]{1,0:T(8,128)(2,1)S(1)}, bf16[512,512]{1,0:T(8,128)(2,1)S(1)}, u32[]{:S(2)}, u32[]{:S(2)}) collective-permute-start(bf16[512,512]{1,0:T(8,128)(2,1)S(1)} %gradient.7), channel_id=1, source_target_pairs={{0,4},{1,5},{2,6},{3,7},{4,0},{5,1},{6,2},{7,3},{8,12},{9,13},{10,... | collective-permute-start | bytes 1572872 | tf_op jit(solution)/shard_map/ppermute | solution.py:197
  36.2 23.0 %copy-start.2 = (f32[512,512]{1,0:T(8,128)S(1)}, f32[512,512]{1,0:T(8,128)}, u32[]{:S(2)}) copy-start(f32[512,512]{1,0:T(8,128)} %refs_2_.1) | copy-start | bytes 3145732
  36.3 23.0 %collective-permute-start.11 = (bf16[512,512]{1,0:T(8,128)(2,1)S(1)}, bf16[512,512]{1,0:T(8,128)(2,1)S(1)}, u32[]{:S(2)}, u32[]{:S(2)}) collective-permute-start(bf16[512,512]{1,0:T(8,128)(2,1)S(1)} %gradient.5.refs_1_), channel_id=1, source_target_pairs={{0,8},{1,9},{2,10},{3,11},{4,12},{5,13},{6,14},{7,15},{8,0},{9,1},... | collective-permute-start | bytes 1572872 | tf_op jit(solution)/shard_map/ppermute | solution.py:197
  39.0 5.0 %collective-permute-start.7 = (bf16[128,512]{1,0:T(8,128)(2,1)S(1)}, bf16[128,512]{1,0:T(8,128)(2,1)S(1)}, u32[]{:S(2)}, u32[]{:S(2)}) collective-permute-start(bf16[128,512]{1,0:T(8,128)(2,1)S(1)} %get-tuple-element.29), channel_id=1, source_target_pairs={{0,1},{1,0},{2,3},{3,2},{4,5},{5,4},{6,7},{7,6},{8,9},{9,8},{10,11... | collective-permute-start | bytes 393224 | tf_op jit(solution)/shard_map/ppermute | solution.py:200
  40.6 5.0 %collective-permute-start.8 = (bf16[128,512]{1,0:T(8,128)(2,1)S(1)}, bf16[128,512]{1,0:T(8,128)(2,1)S(1)}, u32[]{:S(2)}, u32[]{:S(2)}) collective-permute-start(bf16[128,512]{1,0:T(8,128)(2,1)S(1)} %get-tuple-element.30), channel_id=1, source_target_pairs={{0,2},{1,3},{2,0},{3,1},{4,6},{5,7},{6,4},{7,5},{8,10},{9,11},{10,... | collective-permute-start | bytes 393224 | tf_op jit(solution)/shard_map/ppermute | solution.py:200
  41.1 5.9 %collective-permute-start.9 = (bf16[128,512]{1,0:T(8,128)(2,1)S(1)}, bf16[128,512]{1,0:T(8,128)(2,1)S(1)}, u32[]{:S(2)}, u32[]{:S(2)}) collective-permute-start(bf16[128,512]{1,0:T(8,128)(2,1)S(1)} %get-tuple-element.31), channel_id=1, source_target_pairs={{0,3},{1,2},{2,1},{3,0},{4,7},{5,6},{6,5},{7,4},{8,11},{9,10},{10,... | collective-permute-start | bytes 393224 | tf_op jit(solution)/shard_map/ppermute | solution.py:200
  59.9 2.0 %collective-permute-start.12 = (f32[256,512]{1,0:T(8,128)S(1)}, f32[256,512]{1,0:T(8,128)S(1)}, u32[]{:S(2)}, u32[]{:S(2)}) collective-permute-start(f32[256,512]{1,0:T(8,128)S(1)} %drift.1), channel_id=1, source_target_pairs={{0,16},{16,0},{1,17},{17,1},{2,18},{18,2},{3,19},{19,3},{4,20},{20... | collective-permute-start | bytes 1572872 | tf_op jit(solution)/shard_map/ppermute | solution.py:206
  62.0 15.1 %collective-permute-start.16 = (bf16[256,512]{1,0:T(8,128)(2,1)S(1)}, bf16[256,512]{1,0:T(8,128)(2,1)S(1)}, u32[]{:S(2)}, u32[]{:S(2)}) collective-permute-start(bf16[256,512]{1,0:T(8,128)(2,1)S(1)} %outer.1.refs_8_), channel_id=1, source_target_pairs={{0,8},{1,9},{2,10},{3,11},{4,12},{5,13},{6,14},{7,15},{8,0},{9,1},... | collective-permute-start | bytes 786440 | tf_op jit(solution)/shard_map/ppermute | solution.py:197
  62.1 15.1 %collective-permute-start.14 = (bf16[256,512]{1,0:T(8,128)(2,1)S(1)}, bf16[256,512]{1,0:T(8,128)(2,1)S(1)}, u32[]{:S(2)}, u32[]{:S(2)}) collective-permute-start(bf16[256,512]{1,0:T(8,128)(2,1)S(1)} %outer.1.refs_8_), channel_id=1, source_target_pairs={{0,4},{1,5},{2,6},{3,7},{4,0},{5,1},{6,2},{7,3},{8,12},{9,13},{10,... | collective-permute-start | bytes 786440 | tf_op jit(solution)/shard_map/ppermute | solution.py:197
  77.1 8.0 %collective-permute-start.18 = (bf16[256,512]{1,0:T(8,128)(2,1)S(1)}, bf16[256,512]{1,0:T(8,128)(2,1)S(1)}, u32[]{:S(2)}, u32[]{:S(2)}) collective-permute-start(bf16[256,512]{1,0:T(8,128)(2,1)S(1)} %collective-permute-done.16.refs_12_), channel_id=1, source_target_pairs={{0,4},{1,5},{2,6},{3,7},{4,0},{5,1},{6,2},{7,3},{8,12},{9,13},{10,... | collective-permute-start | bytes 786440 | tf_op jit(solution)/shard_map/ppermute | solution.py:197
  77.1 8.0 %collective-permute-start.13 = (bf16[256,512]{1,0:T(8,128)(2,1)S(1)}, bf16[256,512]{1,0:T(8,128)(2,1)S(1)}, u32[]{:S(2)}, u32[]{:S(2)}) collective-permute-start(bf16[256,512]{1,0:T(8,128)(2,1)S(1)} %outer.1.refs_8_), channel_id=1, source_target_pairs={{0,16},{16,0},{1,17},{17,1},{2,18},{18,2},{3,19},{19,3},{4,20},{20... | collective-permute-start | bytes 786440 | tf_op jit(solution)/shard_map/ppermute | solution.py:206
  77.2 7.9 %collective-permute-start.15 = (bf16[256,512]{1,0:T(8,128)(2,1)S(1)}, bf16[256,512]{1,0:T(8,128)(2,1)S(1)}, u32[]{:S(2)}, u32[]{:S(2)}) collective-permute-start(bf16[256,512]{1,0:T(8,128)(2,1)S(1)} %collective-permute-done.14.refs_10_), channel_id=1, source_target_pairs={{0,16},{16,0},{1,17},{17,1},{2,18},{18,2},{3,19},{19,3},{4,20},{20... | collective-permute-start | bytes 786440 | tf_op jit(solution)/shard_map/ppermute | solution.py:206
  77.7 7.5 %collective-permute-start.17 = (bf16[256,512]{1,0:T(8,128)(2,1)S(1)}, bf16[256,512]{1,0:T(8,128)(2,1)S(1)}, u32[]{:S(2)}, u32[]{:S(2)}) collective-permute-start(bf16[256,512]{1,0:T(8,128)(2,1)S(1)} %collective-permute-done.16.refs_12_), channel_id=1, source_target_pairs={{0,16},{16,0},{1,17},{17,1},{2,18},{18,2},{3,19},{19,3},{4,20},{20... | collective-permute-start | bytes 786440 | tf_op jit(solution)/shard_map/ppermute | solution.py:206
  85.1 1.5 %collective-permute-start.19 = (bf16[256,512]{1,0:T(8,128)(2,1)S(1)}, bf16[256,512]{1,0:T(8,128)(2,1)S(1)}, u32[]{:S(2)}, u32[]{:S(2)}) collective-permute-start(bf16[256,512]{1,0:T(8,128)(2,1)S(1)} %collective-permute-done.18.refs_5_), channel_id=1, source_target_pairs={{0,16},{16,0},{1,17},{17,1},{2,18},{18,2},{3,19},{19,3},{4,20},{20... | collective-permute-start | bytes 786440 | tf_op jit(solution)/shard_map/ppermute | solution.py:206
  87.1 6.0 %collective-permute-start.20 = (bf16[128,512]{1,0:T(8,128)(2,1)S(1)}, bf16[128,512]{1,0:T(8,128)(2,1)S(1)}, u32[]{:S(2)}, u32[]{:S(2)}) collective-permute-start(bf16[128,512]{1,0:T(8,128)(2,1)S(1)} %get-tuple-element.35), channel_id=1, source_target_pairs={{0,1},{1,0},{2,3},{3,2},{4,5},{5,4},{6,7},{7,6},{8,9},{9,8},{10,11... | collective-permute-start | bytes 393224 | tf_op jit(solution)/shard_map/ppermute | solution.py:200
  88.6 6.6 %collective-permute-start.21 = (bf16[128,512]{1,0:T(8,128)(2,1)S(1)}, bf16[128,512]{1,0:T(8,128)(2,1)S(1)}, u32[]{:S(2)}, u32[]{:S(2)}) collective-permute-start(bf16[128,512]{1,0:T(8,128)(2,1)S(1)} %get-tuple-element.36), channel_id=1, source_target_pairs={{0,2},{1,3},{2,0},{3,1},{4,6},{5,7},{6,4},{7,5},{8,10},{9,11},{10,... | collective-permute-start | bytes 393224 | tf_op jit(solution)/shard_map/ppermute | solution.py:200
  89.3 7.7 %collective-permute-start.22 = (bf16[128,512]{1,0:T(8,128)(2,1)S(1)}, bf16[128,512]{1,0:T(8,128)(2,1)S(1)}, u32[]{:S(2)}, u32[]{:S(2)}) collective-permute-start(bf16[128,512]{1,0:T(8,128)(2,1)S(1)} %get-tuple-element.37), channel_id=1, source_target_pairs={{0,3},{1,2},{2,1},{3,0},{4,7},{5,6},{6,5},{7,4},{8,11},{9,10},{10,... | collective-permute-start | bytes 393224 | tf_op jit(solution)/shard_map/ppermute | solution.py:200
  (7 other events, 81.0 us)

commit v10 on v9

--- a/solution.py
+++ b/solution.py
@@ -17,7 +17,7 @@
 PLANES = 4
 CHUNK = 32
 CONTRACT_ROWS = (((0,), (0,)), ((), ()))
-AHEAD_FLOPS = 10**12
+AHEAD_FLOPS = 10**10
 VMEM_BYTES = 16 * 1024 * 1024
 
 

time: 97.9 us -> 96.6 us (0.987)
  Pallas kernels: 8.55 us -> 6.71 us
    pallas_call x13, Pallas kernels: 8.55 us -> 6.71 us  [call(): pl.pallas_call(without_after, out_shape=out, in_specs=[pl.BlockSpec(memor...]
  transfers between devices with their start and end apart: 23 -> 23, of which waited for: 19 -> 18; matrix products, arithmetic and copies ran while one was open for 0% -> 0% of each run, Pallas kernels for 7% -> 5%
where the time goes in v10:
time: 96.6 us; the launch traced here: 96.4 us
  waiting for transfers between devices  61.4 us (64%)
  starting transfers between devices  24.9 us (26%)
  Pallas kernels  6.71 us (7%)
  local copies, waits for them, and re-layouts  2.53 us (3%)
    ppermute x6, waiting for transfers between devices, planes(): lax.ppermute(x, 'fsdp', [(p * inner + i, (p ^ bits) * inner + i) for p in...  33 us
    ppermute x12, waiting for transfers between devices, across(): lax.ppermute(x, 'fsdp', [(p * inner + i, p * inner + (i ^ k)) for p in ra...  27.7 us
    ppermute x12, starting transfers between devices, across(): lax.ppermute(x, 'fsdp', [(p * inner + i, p * inner + (i ^ k)) for p in ra...  15.3 us
    ppermute x6, starting transfers between devices, planes(): lax.ppermute(x, 'fsdp', [(p * inner + i, (p ^ bits) * inner + i) for p in...  9.02 us
    pallas_call x13, Pallas kernels, call(): pl.pallas_call(without_after, out_shape=out, in_specs=[pl.BlockSpec(memor...  6.71 us
    unnamed x16, local copies, waits for them, and re-layouts  2.53 us
  transfers between devices with their start and end apart: 23, of which 18 were waited for; matrix products, arithmetic and copies ran while one was open for 0% of the time, Pallas kernels for 5%

profile of v10, /device:TPU:0, one launch (start us, length us, event | category | flops | bytes accessed | tf_op | source)
XLA Modules:
  0.0 96.4 jit_solution(4601925291520352952)
XLA Ops:
  0.6 1.6 %copy-done = bf16[1,128,8192]{2,1,0:T(8,128)(2,1)S(1)} copy-done((bf16[1,128,8192]{2,1,0:T(8,128)(2,1)S(1)}, bf16[1,128,8192]{2,1,0:T(8,128)(2,1)}, u32[]{:S(2)}) %copy-start) | copy-done | bytes 2097176
  3.4 3.0 %collective-permute-start = (bf16[128,1024]{1,0:T(8,128)(2,1)S(1)}, bf16[128,1024]{1,0:T(8,128)(2,1)S(1)}, u32[]{:S(2)}, u32[]{:S(2)}) collective-permute-start(bf16[128,1024]{1,0:T(8,128)(2,1)S(1)} %get-tuple-element.20), channel_id=1, source_target_pairs={{0,1},{1,0},{2,3},{3,2},{4,5},{5,4},{6,7},{7,6},{8,9},{9,8},{10,11... | collective-permute-start | bytes 786440 | tf_op jit(solution)/shard_map/ppermute | solution.py:200
  6.4 1.5 %collective-permute-start.4 = (bf16[128,1024]{1,0:T(8,128)(2,1)S(1)}, bf16[128,1024]{1,0:T(8,128)(2,1)S(1)}, u32[]{:S(2)}, u32[]{:S(2)}) collective-permute-start(bf16[128,1024]{1,0:T(8,128)(2,1)S(1)} %get-tuple-element.26), channel_id=1, source_target_pairs={{0,2},{1,3},{2,0},{3,1},{4,6},{5,7},{6,4},{7,5},{8,10},{9,11},{10,... | collective-permute-start | bytes 786440 | tf_op jit(solution)/shard_map/ppermute | solution.py:200
  7.9 5.6 %collective-permute-done.refs_1_.refs_5_.refs_2_ = bf16[128,1024]{1,0:T(8,128)(2,1)S(1)} collective-permute-done((bf16[128,1024]{1,0:T(8,128)(2,1)S(1)}, bf16[128,1024]{1,0:T(8,128)(2,1)S(1)}, u32[]{:S(2)}, u32[]{:S(2)}) %collective-permute-start) | collective-permute-done | bytes 262176 | tf_op jit(solution)/shard_map/ppermute | solution.py:200
  13.6 2.1 %collective-permute-start.1 = (bf16[128,1024]{1,0:T(8,128)(2,1)S(1)}, bf16[128,1024]{1,0:T(8,128)(2,1)S(1)}, u32[]{:S(2)}, u32[]{:S(2)}) collective-permute-start(bf16[128,1024]{1,0:T(8,128)(2,1)S(1)} %get-tuple-element.22), channel_id=1, source_target_pairs={{0,1},{1,0},{2,3},{3,2},{4,5},{5,4},{6,7},{7,6},{8,9},{9,8},{10,11... | collective-permute-start | bytes 786440 | tf_op jit(solution)/shard_map/ppermute | solution.py:200
  15.7 1.5 %collective-permute-start.2 = (bf16[128,1024]{1,0:T(8,128)(2,1)S(1)}, bf16[128,1024]{1,0:T(8,128)(2,1)S(1)}, u32[]{:S(2)}, u32[]{:S(2)}) collective-permute-start(bf16[128,1024]{1,0:T(8,128)(2,1)S(1)} %get-tuple-element.23), channel_id=1, source_target_pairs={{0,2},{1,3},{2,0},{3,1},{4,6},{5,7},{6,4},{7,5},{8,10},{9,11},{10,... | collective-permute-start | bytes 786440 | tf_op jit(solution)/shard_map/ppermute | solution.py:200
  17.2 2.9 %collective-permute-done.4.refs_2_.refs_6_.refs_3_ = bf16[128,1024]{1,0:T(8,128)(2,1)S(1)} collective-permute-done((bf16[128,1024]{1,0:T(8,128)(2,1)S(1)}, bf16[128,1024]{1,0:T(8,128)(2,1)S(1)}, u32[]{:S(2)}, u32[]{:S(2)}) %collective-permute-start.4) | collective-permute-done | bytes 262176 | tf_op jit(solution)/shard_map/ppermute | solution.py:200
  21.2 1.6 %collective-permute-start.6 = (bf16[512,512]{1,0:T(8,128)(2,1)S(1)}, bf16[512,512]{1,0:T(8,128)(2,1)S(1)}, u32[]{:S(2)}, u32[]{:S(2)}) collective-permute-start(bf16[512,512]{1,0:T(8,128)(2,1)S(1)} %gradient.4), channel_id=1, source_target_pairs={{0,4},{1,5},{2,6},{3,7},{4,0},{5,1},{6,2},{7,3},{8,12},{9,13},{10,... | collective-permute-start | bytes 1572872 | tf_op jit(solution)/shard_map/ppermute | solution.py:197
  22.8 2.0 %collective-permute-done.1.refs_1_.refs_5_ = bf16[128,1024]{1,0:T(8,128)(2,1)S(1)} collective-permute-done((bf16[128,1024]{1,0:T(8,128)(2,1)S(1)}, bf16[128,1024]{1,0:T(8,128)(2,1)S(1)}, u32[]{:S(2)}, u32[]{:S(2)}) %collective-permute-start.1) | collective-permute-done | bytes 262176 | tf_op jit(solution)/shard_map/ppermute | solution.py:200
  24.8 6.2 %collective-permute-done.2.refs_2_.refs_6_ = bf16[128,1024]{1,0:T(8,128)(2,1)S(1)} collective-permute-done((bf16[128,1024]{1,0:T(8,128)(2,1)S(1)}, bf16[128,1024]{1,0:T(8,128)(2,1)S(1)}, u32[]{:S(2)}, u32[]{:S(2)}) %collective-permute-start.2) | collective-permute-done | bytes 262176 | tf_op jit(solution)/shard_map/ppermute | solution.py:200
  31.5 1.6 %collective-permute-start.10 = (bf16[512,512]{1,0:T(8,128)(2,1)S(1)}, bf16[512,512]{1,0:T(8,128)(2,1)S(1)}, u32[]{:S(2)}, u32[]{:S(2)}) collective-permute-start(bf16[512,512]{1,0:T(8,128)(2,1)S(1)} %gradient.7), channel_id=1, source_target_pairs={{0,4},{1,5},{2,6},{3,7},{4,0},{5,1},{6,2},{7,3},{8,12},{9,13},{10,... | collective-permute-start | bytes 1572872 | tf_op jit(solution)/shard_map/ppermute | solution.py:197
  33.7 2.7 %collective-permute-start.11 = (bf16[512,512]{1,0:T(8,128)(2,1)S(1)}, bf16[512,512]{1,0:T(8,128)(2,1)S(1)}, u32[]{:S(2)}, u32[]{:S(2)}) collective-permute-start(bf16[512,512]{1,0:T(8,128)(2,1)S(1)} %gradient.5.refs_1_), channel_id=1, source_target_pairs={{0,8},{1,9},{2,10},{3,11},{4,12},{5,13},{6,14},{7,15},{8,0},{9,1},... | collective-permute-start | bytes 1572872 | tf_op jit(solution)/shard_map/ppermute | solution.py:197
  39.9 2.5 %collective-permute-done.7.refs_1_ = bf16[128,512]{1,0:T(8,128)(2,1)S(1)} collective-permute-done((bf16[128,512]{1,0:T(8,128)(2,1)S(1)}, bf16[128,512]{1,0:T(8,128)(2,1)S(1)}, u32[]{:S(2)}, u32[]{:S(2)}) %collective-permute-start.7) | collective-permute-done | bytes 131104 | tf_op jit(solution)/shard_map/ppermute | solution.py:200
  42.8 1.6 %collective-permute-done.9.refs_3_ = bf16[128,512]{1,0:T(8,128)(2,1)S(1)} collective-permute-done((bf16[128,512]{1,0:T(8,128)(2,1)S(1)}, bf16[128,512]{1,0:T(8,128)(2,1)S(1)}, u32[]{:S(2)}, u32[]{:S(2)}) %collective-permute-start.9) | collective-permute-done | bytes 131104 | tf_op jit(solution)/shard_map/ppermute | solution.py:200
  44.8 9.9 %collective-permute-done.10.refs_1_ = bf16[512,512]{1,0:T(8,128)(2,1)S(1)} collective-permute-done((bf16[512,512]{1,0:T(8,128)(2,1)S(1)}, bf16[512,512]{1,0:T(8,128)(2,1)S(1)}, u32[]{:S(2)}, u32[]{:S(2)}) %collective-permute-start.10) | collective-permute-done | bytes 524320 | tf_op jit(solution)/shard_map/ppermute | solution.py:197
  54.7 3.5 %collective-permute-done.11.refs_2_ = bf16[512,512]{1,0:T(8,128)(2,1)S(1)} collective-permute-done((bf16[512,512]{1,0:T(8,128)(2,1)S(1)}, bf16[512,512]{1,0:T(8,128)(2,1)S(1)}, u32[]{:S(2)}, u32[]{:S(2)}) %collective-permute-start.11) | collective-permute-done | bytes 524320 | tf_op jit(solution)/shard_map/ppermute | solution.py:197
  58.9 1.7 %update.1 = (f32[512,512]{1,0:T(8,128)}, f32[256,512]{1,0:T(8,128)S(1)}) custom-call(f32[512,512]{1,0:T(8,128)S(1)} %gradient.6.refs_0_, bf16[512,512]{1,0:T(8,128)(2,1)S(1)} %collective-permute-done.10.refs_1_, bf16[512,512]{1,0:T(8,128)(2,1)S(1)} %collective-permute-done.11.refs_2_, f32[512,512]{1,0:T(8,128)S(1)} %bitcast.11, f32[512,512]{1,0:T(8,128)S(1)} %bitcast.13, ...), custom_call_target="tpu_custom_call" | custom-call | bytes 7864320 | tf_op jit(solution)/shard_map/update/pallas_call | solution.py:61
  61.0 3.0 %collective-permute-start.14 = (bf16[256,512]{1,0:T(8,128)(2,1)S(1)}, bf16[256,512]{1,0:T(8,128)(2,1)S(1)}, u32[]{:S(2)}, u32[]{:S(2)}) collective-permute-start(bf16[256,512]{1,0:T(8,128)(2,1)S(1)} %outer.1.refs_8_), channel_id=1, source_target_pairs={{0,4},{1,5},{2,6},{3,7},{4,0},{5,1},{6,2},{7,3},{8,12},{9,13},{10,... | collective-permute-start | bytes 786440 | tf_op jit(solution)/shard_map/ppermute | solution.py:197
  64.1 11.9 %collective-permute-done.16.refs_12_ = bf16[256,512]{1,0:T(8,128)(2,1)S(1)} collective-permute-done((bf16[256,512]{1,0:T(8,128)(2,1)S(1)}, bf16[256,512]{1,0:T(8,128)(2,1)S(1)}, u32[]{:S(2)}, u32[]{:S(2)}) %collective-permute-start.16) | collective-permute-done | bytes 262176 | tf_op jit(solution)/shard_map/ppermute | solution.py:197
  76.6 7.5 %collective-permute-done.18.refs_5_ = bf16[256,512]{1,0:T(8,128)(2,1)S(1)} collective-permute-done((bf16[256,512]{1,0:T(8,128)(2,1)S(1)}, bf16[256,512]{1,0:T(8,128)(2,1)S(1)}, u32[]{:S(2)}, u32[]{:S(2)}) %collective-permute-start.18) | collective-permute-done | bytes 262176 | tf_op jit(solution)/shard_map/ppermute | solution.py:197
  86.1 1.5 %collective-permute-start.20 = (bf16[128,512]{1,0:T(8,128)(2,1)S(1)}, bf16[128,512]{1,0:T(8,128)(2,1)S(1)}, u32[]{:S(2)}, u32[]{:S(2)}) collective-permute-start(bf16[128,512]{1,0:T(8,128)(2,1)S(1)} %get-tuple-element.35), channel_id=1, source_target_pairs={{0,1},{1,0},{2,3},{3,2},{4,5},{5,4},{6,7},{7,6},{8,9},{9,8},{10,11... | collective-permute-start | bytes 393224 | tf_op jit(solution)/shard_map/ppermute | solution.py:200
  89.7 2.4 %collective-permute-done.20.refs_1_ = bf16[128,512]{1,0:T(8,128)(2,1)S(1)} collective-permute-done((bf16[128,512]{1,0:T(8,128)(2,1)S(1)}, bf16[128,512]{1,0:T(8,128)(2,1)S(1)}, u32[]{:S(2)}, u32[]{:S(2)}) %collective-permute-start.20) | collective-permute-done | bytes 131104 | tf_op jit(solution)/shard_map/ppermute | solution.py:200
  92.1 1.8 %collective-permute-done.21.refs_2_ = bf16[128,512]{1,0:T(8,128)(2,1)S(1)} collective-permute-done((bf16[128,512]{1,0:T(8,128)(2,1)S(1)}, bf16[128,512]{1,0:T(8,128)(2,1)S(1)}, u32[]{:S(2)}, u32[]{:S(2)}) %collective-permute-start.21) | collective-permute-done | bytes 131104 | tf_op jit(solution)/shard_map/ppermute | solution.py:200
  93.9 1.8 %collective-permute-done.22.refs_3_ = bf16[128,512]{1,0:T(8,128)(2,1)S(1)} collective-permute-done((bf16[128,512]{1,0:T(8,128)(2,1)S(1)}, bf16[128,512]{1,0:T(8,128)(2,1)S(1)}, u32[]{:S(2)}, u32[]{:S(2)}) %collective-permute-start.22) | collective-permute-done | bytes 131104 | tf_op jit(solution)/shard_map/ppermute | solution.py:200
  (51 shorter events, 14.1 us)
Async XLA Ops:
  3.4 10.1 %collective-permute-start = (bf16[128,1024]{1,0:T(8,128)(2,1)S(1)}, bf16[128,1024]{1,0:T(8,128)(2,1)S(1)}, u32[]{:S(2)}, u32[]{:S(2)}) collective-permute-start(bf16[128,1024]{1,0:T(8,128)(2,1)S(1)} %get-tuple-element.20), channel_id=1, source_target_pairs={{0,1},{1,0},{2,3},{3,2},{4,5},{5,4},{6,7},{7,6},{8,9},{9,8},{10,11... | collective-permute-start | bytes 786440 | tf_op jit(solution)/shard_map/ppermute | solution.py:200
  6.4 13.8 %collective-permute-start.4 = (bf16[128,1024]{1,0:T(8,128)(2,1)S(1)}, bf16[128,1024]{1,0:T(8,128)(2,1)S(1)}, u32[]{:S(2)}, u32[]{:S(2)}) collective-permute-start(bf16[128,1024]{1,0:T(8,128)(2,1)S(1)} %get-tuple-element.26), channel_id=1, source_target_pairs={{0,2},{1,3},{2,0},{3,1},{4,6},{5,7},{6,4},{7,5},{8,10},{9,11},{10,... | collective-permute-start | bytes 786440 | tf_op jit(solution)/shard_map/ppermute | solution.py:200
  7.9 12.8 %collective-permute-start.5 = (bf16[128,1024]{1,0:T(8,128)(2,1)S(1)}, bf16[128,1024]{1,0:T(8,128)(2,1)S(1)}, u32[]{:S(2)}, u32[]{:S(2)}) collective-permute-start(bf16[128,1024]{1,0:T(8,128)(2,1)S(1)} %get-tuple-element.27), channel_id=1, source_target_pairs={{0,3},{1,2},{2,1},{3,0},{4,7},{5,6},{6,5},{7,4},{8,11},{9,10},{10,... | collective-permute-start | bytes 786440 | tf_op jit(solution)/shard_map/ppermute | solution.py:200
  13.6 11.2 %collective-permute-start.1 = (bf16[128,1024]{1,0:T(8,128)(2,1)S(1)}, bf16[128,1024]{1,0:T(8,128)(2,1)S(1)}, u32[]{:S(2)}, u32[]{:S(2)}) collective-permute-start(bf16[128,1024]{1,0:T(8,128)(2,1)S(1)} %get-tuple-element.22), channel_id=1, source_target_pairs={{0,1},{1,0},{2,3},{3,2},{4,5},{5,4},{6,7},{7,6},{8,9},{9,8},{10,11... | collective-permute-start | bytes 786440 | tf_op jit(solution)/shard_map/ppermute | solution.py:200
  15.7 15.3 %collective-permute-start.2 = (bf16[128,1024]{1,0:T(8,128)(2,1)S(1)}, bf16[128,1024]{1,0:T(8,128)(2,1)S(1)}, u32[]{:S(2)}, u32[]{:S(2)}) collective-permute-start(bf16[128,1024]{1,0:T(8,128)(2,1)S(1)} %get-tuple-element.23), channel_id=1, source_target_pairs={{0,2},{1,3},{2,0},{3,1},{4,6},{5,7},{6,4},{7,5},{8,10},{9,11},{10,... | collective-permute-start | bytes 786440 | tf_op jit(solution)/shard_map/ppermute | solution.py:200
  17.2 13.8 %collective-permute-start.3 = (bf16[128,1024]{1,0:T(8,128)(2,1)S(1)}, bf16[128,1024]{1,0:T(8,128)(2,1)S(1)}, u32[]{:S(2)}, u32[]{:S(2)}) collective-permute-start(bf16[128,1024]{1,0:T(8,128)(2,1)S(1)} %get-tuple-element.24), channel_id=1, source_target_pairs={{0,3},{1,2},{2,1},{3,0},{4,7},{5,6},{6,5},{7,4},{8,11},{9,10},{10,... | collective-permute-start | bytes 786440 | tf_op jit(solution)/shard_map/ppermute | solution.py:200
  21.2 12.0 %collective-permute-start.6 = (bf16[512,512]{1,0:T(8,128)(2,1)S(1)}, bf16[512,512]{1,0:T(8,128)(2,1)S(1)}, u32[]{:S(2)}, u32[]{:S(2)}) collective-permute-start(bf16[512,512]{1,0:T(8,128)(2,1)S(1)} %gradient.4), channel_id=1, source_target_pairs={{0,4},{1,5},{2,6},{3,7},{4,0},{5,1},{6,2},{7,3},{8,12},{9,13},{10,... | collective-permute-start | bytes 1572872 | tf_op jit(solution)/shard_map/ppermute | solution.py:197
  31.5 23.2 %collective-permute-start.10 = (bf16[512,512]{1,0:T(8,128)(2,1)S(1)}, bf16[512,512]{1,0:T(8,128)(2,1)S(1)}, u32[]{:S(2)}, u32[]{:S(2)}) collective-permute-start(bf16[512,512]{1,0:T(8,128)(2,1)S(1)} %gradient.7), channel_id=1, source_target_pairs={{0,4},{1,5},{2,6},{3,7},{4,0},{5,1},{6,2},{7,3},{8,12},{9,13},{10,... | collective-permute-start | bytes 1572872 | tf_op jit(solution)/shard_map/ppermute | solution.py:197
  33.6 24.6 %copy-start.2 = (f32[512,512]{1,0:T(8,128)S(1)}, f32[512,512]{1,0:T(8,128)}, u32[]{:S(2)}) copy-start(f32[512,512]{1,0:T(8,128)} %refs_2_.1) | copy-start | bytes 3145732
  33.7 24.6 %collective-permute-start.11 = (bf16[512,512]{1,0:T(8,128)(2,1)S(1)}, bf16[512,512]{1,0:T(8,128)(2,1)S(1)}, u32[]{:S(2)}, u32[]{:S(2)}) collective-permute-start(bf16[512,512]{1,0:T(8,128)(2,1)S(1)} %gradient.5.refs_1_), channel_id=1, source_target_pairs={{0,8},{1,9},{2,10},{3,11},{4,12},{5,13},{6,14},{7,15},{8,0},{9,1},... | collective-permute-start | bytes 1572872 | tf_op jit(solution)/shard_map/ppermute | solution.py:197
  36.4 6.1 %collective-permute-start.7 = (bf16[128,512]{1,0:T(8,128)(2,1)S(1)}, bf16[128,512]{1,0:T(8,128)(2,1)S(1)}, u32[]{:S(2)}, u32[]{:S(2)}) collective-permute-start(bf16[128,512]{1,0:T(8,128)(2,1)S(1)} %get-tuple-element.29), channel_id=1, source_target_pairs={{0,1},{1,0},{2,3},{3,2},{4,5},{5,4},{6,7},{7,6},{8,9},{9,8},{10,11... | collective-permute-start | bytes 393224 | tf_op jit(solution)/shard_map/ppermute | solution.py:200
  37.7 5.1 %collective-permute-start.8 = (bf16[128,512]{1,0:T(8,128)(2,1)S(1)}, bf16[128,512]{1,0:T(8,128)(2,1)S(1)}, u32[]{:S(2)}, u32[]{:S(2)}) collective-permute-start(bf16[128,512]{1,0:T(8,128)(2,1)S(1)} %get-tuple-element.30), channel_id=1, source_target_pairs={{0,2},{1,3},{2,0},{3,1},{4,6},{5,7},{6,4},{7,5},{8,10},{9,11},{10,... | collective-permute-start | bytes 393224 | tf_op jit(solution)/shard_map/ppermute | solution.py:200
  38.5 5.9 %collective-permute-start.9 = (bf16[128,512]{1,0:T(8,128)(2,1)S(1)}, bf16[128,512]{1,0:T(8,128)(2,1)S(1)}, u32[]{:S(2)}, u32[]{:S(2)}) collective-permute-start(bf16[128,512]{1,0:T(8,128)(2,1)S(1)} %get-tuple-element.31), channel_id=1, source_target_pairs={{0,3},{1,2},{2,1},{3,0},{4,7},{5,6},{6,5},{7,4},{8,11},{9,10},{10,... | collective-permute-start | bytes 393224 | tf_op jit(solution)/shard_map/ppermute | solution.py:200
  58.8 2.0 %collective-permute-start.12 = (f32[256,512]{1,0:T(8,128)S(1)}, f32[256,512]{1,0:T(8,128)S(1)}, u32[]{:S(2)}, u32[]{:S(2)}) collective-permute-start(f32[256,512]{1,0:T(8,128)S(1)} %drift.1), channel_id=1, source_target_pairs={{0,16},{16,0},{1,17},{17,1},{2,18},{18,2},{3,19},{19,3},{4,20},{20... | collective-permute-start | bytes 1572872 | tf_op jit(solution)/shard_map/ppermute | solution.py:206
  61.0 15.0 %collective-permute-start.16 = (bf16[256,512]{1,0:T(8,128)(2,1)S(1)}, bf16[256,512]{1,0:T(8,128)(2,1)S(1)}, u32[]{:S(2)}, u32[]{:S(2)}) collective-permute-start(bf16[256,512]{1,0:T(8,128)(2,1)S(1)} %outer.1.refs_8_), channel_id=1, source_target_pairs={{0,8},{1,9},{2,10},{3,11},{4,12},{5,13},{6,14},{7,15},{8,0},{9,1},... | collective-permute-start | bytes 786440 | tf_op jit(solution)/shard_map/ppermute | solution.py:197
  61.0 15.1 %collective-permute-start.14 = (bf16[256,512]{1,0:T(8,128)(2,1)S(1)}, bf16[256,512]{1,0:T(8,128)(2,1)S(1)}, u32[]{:S(2)}, u32[]{:S(2)}) collective-permute-start(bf16[256,512]{1,0:T(8,128)(2,1)S(1)} %outer.1.refs_8_), channel_id=1, source_target_pairs={{0,4},{1,5},{2,6},{3,7},{4,0},{5,1},{6,2},{7,3},{8,12},{9,13},{10,... | collective-permute-start | bytes 786440 | tf_op jit(solution)/shard_map/ppermute | solution.py:197
  75.9 8.2 %collective-permute-start.18 = (bf16[256,512]{1,0:T(8,128)(2,1)S(1)}, bf16[256,512]{1,0:T(8,128)(2,1)S(1)}, u32[]{:S(2)}, u32[]{:S(2)}) collective-permute-start(bf16[256,512]{1,0:T(8,128)(2,1)S(1)} %collective-permute-done.16.refs_12_), channel_id=1, source_target_pairs={{0,4},{1,5},{2,6},{3,7},{4,0},{5,1},{6,2},{7,3},{8,12},{9,13},{10,... | collective-permute-start | bytes 786440 | tf_op jit(solution)/shard_map/ppermute | solution.py:197
  75.9 8.2 %collective-permute-start.13 = (bf16[256,512]{1,0:T(8,128)(2,1)S(1)}, bf16[256,512]{1,0:T(8,128)(2,1)S(1)}, u32[]{:S(2)}, u32[]{:S(2)}) collective-permute-start(bf16[256,512]{1,0:T(8,128)(2,1)S(1)} %outer.1.refs_8_), channel_id=1, source_target_pairs={{0,16},{16,0},{1,17},{17,1},{2,18},{18,2},{3,19},{19,3},{4,20},{20... | collective-permute-start | bytes 786440 | tf_op jit(solution)/shard_map/ppermute | solution.py:206
  76.1 8.0 %collective-permute-start.15 = (bf16[256,512]{1,0:T(8,128)(2,1)S(1)}, bf16[256,512]{1,0:T(8,128)(2,1)S(1)}, u32[]{:S(2)}, u32[]{:S(2)}) collective-permute-start(bf16[256,512]{1,0:T(8,128)(2,1)S(1)} %collective-permute-done.14.refs_10_), channel_id=1, source_target_pairs={{0,16},{16,0},{1,17},{17,1},{2,18},{18,2},{3,19},{19,3},{4,20},{20... | collective-permute-start | bytes 786440 | tf_op jit(solution)/shard_map/ppermute | solution.py:206
  76.4 7.7 %collective-permute-start.17 = (bf16[256,512]{1,0:T(8,128)(2,1)S(1)}, bf16[256,512]{1,0:T(8,128)(2,1)S(1)}, u32[]{:S(2)}, u32[]{:S(2)}) collective-permute-start(bf16[256,512]{1,0:T(8,128)(2,1)S(1)} %collective-permute-done.16.refs_12_), channel_id=1, source_target_pairs={{0,16},{16,0},{1,17},{17,1},{2,18},{18,2},{3,19},{19,3},{4,20},{20... | collective-permute-start | bytes 786440 | tf_op jit(solution)/shard_map/ppermute | solution.py:206
  84.1 1.5 %collective-permute-start.19 = (bf16[256,512]{1,0:T(8,128)(2,1)S(1)}, bf16[256,512]{1,0:T(8,128)(2,1)S(1)}, u32[]{:S(2)}, u32[]{:S(2)}) collective-permute-start(bf16[256,512]{1,0:T(8,128)(2,1)S(1)} %collective-permute-done.18.refs_5_), channel_id=1, source_target_pairs={{0,16},{16,0},{1,17},{17,1},{2,18},{18,2},{3,19},{19,3},{4,20},{20... | collective-permute-start | bytes 786440 | tf_op jit(solution)/shard_map/ppermute | solution.py:206
  86.1 6.0 %collective-permute-start.20 = (bf16[128,512]{1,0:T(8,128)(2,1)S(1)}, bf16[128,512]{1,0:T(8,128)(2,1)S(1)}, u32[]{:S(2)}, u32[]{:S(2)}) collective-permute-start(bf16[128,512]{1,0:T(8,128)(2,1)S(1)} %get-tuple-element.35), channel_id=1, source_target_pairs={{0,1},{1,0},{2,3},{3,2},{4,5},{5,4},{6,7},{7,6},{8,9},{9,8},{10,11... | collective-permute-start | bytes 393224 | tf_op jit(solution)/shard_map/ppermute | solution.py:200
  87.6 6.2 %collective-permute-start.21 = (bf16[128,512]{1,0:T(8,128)(2,1)S(1)}, bf16[128,512]{1,0:T(8,128)(2,1)S(1)}, u32[]{:S(2)}, u32[]{:S(2)}) collective-permute-start(bf16[128,512]{1,0:T(8,128)(2,1)S(1)} %get-tuple-element.36), channel_id=1, source_target_pairs={{0,2},{1,3},{2,0},{3,1},{4,6},{5,7},{6,4},{7,5},{8,10},{9,11},{10,... | collective-permute-start | bytes 393224 | tf_op jit(solution)/shard_map/ppermute | solution.py:200
  88.2 7.5 %collective-permute-start.22 = (bf16[128,512]{1,0:T(8,128)(2,1)S(1)}, bf16[128,512]{1,0:T(8,128)(2,1)S(1)}, u32[]{:S(2)}, u32[]{:S(2)}) collective-permute-start(bf16[128,512]{1,0:T(8,128)(2,1)S(1)} %get-tuple-element.37), channel_id=1, source_target_pairs={{0,3},{1,2},{2,1},{3,0},{4,7},{5,6},{6,5},{7,4},{8,11},{9,10},{10,... | collective-permute-start | bytes 393224 | tf_op jit(solution)/shard_map/ppermute | solution.py:200
  (7 other events, 83.2 us)

commit v11 on v10

--- a/solution.py
+++ b/solution.py
@@ -19,6 +19,7 @@
 CONTRACT_ROWS = (((0,), (0,)), ((), ()))
 AHEAD_FLOPS = 10**10
 VMEM_BYTES = 16 * 1024 * 1024
+FIRST_VMEM_BYTES = 61 * 1024 * 1024
 
 
 def outer_update(average, anchor_rows, momentum_rows):
@@ -51,8 +52,9 @@
     return (at // 2 + bits // 2 - 2 * (at // 2) * (bits // 2)) * 2 + low + bits % 2 - 2 * low * (bits % 2)
 
 
-def call(kernel, name, out, inputs, flops, scratch=(), after=(), space=pltpu.VMEM):
-    moved = sum(x.size * x.dtype.itemsize for x in list(inputs) + list(out))
+def call(kernel, name, out, inputs, flops, scratch=(), after=(), space=pltpu.VMEM, moved=None, vmem=VMEM_BYTES):
+    if moved is None:
+        moved = sum(x.size * x.dtype.itemsize for x in list(inputs) + list(out))
     count = len(inputs)
 
     def without_after(*refs):
@@ -64,7 +66,7 @@
         in_specs=[pl.BlockSpec(memory_space=space)] * count + [pl.BlockSpec(memory_space=pl.ANY)] * len(after),
         out_specs=[pl.BlockSpec(memory_space=pltpu.VMEM)] * len(out),
         scratch_shapes=list(scratch),
-        compiler_params=pltpu.CompilerParams(vmem_limit_bytes=VMEM_BYTES),
+        compiler_params=pltpu.CompilerParams(vmem_limit_bytes=vmem),
         cost_estimate=pl.CostEstimate(flops=flops, bytes_accessed=moved, transcendentals=0),
         name=name,
     )(*inputs, *after)
@@ -208,7 +210,7 @@
     out = [jax.ShapeDtypeStruct((tokens, rows + width), jnp.bfloat16)] * inner
     sems = [pltpu.SemaphoreType.DMA((2 * inner,))]
     kernel = partial(pack_first_kernel, inner, rows)
-    first = around(call(kernel, "pack", out, [acts[0], value_cots[0]], 0, sems, space=pltpu.HBM))
+    first = around(call(kernel, "pack", out, [acts[0], value_cots[0]], 0, sems, space=pltpu.HBM, moved=0, vmem=FIRST_VMEM_BYTES))
 
     def pack(blocks, after):
         out = [jax.ShapeDtypeStruct((tokens, len(blocks) * rows), jnp.bfloat16)] * inner

time: 96.6 us -> 96.5 us (level)
  local copies, waits for them, and re-layouts: 2.53 us -> 0.04 us
  Pallas kernels: 6.71 us -> 8.96 us
    unnamed x16 -> x14, local copies, waits for them, and re-layouts: 2.53 us -> 0.04 us
    pallas_call x13, Pallas kernels: 6.71 us -> 8.96 us  [call(): pl.pallas_call(without_after, out_shape=out, in_specs=[pl.BlockSpec(memor...]
where the time goes in v11:
time: 96.5 us; the launch traced here: 96.4 us
  waiting for transfers between devices  61.6 us (64%)
  starting transfers between devices  24.9 us (26%)
  Pallas kernels  8.96 us (9%)
    ppermute x6, waiting for transfers between devices, planes(): lax.ppermute(x, 'fsdp', [(p * inner + i, (p ^ bits) * inner + i) for p in...  33 us
    ppermute x12, waiting for transfers between devices, across(): lax.ppermute(x, 'fsdp', [(p * inner + i, p * inner + (i ^ k)) for p in ra...  27.9 us
    ppermute x12, starting transfers between devices, across(): lax.ppermute(x, 'fsdp', [(p * inner + i, p * inner + (i ^ k)) for p in ra...  15.3 us
    ppermute x6, starting transfers between devices, planes(): lax.ppermute(x, 'fsdp', [(p * inner + i, (p ^ bits) * inner + i) for p in...  9.02 us
    pallas_call x13, Pallas kernels, call(): pl.pallas_call(without_after, out_shape=out, in_specs=[pl.BlockSpec(memor...  8.96 us
  transfers between devices with their start and end apart: 23, of which 18 were waited for; matrix products, arithmetic and copies ran while one was open for 0% of the time, Pallas kernels for 5%

profile of v11, /device:TPU:0, one launch (start us, length us, event | category | flops | bytes accessed | tf_op | source)
XLA Modules:
  0.0 96.4 jit_solution(8631309864245452193)
XLA Ops:
  0.6 2.5 %pack.3 = (bf16[128,1024]{1,0:T(8,128)(2,1)}, bf16[128,1024]{1,0:T(8,128)(2,1)}, bf16[128,1024]{1,0:T(8,128)(2,1)}, bf16[128,1024]{1,0:T(8,128)(2,1)}) custom-call(bf16[128,8192]{1,0:T(8,128)(2,1)} %bitcast.7, bf16[128,512]{1,0:T(8,128)(2,1)} %bitcast.16), custom_call_target="tpu_custom_call" | custom-call | tf_op jit(solution)/shard_map/pack/pallas_call | solution.py:63
  3.1 3.0 %collective-permute-start = (bf16[128,1024]{1,0:T(8,128)(2,1)}, bf16[128,1024]{1,0:T(8,128)(2,1)S(1)}, u32[]{:S(2)}, u32[]{:S(2)}) collective-permute-start(bf16[128,1024]{1,0:T(8,128)(2,1)} %get-tuple-element.20), channel_id=1, source_target_pairs={{0,1},{1,0},{2,3},{3,2},{4,5},{5,4},{6,7},{7,6},{8,9},{9,8},{10,11... | collective-permute-start | bytes 786440 | tf_op jit(solution)/shard_map/ppermute | solution.py:202
  6.1 1.5 %collective-permute-start.4 = (bf16[128,1024]{1,0:T(8,128)(2,1)}, bf16[128,1024]{1,0:T(8,128)(2,1)S(1)}, u32[]{:S(2)}, u32[]{:S(2)}) collective-permute-start(bf16[128,1024]{1,0:T(8,128)(2,1)} %get-tuple-element.26), channel_id=1, source_target_pairs={{0,2},{1,3},{2,0},{3,1},{4,6},{5,7},{6,4},{7,5},{8,10},{9,11},{10,... | collective-permute-start | bytes 786440 | tf_op jit(solution)/shard_map/ppermute | solution.py:202
  7.7 5.8 %collective-permute-done.refs_1_.refs_5_.refs_2_ = bf16[128,1024]{1,0:T(8,128)(2,1)S(1)} collective-permute-done((bf16[128,1024]{1,0:T(8,128)(2,1)}, bf16[128,1024]{1,0:T(8,128)(2,1)S(1)}, u32[]{:S(2)}, u32[]{:S(2)}) %collective-permute-start) | collective-permute-done | bytes 262176 | tf_op jit(solution)/shard_map/ppermute | solution.py:202
  13.6 2.1 %collective-permute-start.1 = (bf16[128,1024]{1,0:T(8,128)(2,1)S(1)}, bf16[128,1024]{1,0:T(8,128)(2,1)S(1)}, u32[]{:S(2)}, u32[]{:S(2)}) collective-permute-start(bf16[128,1024]{1,0:T(8,128)(2,1)S(1)} %get-tuple-element.22), channel_id=1, source_target_pairs={{0,1},{1,0},{2,3},{3,2},{4,5},{5,4},{6,7},{7,6},{8,9},{9,8},{10,11... | collective-permute-start | bytes 786440 | tf_op jit(solution)/shard_map/ppermute | solution.py:202
  15.7 1.5 %collective-permute-start.2 = (bf16[128,1024]{1,0:T(8,128)(2,1)S(1)}, bf16[128,1024]{1,0:T(8,128)(2,1)S(1)}, u32[]{:S(2)}, u32[]{:S(2)}) collective-permute-start(bf16[128,1024]{1,0:T(8,128)(2,1)S(1)} %get-tuple-element.23), channel_id=1, source_target_pairs={{0,2},{1,3},{2,0},{3,1},{4,6},{5,7},{6,4},{7,5},{8,10},{9,11},{10,... | collective-permute-start | bytes 786440 | tf_op jit(solution)/shard_map/ppermute | solution.py:202
  17.2 3.0 %collective-permute-done.4.refs_2_.refs_6_.refs_3_ = bf16[128,1024]{1,0:T(8,128)(2,1)S(1)} collective-permute-done((bf16[128,1024]{1,0:T(8,128)(2,1)}, bf16[128,1024]{1,0:T(8,128)(2,1)S(1)}, u32[]{:S(2)}, u32[]{:S(2)}) %collective-permute-start.4) | collective-permute-done | bytes 262176 | tf_op jit(solution)/shard_map/ppermute | solution.py:202
  21.2 1.6 %collective-permute-start.6 = (bf16[512,512]{1,0:T(8,128)(2,1)S(1)}, bf16[512,512]{1,0:T(8,128)(2,1)S(1)}, u32[]{:S(2)}, u32[]{:S(2)}) collective-permute-start(bf16[512,512]{1,0:T(8,128)(2,1)S(1)} %gradient.4), channel_id=1, source_target_pairs={{0,4},{1,5},{2,6},{3,7},{4,0},{5,1},{6,2},{7,3},{8,12},{9,13},{10,... | collective-permute-start | bytes 1572872 | tf_op jit(solution)/shard_map/ppermute | solution.py:199
  22.8 2.0 %collective-permute-done.1.refs_1_.refs_5_ = bf16[128,1024]{1,0:T(8,128)(2,1)S(1)} collective-permute-done((bf16[128,1024]{1,0:T(8,128)(2,1)S(1)}, bf16[128,1024]{1,0:T(8,128)(2,1)S(1)}, u32[]{:S(2)}, u32[]{:S(2)}) %collective-permute-start.1) | collective-permute-done | bytes 262176 | tf_op jit(solution)/shard_map/ppermute | solution.py:202
  24.8 6.2 %collective-permute-done.2.refs_2_.refs_6_ = bf16[128,1024]{1,0:T(8,128)(2,1)S(1)} collective-permute-done((bf16[128,1024]{1,0:T(8,128)(2,1)S(1)}, bf16[128,1024]{1,0:T(8,128)(2,1)S(1)}, u32[]{:S(2)}, u32[]{:S(2)}) %collective-permute-start.2) | collective-permute-done | bytes 262176 | tf_op jit(solution)/shard_map/ppermute | solution.py:202
  31.5 1.6 %collective-permute-start.10 = (bf16[512,512]{1,0:T(8,128)(2,1)S(1)}, bf16[512,512]{1,0:T(8,128)(2,1)S(1)}, u32[]{:S(2)}, u32[]{:S(2)}) collective-permute-start(bf16[512,512]{1,0:T(8,128)(2,1)S(1)} %gradient.7), channel_id=1, source_target_pairs={{0,4},{1,5},{2,6},{3,7},{4,0},{5,1},{6,2},{7,3},{8,12},{9,13},{10,... | collective-permute-start | bytes 1572872 | tf_op jit(solution)/shard_map/ppermute | solution.py:199
  33.6 2.7 %collective-permute-start.11 = (bf16[512,512]{1,0:T(8,128)(2,1)S(1)}, bf16[512,512]{1,0:T(8,128)(2,1)S(1)}, u32[]{:S(2)}, u32[]{:S(2)}) collective-permute-start(bf16[512,512]{1,0:T(8,128)(2,1)S(1)} %gradient.5.refs_1_), channel_id=1, source_target_pairs={{0,8},{1,9},{2,10},{3,11},{4,12},{5,13},{6,14},{7,15},{8,0},{9,1},... | collective-permute-start | bytes 1572872 | tf_op jit(solution)/shard_map/ppermute | solution.py:199
  39.9 2.5 %collective-permute-done.7.refs_1_ = bf16[128,512]{1,0:T(8,128)(2,1)S(1)} collective-permute-done((bf16[128,512]{1,0:T(8,128)(2,1)S(1)}, bf16[128,512]{1,0:T(8,128)(2,1)S(1)}, u32[]{:S(2)}, u32[]{:S(2)}) %collective-permute-start.7) | collective-permute-done | bytes 131104 | tf_op jit(solution)/shard_map/ppermute | solution.py:202
  42.7 1.6 %collective-permute-done.9.refs_3_ = bf16[128,512]{1,0:T(8,128)(2,1)S(1)} collective-permute-done((bf16[128,512]{1,0:T(8,128)(2,1)S(1)}, bf16[128,512]{1,0:T(8,128)(2,1)S(1)}, u32[]{:S(2)}, u32[]{:S(2)}) %collective-permute-start.9) | collective-permute-done | bytes 131104 | tf_op jit(solution)/shard_map/ppermute | solution.py:202
  44.8 9.9 %collective-permute-done.10.refs_1_ = bf16[512,512]{1,0:T(8,128)(2,1)S(1)} collective-permute-done((bf16[512,512]{1,0:T(8,128)(2,1)S(1)}, bf16[512,512]{1,0:T(8,128)(2,1)S(1)}, u32[]{:S(2)}, u32[]{:S(2)}) %collective-permute-start.10) | collective-permute-done | bytes 524320 | tf_op jit(solution)/shard_map/ppermute | solution.py:199
  54.7 3.6 %collective-permute-done.11.refs_2_ = bf16[512,512]{1,0:T(8,128)(2,1)S(1)} collective-permute-done((bf16[512,512]{1,0:T(8,128)(2,1)S(1)}, bf16[512,512]{1,0:T(8,128)(2,1)S(1)}, u32[]{:S(2)}, u32[]{:S(2)}) %collective-permute-start.11) | collective-permute-done | bytes 524320 | tf_op jit(solution)/shard_map/ppermute | solution.py:199
  58.9 1.7 %update.1 = (f32[512,512]{1,0:T(8,128)}, f32[256,512]{1,0:T(8,128)S(1)}) custom-call(f32[512,512]{1,0:T(8,128)S(1)} %gradient.6.refs_0_, bf16[512,512]{1,0:T(8,128)(2,1)S(1)} %collective-permute-done.10.refs_1_, bf16[512,512]{1,0:T(8,128)(2,1)S(1)} %collective-permute-done.11.refs_2_, f32[512,512]{1,0:T(8,128)S(1)} %bitcast.11, f32[512,512]{1,0:T(8,128)S(1)} %bitcast.13, ...), custom_call_target="tpu_custom_call" | custom-call | bytes 7864320 | tf_op jit(solution)/shard_map/update/pallas_call | solution.py:63
  61.0 3.0 %collective-permute-start.14 = (bf16[256,512]{1,0:T(8,128)(2,1)S(1)}, bf16[256,512]{1,0:T(8,128)(2,1)S(1)}, u32[]{:S(2)}, u32[]{:S(2)}) collective-permute-start(bf16[256,512]{1,0:T(8,128)(2,1)S(1)} %outer.1.refs_8_), channel_id=1, source_target_pairs={{0,4},{1,5},{2,6},{3,7},{4,0},{5,1},{6,2},{7,3},{8,12},{9,13},{10,... | collective-permute-start | bytes 786440 | tf_op jit(solution)/shard_map/ppermute | solution.py:199
  64.0 11.9 %collective-permute-done.16.refs_12_ = bf16[256,512]{1,0:T(8,128)(2,1)S(1)} collective-permute-done((bf16[256,512]{1,0:T(8,128)(2,1)S(1)}, bf16[256,512]{1,0:T(8,128)(2,1)S(1)}, u32[]{:S(2)}, u32[]{:S(2)}) %collective-permute-start.16) | collective-permute-done | bytes 262176 | tf_op jit(solution)/shard_map/ppermute | solution.py:199
  76.6 7.5 %collective-permute-done.18.refs_5_ = bf16[256,512]{1,0:T(8,128)(2,1)S(1)} collective-permute-done((bf16[256,512]{1,0:T(8,128)(2,1)S(1)}, bf16[256,512]{1,0:T(8,128)(2,1)S(1)}, u32[]{:S(2)}, u32[]{:S(2)}) %collective-permute-start.18) | collective-permute-done | bytes 262176 | tf_op jit(solution)/shard_map/ppermute | solution.py:199
  86.1 1.5 %collective-permute-start.20 = (bf16[128,512]{1,0:T(8,128)(2,1)S(1)}, bf16[128,512]{1,0:T(8,128)(2,1)S(1)}, u32[]{:S(2)}, u32[]{:S(2)}) collective-permute-start(bf16[128,512]{1,0:T(8,128)(2,1)S(1)} %get-tuple-element.35), channel_id=1, source_target_pairs={{0,1},{1,0},{2,3},{3,2},{4,5},{5,4},{6,7},{7,6},{8,9},{9,8},{10,11... | collective-permute-start | bytes 393224 | tf_op jit(solution)/shard_map/ppermute | solution.py:202
  89.6 2.4 %collective-permute-done.20.refs_1_ = bf16[128,512]{1,0:T(8,128)(2,1)S(1)} collective-permute-done((bf16[128,512]{1,0:T(8,128)(2,1)S(1)}, bf16[128,512]{1,0:T(8,128)(2,1)S(1)}, u32[]{:S(2)}, u32[]{:S(2)}) %collective-permute-start.20) | collective-permute-done | bytes 131104 | tf_op jit(solution)/shard_map/ppermute | solution.py:202
  92.1 1.8 %collective-permute-done.21.refs_2_ = bf16[128,512]{1,0:T(8,128)(2,1)S(1)} collective-permute-done((bf16[128,512]{1,0:T(8,128)(2,1)S(1)}, bf16[128,512]{1,0:T(8,128)(2,1)S(1)}, u32[]{:S(2)}, u32[]{:S(2)}) %collective-permute-start.21) | collective-permute-done | bytes 131104 | tf_op jit(solution)/shard_map/ppermute | solution.py:202
  93.9 1.8 %collective-permute-done.22.refs_3_ = bf16[128,512]{1,0:T(8,128)(2,1)S(1)} collective-permute-done((bf16[128,512]{1,0:T(8,128)(2,1)S(1)}, bf16[128,512]{1,0:T(8,128)(2,1)S(1)}, u32[]{:S(2)}, u32[]{:S(2)}) %collective-permute-start.22) | collective-permute-done | bytes 131104 | tf_op jit(solution)/shard_map/ppermute | solution.py:202
  (49 shorter events, 12.9 us)
Async XLA Ops:
  3.1 10.3 %collective-permute-start = (bf16[128,1024]{1,0:T(8,128)(2,1)}, bf16[128,1024]{1,0:T(8,128)(2,1)S(1)}, u32[]{:S(2)}, u32[]{:S(2)}) collective-permute-start(bf16[128,1024]{1,0:T(8,128)(2,1)} %get-tuple-element.20), channel_id=1, source_target_pairs={{0,1},{1,0},{2,3},{3,2},{4,5},{5,4},{6,7},{7,6},{8,9},{9,8},{10,11... | collective-permute-start | bytes 786440 | tf_op jit(solution)/shard_map/ppermute | solution.py:202
  6.1 14.1 %collective-permute-start.4 = (bf16[128,1024]{1,0:T(8,128)(2,1)}, bf16[128,1024]{1,0:T(8,128)(2,1)S(1)}, u32[]{:S(2)}, u32[]{:S(2)}) collective-permute-start(bf16[128,1024]{1,0:T(8,128)(2,1)} %get-tuple-element.26), channel_id=1, source_target_pairs={{0,2},{1,3},{2,0},{3,1},{4,6},{5,7},{6,4},{7,5},{8,10},{9,11},{10,... | collective-permute-start | bytes 786440 | tf_op jit(solution)/shard_map/ppermute | solution.py:202
  7.7 13.0 %collective-permute-start.5 = (bf16[128,1024]{1,0:T(8,128)(2,1)}, bf16[128,1024]{1,0:T(8,128)(2,1)S(1)}, u32[]{:S(2)}, u32[]{:S(2)}) collective-permute-start(bf16[128,1024]{1,0:T(8,128)(2,1)} %get-tuple-element.27), channel_id=1, source_target_pairs={{0,3},{1,2},{2,1},{3,0},{4,7},{5,6},{6,5},{7,4},{8,11},{9,10},{10,... | collective-permute-start | bytes 786440 | tf_op jit(solution)/shard_map/ppermute | solution.py:202
  13.6 11.2 %collective-permute-start.1 = (bf16[128,1024]{1,0:T(8,128)(2,1)S(1)}, bf16[128,1024]{1,0:T(8,128)(2,1)S(1)}, u32[]{:S(2)}, u32[]{:S(2)}) collective-permute-start(bf16[128,1024]{1,0:T(8,128)(2,1)S(1)} %get-tuple-element.22), channel_id=1, source_target_pairs={{0,1},{1,0},{2,3},{3,2},{4,5},{5,4},{6,7},{7,6},{8,9},{9,8},{10,11... | collective-permute-start | bytes 786440 | tf_op jit(solution)/shard_map/ppermute | solution.py:202
  15.7 15.3 %collective-permute-start.2 = (bf16[128,1024]{1,0:T(8,128)(2,1)S(1)}, bf16[128,1024]{1,0:T(8,128)(2,1)S(1)}, u32[]{:S(2)}, u32[]{:S(2)}) collective-permute-start(bf16[128,1024]{1,0:T(8,128)(2,1)S(1)} %get-tuple-element.23), channel_id=1, source_target_pairs={{0,2},{1,3},{2,0},{3,1},{4,6},{5,7},{6,4},{7,5},{8,10},{9,11},{10,... | collective-permute-start | bytes 786440 | tf_op jit(solution)/shard_map/ppermute | solution.py:202
  17.2 13.8 %collective-permute-start.3 = (bf16[128,1024]{1,0:T(8,128)(2,1)S(1)}, bf16[128,1024]{1,0:T(8,128)(2,1)S(1)}, u32[]{:S(2)}, u32[]{:S(2)}) collective-permute-start(bf16[128,1024]{1,0:T(8,128)(2,1)S(1)} %get-tuple-element.24), channel_id=1, source_target_pairs={{0,3},{1,2},{2,1},{3,0},{4,7},{5,6},{6,5},{7,4},{8,11},{9,10},{10,... | collective-permute-start | bytes 786440 | tf_op jit(solution)/shard_map/ppermute | solution.py:202
  21.2 11.9 %collective-permute-start.6 = (bf16[512,512]{1,0:T(8,128)(2,1)S(1)}, bf16[512,512]{1,0:T(8,128)(2,1)S(1)}, u32[]{:S(2)}, u32[]{:S(2)}) collective-permute-start(bf16[512,512]{1,0:T(8,128)(2,1)S(1)} %gradient.4), channel_id=1, source_target_pairs={{0,4},{1,5},{2,6},{3,7},{4,0},{5,1},{6,2},{7,3},{8,12},{9,13},{10,... | collective-permute-start | bytes 1572872 | tf_op jit(solution)/shard_map/ppermute | solution.py:199
  31.5 23.2 %collective-permute-start.10 = (bf16[512,512]{1,0:T(8,128)(2,1)S(1)}, bf16[512,512]{1,0:T(8,128)(2,1)S(1)}, u32[]{:S(2)}, u32[]{:S(2)}) collective-permute-start(bf16[512,512]{1,0:T(8,128)(2,1)S(1)} %gradient.7), channel_id=1, source_target_pairs={{0,4},{1,5},{2,6},{3,7},{4,0},{5,1},{6,2},{7,3},{8,12},{9,13},{10,... | collective-permute-start | bytes 1572872 | tf_op jit(solution)/shard_map/ppermute | solution.py:199
  33.6 24.6 %copy-start.1 = (f32[512,512]{1,0:T(8,128)S(1)}, f32[512,512]{1,0:T(8,128)}, u32[]{:S(2)}) copy-start(f32[512,512]{1,0:T(8,128)} %refs_2_.1) | copy-start | bytes 3145732
  33.6 24.6 %collective-permute-start.11 = (bf16[512,512]{1,0:T(8,128)(2,1)S(1)}, bf16[512,512]{1,0:T(8,128)(2,1)S(1)}, u32[]{:S(2)}, u32[]{:S(2)}) collective-permute-start(bf16[512,512]{1,0:T(8,128)(2,1)S(1)} %gradient.5.refs_1_), channel_id=1, source_target_pairs={{0,8},{1,9},{2,10},{3,11},{4,12},{5,13},{6,14},{7,15},{8,0},{9,1},... | collective-permute-start | bytes 1572872 | tf_op jit(solution)/shard_map/ppermute | solution.py:199
  36.3 6.0 %collective-permute-start.7 = (bf16[128,512]{1,0:T(8,128)(2,1)S(1)}, bf16[128,512]{1,0:T(8,128)(2,1)S(1)}, u32[]{:S(2)}, u32[]{:S(2)}) collective-permute-start(bf16[128,512]{1,0:T(8,128)(2,1)S(1)} %get-tuple-element.29), channel_id=1, source_target_pairs={{0,1},{1,0},{2,3},{3,2},{4,5},{5,4},{6,7},{7,6},{8,9},{9,8},{10,11... | collective-permute-start | bytes 393224 | tf_op jit(solution)/shard_map/ppermute | solution.py:202
  37.7 5.1 %collective-permute-start.8 = (bf16[128,512]{1,0:T(8,128)(2,1)S(1)}, bf16[128,512]{1,0:T(8,128)(2,1)S(1)}, u32[]{:S(2)}, u32[]{:S(2)}) collective-permute-start(bf16[128,512]{1,0:T(8,128)(2,1)S(1)} %get-tuple-element.30), channel_id=1, source_target_pairs={{0,2},{1,3},{2,0},{3,1},{4,6},{5,7},{6,4},{7,5},{8,10},{9,11},{10,... | collective-permute-start | bytes 393224 | tf_op jit(solution)/shard_map/ppermute | solution.py:202
  38.4 5.9 %collective-permute-start.9 = (bf16[128,512]{1,0:T(8,128)(2,1)S(1)}, bf16[128,512]{1,0:T(8,128)(2,1)S(1)}, u32[]{:S(2)}, u32[]{:S(2)}) collective-permute-start(bf16[128,512]{1,0:T(8,128)(2,1)S(1)} %get-tuple-element.31), channel_id=1, source_target_pairs={{0,3},{1,2},{2,1},{3,0},{4,7},{5,6},{6,5},{7,4},{8,11},{9,10},{10,... | collective-permute-start | bytes 393224 | tf_op jit(solution)/shard_map/ppermute | solution.py:202
  58.8 2.0 %collective-permute-start.12 = (f32[256,512]{1,0:T(8,128)S(1)}, f32[256,512]{1,0:T(8,128)S(1)}, u32[]{:S(2)}, u32[]{:S(2)}) collective-permute-start(f32[256,512]{1,0:T(8,128)S(1)} %drift.1), channel_id=1, source_target_pairs={{0,16},{16,0},{1,17},{17,1},{2,18},{18,2},{3,19},{19,3},{4,20},{20... | collective-permute-start | bytes 1572872 | tf_op jit(solution)/shard_map/ppermute | solution.py:208
  60.9 15.0 %collective-permute-start.16 = (bf16[256,512]{1,0:T(8,128)(2,1)S(1)}, bf16[256,512]{1,0:T(8,128)(2,1)S(1)}, u32[]{:S(2)}, u32[]{:S(2)}) collective-permute-start(bf16[256,512]{1,0:T(8,128)(2,1)S(1)} %outer.1.refs_8_), channel_id=1, source_target_pairs={{0,8},{1,9},{2,10},{3,11},{4,12},{5,13},{6,14},{7,15},{8,0},{9,1},... | collective-permute-start | bytes 786440 | tf_op jit(solution)/shard_map/ppermute | solution.py:199
  61.0 15.0 %collective-permute-start.14 = (bf16[256,512]{1,0:T(8,128)(2,1)S(1)}, bf16[256,512]{1,0:T(8,128)(2,1)S(1)}, u32[]{:S(2)}, u32[]{:S(2)}) collective-permute-start(bf16[256,512]{1,0:T(8,128)(2,1)S(1)} %outer.1.refs_8_), channel_id=1, source_target_pairs={{0,4},{1,5},{2,6},{3,7},{4,0},{5,1},{6,2},{7,3},{8,12},{9,13},{10,... | collective-permute-start | bytes 786440 | tf_op jit(solution)/shard_map/ppermute | solution.py:199
  75.9 8.2 %collective-permute-start.18 = (bf16[256,512]{1,0:T(8,128)(2,1)S(1)}, bf16[256,512]{1,0:T(8,128)(2,1)S(1)}, u32[]{:S(2)}, u32[]{:S(2)}) collective-permute-start(bf16[256,512]{1,0:T(8,128)(2,1)S(1)} %collective-permute-done.16.refs_12_), channel_id=1, source_target_pairs={{0,4},{1,5},{2,6},{3,7},{4,0},{5,1},{6,2},{7,3},{8,12},{9,13},{10,... | collective-permute-start | bytes 786440 | tf_op jit(solution)/shard_map/ppermute | solution.py:199
  75.9 8.2 %collective-permute-start.13 = (bf16[256,512]{1,0:T(8,128)(2,1)S(1)}, bf16[256,512]{1,0:T(8,128)(2,1)S(1)}, u32[]{:S(2)}, u32[]{:S(2)}) collective-permute-start(bf16[256,512]{1,0:T(8,128)(2,1)S(1)} %outer.1.refs_8_), channel_id=1, source_target_pairs={{0,16},{16,0},{1,17},{17,1},{2,18},{18,2},{3,19},{19,3},{4,20},{20... | collective-permute-start | bytes 786440 | tf_op jit(solution)/shard_map/ppermute | solution.py:208
  76.1 8.0 %collective-permute-start.15 = (bf16[256,512]{1,0:T(8,128)(2,1)S(1)}, bf16[256,512]{1,0:T(8,128)(2,1)S(1)}, u32[]{:S(2)}, u32[]{:S(2)}) collective-permute-start(bf16[256,512]{1,0:T(8,128)(2,1)S(1)} %collective-permute-done.14.refs_10_), channel_id=1, source_target_pairs={{0,16},{16,0},{1,17},{17,1},{2,18},{18,2},{3,19},{19,3},{4,20},{20... | collective-permute-start | bytes 786440 | tf_op jit(solution)/shard_map/ppermute | solution.py:208
  76.4 7.7 %collective-permute-start.17 = (bf16[256,512]{1,0:T(8,128)(2,1)S(1)}, bf16[256,512]{1,0:T(8,128)(2,1)S(1)}, u32[]{:S(2)}, u32[]{:S(2)}) collective-permute-start(bf16[256,512]{1,0:T(8,128)(2,1)S(1)} %collective-permute-done.16.refs_12_), channel_id=1, source_target_pairs={{0,16},{16,0},{1,17},{17,1},{2,18},{18,2},{3,19},{19,3},{4,20},{20... | collective-permute-start | bytes 786440 | tf_op jit(solution)/shard_map/ppermute | solution.py:208
  84.1 1.5 %collective-permute-start.19 = (bf16[256,512]{1,0:T(8,128)(2,1)S(1)}, bf16[256,512]{1,0:T(8,128)(2,1)S(1)}, u32[]{:S(2)}, u32[]{:S(2)}) collective-permute-start(bf16[256,512]{1,0:T(8,128)(2,1)S(1)} %collective-permute-done.18.refs_5_), channel_id=1, source_target_pairs={{0,16},{16,0},{1,17},{17,1},{2,18},{18,2},{3,19},{19,3},{4,20},{20... | collective-permute-start | bytes 786440 | tf_op jit(solution)/shard_map/ppermute | solution.py:208
  86.1 6.0 %collective-permute-start.20 = (bf16[128,512]{1,0:T(8,128)(2,1)S(1)}, bf16[128,512]{1,0:T(8,128)(2,1)S(1)}, u32[]{:S(2)}, u32[]{:S(2)}) collective-permute-start(bf16[128,512]{1,0:T(8,128)(2,1)S(1)} %get-tuple-element.35), channel_id=1, source_target_pairs={{0,1},{1,0},{2,3},{3,2},{4,5},{5,4},{6,7},{7,6},{8,9},{9,8},{10,11... | collective-permute-start | bytes 393224 | tf_op jit(solution)/shard_map/ppermute | solution.py:202
  87.6 6.3 %collective-permute-start.21 = (bf16[128,512]{1,0:T(8,128)(2,1)S(1)}, bf16[128,512]{1,0:T(8,128)(2,1)S(1)}, u32[]{:S(2)}, u32[]{:S(2)}) collective-permute-start(bf16[128,512]{1,0:T(8,128)(2,1)S(1)} %get-tuple-element.36), channel_id=1, source_target_pairs={{0,2},{1,3},{2,0},{3,1},{4,6},{5,7},{6,4},{7,5},{8,10},{9,11},{10,... | collective-permute-start | bytes 393224 | tf_op jit(solution)/shard_map/ppermute | solution.py:202
  88.2 7.5 %collective-permute-start.22 = (bf16[128,512]{1,0:T(8,128)(2,1)S(1)}, bf16[128,512]{1,0:T(8,128)(2,1)S(1)}, u32[]{:S(2)}, u32[]{:S(2)}) collective-permute-start(bf16[128,512]{1,0:T(8,128)(2,1)S(1)} %get-tuple-element.37), channel_id=1, source_target_pairs={{0,3},{1,2},{2,1},{3,0},{4,7},{5,6},{6,5},{7,4},{8,11},{9,10},{10,... | collective-permute-start | bytes 393224 | tf_op jit(solution)/shard_map/ppermute | solution.py:202
  (6 other events, 106.3 us)

commit v12 on v11

--- a/solution.py
+++ b/solution.py
@@ -256,7 +256,7 @@
         [early] + first + [mine3, swap(mine3)],
         flops,
     )
-    terms = [own] + [across(sums[k - 1], k) for k in range(1, inner)]
+    terms = [own] + [across(sums[k - 1], k) for k in reversed(range(1, inner))]
     (values,) = call(sum_kernel, "sum", [block], terms, 0)
     return (first_next[None], values[None])
 

time: 96.5 us -> 96.6 us (level)
  no operation moved by 1% of the time
where the time goes in v12:
time: 96.6 us; the launch traced here: 96.4 us
  waiting for transfers between devices  61.7 us (64%)
  starting transfers between devices  24.9 us (26%)
  Pallas kernels  8.96 us (9%)
    ppermute x6, waiting for transfers between devices, planes(): lax.ppermute(x, 'fsdp', [(p * inner + i, (p ^ bits) * inner + i) for p in...  33 us
    ppermute x12, waiting for transfers between devices, across(): lax.ppermute(x, 'fsdp', [(p * inner + i, p * inner + (i ^ k)) for p in ra...  27.9 us
    ppermute x12, starting transfers between devices, across(): lax.ppermute(x, 'fsdp', [(p * inner + i, p * inner + (i ^ k)) for p in ra...  15.3 us
    ppermute x6, starting transfers between devices, planes(): lax.ppermute(x, 'fsdp', [(p * inner + i, (p ^ bits) * inner + i) for p in...  9.02 us
    pallas_call x13, Pallas kernels, call(): pl.pallas_call(without_after, out_shape=out, in_specs=[pl.BlockSpec(memor...  8.96 us
  transfers between devices with their start and end apart: 23, of which 18 were waited for; matrix products, arithmetic and copies ran while one was open for 0% of the time, Pallas kernels for 5%

profile of v12, /device:TPU:0, one launch (start us, length us, event | category | flops | bytes accessed | tf_op | source)
XLA Modules:
  0.0 96.4 jit_solution(14529047011812184185)
XLA Ops:
  0.6 2.5 %pack.3 = (bf16[128,1024]{1,0:T(8,128)(2,1)}, bf16[128,1024]{1,0:T(8,128)(2,1)}, bf16[128,1024]{1,0:T(8,128)(2,1)}, bf16[128,1024]{1,0:T(8,128)(2,1)}) custom-call(bf16[128,8192]{1,0:T(8,128)(2,1)} %bitcast.7, bf16[128,512]{1,0:T(8,128)(2,1)} %bitcast.16), custom_call_target="tpu_custom_call" | custom-call | tf_op jit(solution)/shard_map/pack/pallas_call | solution.py:63
  3.1 3.0 %collective-permute-start = (bf16[128,1024]{1,0:T(8,128)(2,1)}, bf16[128,1024]{1,0:T(8,128)(2,1)S(1)}, u32[]{:S(2)}, u32[]{:S(2)}) collective-permute-start(bf16[128,1024]{1,0:T(8,128)(2,1)} %get-tuple-element.20), channel_id=1, source_target_pairs={{0,1},{1,0},{2,3},{3,2},{4,5},{5,4},{6,7},{7,6},{8,9},{9,8},{10,11... | collective-permute-start | bytes 786440 | tf_op jit(solution)/shard_map/ppermute | solution.py:202
  6.1 1.5 %collective-permute-start.4 = (bf16[128,1024]{1,0:T(8,128)(2,1)}, bf16[128,1024]{1,0:T(8,128)(2,1)S(1)}, u32[]{:S(2)}, u32[]{:S(2)}) collective-permute-start(bf16[128,1024]{1,0:T(8,128)(2,1)} %get-tuple-element.26), channel_id=1, source_target_pairs={{0,2},{1,3},{2,0},{3,1},{4,6},{5,7},{6,4},{7,5},{8,10},{9,11},{10,... | collective-permute-start | bytes 786440 | tf_op jit(solution)/shard_map/ppermute | solution.py:202
  7.7 5.8 %collective-permute-done.refs_1_.refs_5_.refs_2_ = bf16[128,1024]{1,0:T(8,128)(2,1)S(1)} collective-permute-done((bf16[128,1024]{1,0:T(8,128)(2,1)}, bf16[128,1024]{1,0:T(8,128)(2,1)S(1)}, u32[]{:S(2)}, u32[]{:S(2)}) %collective-permute-start) | collective-permute-done | bytes 262176 | tf_op jit(solution)/shard_map/ppermute | solution.py:202
  13.6 2.1 %collective-permute-start.1 = (bf16[128,1024]{1,0:T(8,128)(2,1)S(1)}, bf16[128,1024]{1,0:T(8,128)(2,1)S(1)}, u32[]{:S(2)}, u32[]{:S(2)}) collective-permute-start(bf16[128,1024]{1,0:T(8,128)(2,1)S(1)} %get-tuple-element.22), channel_id=1, source_target_pairs={{0,1},{1,0},{2,3},{3,2},{4,5},{5,4},{6,7},{7,6},{8,9},{9,8},{10,11... | collective-permute-start | bytes 786440 | tf_op jit(solution)/shard_map/ppermute | solution.py:202
  15.7 1.5 %collective-permute-start.2 = (bf16[128,1024]{1,0:T(8,128)(2,1)S(1)}, bf16[128,1024]{1,0:T(8,128)(2,1)S(1)}, u32[]{:S(2)}, u32[]{:S(2)}) collective-permute-start(bf16[128,1024]{1,0:T(8,128)(2,1)S(1)} %get-tuple-element.23), channel_id=1, source_target_pairs={{0,2},{1,3},{2,0},{3,1},{4,6},{5,7},{6,4},{7,5},{8,10},{9,11},{10,... | collective-permute-start | bytes 786440 | tf_op jit(solution)/shard_map/ppermute | solution.py:202
  17.2 3.0 %collective-permute-done.4.refs_2_.refs_6_.refs_3_ = bf16[128,1024]{1,0:T(8,128)(2,1)S(1)} collective-permute-done((bf16[128,1024]{1,0:T(8,128)(2,1)}, bf16[128,1024]{1,0:T(8,128)(2,1)S(1)}, u32[]{:S(2)}, u32[]{:S(2)}) %collective-permute-start.4) | collective-permute-done | bytes 262176 | tf_op jit(solution)/shard_map/ppermute | solution.py:202
  21.2 1.6 %collective-permute-start.6 = (bf16[512,512]{1,0:T(8,128)(2,1)S(1)}, bf16[512,512]{1,0:T(8,128)(2,1)S(1)}, u32[]{:S(2)}, u32[]{:S(2)}) collective-permute-start(bf16[512,512]{1,0:T(8,128)(2,1)S(1)} %gradient.4), channel_id=1, source_target_pairs={{0,4},{1,5},{2,6},{3,7},{4,0},{5,1},{6,2},{7,3},{8,12},{9,13},{10,... | collective-permute-start | bytes 1572872 | tf_op jit(solution)/shard_map/ppermute | solution.py:199
  22.8 2.0 %collective-permute-done.1.refs_1_.refs_5_ = bf16[128,1024]{1,0:T(8,128)(2,1)S(1)} collective-permute-done((bf16[128,1024]{1,0:T(8,128)(2,1)S(1)}, bf16[128,1024]{1,0:T(8,128)(2,1)S(1)}, u32[]{:S(2)}, u32[]{:S(2)}) %collective-permute-start.1) | collective-permute-done | bytes 262176 | tf_op jit(solution)/shard_map/ppermute | solution.py:202
  24.8 6.2 %collective-permute-done.2.refs_2_.refs_6_ = bf16[128,1024]{1,0:T(8,128)(2,1)S(1)} collective-permute-done((bf16[128,1024]{1,0:T(8,128)(2,1)S(1)}, bf16[128,1024]{1,0:T(8,128)(2,1)S(1)}, u32[]{:S(2)}, u32[]{:S(2)}) %collective-permute-start.2) | collective-permute-done | bytes 262176 | tf_op jit(solution)/shard_map/ppermute | solution.py:202
  31.5 1.6 %collective-permute-start.10 = (bf16[512,512]{1,0:T(8,128)(2,1)S(1)}, bf16[512,512]{1,0:T(8,128)(2,1)S(1)}, u32[]{:S(2)}, u32[]{:S(2)}) collective-permute-start(bf16[512,512]{1,0:T(8,128)(2,1)S(1)} %gradient.7), channel_id=1, source_target_pairs={{0,4},{1,5},{2,6},{3,7},{4,0},{5,1},{6,2},{7,3},{8,12},{9,13},{10,... | collective-permute-start | bytes 1572872 | tf_op jit(solution)/shard_map/ppermute | solution.py:199
  33.6 2.7 %collective-permute-start.11 = (bf16[512,512]{1,0:T(8,128)(2,1)S(1)}, bf16[512,512]{1,0:T(8,128)(2,1)S(1)}, u32[]{:S(2)}, u32[]{:S(2)}) collective-permute-start(bf16[512,512]{1,0:T(8,128)(2,1)S(1)} %gradient.5.refs_1_), channel_id=1, source_target_pairs={{0,8},{1,9},{2,10},{3,11},{4,12},{5,13},{6,14},{7,15},{8,0},{9,1},... | collective-permute-start | bytes 1572872 | tf_op jit(solution)/shard_map/ppermute | solution.py:199
  39.9 2.5 %collective-permute-done.7.refs_1_ = bf16[128,512]{1,0:T(8,128)(2,1)S(1)} collective-permute-done((bf16[128,512]{1,0:T(8,128)(2,1)S(1)}, bf16[128,512]{1,0:T(8,128)(2,1)S(1)}, u32[]{:S(2)}, u32[]{:S(2)}) %collective-permute-start.7) | collective-permute-done | bytes 131104 | tf_op jit(solution)/shard_map/ppermute | solution.py:202
  42.7 1.6 %collective-permute-done.9.refs_3_ = bf16[128,512]{1,0:T(8,128)(2,1)S(1)} collective-permute-done((bf16[128,512]{1,0:T(8,128)(2,1)S(1)}, bf16[128,512]{1,0:T(8,128)(2,1)S(1)}, u32[]{:S(2)}, u32[]{:S(2)}) %collective-permute-start.9) | collective-permute-done | bytes 131104 | tf_op jit(solution)/shard_map/ppermute | solution.py:202
  44.8 9.9 %collective-permute-done.10.refs_1_ = bf16[512,512]{1,0:T(8,128)(2,1)S(1)} collective-permute-done((bf16[512,512]{1,0:T(8,128)(2,1)S(1)}, bf16[512,512]{1,0:T(8,128)(2,1)S(1)}, u32[]{:S(2)}, u32[]{:S(2)}) %collective-permute-start.10) | collective-permute-done | bytes 524320 | tf_op jit(solution)/shard_map/ppermute | solution.py:199
  54.7 3.6 %collective-permute-done.11.refs_2_ = bf16[512,512]{1,0:T(8,128)(2,1)S(1)} collective-permute-done((bf16[512,512]{1,0:T(8,128)(2,1)S(1)}, bf16[512,512]{1,0:T(8,128)(2,1)S(1)}, u32[]{:S(2)}, u32[]{:S(2)}) %collective-permute-start.11) | collective-permute-done | bytes 524320 | tf_op jit(solution)/shard_map/ppermute | solution.py:199
  58.9 1.7 %update.1 = (f32[512,512]{1,0:T(8,128)}, f32[256,512]{1,0:T(8,128)S(1)}) custom-call(f32[512,512]{1,0:T(8,128)S(1)} %gradient.6.refs_0_, bf16[512,512]{1,0:T(8,128)(2,1)S(1)} %collective-permute-done.10.refs_1_, bf16[512,512]{1,0:T(8,128)(2,1)S(1)} %collective-permute-done.11.refs_2_, f32[512,512]{1,0:T(8,128)S(1)} %bitcast.11, f32[512,512]{1,0:T(8,128)S(1)} %bitcast.13, ...), custom_call_target="tpu_custom_call" | custom-call | bytes 7864320 | tf_op jit(solution)/shard_map/update/pallas_call | solution.py:63
  61.0 3.0 %collective-permute-start.14 = (bf16[256,512]{1,0:T(8,128)(2,1)S(1)}, bf16[256,512]{1,0:T(8,128)(2,1)S(1)}, u32[]{:S(2)}, u32[]{:S(2)}) collective-permute-start(bf16[256,512]{1,0:T(8,128)(2,1)S(1)} %outer.1.refs_8_), channel_id=1, source_target_pairs={{0,4},{1,5},{2,6},{3,7},{4,0},{5,1},{6,2},{7,3},{8,12},{9,13},{10,... | collective-permute-start | bytes 786440 | tf_op jit(solution)/shard_map/ppermute | solution.py:199
  64.0 11.9 %collective-permute-done.16.refs_12_ = bf16[256,512]{1,0:T(8,128)(2,1)S(1)} collective-permute-done((bf16[256,512]{1,0:T(8,128)(2,1)S(1)}, bf16[256,512]{1,0:T(8,128)(2,1)S(1)}, u32[]{:S(2)}, u32[]{:S(2)}) %collective-permute-start.16) | collective-permute-done | bytes 262176 | tf_op jit(solution)/shard_map/ppermute | solution.py:199
  76.6 7.5 %collective-permute-done.18.refs_5_ = bf16[256,512]{1,0:T(8,128)(2,1)S(1)} collective-permute-done((bf16[256,512]{1,0:T(8,128)(2,1)S(1)}, bf16[256,512]{1,0:T(8,128)(2,1)S(1)}, u32[]{:S(2)}, u32[]{:S(2)}) %collective-permute-start.18) | collective-permute-done | bytes 262176 | tf_op jit(solution)/shard_map/ppermute | solution.py:199
  86.1 1.5 %collective-permute-start.20 = (bf16[128,512]{1,0:T(8,128)(2,1)S(1)}, bf16[128,512]{1,0:T(8,128)(2,1)S(1)}, u32[]{:S(2)}, u32[]{:S(2)}) collective-permute-start(bf16[128,512]{1,0:T(8,128)(2,1)S(1)} %get-tuple-element.35), channel_id=1, source_target_pairs={{0,3},{1,2},{2,1},{3,0},{4,7},{5,6},{6,5},{7,4},{8,11},{9,10},{10,... | collective-permute-start | bytes 393224 | tf_op jit(solution)/shard_map/ppermute | solution.py:202
  87.6 1.5 %collective-permute-start.21 = (bf16[128,512]{1,0:T(8,128)(2,1)S(1)}, bf16[128,512]{1,0:T(8,128)(2,1)S(1)}, u32[]{:S(2)}, u32[]{:S(2)}) collective-permute-start(bf16[128,512]{1,0:T(8,128)(2,1)S(1)} %get-tuple-element.36), channel_id=1, source_target_pairs={{0,2},{1,3},{2,0},{3,1},{4,6},{5,7},{6,4},{7,5},{8,10},{9,11},{10,... | collective-permute-start | bytes 393224 | tf_op jit(solution)/shard_map/ppermute | solution.py:202
  89.6 3.8 %collective-permute-done.20.refs_1_ = bf16[128,512]{1,0:T(8,128)(2,1)S(1)} collective-permute-done((bf16[128,512]{1,0:T(8,128)(2,1)S(1)}, bf16[128,512]{1,0:T(8,128)(2,1)S(1)}, u32[]{:S(2)}, u32[]{:S(2)}) %collective-permute-start.20) | collective-permute-done | bytes 131104 | tf_op jit(solution)/shard_map/ppermute | solution.py:202
  93.4 2.0 %collective-permute-done.21.refs_2_ = bf16[128,512]{1,0:T(8,128)(2,1)S(1)} collective-permute-done((bf16[128,512]{1,0:T(8,128)(2,1)S(1)}, bf16[128,512]{1,0:T(8,128)(2,1)S(1)}, u32[]{:S(2)}, u32[]{:S(2)}) %collective-permute-start.21) | collective-permute-done | bytes 131104 | tf_op jit(solution)/shard_map/ppermute | solution.py:202
  (49 shorter events, 11.8 us)
Async XLA Ops:
  3.1 10.3 %collective-permute-start = (bf16[128,1024]{1,0:T(8,128)(2,1)}, bf16[128,1024]{1,0:T(8,128)(2,1)S(1)}, u32[]{:S(2)}, u32[]{:S(2)}) collective-permute-start(bf16[128,1024]{1,0:T(8,128)(2,1)} %get-tuple-element.20), channel_id=1, source_target_pairs={{0,1},{1,0},{2,3},{3,2},{4,5},{5,4},{6,7},{7,6},{8,9},{9,8},{10,11... | collective-permute-start | bytes 786440 | tf_op jit(solution)/shard_map/ppermute | solution.py:202
  6.1 14.1 %collective-permute-start.4 = (bf16[128,1024]{1,0:T(8,128)(2,1)}, bf16[128,1024]{1,0:T(8,128)(2,1)S(1)}, u32[]{:S(2)}, u32[]{:S(2)}) collective-permute-start(bf16[128,1024]{1,0:T(8,128)(2,1)} %get-tuple-element.26), channel_id=1, source_target_pairs={{0,2},{1,3},{2,0},{3,1},{4,6},{5,7},{6,4},{7,5},{8,10},{9,11},{10,... | collective-permute-start | bytes 786440 | tf_op jit(solution)/shard_map/ppermute | solution.py:202
  7.7 13.0 %collective-permute-start.5 = (bf16[128,1024]{1,0:T(8,128)(2,1)}, bf16[128,1024]{1,0:T(8,128)(2,1)S(1)}, u32[]{:S(2)}, u32[]{:S(2)}) collective-permute-start(bf16[128,1024]{1,0:T(8,128)(2,1)} %get-tuple-element.27), channel_id=1, source_target_pairs={{0,3},{1,2},{2,1},{3,0},{4,7},{5,6},{6,5},{7,4},{8,11},{9,10},{10,... | collective-permute-start | bytes 786440 | tf_op jit(solution)/shard_map/ppermute | solution.py:202
  13.6 11.2 %collective-permute-start.1 = (bf16[128,1024]{1,0:T(8,128)(2,1)S(1)}, bf16[128,1024]{1,0:T(8,128)(2,1)S(1)}, u32[]{:S(2)}, u32[]{:S(2)}) collective-permute-start(bf16[128,1024]{1,0:T(8,128)(2,1)S(1)} %get-tuple-element.22), channel_id=1, source_target_pairs={{0,1},{1,0},{2,3},{3,2},{4,5},{5,4},{6,7},{7,6},{8,9},{9,8},{10,11... | collective-permute-start | bytes 786440 | tf_op jit(solution)/shard_map/ppermute | solution.py:202
  15.7 15.3 %collective-permute-start.2 = (bf16[128,1024]{1,0:T(8,128)(2,1)S(1)}, bf16[128,1024]{1,0:T(8,128)(2,1)S(1)}, u32[]{:S(2)}, u32[]{:S(2)}) collective-permute-start(bf16[128,1024]{1,0:T(8,128)(2,1)S(1)} %get-tuple-element.23), channel_id=1, source_target_pairs={{0,2},{1,3},{2,0},{3,1},{4,6},{5,7},{6,4},{7,5},{8,10},{9,11},{10,... | collective-permute-start | bytes 786440 | tf_op jit(solution)/shard_map/ppermute | solution.py:202
  17.2 13.8 %collective-permute-start.3 = (bf16[128,1024]{1,0:T(8,128)(2,1)S(1)}, bf16[128,1024]{1,0:T(8,128)(2,1)S(1)}, u32[]{:S(2)}, u32[]{:S(2)}) collective-permute-start(bf16[128,1024]{1,0:T(8,128)(2,1)S(1)} %get-tuple-element.24), channel_id=1, source_target_pairs={{0,3},{1,2},{2,1},{3,0},{4,7},{5,6},{6,5},{7,4},{8,11},{9,10},{10,... | collective-permute-start | bytes 786440 | tf_op jit(solution)/shard_map/ppermute | solution.py:202
  21.2 11.9 %collective-permute-start.6 = (bf16[512,512]{1,0:T(8,128)(2,1)S(1)}, bf16[512,512]{1,0:T(8,128)(2,1)S(1)}, u32[]{:S(2)}, u32[]{:S(2)}) collective-permute-start(bf16[512,512]{1,0:T(8,128)(2,1)S(1)} %gradient.4), channel_id=1, source_target_pairs={{0,4},{1,5},{2,6},{3,7},{4,0},{5,1},{6,2},{7,3},{8,12},{9,13},{10,... | collective-permute-start | bytes 1572872 | tf_op jit(solution)/shard_map/ppermute | solution.py:199
  31.5 23.2 %collective-permute-start.10 = (bf16[512,512]{1,0:T(8,128)(2,1)S(1)}, bf16[512,512]{1,0:T(8,128)(2,1)S(1)}, u32[]{:S(2)}, u32[]{:S(2)}) collective-permute-start(bf16[512,512]{1,0:T(8,128)(2,1)S(1)} %gradient.7), channel_id=1, source_target_pairs={{0,4},{1,5},{2,6},{3,7},{4,0},{5,1},{6,2},{7,3},{8,12},{9,13},{10,... | collective-permute-start | bytes 1572872 | tf_op jit(solution)/shard_map/ppermute | solution.py:199
  33.6 24.6 %copy-start.1 = (f32[512,512]{1,0:T(8,128)S(1)}, f32[512,512]{1,0:T(8,128)}, u32[]{:S(2)}) copy-start(f32[512,512]{1,0:T(8,128)} %refs_2_.1) | copy-start | bytes 3145732
  33.6 24.6 %collective-permute-start.11 = (bf16[512,512]{1,0:T(8,128)(2,1)S(1)}, bf16[512,512]{1,0:T(8,128)(2,1)S(1)}, u32[]{:S(2)}, u32[]{:S(2)}) collective-permute-start(bf16[512,512]{1,0:T(8,128)(2,1)S(1)} %gradient.5.refs_1_), channel_id=1, source_target_pairs={{0,8},{1,9},{2,10},{3,11},{4,12},{5,13},{6,14},{7,15},{8,0},{9,1},... | collective-permute-start | bytes 1572872 | tf_op jit(solution)/shard_map/ppermute | solution.py:199
  36.3 6.0 %collective-permute-start.7 = (bf16[128,512]{1,0:T(8,128)(2,1)S(1)}, bf16[128,512]{1,0:T(8,128)(2,1)S(1)}, u32[]{:S(2)}, u32[]{:S(2)}) collective-permute-start(bf16[128,512]{1,0:T(8,128)(2,1)S(1)} %get-tuple-element.29), channel_id=1, source_target_pairs={{0,1},{1,0},{2,3},{3,2},{4,5},{5,4},{6,7},{7,6},{8,9},{9,8},{10,11... | collective-permute-start | bytes 393224 | tf_op jit(solution)/shard_map/ppermute | solution.py:202
  37.7 5.1 %collective-permute-start.8 = (bf16[128,512]{1,0:T(8,128)(2,1)S(1)}, bf16[128,512]{1,0:T(8,128)(2,1)S(1)}, u32[]{:S(2)}, u32[]{:S(2)}) collective-permute-start(bf16[128,512]{1,0:T(8,128)(2,1)S(1)} %get-tuple-element.30), channel_id=1, source_target_pairs={{0,2},{1,3},{2,0},{3,1},{4,6},{5,7},{6,4},{7,5},{8,10},{9,11},{10,... | collective-permute-start | bytes 393224 | tf_op jit(solution)/shard_map/ppermute | solution.py:202
  38.4 5.9 %collective-permute-start.9 = (bf16[128,512]{1,0:T(8,128)(2,1)S(1)}, bf16[128,512]{1,0:T(8,128)(2,1)S(1)}, u32[]{:S(2)}, u32[]{:S(2)}) collective-permute-start(bf16[128,512]{1,0:T(8,128)(2,1)S(1)} %get-tuple-element.31), channel_id=1, source_target_pairs={{0,3},{1,2},{2,1},{3,0},{4,7},{5,6},{6,5},{7,4},{8,11},{9,10},{10,... | collective-permute-start | bytes 393224 | tf_op jit(solution)/shard_map/ppermute | solution.py:202
  58.8 2.0 %collective-permute-start.12 = (f32[256,512]{1,0:T(8,128)S(1)}, f32[256,512]{1,0:T(8,128)S(1)}, u32[]{:S(2)}, u32[]{:S(2)}) collective-permute-start(f32[256,512]{1,0:T(8,128)S(1)} %drift.1), channel_id=1, source_target_pairs={{0,16},{16,0},{1,17},{17,1},{2,18},{18,2},{3,19},{19,3},{4,20},{20... | collective-permute-start | bytes 1572872 | tf_op jit(solution)/shard_map/ppermute | solution.py:208
  60.9 15.0 %collective-permute-start.16 = (bf16[256,512]{1,0:T(8,128)(2,1)S(1)}, bf16[256,512]{1,0:T(8,128)(2,1)S(1)}, u32[]{:S(2)}, u32[]{:S(2)}) collective-permute-start(bf16[256,512]{1,0:T(8,128)(2,1)S(1)} %outer.1.refs_8_), channel_id=1, source_target_pairs={{0,8},{1,9},{2,10},{3,11},{4,12},{5,13},{6,14},{7,15},{8,0},{9,1},... | collective-permute-start | bytes 786440 | tf_op jit(solution)/shard_map/ppermute | solution.py:199
  61.0 15.0 %collective-permute-start.14 = (bf16[256,512]{1,0:T(8,128)(2,1)S(1)}, bf16[256,512]{1,0:T(8,128)(2,1)S(1)}, u32[]{:S(2)}, u32[]{:S(2)}) collective-permute-start(bf16[256,512]{1,0:T(8,128)(2,1)S(1)} %outer.1.refs_8_), channel_id=1, source_target_pairs={{0,4},{1,5},{2,6},{3,7},{4,0},{5,1},{6,2},{7,3},{8,12},{9,13},{10,... | collective-permute-start | bytes 786440 | tf_op jit(solution)/shard_map/ppermute | solution.py:199
  75.9 8.2 %collective-permute-start.18 = (bf16[256,512]{1,0:T(8,128)(2,1)S(1)}, bf16[256,512]{1,0:T(8,128)(2,1)S(1)}, u32[]{:S(2)}, u32[]{:S(2)}) collective-permute-start(bf16[256,512]{1,0:T(8,128)(2,1)S(1)} %collective-permute-done.16.refs_12_), channel_id=1, source_target_pairs={{0,4},{1,5},{2,6},{3,7},{4,0},{5,1},{6,2},{7,3},{8,12},{9,13},{10,... | collective-permute-start | bytes 786440 | tf_op jit(solution)/shard_map/ppermute | solution.py:199
  75.9 8.2 %collective-permute-start.13 = (bf16[256,512]{1,0:T(8,128)(2,1)S(1)}, bf16[256,512]{1,0:T(8,128)(2,1)S(1)}, u32[]{:S(2)}, u32[]{:S(2)}) collective-permute-start(bf16[256,512]{1,0:T(8,128)(2,1)S(1)} %outer.1.refs_8_), channel_id=1, source_target_pairs={{0,16},{16,0},{1,17},{17,1},{2,18},{18,2},{3,19},{19,3},{4,20},{20... | collective-permute-start | bytes 786440 | tf_op jit(solution)/shard_map/ppermute | solution.py:208
  76.1 8.0 %collective-permute-start.15 = (bf16[256,512]{1,0:T(8,128)(2,1)S(1)}, bf16[256,512]{1,0:T(8,128)(2,1)S(1)}, u32[]{:S(2)}, u32[]{:S(2)}) collective-permute-start(bf16[256,512]{1,0:T(8,128)(2,1)S(1)} %collective-permute-done.14.refs_10_), channel_id=1, source_target_pairs={{0,16},{16,0},{1,17},{17,1},{2,18},{18,2},{3,19},{19,3},{4,20},{20... | collective-permute-start | bytes 786440 | tf_op jit(solution)/shard_map/ppermute | solution.py:208
  76.4 7.7 %collective-permute-start.17 = (bf16[256,512]{1,0:T(8,128)(2,1)S(1)}, bf16[256,512]{1,0:T(8,128)(2,1)S(1)}, u32[]{:S(2)}, u32[]{:S(2)}) collective-permute-start(bf16[256,512]{1,0:T(8,128)(2,1)S(1)} %collective-permute-done.16.refs_12_), channel_id=1, source_target_pairs={{0,16},{16,0},{1,17},{17,1},{2,18},{18,2},{3,19},{19,3},{4,20},{20... | collective-permute-start | bytes 786440 | tf_op jit(solution)/shard_map/ppermute | solution.py:208
  84.1 1.5 %collective-permute-start.19 = (bf16[256,512]{1,0:T(8,128)(2,1)S(1)}, bf16[256,512]{1,0:T(8,128)(2,1)S(1)}, u32[]{:S(2)}, u32[]{:S(2)}) collective-permute-start(bf16[256,512]{1,0:T(8,128)(2,1)S(1)} %collective-permute-done.18.refs_5_), channel_id=1, source_target_pairs={{0,16},{16,0},{1,17},{17,1},{2,18},{18,2},{3,19},{19,3},{4,20},{20... | collective-permute-start | bytes 786440 | tf_op jit(solution)/shard_map/ppermute | solution.py:208
  86.1 7.3 %collective-permute-start.20 = (bf16[128,512]{1,0:T(8,128)(2,1)S(1)}, bf16[128,512]{1,0:T(8,128)(2,1)S(1)}, u32[]{:S(2)}, u32[]{:S(2)}) collective-permute-start(bf16[128,512]{1,0:T(8,128)(2,1)S(1)} %get-tuple-element.35), channel_id=1, source_target_pairs={{0,3},{1,2},{2,1},{3,0},{4,7},{5,6},{6,5},{7,4},{8,11},{9,10},{10,... | collective-permute-start | bytes 393224 | tf_op jit(solution)/shard_map/ppermute | solution.py:202
  87.6 7.8 %collective-permute-start.21 = (bf16[128,512]{1,0:T(8,128)(2,1)S(1)}, bf16[128,512]{1,0:T(8,128)(2,1)S(1)}, u32[]{:S(2)}, u32[]{:S(2)}) collective-permute-start(bf16[128,512]{1,0:T(8,128)(2,1)S(1)} %get-tuple-element.36), channel_id=1, source_target_pairs={{0,2},{1,3},{2,0},{3,1},{4,6},{5,7},{6,4},{7,5},{8,10},{9,11},{10,... | collective-permute-start | bytes 393224 | tf_op jit(solution)/shard_map/ppermute | solution.py:202
  89.1 6.6 %collective-permute-start.22 = (bf16[128,512]{1,0:T(8,128)(2,1)S(1)}, bf16[128,512]{1,0:T(8,128)(2,1)S(1)}, u32[]{:S(2)}, u32[]{:S(2)}) collective-permute-start(bf16[128,512]{1,0:T(8,128)(2,1)S(1)} %get-tuple-element.37), channel_id=1, source_target_pairs={{0,1},{1,0},{2,3},{3,2},{4,5},{5,4},{6,7},{7,6},{8,9},{9,8},{10,11... | collective-permute-start | bytes 393224 | tf_op jit(solution)/shard_map/ppermute | solution.py:202
  (6 other events, 106.3 us)

commit v13 on v11

--- a/solution.py
+++ b/solution.py
@@ -150,6 +150,10 @@
     half = out.shape[0]
     at = pl.ds(pl.multiple_of(lax.axis_index("rep") * half, half), half)
     out[...] = outer_update((drift[...] + other[...]) / 2, anchor[at, :], momentum[at, :])
+
+
+def copy_kernel(ref, out):
+    out[...] = ref[...]
 
 
 def product(messages, rows, pieces):
@@ -237,9 +241,11 @@
     new_half = jax.ShapeDtypeStruct((half, width), jnp.bfloat16)
     (mine,) = call(outer_kernel, "outer", [new_half], [drift, drift_in, anchor, outer_momentum], 0)
     mine2 = planes(mine, 2)
-    mine1 = planes(mine, 1)
+    other = swap(mine)
+    (again,) = call(copy_kernel, "again", [new_half], [mine], 0, after=[other])
+    mine1 = planes(again, 1)
     mine3 = planes(mine2, 1)
-    pieces = [y for x in (mine, mine1, mine2) for y in (x, swap(x))]
+    pieces = [mine, other] + [y for x in (mine1, mine2) for y in (x, swap(x))]
     flops = 2 * inner * tokens * rows * width
     (early,) = call(
         partial(early_values_kernel, inner, rows),

time: 96.5 us -> 96.8 us (level)
  waiting for transfers between devices: 61.6 us -> 63.4 us
  starting transfers between devices: 24.9 us -> 23.5 us
    ppermute x5, waiting for transfers between devices: 0.78 us -> 2.09 us  [swap(): return lax.ppermute(x, 'rep', [(0, 1), (1, 0)])]
    ppermute x6, starting transfers between devices: 9.02 us -> 7.73 us  [planes(): lax.ppermute(x, 'fsdp', [(p * inner + i, (p ^ bits) * inner + i) for p in...]
    pallas_call x13 -> x14, Pallas kernels: 8.96 us -> 8.98 us  [call(): pl.pallas_call(without_after, out_shape=out, in_specs=[pl.BlockSpec(memor...]
  transfers between devices with their start and end apart: 23 -> 23, of which waited for: 18 -> 19; matrix products, arithmetic and copies ran while one was open for 0% -> 0% of each run, Pallas kernels for 5% -> 5%
where the time goes in v13:
time: 96.8 us; the launch traced here: 96.7 us
  waiting for transfers between devices  63.4 us (65%)
  starting transfers between devices  23.5 us (24%)
  Pallas kernels  8.98 us (9%)
    ppermute x6, waiting for transfers between devices, planes(): lax.ppermute(x, 'fsdp', [(p * inner + i, (p ^ bits) * inner + i) for p in...  33.4 us
    ppermute x12, waiting for transfers between devices, across(): lax.ppermute(x, 'fsdp', [(p * inner + i, p * inner + (i ^ k)) for p in ra...  27.9 us
    ppermute x12, starting transfers between devices, across(): lax.ppermute(x, 'fsdp', [(p * inner + i, p * inner + (i ^ k)) for p in ra...  15.3 us
    pallas_call x14, Pallas kernels, call(): pl.pallas_call(without_after, out_shape=out, in_specs=[pl.BlockSpec(memor...  8.98 us
    ppermute x6, starting transfers between devices, planes(): lax.ppermute(x, 'fsdp', [(p * inner + i, (p ^ bits) * inner + i) for p in...  7.73 us
    ppermute x5, waiting for transfers between devices, swap(): return lax.ppermute(x, 'rep', [(0, 1), (1, 0)])  2.09 us
  transfers between devices with their start and end apart: 23, of which 19 were waited for; matrix products, arithmetic and copies ran while one was open for 0% of the time, Pallas kernels for 5%

profile of v13, /device:TPU:0, one launch (start us, length us, event | category | flops | bytes accessed | tf_op | source)
XLA Modules:
  0.0 96.7 jit_solution(228048118659430749)
XLA Ops:
  0.6 2.5 %pack.3 = (bf16[128,1024]{1,0:T(8,128)(2,1)}, bf16[128,1024]{1,0:T(8,128)(2,1)}, bf16[128,1024]{1,0:T(8,128)(2,1)}, bf16[128,1024]{1,0:T(8,128)(2,1)}) custom-call(bf16[128,8192]{1,0:T(8,128)(2,1)} %bitcast.7, bf16[128,512]{1,0:T(8,128)(2,1)} %bitcast.16), custom_call_target="tpu_custom_call" | custom-call | tf_op jit(solution)/shard_map/pack/pallas_call | solution.py:63
  3.1 3.0 %collective-permute-start = (bf16[128,1024]{1,0:T(8,128)(2,1)}, bf16[128,1024]{1,0:T(8,128)(2,1)S(1)}, u32[]{:S(2)}, u32[]{:S(2)}) collective-permute-start(bf16[128,1024]{1,0:T(8,128)(2,1)} %get-tuple-element.20), channel_id=1, source_target_pairs={{0,1},{1,0},{2,3},{3,2},{4,5},{5,4},{6,7},{7,6},{8,9},{9,8},{10,11... | collective-permute-start | bytes 786440 | tf_op jit(solution)/shard_map/ppermute | solution.py:206
  6.1 1.5 %collective-permute-start.4 = (bf16[128,1024]{1,0:T(8,128)(2,1)}, bf16[128,1024]{1,0:T(8,128)(2,1)S(1)}, u32[]{:S(2)}, u32[]{:S(2)}) collective-permute-start(bf16[128,1024]{1,0:T(8,128)(2,1)} %get-tuple-element.26), channel_id=1, source_target_pairs={{0,2},{1,3},{2,0},{3,1},{4,6},{5,7},{6,4},{7,5},{8,10},{9,11},{10,... | collective-permute-start | bytes 786440 | tf_op jit(solution)/shard_map/ppermute | solution.py:206
  7.7 5.8 %collective-permute-done.refs_1_.refs_5_.refs_2_ = bf16[128,1024]{1,0:T(8,128)(2,1)S(1)} collective-permute-done((bf16[128,1024]{1,0:T(8,128)(2,1)}, bf16[128,1024]{1,0:T(8,128)(2,1)S(1)}, u32[]{:S(2)}, u32[]{:S(2)}) %collective-permute-start) | collective-permute-done | bytes 262176 | tf_op jit(solution)/shard_map/ppermute | solution.py:206
  13.6 2.1 %collective-permute-start.1 = (bf16[128,1024]{1,0:T(8,128)(2,1)S(1)}, bf16[128,1024]{1,0:T(8,128)(2,1)S(1)}, u32[]{:S(2)}, u32[]{:S(2)}) collective-permute-start(bf16[128,1024]{1,0:T(8,128)(2,1)S(1)} %get-tuple-element.22), channel_id=1, source_target_pairs={{0,1},{1,0},{2,3},{3,2},{4,5},{5,4},{6,7},{7,6},{8,9},{9,8},{10,11... | collective-permute-start | bytes 786440 | tf_op jit(solution)/shard_map/ppermute | solution.py:206
  15.7 1.5 %collective-permute-start.2 = (bf16[128,1024]{1,0:T(8,128)(2,1)S(1)}, bf16[128,1024]{1,0:T(8,128)(2,1)S(1)}, u32[]{:S(2)}, u32[]{:S(2)}) collective-permute-start(bf16[128,1024]{1,0:T(8,128)(2,1)S(1)} %get-tuple-element.23), channel_id=1, source_target_pairs={{0,2},{1,3},{2,0},{3,1},{4,6},{5,7},{6,4},{7,5},{8,10},{9,11},{10,... | collective-permute-start | bytes 786440 | tf_op jit(solution)/shard_map/ppermute | solution.py:206
  17.2 3.0 %collective-permute-done.4.refs_2_.refs_6_.refs_3_ = bf16[128,1024]{1,0:T(8,128)(2,1)S(1)} collective-permute-done((bf16[128,1024]{1,0:T(8,128)(2,1)}, bf16[128,1024]{1,0:T(8,128)(2,1)S(1)}, u32[]{:S(2)}, u32[]{:S(2)}) %collective-permute-start.4) | collective-permute-done | bytes 262176 | tf_op jit(solution)/shard_map/ppermute | solution.py:206
  21.2 1.6 %collective-permute-start.6 = (bf16[512,512]{1,0:T(8,128)(2,1)S(1)}, bf16[512,512]{1,0:T(8,128)(2,1)S(1)}, u32[]{:S(2)}, u32[]{:S(2)}) collective-permute-start(bf16[512,512]{1,0:T(8,128)(2,1)S(1)} %gradient.4), channel_id=1, source_target_pairs={{0,4},{1,5},{2,6},{3,7},{4,0},{5,1},{6,2},{7,3},{8,12},{9,13},{10,... | collective-permute-start | bytes 1572872 | tf_op jit(solution)/shard_map/ppermute | solution.py:203
  22.8 2.0 %collective-permute-done.1.refs_1_.refs_5_ = bf16[128,1024]{1,0:T(8,128)(2,1)S(1)} collective-permute-done((bf16[128,1024]{1,0:T(8,128)(2,1)S(1)}, bf16[128,1024]{1,0:T(8,128)(2,1)S(1)}, u32[]{:S(2)}, u32[]{:S(2)}) %collective-permute-start.1) | collective-permute-done | bytes 262176 | tf_op jit(solution)/shard_map/ppermute | solution.py:206
  24.8 6.2 %collective-permute-done.2.refs_2_.refs_6_ = bf16[128,1024]{1,0:T(8,128)(2,1)S(1)} collective-permute-done((bf16[128,1024]{1,0:T(8,128)(2,1)S(1)}, bf16[128,1024]{1,0:T(8,128)(2,1)S(1)}, u32[]{:S(2)}, u32[]{:S(2)}) %collective-permute-start.2) | collective-permute-done | bytes 262176 | tf_op jit(solution)/shard_map/ppermute | solution.py:206
  31.5 1.6 %collective-permute-start.10 = (bf16[512,512]{1,0:T(8,128)(2,1)S(1)}, bf16[512,512]{1,0:T(8,128)(2,1)S(1)}, u32[]{:S(2)}, u32[]{:S(2)}) collective-permute-start(bf16[512,512]{1,0:T(8,128)(2,1)S(1)} %gradient.7), channel_id=1, source_target_pairs={{0,4},{1,5},{2,6},{3,7},{4,0},{5,1},{6,2},{7,3},{8,12},{9,13},{10,... | collective-permute-start | bytes 1572872 | tf_op jit(solution)/shard_map/ppermute | solution.py:203
  33.6 2.7 %collective-permute-start.11 = (bf16[512,512]{1,0:T(8,128)(2,1)S(1)}, bf16[512,512]{1,0:T(8,128)(2,1)S(1)}, u32[]{:S(2)}, u32[]{:S(2)}) collective-permute-start(bf16[512,512]{1,0:T(8,128)(2,1)S(1)} %gradient.5.refs_1_), channel_id=1, source_target_pairs={{0,8},{1,9},{2,10},{3,11},{4,12},{5,13},{6,14},{7,15},{8,0},{9,1},... | collective-permute-start | bytes 1572872 | tf_op jit(solution)/shard_map/ppermute | solution.py:203
  39.9 2.5 %collective-permute-done.7.refs_1_ = bf16[128,512]{1,0:T(8,128)(2,1)S(1)} collective-permute-done((bf16[128,512]{1,0:T(8,128)(2,1)S(1)}, bf16[128,512]{1,0:T(8,128)(2,1)S(1)}, u32[]{:S(2)}, u32[]{:S(2)}) %collective-permute-start.7) | collective-permute-done | bytes 131104 | tf_op jit(solution)/shard_map/ppermute | solution.py:206
  42.7 1.6 %collective-permute-done.9.refs_3_ = bf16[128,512]{1,0:T(8,128)(2,1)S(1)} collective-permute-done((bf16[128,512]{1,0:T(8,128)(2,1)S(1)}, bf16[128,512]{1,0:T(8,128)(2,1)S(1)}, u32[]{:S(2)}, u32[]{:S(2)}) %collective-permute-start.9) | collective-permute-done | bytes 131104 | tf_op jit(solution)/shard_map/ppermute | solution.py:206
  44.8 9.9 %collective-permute-done.10.refs_1_ = bf16[512,512]{1,0:T(8,128)(2,1)S(1)} collective-permute-done((bf16[512,512]{1,0:T(8,128)(2,1)S(1)}, bf16[512,512]{1,0:T(8,128)(2,1)S(1)}, u32[]{:S(2)}, u32[]{:S(2)}) %collective-permute-start.10) | collective-permute-done | bytes 524320 | tf_op jit(solution)/shard_map/ppermute | solution.py:203
  54.7 3.6 %collective-permute-done.11.refs_2_ = bf16[512,512]{1,0:T(8,128)(2,1)S(1)} collective-permute-done((bf16[512,512]{1,0:T(8,128)(2,1)S(1)}, bf16[512,512]{1,0:T(8,128)(2,1)S(1)}, u32[]{:S(2)}, u32[]{:S(2)}) %collective-permute-start.11) | collective-permute-done | bytes 524320 | tf_op jit(solution)/shard_map/ppermute | solution.py:203
  58.9 1.7 %update.1 = (f32[512,512]{1,0:T(8,128)}, f32[256,512]{1,0:T(8,128)S(1)}) custom-call(f32[512,512]{1,0:T(8,128)S(1)} %gradient.6.refs_0_, bf16[512,512]{1,0:T(8,128)(2,1)S(1)} %collective-permute-done.10.refs_1_, bf16[512,512]{1,0:T(8,128)(2,1)S(1)} %collective-permute-done.11.refs_2_, f32[512,512]{1,0:T(8,128)S(1)} %bitcast.11, f32[512,512]{1,0:T(8,128)S(1)} %bitcast.13, ...), custom_call_target="tpu_custom_call" | custom-call | bytes 7864320 | tf_op jit(solution)/shard_map/update/pallas_call | solution.py:63
  62.6 1.8 %collective-permute-start.14 = (bf16[256,512]{1,0:T(8,128)(2,1)S(1)}, bf16[256,512]{1,0:T(8,128)(2,1)S(1)}, u32[]{:S(2)}, u32[]{:S(2)}) collective-permute-start(bf16[256,512]{1,0:T(8,128)(2,1)S(1)} %again.1), channel_id=1, source_target_pairs={{0,4},{1,5},{2,6},{3,7},{4,0},{5,1},{6,2},{7,3},{8,12},{9,13},{10,... | collective-permute-start | bytes 786440 | tf_op jit(solution)/shard_map/ppermute | solution.py:203
  64.4 11.8 %collective-permute-done.16.refs_12_ = bf16[256,512]{1,0:T(8,128)(2,1)S(1)} collective-permute-done((bf16[256,512]{1,0:T(8,128)(2,1)S(1)}, bf16[256,512]{1,0:T(8,128)(2,1)S(1)}, u32[]{:S(2)}, u32[]{:S(2)}) %collective-permute-start.16) | collective-permute-done | bytes 262176 | tf_op jit(solution)/shard_map/ppermute | solution.py:203
  76.7 7.7 %collective-permute-done.18.refs_5_ = bf16[256,512]{1,0:T(8,128)(2,1)S(1)} collective-permute-done((bf16[256,512]{1,0:T(8,128)(2,1)S(1)}, bf16[256,512]{1,0:T(8,128)(2,1)S(1)}, u32[]{:S(2)}, u32[]{:S(2)}) %collective-permute-start.18) | collective-permute-done | bytes 262176 | tf_op jit(solution)/shard_map/ppermute | solution.py:203
  86.4 1.5 %collective-permute-start.20 = (bf16[128,512]{1,0:T(8,128)(2,1)S(1)}, bf16[128,512]{1,0:T(8,128)(2,1)S(1)}, u32[]{:S(2)}, u32[]{:S(2)}) collective-permute-start(bf16[128,512]{1,0:T(8,128)(2,1)S(1)} %get-tuple-element.35), channel_id=1, source_target_pairs={{0,1},{1,0},{2,3},{3,2},{4,5},{5,4},{6,7},{7,6},{8,9},{9,8},{10,11... | collective-permute-start | bytes 393224 | tf_op jit(solution)/shard_map/ppermute | solution.py:206
  89.9 2.4 %collective-permute-done.20.refs_1_ = bf16[128,512]{1,0:T(8,128)(2,1)S(1)} collective-permute-done((bf16[128,512]{1,0:T(8,128)(2,1)S(1)}, bf16[128,512]{1,0:T(8,128)(2,1)S(1)}, u32[]{:S(2)}, u32[]{:S(2)}) %collective-permute-start.20) | collective-permute-done | bytes 131104 | tf_op jit(solution)/shard_map/ppermute | solution.py:206
  92.3 1.8 %collective-permute-done.21.refs_2_ = bf16[128,512]{1,0:T(8,128)(2,1)S(1)} collective-permute-done((bf16[128,512]{1,0:T(8,128)(2,1)S(1)}, bf16[128,512]{1,0:T(8,128)(2,1)S(1)}, u32[]{:S(2)}, u32[]{:S(2)}) %collective-permute-start.21) | collective-permute-done | bytes 131104 | tf_op jit(solution)/shard_map/ppermute | solution.py:206
  94.1 1.8 %collective-permute-done.22.refs_3_ = bf16[128,512]{1,0:T(8,128)(2,1)S(1)} collective-permute-done((bf16[128,512]{1,0:T(8,128)(2,1)S(1)}, bf16[128,512]{1,0:T(8,128)(2,1)S(1)}, u32[]{:S(2)}, u32[]{:S(2)}) %collective-permute-start.22) | collective-permute-done | bytes 131104 | tf_op jit(solution)/shard_map/ppermute | solution.py:206
  (50 shorter events, 14.3 us)
Async XLA Ops:
  3.1 10.3 %collective-permute-start = (bf16[128,1024]{1,0:T(8,128)(2,1)}, bf16[128,1024]{1,0:T(8,128)(2,1)S(1)}, u32[]{:S(2)}, u32[]{:S(2)}) collective-permute-start(bf16[128,1024]{1,0:T(8,128)(2,1)} %get-tuple-element.20), channel_id=1, source_target_pairs={{0,1},{1,0},{2,3},{3,2},{4,5},{5,4},{6,7},{7,6},{8,9},{9,8},{10,11... | collective-permute-start | bytes 786440 | tf_op jit(solution)/shard_map/ppermute | solution.py:206
  6.1 14.1 %collective-permute-start.4 = (bf16[128,1024]{1,0:T(8,128)(2,1)}, bf16[128,1024]{1,0:T(8,128)(2,1)S(1)}, u32[]{:S(2)}, u32[]{:S(2)}) collective-permute-start(bf16[128,1024]{1,0:T(8,128)(2,1)} %get-tuple-element.26), channel_id=1, source_target_pairs={{0,2},{1,3},{2,0},{3,1},{4,6},{5,7},{6,4},{7,5},{8,10},{9,11},{10,... | collective-permute-start | bytes 786440 | tf_op jit(solution)/shard_map/ppermute | solution.py:206
  7.7 13.0 %collective-permute-start.5 = (bf16[128,1024]{1,0:T(8,128)(2,1)}, bf16[128,1024]{1,0:T(8,128)(2,1)S(1)}, u32[]{:S(2)}, u32[]{:S(2)}) collective-permute-start(bf16[128,1024]{1,0:T(8,128)(2,1)} %get-tuple-element.27), channel_id=1, source_target_pairs={{0,3},{1,2},{2,1},{3,0},{4,7},{5,6},{6,5},{7,4},{8,11},{9,10},{10,... | collective-permute-start | bytes 786440 | tf_op jit(solution)/shard_map/ppermute | solution.py:206
  13.6 11.2 %collective-permute-start.1 = (bf16[128,1024]{1,0:T(8,128)(2,1)S(1)}, bf16[128,1024]{1,0:T(8,128)(2,1)S(1)}, u32[]{:S(2)}, u32[]{:S(2)}) collective-permute-start(bf16[128,1024]{1,0:T(8,128)(2,1)S(1)} %get-tuple-element.22), channel_id=1, source_target_pairs={{0,1},{1,0},{2,3},{3,2},{4,5},{5,4},{6,7},{7,6},{8,9},{9,8},{10,11... | collective-permute-start | bytes 786440 | tf_op jit(solution)/shard_map/ppermute | solution.py:206
  15.7 15.3 %collective-permute-start.2 = (bf16[128,1024]{1,0:T(8,128)(2,1)S(1)}, bf16[128,1024]{1,0:T(8,128)(2,1)S(1)}, u32[]{:S(2)}, u32[]{:S(2)}) collective-permute-start(bf16[128,1024]{1,0:T(8,128)(2,1)S(1)} %get-tuple-element.23), channel_id=1, source_target_pairs={{0,2},{1,3},{2,0},{3,1},{4,6},{5,7},{6,4},{7,5},{8,10},{9,11},{10,... | collective-permute-start | bytes 786440 | tf_op jit(solution)/shard_map/ppermute | solution.py:206
  17.2 13.8 %collective-permute-start.3 = (bf16[128,1024]{1,0:T(8,128)(2,1)S(1)}, bf16[128,1024]{1,0:T(8,128)(2,1)S(1)}, u32[]{:S(2)}, u32[]{:S(2)}) collective-permute-start(bf16[128,1024]{1,0:T(8,128)(2,1)S(1)} %get-tuple-element.24), channel_id=1, source_target_pairs={{0,3},{1,2},{2,1},{3,0},{4,7},{5,6},{6,5},{7,4},{8,11},{9,10},{10,... | collective-permute-start | bytes 786440 | tf_op jit(solution)/shard_map/ppermute | solution.py:206
  21.2 11.9 %collective-permute-start.6 = (bf16[512,512]{1,0:T(8,128)(2,1)S(1)}, bf16[512,512]{1,0:T(8,128)(2,1)S(1)}, u32[]{:S(2)}, u32[]{:S(2)}) collective-permute-start(bf16[512,512]{1,0:T(8,128)(2,1)S(1)} %gradient.4), channel_id=1, source_target_pairs={{0,4},{1,5},{2,6},{3,7},{4,0},{5,1},{6,2},{7,3},{8,12},{9,13},{10,... | collective-permute-start | bytes 1572872 | tf_op jit(solution)/shard_map/ppermute | solution.py:203
  31.5 23.2 %collective-permute-start.10 = (bf16[512,512]{1,0:T(8,128)(2,1)S(1)}, bf16[512,512]{1,0:T(8,128)(2,1)S(1)}, u32[]{:S(2)}, u32[]{:S(2)}) collective-permute-start(bf16[512,512]{1,0:T(8,128)(2,1)S(1)} %gradient.7), channel_id=1, source_target_pairs={{0,4},{1,5},{2,6},{3,7},{4,0},{5,1},{6,2},{7,3},{8,12},{9,13},{10,... | collective-permute-start | bytes 1572872 | tf_op jit(solution)/shard_map/ppermute | solution.py:203
  33.6 24.6 %copy-start.1 = (f32[512,512]{1,0:T(8,128)S(1)}, f32[512,512]{1,0:T(8,128)}, u32[]{:S(2)}) copy-start(f32[512,512]{1,0:T(8,128)} %refs_2_.1) | copy-start | bytes 3145732
  33.6 24.6 %collective-permute-start.11 = (bf16[512,512]{1,0:T(8,128)(2,1)S(1)}, bf16[512,512]{1,0:T(8,128)(2,1)S(1)}, u32[]{:S(2)}, u32[]{:S(2)}) collective-permute-start(bf16[512,512]{1,0:T(8,128)(2,1)S(1)} %gradient.5.refs_1_), channel_id=1, source_target_pairs={{0,8},{1,9},{2,10},{3,11},{4,12},{5,13},{6,14},{7,15},{8,0},{9,1},... | collective-permute-start | bytes 1572872 | tf_op jit(solution)/shard_map/ppermute | solution.py:203
  36.3 6.0 %collective-permute-start.7 = (bf16[128,512]{1,0:T(8,128)(2,1)S(1)}, bf16[128,512]{1,0:T(8,128)(2,1)S(1)}, u32[]{:S(2)}, u32[]{:S(2)}) collective-permute-start(bf16[128,512]{1,0:T(8,128)(2,1)S(1)} %get-tuple-element.29), channel_id=1, source_target_pairs={{0,1},{1,0},{2,3},{3,2},{4,5},{5,4},{6,7},{7,6},{8,9},{9,8},{10,11... | collective-permute-start | bytes 393224 | tf_op jit(solution)/shard_map/ppermute | solution.py:206
  37.7 5.1 %collective-permute-start.8 = (bf16[128,512]{1,0:T(8,128)(2,1)S(1)}, bf16[128,512]{1,0:T(8,128)(2,1)S(1)}, u32[]{:S(2)}, u32[]{:S(2)}) collective-permute-start(bf16[128,512]{1,0:T(8,128)(2,1)S(1)} %get-tuple-element.30), channel_id=1, source_target_pairs={{0,2},{1,3},{2,0},{3,1},{4,6},{5,7},{6,4},{7,5},{8,10},{9,11},{10,... | collective-permute-start | bytes 393224 | tf_op jit(solution)/shard_map/ppermute | solution.py:206
  38.4 5.9 %collective-permute-start.9 = (bf16[128,512]{1,0:T(8,128)(2,1)S(1)}, bf16[128,512]{1,0:T(8,128)(2,1)S(1)}, u32[]{:S(2)}, u32[]{:S(2)}) collective-permute-start(bf16[128,512]{1,0:T(8,128)(2,1)S(1)} %get-tuple-element.31), channel_id=1, source_target_pairs={{0,3},{1,2},{2,1},{3,0},{4,7},{5,6},{6,5},{7,4},{8,11},{9,10},{10,... | collective-permute-start | bytes 393224 | tf_op jit(solution)/shard_map/ppermute | solution.py:206
  58.8 2.0 %collective-permute-start.12 = (f32[256,512]{1,0:T(8,128)S(1)}, f32[256,512]{1,0:T(8,128)S(1)}, u32[]{:S(2)}, u32[]{:S(2)}) collective-permute-start(f32[256,512]{1,0:T(8,128)S(1)} %drift.1), channel_id=1, source_target_pairs={{0,16},{16,0},{1,17},{17,1},{2,18},{18,2},{3,19},{19,3},{4,20},{20... | collective-permute-start | bytes 1572872 | tf_op jit(solution)/shard_map/ppermute | solution.py:212
  60.9 1.6 %collective-permute-start.13 = (bf16[256,512]{1,0:T(8,128)(2,1)S(1)}, bf16[256,512]{1,0:T(8,128)(2,1)S(1)}, u32[]{:S(2)}, u32[]{:S(2)}) collective-permute-start(bf16[256,512]{1,0:T(8,128)(2,1)S(1)} %outer.1.refs_0_.refs_8_), channel_id=1, source_target_pairs={{0,16},{16,0},{1,17},{17,1},{2,18},{18,2},{3,19},{19,3},{4,20},{20... | collective-permute-start | bytes 786440 | tf_op jit(solution)/shard_map/ppermute | solution.py:212
  61.2 14.9 %collective-permute-start.16 = (bf16[256,512]{1,0:T(8,128)(2,1)S(1)}, bf16[256,512]{1,0:T(8,128)(2,1)S(1)}, u32[]{:S(2)}, u32[]{:S(2)}) collective-permute-start(bf16[256,512]{1,0:T(8,128)(2,1)S(1)} %outer.1.refs_0_.refs_8_), channel_id=1, source_target_pairs={{0,8},{1,9},{2,10},{3,11},{4,12},{5,13},{6,14},{7,15},{8,0},{9,1},... | collective-permute-start | bytes 786440 | tf_op jit(solution)/shard_map/ppermute | solution.py:203
  62.6 14.1 %collective-permute-start.14 = (bf16[256,512]{1,0:T(8,128)(2,1)S(1)}, bf16[256,512]{1,0:T(8,128)(2,1)S(1)}, u32[]{:S(2)}, u32[]{:S(2)}) collective-permute-start(bf16[256,512]{1,0:T(8,128)(2,1)S(1)} %again.1), channel_id=1, source_target_pairs={{0,4},{1,5},{2,6},{3,7},{4,0},{5,1},{6,2},{7,3},{8,12},{9,13},{10,... | collective-permute-start | bytes 786440 | tf_op jit(solution)/shard_map/ppermute | solution.py:203
  76.2 8.2 %collective-permute-start.18 = (bf16[256,512]{1,0:T(8,128)(2,1)S(1)}, bf16[256,512]{1,0:T(8,128)(2,1)S(1)}, u32[]{:S(2)}, u32[]{:S(2)}) collective-permute-start(bf16[256,512]{1,0:T(8,128)(2,1)S(1)} %collective-permute-done.16.refs_12_), channel_id=1, source_target_pairs={{0,4},{1,5},{2,6},{3,7},{4,0},{5,1},{6,2},{7,3},{8,12},{9,13},{10,... | collective-permute-start | bytes 786440 | tf_op jit(solution)/shard_map/ppermute | solution.py:203
  76.2 8.2 %collective-permute-start.17 = (bf16[256,512]{1,0:T(8,128)(2,1)S(1)}, bf16[256,512]{1,0:T(8,128)(2,1)S(1)}, u32[]{:S(2)}, u32[]{:S(2)}) collective-permute-start(bf16[256,512]{1,0:T(8,128)(2,1)S(1)} %collective-permute-done.16.refs_12_), channel_id=1, source_target_pairs={{0,16},{16,0},{1,17},{17,1},{2,18},{18,2},{3,19},{19,3},{4,20},{20... | collective-permute-start | bytes 786440 | tf_op jit(solution)/shard_map/ppermute | solution.py:212
  76.7 7.7 %collective-permute-start.15 = (bf16[256,512]{1,0:T(8,128)(2,1)S(1)}, bf16[256,512]{1,0:T(8,128)(2,1)S(1)}, u32[]{:S(2)}, u32[]{:S(2)}) collective-permute-start(bf16[256,512]{1,0:T(8,128)(2,1)S(1)} %collective-permute-done.14.refs_10_), channel_id=1, source_target_pairs={{0,16},{16,0},{1,17},{17,1},{2,18},{18,2},{3,19},{19,3},{4,20},{20... | collective-permute-start | bytes 786440 | tf_op jit(solution)/shard_map/ppermute | solution.py:212
  84.4 1.5 %collective-permute-start.19 = (bf16[256,512]{1,0:T(8,128)(2,1)S(1)}, bf16[256,512]{1,0:T(8,128)(2,1)S(1)}, u32[]{:S(2)}, u32[]{:S(2)}) collective-permute-start(bf16[256,512]{1,0:T(8,128)(2,1)S(1)} %collective-permute-done.18.refs_5_), channel_id=1, source_target_pairs={{0,16},{16,0},{1,17},{17,1},{2,18},{18,2},{3,19},{19,3},{4,20},{20... | collective-permute-start | bytes 786440 | tf_op jit(solution)/shard_map/ppermute | solution.py:212
  86.4 6.0 %collective-permute-start.20 = (bf16[128,512]{1,0:T(8,128)(2,1)S(1)}, bf16[128,512]{1,0:T(8,128)(2,1)S(1)}, u32[]{:S(2)}, u32[]{:S(2)}) collective-permute-start(bf16[128,512]{1,0:T(8,128)(2,1)S(1)} %get-tuple-element.35), channel_id=1, source_target_pairs={{0,1},{1,0},{2,3},{3,2},{4,5},{5,4},{6,7},{7,6},{8,9},{9,8},{10,11... | collective-permute-start | bytes 393224 | tf_op jit(solution)/shard_map/ppermute | solution.py:206
  87.9 6.3 %collective-permute-start.21 = (bf16[128,512]{1,0:T(8,128)(2,1)S(1)}, bf16[128,512]{1,0:T(8,128)(2,1)S(1)}, u32[]{:S(2)}, u32[]{:S(2)}) collective-permute-start(bf16[128,512]{1,0:T(8,128)(2,1)S(1)} %get-tuple-element.36), channel_id=1, source_target_pairs={{0,2},{1,3},{2,0},{3,1},{4,6},{5,7},{6,4},{7,5},{8,10},{9,11},{10,... | collective-permute-start | bytes 393224 | tf_op jit(solution)/shard_map/ppermute | solution.py:206
  88.4 7.5 %collective-permute-start.22 = (bf16[128,512]{1,0:T(8,128)(2,1)S(1)}, bf16[128,512]{1,0:T(8,128)(2,1)S(1)}, u32[]{:S(2)}, u32[]{:S(2)}) collective-permute-start(bf16[128,512]{1,0:T(8,128)(2,1)S(1)} %get-tuple-element.37), channel_id=1, source_target_pairs={{0,3},{1,2},{2,1},{3,0},{4,7},{5,6},{6,5},{7,4},{8,11},{9,10},{10,... | collective-permute-start | bytes 393224 | tf_op jit(solution)/shard_map/ppermute | solution.py:206
  (6 other events, 106.3 us)

commit v14 on v11

--- a/solution.py
+++ b/solution.py
@@ -17,7 +17,6 @@
 PLANES = 4
 CHUNK = 32
 CONTRACT_ROWS = (((0,), (0,)), ((), ()))
-AHEAD_FLOPS = 10**10
 VMEM_BYTES = 16 * 1024 * 1024
 FIRST_VMEM_BYTES = 61 * 1024 * 1024
 
@@ -220,12 +219,13 @@
     full = jax.ShapeDtypeStruct((rows, width), jnp.float32)
     sent = jax.ShapeDtypeStruct((rows, width), jnp.bfloat16)
 
-    def gradient(message, at, out, arrived=(), flops=2 * inner * tokens * rows * width):
+    def gradient(message, at, out, arrived=()):
         kernel = partial(gradient_kernel, inner, rows, at)
+        flops = 2 * inner * tokens * rows * width
         return call(kernel, "gradient", [out], message + first + list(arrived), flops)[0]
 
     beside_far = planes(gradient(first, 0, sent), 1)
-    beside = planes(gradient(second, rows, sent, flops=AHEAD_FLOPS), 1)
+    beside = planes(gradient(second, rows, sent), 1)
     for_far = gradient(second, 0, sent, [beside_far])
     far = planes(for_far, 2)
     last = around(pack((0,), [for_far]))

time: 96.5 us -> 96.2 us (level)
  waiting for transfers between devices: 61.6 us -> 58.3 us
  starting transfers between devices: 24.9 us -> 27 us
    ppermute x6, waiting for transfers between devices: 33 us -> 24.7 us  [planes(): lax.ppermute(x, 'fsdp', [(p * inner + i, (p ^ bits) * inner + i) for p in...]
    ppermute x12, waiting for transfers between devices: 27.9 us -> 32.8 us  [across(): lax.ppermute(x, 'fsdp', [(p * inner + i, p * inner + (i ^ k)) for p in ra...]
    ppermute x6, starting transfers between devices: 9.02 us -> 10.7 us  [planes(): lax.ppermute(x, 'fsdp', [(p * inner + i, (p ^ bits) * inner + i) for p in...]
  transfers between devices with their start and end apart: 23 -> 23, of which waited for: 18 -> 15; matrix products, arithmetic and copies ran while one was open for 0% -> 0% of each run, Pallas kernels for 5% -> 4%
where the time goes in v14:
time: 96.2 us; the launch traced here: 96.1 us
  waiting for transfers between devices  58.3 us (61%)
  starting transfers between devices  27 us (28%)
  Pallas kernels  8.95 us (9%)
  local copies, waits for them, and re-layouts  0.99 us (1%)
    ppermute x12, waiting for transfers between devices, across(): lax.ppermute(x, 'fsdp', [(p * inner + i, p * inner + (i ^ k)) for p in ra...  32.8 us
    ppermute x6, waiting for transfers between devices, planes(): lax.ppermute(x, 'fsdp', [(p * inner + i, (p ^ bits) * inner + i) for p in...  24.7 us
    ppermute x12, starting transfers between devices, across(): lax.ppermute(x, 'fsdp', [(p * inner + i, p * inner + (i ^ k)) for p in ra...  15.7 us
    ppermute x6, starting transfers between devices, planes(): lax.ppermute(x, 'fsdp', [(p * inner + i, (p ^ bits) * inner + i) for p in...  10.7 us
    pallas_call x13, Pallas kernels, call(): pl.pallas_call(without_after, out_shape=out, in_specs=[pl.BlockSpec(memor...  8.95 us
  transfers between devices with their start and end apart: 23, of which 15 were waited for; matrix products, arithmetic and copies ran while one was open for 0% of the time, Pallas kernels for 4%

profile of v14, /device:TPU:0, one launch (start us, length us, event | category | flops | bytes accessed | tf_op | source)
XLA Modules:
  0.0 96.1 jit_solution(10918601069317957819)
XLA Ops:
  0.6 2.5 %pack.3 = (bf16[128,1024]{1,0:T(8,128)(2,1)}, bf16[128,1024]{1,0:T(8,128)(2,1)}, bf16[128,1024]{1,0:T(8,128)(2,1)}, bf16[128,1024]{1,0:T(8,128)(2,1)}) custom-call(bf16[128,8192]{1,0:T(8,128)(2,1)} %bitcast.7, bf16[128,512]{1,0:T(8,128)(2,1)} %bitcast.16), custom_call_target="tpu_custom_call" | custom-call | tf_op jit(solution)/shard_map/pack/pallas_call | solution.py:62
  3.1 3.0 %collective-permute-start = (bf16[128,1024]{1,0:T(8,128)(2,1)}, bf16[128,1024]{1,0:T(8,128)(2,1)S(1)}, u32[]{:S(2)}, u32[]{:S(2)}) collective-permute-start(bf16[128,1024]{1,0:T(8,128)(2,1)} %get-tuple-element.20), channel_id=1, source_target_pairs={{0,1},{1,0},{2,3},{3,2},{4,5},{5,4},{6,7},{7,6},{8,9},{9,8},{10,11... | collective-permute-start | bytes 786440 | tf_op jit(solution)/shard_map/ppermute | solution.py:201
  6.1 1.5 %collective-permute-start.4 = (bf16[128,1024]{1,0:T(8,128)(2,1)}, bf16[128,1024]{1,0:T(8,128)(2,1)S(1)}, u32[]{:S(2)}, u32[]{:S(2)}) collective-permute-start(bf16[128,1024]{1,0:T(8,128)(2,1)} %get-tuple-element.26), channel_id=1, source_target_pairs={{0,2},{1,3},{2,0},{3,1},{4,6},{5,7},{6,4},{7,5},{8,10},{9,11},{10,... | collective-permute-start | bytes 786440 | tf_op jit(solution)/shard_map/ppermute | solution.py:201
  7.7 5.8 %collective-permute-done.refs_1_.refs_5_.refs_2_ = bf16[128,1024]{1,0:T(8,128)(2,1)S(1)} collective-permute-done((bf16[128,1024]{1,0:T(8,128)(2,1)}, bf16[128,1024]{1,0:T(8,128)(2,1)S(1)}, u32[]{:S(2)}, u32[]{:S(2)}) %collective-permute-start) | collective-permute-done | bytes 262176 | tf_op jit(solution)/shard_map/ppermute | solution.py:201
  13.5 6.2 %collective-permute-done.4.refs_2_.refs_6_.refs_3_ = bf16[128,1024]{1,0:T(8,128)(2,1)S(1)} collective-permute-done((bf16[128,1024]{1,0:T(8,128)(2,1)}, bf16[128,1024]{1,0:T(8,128)(2,1)S(1)}, u32[]{:S(2)}, u32[]{:S(2)}) %collective-permute-start.4) | collective-permute-done | bytes 262176 | tf_op jit(solution)/shard_map/ppermute | solution.py:201
  21.1 1.6 %collective-permute-start.6 = (bf16[512,512]{1,0:T(8,128)(2,1)S(1)}, bf16[512,512]{1,0:T(8,128)(2,1)S(1)}, u32[]{:S(2)}, u32[]{:S(2)}) collective-permute-start(bf16[512,512]{1,0:T(8,128)(2,1)S(1)} %gradient.4), channel_id=1, source_target_pairs={{0,4},{1,5},{2,6},{3,7},{4,0},{5,1},{6,2},{7,3},{8,12},{9,13},{10,... | collective-permute-start | bytes 1572872 | tf_op jit(solution)/shard_map/ppermute | solution.py:198
  25.0 1.4 %collective-permute-start.3 = (bf16[128,1024]{1,0:T(8,128)(2,1)S(1)}, bf16[128,1024]{1,0:T(8,128)(2,1)S(1)}, u32[]{:S(2)}, u32[]{:S(2)}) collective-permute-start(bf16[128,1024]{1,0:T(8,128)(2,1)S(1)} %get-tuple-element.24), channel_id=1, source_target_pairs={{0,3},{1,2},{2,1},{3,0},{4,7},{5,6},{6,5},{7,4},{8,11},{9,10},{10,... | collective-permute-start | bytes 786440 | tf_op jit(solution)/shard_map/ppermute | solution.py:201
  26.4 5.8 %collective-permute-done.1.refs_1_.refs_5_ = bf16[128,1024]{1,0:T(8,128)(2,1)S(1)} collective-permute-done((bf16[128,1024]{1,0:T(8,128)(2,1)S(1)}, bf16[128,1024]{1,0:T(8,128)(2,1)S(1)}, u32[]{:S(2)}, u32[]{:S(2)}) %collective-permute-start.1) | collective-permute-done | bytes 262176 | tf_op jit(solution)/shard_map/ppermute | solution.py:201
  32.2 4.2 %collective-permute-done.2.refs_2_.refs_6_ = bf16[128,1024]{1,0:T(8,128)(2,1)S(1)} collective-permute-done((bf16[128,1024]{1,0:T(8,128)(2,1)S(1)}, bf16[128,1024]{1,0:T(8,128)(2,1)S(1)}, u32[]{:S(2)}, u32[]{:S(2)}) %collective-permute-start.2) | collective-permute-done | bytes 262176 | tf_op jit(solution)/shard_map/ppermute | solution.py:201
  37.9 2.6 %collective-permute-start.11 = (bf16[512,512]{1,0:T(8,128)(2,1)S(1)}, bf16[512,512]{1,0:T(8,128)(2,1)S(1)}, u32[]{:S(2)}, u32[]{:S(2)}) collective-permute-start(bf16[512,512]{1,0:T(8,128)(2,1)S(1)} %gradient.5.refs_1_), channel_id=1, source_target_pairs={{0,8},{1,9},{2,10},{3,11},{4,12},{5,13},{6,14},{7,15},{8,0},{9,1},... | collective-permute-start | bytes 1572872 | tf_op jit(solution)/shard_map/ppermute | solution.py:198
  41.3 1.5 %collective-permute-start.8 = (bf16[128,512]{1,0:T(8,128)(2,1)S(1)}, bf16[128,512]{1,0:T(8,128)(2,1)S(1)}, u32[]{:S(2)}, u32[]{:S(2)}) collective-permute-start(bf16[128,512]{1,0:T(8,128)(2,1)S(1)} %get-tuple-element.30), channel_id=1, source_target_pairs={{0,2},{1,3},{2,0},{3,1},{4,6},{5,7},{6,4},{7,5},{8,10},{9,11},{10,... | collective-permute-start | bytes 393224 | tf_op jit(solution)/shard_map/ppermute | solution.py:201
  42.8 1.4 %collective-permute-start.9 = (bf16[128,512]{1,0:T(8,128)(2,1)S(1)}, bf16[128,512]{1,0:T(8,128)(2,1)S(1)}, u32[]{:S(2)}, u32[]{:S(2)}) collective-permute-start(bf16[128,512]{1,0:T(8,128)(2,1)S(1)} %get-tuple-element.31), channel_id=1, source_target_pairs={{0,3},{1,2},{2,1},{3,0},{4,7},{5,6},{6,5},{7,4},{8,11},{9,10},{10,... | collective-permute-start | bytes 393224 | tf_op jit(solution)/shard_map/ppermute | solution.py:201
  44.2 1.5 %collective-permute-done.7.refs_1_ = bf16[128,512]{1,0:T(8,128)(2,1)S(1)} collective-permute-done((bf16[128,512]{1,0:T(8,128)(2,1)S(1)}, bf16[128,512]{1,0:T(8,128)(2,1)S(1)}, u32[]{:S(2)}, u32[]{:S(2)}) %collective-permute-start.7) | collective-permute-done | bytes 131104 | tf_op jit(solution)/shard_map/ppermute | solution.py:201
  46.2 2.4 %collective-permute-done.9.refs_3_ = bf16[128,512]{1,0:T(8,128)(2,1)S(1)} collective-permute-done((bf16[128,512]{1,0:T(8,128)(2,1)S(1)}, bf16[128,512]{1,0:T(8,128)(2,1)S(1)}, u32[]{:S(2)}, u32[]{:S(2)}) %collective-permute-start.9) | collective-permute-done | bytes 131104 | tf_op jit(solution)/shard_map/ppermute | solution.py:201
  49.1 8.5 %collective-permute-done.10.refs_1_ = bf16[512,512]{1,0:T(8,128)(2,1)S(1)} collective-permute-done((bf16[512,512]{1,0:T(8,128)(2,1)S(1)}, bf16[512,512]{1,0:T(8,128)(2,1)S(1)}, u32[]{:S(2)}, u32[]{:S(2)}) %collective-permute-start.10) | collective-permute-done | bytes 524320 | tf_op jit(solution)/shard_map/ppermute | solution.py:198
  58.2 1.7 %update.1 = (f32[512,512]{1,0:T(8,128)}, f32[256,512]{1,0:T(8,128)S(1)}) custom-call(f32[512,512]{1,0:T(8,128)S(1)} %gradient.6.refs_0_, bf16[512,512]{1,0:T(8,128)(2,1)S(1)} %collective-permute-done.10.refs_1_, bf16[512,512]{1,0:T(8,128)(2,1)S(1)} %collective-permute-done.11.refs_2_, f32[512,512]{1,0:T(8,128)S(1)} %bitcast.11, f32[512,512]{1,0:T(8,128)S(1)} %bitcast.13, ...), custom_call_target="tpu_custom_call" | custom-call | bytes 7864320 | tf_op jit(solution)/shard_map/update/pallas_call | solution.py:62
  60.3 1.5 %collective-permute-start.16 = (bf16[256,512]{1,0:T(8,128)(2,1)S(1)}, bf16[256,512]{1,0:T(8,128)(2,1)S(1)}, u32[]{:S(2)}, u32[]{:S(2)}) collective-permute-start(bf16[256,512]{1,0:T(8,128)(2,1)S(1)} %outer.1.refs_8_), channel_id=1, source_target_pairs={{0,8},{1,9},{2,10},{3,11},{4,12},{5,13},{6,14},{7,15},{8,0},{9,1},... | collective-permute-start | bytes 786440 | tf_op jit(solution)/shard_map/ppermute | solution.py:198
  61.8 4.4 %collective-permute-start.14 = (bf16[256,512]{1,0:T(8,128)(2,1)S(1)}, bf16[256,512]{1,0:T(8,128)(2,1)S(1)}, u32[]{:S(2)}, u32[]{:S(2)}) collective-permute-start(bf16[256,512]{1,0:T(8,128)(2,1)S(1)} %outer.1.refs_8_), channel_id=1, source_target_pairs={{0,4},{1,5},{2,6},{3,7},{4,0},{5,1},{6,2},{7,3},{8,12},{9,13},{10,... | collective-permute-start | bytes 786440 | tf_op jit(solution)/shard_map/ppermute | solution.py:198
  66.3 9.2 %collective-permute-done.16.refs_12_ = bf16[256,512]{1,0:T(8,128)(2,1)S(1)} collective-permute-done((bf16[256,512]{1,0:T(8,128)(2,1)S(1)}, bf16[256,512]{1,0:T(8,128)(2,1)S(1)}, u32[]{:S(2)}, u32[]{:S(2)}) %collective-permute-start.16) | collective-permute-done | bytes 262176 | tf_op jit(solution)/shard_map/ppermute | solution.py:198
  76.0 7.0 %collective-permute-done.18.refs_5_ = bf16[256,512]{1,0:T(8,128)(2,1)S(1)} collective-permute-done((bf16[256,512]{1,0:T(8,128)(2,1)S(1)}, bf16[256,512]{1,0:T(8,128)(2,1)S(1)}, u32[]{:S(2)}, u32[]{:S(2)}) %collective-permute-start.18) | collective-permute-done | bytes 262176 | tf_op jit(solution)/shard_map/ppermute | solution.py:198
  85.0 2.3 %collective-permute-start.20 = (bf16[128,512]{1,0:T(8,128)(2,1)S(1)}, bf16[128,512]{1,0:T(8,128)(2,1)S(1)}, u32[]{:S(2)}, u32[]{:S(2)}) collective-permute-start(bf16[128,512]{1,0:T(8,128)(2,1)S(1)} %get-tuple-element.35), channel_id=1, source_target_pairs={{0,1},{1,0},{2,3},{3,2},{4,5},{5,4},{6,7},{7,6},{8,9},{9,8},{10,11... | collective-permute-start | bytes 393224 | tf_op jit(solution)/shard_map/ppermute | solution.py:201
  87.3 1.7 %collective-permute-start.21 = (bf16[128,512]{1,0:T(8,128)(2,1)S(1)}, bf16[128,512]{1,0:T(8,128)(2,1)S(1)}, u32[]{:S(2)}, u32[]{:S(2)}) collective-permute-start(bf16[128,512]{1,0:T(8,128)(2,1)S(1)} %get-tuple-element.36), channel_id=1, source_target_pairs={{0,2},{1,3},{2,0},{3,1},{4,6},{5,7},{6,4},{7,5},{8,10},{9,11},{10,... | collective-permute-start | bytes 393224 | tf_op jit(solution)/shard_map/ppermute | solution.py:201
  89.0 2.2 %collective-permute-done.20.refs_1_ = bf16[128,512]{1,0:T(8,128)(2,1)S(1)} collective-permute-done((bf16[128,512]{1,0:T(8,128)(2,1)S(1)}, bf16[128,512]{1,0:T(8,128)(2,1)S(1)}, u32[]{:S(2)}, u32[]{:S(2)}) %collective-permute-start.20) | collective-permute-done | bytes 131104 | tf_op jit(solution)/shard_map/ppermute | solution.py:201
  91.2 4.2 %collective-permute-done.21.refs_2_ = bf16[128,512]{1,0:T(8,128)(2,1)S(1)} collective-permute-done((bf16[128,512]{1,0:T(8,128)(2,1)S(1)}, bf16[128,512]{1,0:T(8,128)(2,1)S(1)}, u32[]{:S(2)}, u32[]{:S(2)}) %collective-permute-start.21) | collective-permute-done | bytes 131104 | tf_op jit(solution)/shard_map/ppermute | solution.py:201
  (51 shorter events, 11.2 us)
Async XLA Ops:
  3.1 10.3 %collective-permute-start = (bf16[128,1024]{1,0:T(8,128)(2,1)}, bf16[128,1024]{1,0:T(8,128)(2,1)S(1)}, u32[]{:S(2)}, u32[]{:S(2)}) collective-permute-start(bf16[128,1024]{1,0:T(8,128)(2,1)} %get-tuple-element.20), channel_id=1, source_target_pairs={{0,1},{1,0},{2,3},{3,2},{4,5},{5,4},{6,7},{7,6},{8,9},{9,8},{10,11... | collective-permute-start | bytes 786440 | tf_op jit(solution)/shard_map/ppermute | solution.py:201
  6.1 13.6 %collective-permute-start.4 = (bf16[128,1024]{1,0:T(8,128)(2,1)}, bf16[128,1024]{1,0:T(8,128)(2,1)S(1)}, u32[]{:S(2)}, u32[]{:S(2)}) collective-permute-start(bf16[128,1024]{1,0:T(8,128)(2,1)} %get-tuple-element.26), channel_id=1, source_target_pairs={{0,2},{1,3},{2,0},{3,1},{4,6},{5,7},{6,4},{7,5},{8,10},{9,11},{10,... | collective-permute-start | bytes 786440 | tf_op jit(solution)/shard_map/ppermute | solution.py:201
  7.6 12.1 %collective-permute-start.5 = (bf16[128,1024]{1,0:T(8,128)(2,1)}, bf16[128,1024]{1,0:T(8,128)(2,1)S(1)}, u32[]{:S(2)}, u32[]{:S(2)}) collective-permute-start(bf16[128,1024]{1,0:T(8,128)(2,1)} %get-tuple-element.27), channel_id=1, source_target_pairs={{0,3},{1,2},{2,1},{3,0},{4,7},{5,6},{6,5},{7,4},{8,11},{9,10},{10,... | collective-permute-start | bytes 786440 | tf_op jit(solution)/shard_map/ppermute | solution.py:201
  21.1 16.3 %collective-permute-start.6 = (bf16[512,512]{1,0:T(8,128)(2,1)S(1)}, bf16[512,512]{1,0:T(8,128)(2,1)S(1)}, u32[]{:S(2)}, u32[]{:S(2)}) collective-permute-start(bf16[512,512]{1,0:T(8,128)(2,1)S(1)} %gradient.4), channel_id=1, source_target_pairs={{0,4},{1,5},{2,6},{3,7},{4,0},{5,1},{6,2},{7,3},{8,12},{9,13},{10,... | collective-permute-start | bytes 1572872 | tf_op jit(solution)/shard_map/ppermute | solution.py:198
  22.9 9.3 %collective-permute-start.1 = (bf16[128,1024]{1,0:T(8,128)(2,1)S(1)}, bf16[128,1024]{1,0:T(8,128)(2,1)S(1)}, u32[]{:S(2)}, u32[]{:S(2)}) collective-permute-start(bf16[128,1024]{1,0:T(8,128)(2,1)S(1)} %get-tuple-element.22), channel_id=1, source_target_pairs={{0,1},{1,0},{2,3},{3,2},{4,5},{5,4},{6,7},{7,6},{8,9},{9,8},{10,11... | collective-permute-start | bytes 786440 | tf_op jit(solution)/shard_map/ppermute | solution.py:201
  24.2 12.2 %collective-permute-start.2 = (bf16[128,1024]{1,0:T(8,128)(2,1)S(1)}, bf16[128,1024]{1,0:T(8,128)(2,1)S(1)}, u32[]{:S(2)}, u32[]{:S(2)}) collective-permute-start(bf16[128,1024]{1,0:T(8,128)(2,1)S(1)} %get-tuple-element.23), channel_id=1, source_target_pairs={{0,2},{1,3},{2,0},{3,1},{4,6},{5,7},{6,4},{7,5},{8,10},{9,11},{10,... | collective-permute-start | bytes 786440 | tf_op jit(solution)/shard_map/ppermute | solution.py:201
  25.0 11.4 %collective-permute-start.3 = (bf16[128,1024]{1,0:T(8,128)(2,1)S(1)}, bf16[128,1024]{1,0:T(8,128)(2,1)S(1)}, u32[]{:S(2)}, u32[]{:S(2)}) collective-permute-start(bf16[128,1024]{1,0:T(8,128)(2,1)S(1)} %get-tuple-element.24), channel_id=1, source_target_pairs={{0,3},{1,2},{2,1},{3,0},{4,7},{5,6},{6,5},{7,4},{8,11},{9,10},{10,... | collective-permute-start | bytes 786440 | tf_op jit(solution)/shard_map/ppermute | solution.py:201
  36.9 20.7 %collective-permute-start.10 = (bf16[512,512]{1,0:T(8,128)(2,1)S(1)}, bf16[512,512]{1,0:T(8,128)(2,1)S(1)}, u32[]{:S(2)}, u32[]{:S(2)}) collective-permute-start(bf16[512,512]{1,0:T(8,128)(2,1)S(1)} %gradient.7), channel_id=1, source_target_pairs={{0,4},{1,5},{2,6},{3,7},{4,0},{5,1},{6,2},{7,3},{8,12},{9,13},{10,... | collective-permute-start | bytes 1572872 | tf_op jit(solution)/shard_map/ppermute | solution.py:198
  37.9 19.6 %collective-permute-start.11 = (bf16[512,512]{1,0:T(8,128)(2,1)S(1)}, bf16[512,512]{1,0:T(8,128)(2,1)S(1)}, u32[]{:S(2)}, u32[]{:S(2)}) collective-permute-start(bf16[512,512]{1,0:T(8,128)(2,1)S(1)} %gradient.5.refs_1_), channel_id=1, source_target_pairs={{0,8},{1,9},{2,10},{3,11},{4,12},{5,13},{6,14},{7,15},{8,0},{9,1},... | collective-permute-start | bytes 1572872 | tf_op jit(solution)/shard_map/ppermute | solution.py:198
  40.6 5.0 %collective-permute-start.7 = (bf16[128,512]{1,0:T(8,128)(2,1)S(1)}, bf16[128,512]{1,0:T(8,128)(2,1)S(1)}, u32[]{:S(2)}, u32[]{:S(2)}) collective-permute-start(bf16[128,512]{1,0:T(8,128)(2,1)S(1)} %get-tuple-element.29), channel_id=1, source_target_pairs={{0,1},{1,0},{2,3},{3,2},{4,5},{5,4},{6,7},{7,6},{8,9},{9,8},{10,11... | collective-permute-start | bytes 393224 | tf_op jit(solution)/shard_map/ppermute | solution.py:201
  41.3 5.0 %collective-permute-start.8 = (bf16[128,512]{1,0:T(8,128)(2,1)S(1)}, bf16[128,512]{1,0:T(8,128)(2,1)S(1)}, u32[]{:S(2)}, u32[]{:S(2)}) collective-permute-start(bf16[128,512]{1,0:T(8,128)(2,1)S(1)} %get-tuple-element.30), channel_id=1, source_target_pairs={{0,2},{1,3},{2,0},{3,1},{4,6},{5,7},{6,4},{7,5},{8,10},{9,11},{10,... | collective-permute-start | bytes 393224 | tf_op jit(solution)/shard_map/ppermute | solution.py:201
  42.8 5.9 %collective-permute-start.9 = (bf16[128,512]{1,0:T(8,128)(2,1)S(1)}, bf16[128,512]{1,0:T(8,128)(2,1)S(1)}, u32[]{:S(2)}, u32[]{:S(2)}) collective-permute-start(bf16[128,512]{1,0:T(8,128)(2,1)S(1)} %get-tuple-element.31), channel_id=1, source_target_pairs={{0,3},{1,2},{2,1},{3,0},{4,7},{5,6},{6,5},{7,4},{8,11},{9,10},{10,... | collective-permute-start | bytes 393224 | tf_op jit(solution)/shard_map/ppermute | solution.py:201
  58.2 2.0 %collective-permute-start.12 = (f32[256,512]{1,0:T(8,128)S(1)}, f32[256,512]{1,0:T(8,128)S(1)}, u32[]{:S(2)}, u32[]{:S(2)}) collective-permute-start(f32[256,512]{1,0:T(8,128)S(1)} %drift.1), channel_id=1, source_target_pairs={{0,16},{16,0},{1,17},{17,1},{2,18},{18,2},{3,19},{19,3},{4,20},{20... | collective-permute-start | bytes 1572872 | tf_op jit(solution)/shard_map/ppermute | solution.py:207
  60.3 24.3 %copy-start.2 = (bf16[128,1024]{1,0:T(8,128)(2,1)S(1)}, bf16[128,1024]{1,0:T(8,128)(2,1)}, u32[]{:S(2)}) copy-start(bf16[128,1024]{1,0:T(8,128)(2,1)} %get-tuple-element.25.refs_0_.refs_4_.refs_1_) | copy-start | bytes 786436
  60.3 15.1 %collective-permute-start.16 = (bf16[256,512]{1,0:T(8,128)(2,1)S(1)}, bf16[256,512]{1,0:T(8,128)(2,1)S(1)}, u32[]{:S(2)}, u32[]{:S(2)}) collective-permute-start(bf16[256,512]{1,0:T(8,128)(2,1)S(1)} %outer.1.refs_8_), channel_id=1, source_target_pairs={{0,8},{1,9},{2,10},{3,11},{4,12},{5,13},{6,14},{7,15},{8,0},{9,1},... | collective-permute-start | bytes 786440 | tf_op jit(solution)/shard_map/ppermute | solution.py:198
  61.8 13.7 %collective-permute-start.14 = (bf16[256,512]{1,0:T(8,128)(2,1)S(1)}, bf16[256,512]{1,0:T(8,128)(2,1)S(1)}, u32[]{:S(2)}, u32[]{:S(2)}) collective-permute-start(bf16[256,512]{1,0:T(8,128)(2,1)S(1)} %outer.1.refs_8_), channel_id=1, source_target_pairs={{0,4},{1,5},{2,6},{3,7},{4,0},{5,1},{6,2},{7,3},{8,12},{9,13},{10,... | collective-permute-start | bytes 786440 | tf_op jit(solution)/shard_map/ppermute | solution.py:198
  75.5 7.6 %collective-permute-start.18 = (bf16[256,512]{1,0:T(8,128)(2,1)S(1)}, bf16[256,512]{1,0:T(8,128)(2,1)S(1)}, u32[]{:S(2)}, u32[]{:S(2)}) collective-permute-start(bf16[256,512]{1,0:T(8,128)(2,1)S(1)} %collective-permute-done.16.refs_12_), channel_id=1, source_target_pairs={{0,4},{1,5},{2,6},{3,7},{4,0},{5,1},{6,2},{7,3},{8,12},{9,13},{10,... | collective-permute-start | bytes 786440 | tf_op jit(solution)/shard_map/ppermute | solution.py:198
  75.5 7.6 %collective-permute-start.13 = (bf16[256,512]{1,0:T(8,128)(2,1)S(1)}, bf16[256,512]{1,0:T(8,128)(2,1)S(1)}, u32[]{:S(2)}, u32[]{:S(2)}) collective-permute-start(bf16[256,512]{1,0:T(8,128)(2,1)S(1)} %outer.1.refs_8_), channel_id=1, source_target_pairs={{0,16},{16,0},{1,17},{17,1},{2,18},{18,2},{3,19},{19,3},{4,20},{20... | collective-permute-start | bytes 786440 | tf_op jit(solution)/shard_map/ppermute | solution.py:207
  75.5 7.5 %collective-permute-start.15 = (bf16[256,512]{1,0:T(8,128)(2,1)S(1)}, bf16[256,512]{1,0:T(8,128)(2,1)S(1)}, u32[]{:S(2)}, u32[]{:S(2)}) collective-permute-start(bf16[256,512]{1,0:T(8,128)(2,1)S(1)} %collective-permute-done.14.refs_10_), channel_id=1, source_target_pairs={{0,16},{16,0},{1,17},{17,1},{2,18},{18,2},{3,19},{19,3},{4,20},{20... | collective-permute-start | bytes 786440 | tf_op jit(solution)/shard_map/ppermute | solution.py:207
  76.0 7.1 %collective-permute-start.17 = (bf16[256,512]{1,0:T(8,128)(2,1)S(1)}, bf16[256,512]{1,0:T(8,128)(2,1)S(1)}, u32[]{:S(2)}, u32[]{:S(2)}) collective-permute-start(bf16[256,512]{1,0:T(8,128)(2,1)S(1)} %collective-permute-done.16.refs_12_), channel_id=1, source_target_pairs={{0,16},{16,0},{1,17},{17,1},{2,18},{18,2},{3,19},{19,3},{4,20},{20... | collective-permute-start | bytes 786440 | tf_op jit(solution)/shard_map/ppermute | solution.py:207
  83.0 1.5 %collective-permute-start.19 = (bf16[256,512]{1,0:T(8,128)(2,1)S(1)}, bf16[256,512]{1,0:T(8,128)(2,1)S(1)}, u32[]{:S(2)}, u32[]{:S(2)}) collective-permute-start(bf16[256,512]{1,0:T(8,128)(2,1)S(1)} %collective-permute-done.18.refs_5_), channel_id=1, source_target_pairs={{0,16},{16,0},{1,17},{17,1},{2,18},{18,2},{3,19},{19,3},{4,20},{20... | collective-permute-start | bytes 786440 | tf_op jit(solution)/shard_map/ppermute | solution.py:207
  85.0 6.2 %collective-permute-start.20 = (bf16[128,512]{1,0:T(8,128)(2,1)S(1)}, bf16[128,512]{1,0:T(8,128)(2,1)S(1)}, u32[]{:S(2)}, u32[]{:S(2)}) collective-permute-start(bf16[128,512]{1,0:T(8,128)(2,1)S(1)} %get-tuple-element.35), channel_id=1, source_target_pairs={{0,1},{1,0},{2,3},{3,2},{4,5},{5,4},{6,7},{7,6},{8,9},{9,8},{10,11... | collective-permute-start | bytes 393224 | tf_op jit(solution)/shard_map/ppermute | solution.py:201
  87.3 8.1 %collective-permute-start.21 = (bf16[128,512]{1,0:T(8,128)(2,1)S(1)}, bf16[128,512]{1,0:T(8,128)(2,1)S(1)}, u32[]{:S(2)}, u32[]{:S(2)}) collective-permute-start(bf16[128,512]{1,0:T(8,128)(2,1)S(1)} %get-tuple-element.36), channel_id=1, source_target_pairs={{0,2},{1,3},{2,0},{3,1},{4,6},{5,7},{6,4},{7,5},{8,10},{9,11},{10,... | collective-permute-start | bytes 393224 | tf_op jit(solution)/shard_map/ppermute | solution.py:201
  89.0 6.3 %collective-permute-start.22 = (bf16[128,512]{1,0:T(8,128)(2,1)S(1)}, bf16[128,512]{1,0:T(8,128)(2,1)S(1)}, u32[]{:S(2)}, u32[]{:S(2)}) collective-permute-start(bf16[128,512]{1,0:T(8,128)(2,1)S(1)} %get-tuple-element.37), channel_id=1, source_target_pairs={{0,3},{1,2},{2,1},{3,0},{4,7},{5,6},{6,5},{7,4},{8,11},{9,10},{10,... | collective-permute-start | bytes 393224 | tf_op jit(solution)/shard_map/ppermute | solution.py:201
  (7 other events, 103.8 us)

commit v15 on v14

--- a/solution.py
+++ b/solution.py
@@ -18,7 +18,6 @@
 CHUNK = 32
 CONTRACT_ROWS = (((0,), (0,)), ((), ()))
 VMEM_BYTES = 16 * 1024 * 1024
-FIRST_VMEM_BYTES = 61 * 1024 * 1024
 
 
 def outer_update(average, anchor_rows, momentum_rows):
@@ -51,9 +50,8 @@
     return (at // 2 + bits // 2 - 2 * (at // 2) * (bits // 2)) * 2 + low + bits % 2 - 2 * low * (bits % 2)
 
 
-def call(kernel, name, out, inputs, flops, scratch=(), after=(), space=pltpu.VMEM, moved=None, vmem=VMEM_BYTES):
-    if moved is None:
-        moved = sum(x.size * x.dtype.itemsize for x in list(inputs) + list(out))
+def call(kernel, name, out, inputs, flops, scratch=(), after=()):
+    moved = sum(x.size * x.dtype.itemsize for x in list(inputs) + list(out))
     count = len(inputs)
 
     def without_after(*refs):
@@ -62,10 +60,10 @@
     return pl.pallas_call(
         without_after,
         out_shape=out,
-        in_specs=[pl.BlockSpec(memory_space=space)] * count + [pl.BlockSpec(memory_space=pl.ANY)] * len(after),
+        in_specs=[pl.BlockSpec(memory_space=pltpu.VMEM)] * count + [pl.BlockSpec(memory_space=pl.ANY)] * len(after),
         out_specs=[pl.BlockSpec(memory_space=pltpu.VMEM)] * len(out),
         scratch_shapes=list(scratch),
-        compiler_params=pltpu.CompilerParams(vmem_limit_bytes=vmem),
+        compiler_params=pltpu.CompilerParams(vmem_limit_bytes=VMEM_BYTES),
         cost_estimate=pl.CostEstimate(flops=flops, bytes_accessed=moved, transcendentals=0),
         name=name,
     )(*inputs, *after)
@@ -76,17 +74,10 @@
     return pl.multiple_of((flip(f // inner, bits) * inner + flip(lax.rem(f, inner), k)) * rows, rows)
 
 
-def pack_first_kernel(inner, rows, acts_ref, cots_ref, *refs):
-    outs, sems = refs[:inner], refs[inner]
-    copies = []
+def pack_first_kernel(inner, rows, acts_ref, cots_ref, *outs):
     for k in range(inner):
-        block = acts_ref.at[:, pl.ds(block_start(inner, rows, 3, k), rows)]
-        copies.append(pltpu.make_async_copy(block, outs[k].at[:, :rows], sems.at[2 * k]))
-        copies.append(pltpu.make_async_copy(cots_ref, outs[k].at[:, rows:], sems.at[2 * k + 1]))
-    for copy in copies:
-        copy.start()
-    for copy in copies:
-        copy.wait()
+        outs[k][:, :rows] = acts_ref[:, pl.ds(block_start(inner, rows, 3, k), rows)]
+        outs[k][:, rows:] = cots_ref[...]
 
 
 def pack_kernel(inner, rows, blocks, acts_ref, *outs):
@@ -207,9 +198,7 @@
         return lax.ppermute(x, "rep", [(0, 1), (1, 0)])
 
     out = [jax.ShapeDtypeStruct((tokens, rows + width), jnp.bfloat16)] * inner
-    sems = [pltpu.SemaphoreType.DMA((2 * inner,))]
-    kernel = partial(pack_first_kernel, inner, rows)
-    first = around(call(kernel, "pack", out, [acts[0], value_cots[0]], 0, sems, space=pltpu.HBM, moved=0, vmem=FIRST_VMEM_BYTES))
+    first = around(call(partial(pack_first_kernel, inner, rows), "pack", out, [acts[0], value_cots[0]], 0))
 
     def pack(blocks, after):
         out = [jax.ShapeDtypeStruct((tokens, len(blocks) * rows), jnp.bfloat16)] * inner

time: 96.2 us -> 95.1 us (0.989)
  Pallas kernels: 8.95 us -> 6.54 us
  local copies, waits for them, and re-layouts: 0.99 us -> 2.52 us
    pallas_call x13, Pallas kernels: 8.95 us -> 6.54 us  [call(): pl.pallas_call(without_after, out_shape=out, in_specs=[pl.BlockSpec(memor...]
    unnamed x16, local copies, waits for them, and re-layouts: 0.99 us -> 2.52 us
where the time goes in v15:
time: 95.1 us; the launch traced here: 95 us
  waiting for transfers between devices  58.1 us (61%)
  starting transfers between devices  27 us (28%)
  Pallas kernels  6.54 us (7%)
  local copies, waits for them, and re-layouts  2.52 us (3%)
    ppermute x12, waiting for transfers between devices, across(): lax.ppermute(x, 'fsdp', [(p * inner + i, p * inner + (i ^ k)) for p in ra...  32.6 us
    ppermute x6, waiting for transfers between devices, planes(): lax.ppermute(x, 'fsdp', [(p * inner + i, (p ^ bits) * inner + i) for p in...  24.7 us
    ppermute x12, starting transfers between devices, across(): lax.ppermute(x, 'fsdp', [(p * inner + i, p * inner + (i ^ k)) for p in ra...  15.7 us
    ppermute x6, starting transfers between devices, planes(): lax.ppermute(x, 'fsdp', [(p * inner + i, (p ^ bits) * inner + i) for p in...  10.8 us
    pallas_call x13, Pallas kernels, call(): pl.pallas_call(without_after, out_shape=out, in_specs=[pl.BlockSpec(memor...  6.54 us
    unnamed x16, local copies, waits for them, and re-layouts  2.52 us
  transfers between devices with their start and end apart: 23, of which 15 were waited for; matrix products, arithmetic and copies ran while one was open for 0% of the time, Pallas kernels for 4%

profile of v15, /device:TPU:0, one launch (start us, length us, event | category | flops | bytes accessed | tf_op | source)
XLA Modules:
  0.0 95.0 jit_solution(15680489956829713354)
XLA Ops:
  0.6 1.6 %copy-done = bf16[1,128,8192]{2,1,0:T(8,128)(2,1)S(1)} copy-done((bf16[1,128,8192]{2,1,0:T(8,128)(2,1)S(1)}, bf16[1,128,8192]{2,1,0:T(8,128)(2,1)}, u32[]{:S(2)}) %copy-start) | copy-done | bytes 2097176
  3.2 3.0 %collective-permute-start = (bf16[128,1024]{1,0:T(8,128)(2,1)S(1)}, bf16[128,1024]{1,0:T(8,128)(2,1)S(1)}, u32[]{:S(2)}, u32[]{:S(2)}) collective-permute-start(bf16[128,1024]{1,0:T(8,128)(2,1)S(1)} %get-tuple-element.20), channel_id=1, source_target_pairs={{0,1},{1,0},{2,3},{3,2},{4,5},{5,4},{6,7},{7,6},{8,9},{9,8},{10,11... | collective-permute-start | bytes 786440 | tf_op jit(solution)/shard_map/ppermute | solution.py:192
  6.2 1.5 %collective-permute-start.4 = (bf16[128,1024]{1,0:T(8,128)(2,1)S(1)}, bf16[128,1024]{1,0:T(8,128)(2,1)S(1)}, u32[]{:S(2)}, u32[]{:S(2)}) collective-permute-start(bf16[128,1024]{1,0:T(8,128)(2,1)S(1)} %get-tuple-element.26), channel_id=1, source_target_pairs={{0,2},{1,3},{2,0},{3,1},{4,6},{5,7},{6,4},{7,5},{8,10},{9,11},{10,... | collective-permute-start | bytes 786440 | tf_op jit(solution)/shard_map/ppermute | solution.py:192
  7.8 5.6 %collective-permute-done.refs_1_.refs_5_.refs_2_ = bf16[128,1024]{1,0:T(8,128)(2,1)S(1)} collective-permute-done((bf16[128,1024]{1,0:T(8,128)(2,1)S(1)}, bf16[128,1024]{1,0:T(8,128)(2,1)S(1)}, u32[]{:S(2)}, u32[]{:S(2)}) %collective-permute-start) | collective-permute-done | bytes 262176 | tf_op jit(solution)/shard_map/ppermute | solution.py:192
  13.4 6.2 %collective-permute-done.4.refs_2_.refs_6_.refs_3_ = bf16[128,1024]{1,0:T(8,128)(2,1)S(1)} collective-permute-done((bf16[128,1024]{1,0:T(8,128)(2,1)S(1)}, bf16[128,1024]{1,0:T(8,128)(2,1)S(1)}, u32[]{:S(2)}, u32[]{:S(2)}) %collective-permute-start.4) | collective-permute-done | bytes 262176 | tf_op jit(solution)/shard_map/ppermute | solution.py:192
  20.1 1.6 %collective-permute-start.6 = (bf16[512,512]{1,0:T(8,128)(2,1)S(1)}, bf16[512,512]{1,0:T(8,128)(2,1)S(1)}, u32[]{:S(2)}, u32[]{:S(2)}) collective-permute-start(bf16[512,512]{1,0:T(8,128)(2,1)S(1)} %gradient.4), channel_id=1, source_target_pairs={{0,4},{1,5},{2,6},{3,7},{4,0},{5,1},{6,2},{7,3},{8,12},{9,13},{10,... | collective-permute-start | bytes 1572872 | tf_op jit(solution)/shard_map/ppermute | solution.py:189
  23.9 1.4 %collective-permute-start.3 = (bf16[128,1024]{1,0:T(8,128)(2,1)S(1)}, bf16[128,1024]{1,0:T(8,128)(2,1)S(1)}, u32[]{:S(2)}, u32[]{:S(2)}) collective-permute-start(bf16[128,1024]{1,0:T(8,128)(2,1)S(1)} %get-tuple-element.24), channel_id=1, source_target_pairs={{0,3},{1,2},{2,1},{3,0},{4,7},{5,6},{6,5},{7,4},{8,11},{9,10},{10,... | collective-permute-start | bytes 786440 | tf_op jit(solution)/shard_map/ppermute | solution.py:192
  25.4 5.8 %collective-permute-done.1.refs_1_.refs_5_ = bf16[128,1024]{1,0:T(8,128)(2,1)S(1)} collective-permute-done((bf16[128,1024]{1,0:T(8,128)(2,1)S(1)}, bf16[128,1024]{1,0:T(8,128)(2,1)S(1)}, u32[]{:S(2)}, u32[]{:S(2)}) %collective-permute-start.1) | collective-permute-done | bytes 262176 | tf_op jit(solution)/shard_map/ppermute | solution.py:192
  31.1 4.2 %collective-permute-done.2.refs_2_.refs_6_ = bf16[128,1024]{1,0:T(8,128)(2,1)S(1)} collective-permute-done((bf16[128,1024]{1,0:T(8,128)(2,1)S(1)}, bf16[128,1024]{1,0:T(8,128)(2,1)S(1)}, u32[]{:S(2)}, u32[]{:S(2)}) %collective-permute-start.2) | collective-permute-done | bytes 262176 | tf_op jit(solution)/shard_map/ppermute | solution.py:192
  36.9 2.7 %collective-permute-start.11 = (bf16[512,512]{1,0:T(8,128)(2,1)S(1)}, bf16[512,512]{1,0:T(8,128)(2,1)S(1)}, u32[]{:S(2)}, u32[]{:S(2)}) collective-permute-start(bf16[512,512]{1,0:T(8,128)(2,1)S(1)} %gradient.5.refs_1_), channel_id=1, source_target_pairs={{0,8},{1,9},{2,10},{3,11},{4,12},{5,13},{6,14},{7,15},{8,0},{9,1},... | collective-permute-start | bytes 1572872 | tf_op jit(solution)/shard_map/ppermute | solution.py:189
  40.2 1.5 %collective-permute-start.8 = (bf16[128,512]{1,0:T(8,128)(2,1)S(1)}, bf16[128,512]{1,0:T(8,128)(2,1)S(1)}, u32[]{:S(2)}, u32[]{:S(2)}) collective-permute-start(bf16[128,512]{1,0:T(8,128)(2,1)S(1)} %get-tuple-element.30), channel_id=1, source_target_pairs={{0,2},{1,3},{2,0},{3,1},{4,6},{5,7},{6,4},{7,5},{8,10},{9,11},{10,... | collective-permute-start | bytes 393224 | tf_op jit(solution)/shard_map/ppermute | solution.py:192
  41.7 1.4 %collective-permute-start.9 = (bf16[128,512]{1,0:T(8,128)(2,1)S(1)}, bf16[128,512]{1,0:T(8,128)(2,1)S(1)}, u32[]{:S(2)}, u32[]{:S(2)}) collective-permute-start(bf16[128,512]{1,0:T(8,128)(2,1)S(1)} %get-tuple-element.31), channel_id=1, source_target_pairs={{0,3},{1,2},{2,1},{3,0},{4,7},{5,6},{6,5},{7,4},{8,11},{9,10},{10,... | collective-permute-start | bytes 393224 | tf_op jit(solution)/shard_map/ppermute | solution.py:192
  43.1 1.5 %collective-permute-done.7.refs_1_ = bf16[128,512]{1,0:T(8,128)(2,1)S(1)} collective-permute-done((bf16[128,512]{1,0:T(8,128)(2,1)S(1)}, bf16[128,512]{1,0:T(8,128)(2,1)S(1)}, u32[]{:S(2)}, u32[]{:S(2)}) %collective-permute-start.7) | collective-permute-done | bytes 131104 | tf_op jit(solution)/shard_map/ppermute | solution.py:192
  45.2 2.4 %collective-permute-done.9.refs_3_ = bf16[128,512]{1,0:T(8,128)(2,1)S(1)} collective-permute-done((bf16[128,512]{1,0:T(8,128)(2,1)S(1)}, bf16[128,512]{1,0:T(8,128)(2,1)S(1)}, u32[]{:S(2)}, u32[]{:S(2)}) %collective-permute-start.9) | collective-permute-done | bytes 131104 | tf_op jit(solution)/shard_map/ppermute | solution.py:192
  48.0 8.5 %collective-permute-done.10.refs_1_ = bf16[512,512]{1,0:T(8,128)(2,1)S(1)} collective-permute-done((bf16[512,512]{1,0:T(8,128)(2,1)S(1)}, bf16[512,512]{1,0:T(8,128)(2,1)S(1)}, u32[]{:S(2)}, u32[]{:S(2)}) %collective-permute-start.10) | collective-permute-done | bytes 524320 | tf_op jit(solution)/shard_map/ppermute | solution.py:189
  57.2 1.7 %update.1 = (f32[512,512]{1,0:T(8,128)}, f32[256,512]{1,0:T(8,128)S(1)}) custom-call(f32[512,512]{1,0:T(8,128)S(1)} %gradient.6.refs_0_, bf16[512,512]{1,0:T(8,128)(2,1)S(1)} %collective-permute-done.10.refs_1_, bf16[512,512]{1,0:T(8,128)(2,1)S(1)} %collective-permute-done.11.refs_2_, f32[512,512]{1,0:T(8,128)S(1)} %bitcast.11, f32[512,512]{1,0:T(8,128)S(1)} %bitcast.13, ...), custom_call_target="tpu_custom_call" | custom-call | bytes 7864320 | tf_op jit(solution)/shard_map/update/pallas_call | solution.py:60
  59.2 1.5 %collective-permute-start.16 = (bf16[256,512]{1,0:T(8,128)(2,1)S(1)}, bf16[256,512]{1,0:T(8,128)(2,1)S(1)}, u32[]{:S(2)}, u32[]{:S(2)}) collective-permute-start(bf16[256,512]{1,0:T(8,128)(2,1)S(1)} %outer.1.refs_8_), channel_id=1, source_target_pairs={{0,8},{1,9},{2,10},{3,11},{4,12},{5,13},{6,14},{7,15},{8,0},{9,1},... | collective-permute-start | bytes 786440 | tf_op jit(solution)/shard_map/ppermute | solution.py:189
  60.8 4.4 %collective-permute-start.14 = (bf16[256,512]{1,0:T(8,128)(2,1)S(1)}, bf16[256,512]{1,0:T(8,128)(2,1)S(1)}, u32[]{:S(2)}, u32[]{:S(2)}) collective-permute-start(bf16[256,512]{1,0:T(8,128)(2,1)S(1)} %outer.1.refs_8_), channel_id=1, source_target_pairs={{0,4},{1,5},{2,6},{3,7},{4,0},{5,1},{6,2},{7,3},{8,12},{9,13},{10,... | collective-permute-start | bytes 786440 | tf_op jit(solution)/shard_map/ppermute | solution.py:189
  65.2 9.2 %collective-permute-done.16.refs_12_ = bf16[256,512]{1,0:T(8,128)(2,1)S(1)} collective-permute-done((bf16[256,512]{1,0:T(8,128)(2,1)S(1)}, bf16[256,512]{1,0:T(8,128)(2,1)S(1)}, u32[]{:S(2)}, u32[]{:S(2)}) %collective-permute-start.16) | collective-permute-done | bytes 262176 | tf_op jit(solution)/shard_map/ppermute | solution.py:189
  75.0 7.0 %collective-permute-done.18.refs_5_ = bf16[256,512]{1,0:T(8,128)(2,1)S(1)} collective-permute-done((bf16[256,512]{1,0:T(8,128)(2,1)S(1)}, bf16[256,512]{1,0:T(8,128)(2,1)S(1)}, u32[]{:S(2)}, u32[]{:S(2)}) %collective-permute-start.18) | collective-permute-done | bytes 262176 | tf_op jit(solution)/shard_map/ppermute | solution.py:189
  83.9 2.3 %collective-permute-start.20 = (bf16[128,512]{1,0:T(8,128)(2,1)S(1)}, bf16[128,512]{1,0:T(8,128)(2,1)S(1)}, u32[]{:S(2)}, u32[]{:S(2)}) collective-permute-start(bf16[128,512]{1,0:T(8,128)(2,1)S(1)} %get-tuple-element.35), channel_id=1, source_target_pairs={{0,1},{1,0},{2,3},{3,2},{4,5},{5,4},{6,7},{7,6},{8,9},{9,8},{10,11... | collective-permute-start | bytes 393224 | tf_op jit(solution)/shard_map/ppermute | solution.py:192
  86.2 1.7 %collective-permute-start.21 = (bf16[128,512]{1,0:T(8,128)(2,1)S(1)}, bf16[128,512]{1,0:T(8,128)(2,1)S(1)}, u32[]{:S(2)}, u32[]{:S(2)}) collective-permute-start(bf16[128,512]{1,0:T(8,128)(2,1)S(1)} %get-tuple-element.36), channel_id=1, source_target_pairs={{0,2},{1,3},{2,0},{3,1},{4,6},{5,7},{6,4},{7,5},{8,10},{9,11},{10,... | collective-permute-start | bytes 393224 | tf_op jit(solution)/shard_map/ppermute | solution.py:192
  87.9 2.1 %collective-permute-done.20.refs_1_ = bf16[128,512]{1,0:T(8,128)(2,1)S(1)} collective-permute-done((bf16[128,512]{1,0:T(8,128)(2,1)S(1)}, bf16[128,512]{1,0:T(8,128)(2,1)S(1)}, u32[]{:S(2)}, u32[]{:S(2)}) %collective-permute-start.20) | collective-permute-done | bytes 131104 | tf_op jit(solution)/shard_map/ppermute | solution.py:192
  90.1 4.2 %collective-permute-done.21.refs_2_ = bf16[128,512]{1,0:T(8,128)(2,1)S(1)} collective-permute-done((bf16[128,512]{1,0:T(8,128)(2,1)S(1)}, bf16[128,512]{1,0:T(8,128)(2,1)S(1)}, u32[]{:S(2)}, u32[]{:S(2)}) %collective-permute-start.21) | collective-permute-done | bytes 131104 | tf_op jit(solution)/shard_map/ppermute | solution.py:192
  (51 shorter events, 11.2 us)
Async XLA Ops:
  3.2 10.1 %collective-permute-start = (bf16[128,1024]{1,0:T(8,128)(2,1)S(1)}, bf16[128,1024]{1,0:T(8,128)(2,1)S(1)}, u32[]{:S(2)}, u32[]{:S(2)}) collective-permute-start(bf16[128,1024]{1,0:T(8,128)(2,1)S(1)} %get-tuple-element.20), channel_id=1, source_target_pairs={{0,1},{1,0},{2,3},{3,2},{4,5},{5,4},{6,7},{7,6},{8,9},{9,8},{10,11... | collective-permute-start | bytes 786440 | tf_op jit(solution)/shard_map/ppermute | solution.py:192
  6.2 13.4 %collective-permute-start.4 = (bf16[128,1024]{1,0:T(8,128)(2,1)S(1)}, bf16[128,1024]{1,0:T(8,128)(2,1)S(1)}, u32[]{:S(2)}, u32[]{:S(2)}) collective-permute-start(bf16[128,1024]{1,0:T(8,128)(2,1)S(1)} %get-tuple-element.26), channel_id=1, source_target_pairs={{0,2},{1,3},{2,0},{3,1},{4,6},{5,7},{6,4},{7,5},{8,10},{9,11},{10,... | collective-permute-start | bytes 786440 | tf_op jit(solution)/shard_map/ppermute | solution.py:192
  7.7 11.9 %collective-permute-start.5 = (bf16[128,1024]{1,0:T(8,128)(2,1)S(1)}, bf16[128,1024]{1,0:T(8,128)(2,1)S(1)}, u32[]{:S(2)}, u32[]{:S(2)}) collective-permute-start(bf16[128,1024]{1,0:T(8,128)(2,1)S(1)} %get-tuple-element.27), channel_id=1, source_target_pairs={{0,3},{1,2},{2,1},{3,0},{4,7},{5,6},{6,5},{7,4},{8,11},{9,10},{10,... | collective-permute-start | bytes 786440 | tf_op jit(solution)/shard_map/ppermute | solution.py:192
  20.1 16.3 %collective-permute-start.6 = (bf16[512,512]{1,0:T(8,128)(2,1)S(1)}, bf16[512,512]{1,0:T(8,128)(2,1)S(1)}, u32[]{:S(2)}, u32[]{:S(2)}) collective-permute-start(bf16[512,512]{1,0:T(8,128)(2,1)S(1)} %gradient.4), channel_id=1, source_target_pairs={{0,4},{1,5},{2,6},{3,7},{4,0},{5,1},{6,2},{7,3},{8,12},{9,13},{10,... | collective-permute-start | bytes 1572872 | tf_op jit(solution)/shard_map/ppermute | solution.py:189
  21.8 9.3 %collective-permute-start.1 = (bf16[128,1024]{1,0:T(8,128)(2,1)S(1)}, bf16[128,1024]{1,0:T(8,128)(2,1)S(1)}, u32[]{:S(2)}, u32[]{:S(2)}) collective-permute-start(bf16[128,1024]{1,0:T(8,128)(2,1)S(1)} %get-tuple-element.22), channel_id=1, source_target_pairs={{0,1},{1,0},{2,3},{3,2},{4,5},{5,4},{6,7},{7,6},{8,9},{9,8},{10,11... | collective-permute-start | bytes 786440 | tf_op jit(solution)/shard_map/ppermute | solution.py:192
  23.1 12.2 %collective-permute-start.2 = (bf16[128,1024]{1,0:T(8,128)(2,1)S(1)}, bf16[128,1024]{1,0:T(8,128)(2,1)S(1)}, u32[]{:S(2)}, u32[]{:S(2)}) collective-permute-start(bf16[128,1024]{1,0:T(8,128)(2,1)S(1)} %get-tuple-element.23), channel_id=1, source_target_pairs={{0,2},{1,3},{2,0},{3,1},{4,6},{5,7},{6,4},{7,5},{8,10},{9,11},{10,... | collective-permute-start | bytes 786440 | tf_op jit(solution)/shard_map/ppermute | solution.py:192
  23.9 11.4 %collective-permute-start.3 = (bf16[128,1024]{1,0:T(8,128)(2,1)S(1)}, bf16[128,1024]{1,0:T(8,128)(2,1)S(1)}, u32[]{:S(2)}, u32[]{:S(2)}) collective-permute-start(bf16[128,1024]{1,0:T(8,128)(2,1)S(1)} %get-tuple-element.24), channel_id=1, source_target_pairs={{0,3},{1,2},{2,1},{3,0},{4,7},{5,6},{6,5},{7,4},{8,11},{9,10},{10,... | collective-permute-start | bytes 786440 | tf_op jit(solution)/shard_map/ppermute | solution.py:192
  35.8 20.7 %collective-permute-start.10 = (bf16[512,512]{1,0:T(8,128)(2,1)S(1)}, bf16[512,512]{1,0:T(8,128)(2,1)S(1)}, u32[]{:S(2)}, u32[]{:S(2)}) collective-permute-start(bf16[512,512]{1,0:T(8,128)(2,1)S(1)} %gradient.7), channel_id=1, source_target_pairs={{0,4},{1,5},{2,6},{3,7},{4,0},{5,1},{6,2},{7,3},{8,12},{9,13},{10,... | collective-permute-start | bytes 1572872 | tf_op jit(solution)/shard_map/ppermute | solution.py:189
  36.8 19.7 %copy-start.2 = (f32[512,512]{1,0:T(8,128)S(1)}, f32[512,512]{1,0:T(8,128)}, u32[]{:S(2)}) copy-start(f32[512,512]{1,0:T(8,128)} %refs_2_.1) | copy-start | bytes 3145732
  36.9 19.6 %collective-permute-start.11 = (bf16[512,512]{1,0:T(8,128)(2,1)S(1)}, bf16[512,512]{1,0:T(8,128)(2,1)S(1)}, u32[]{:S(2)}, u32[]{:S(2)}) collective-permute-start(bf16[512,512]{1,0:T(8,128)(2,1)S(1)} %gradient.5.refs_1_), channel_id=1, source_target_pairs={{0,8},{1,9},{2,10},{3,11},{4,12},{5,13},{6,14},{7,15},{8,0},{9,1},... | collective-permute-start | bytes 1572872 | tf_op jit(solution)/shard_map/ppermute | solution.py:189
  39.6 5.0 %collective-permute-start.7 = (bf16[128,512]{1,0:T(8,128)(2,1)S(1)}, bf16[128,512]{1,0:T(8,128)(2,1)S(1)}, u32[]{:S(2)}, u32[]{:S(2)}) collective-permute-start(bf16[128,512]{1,0:T(8,128)(2,1)S(1)} %get-tuple-element.29), channel_id=1, source_target_pairs={{0,1},{1,0},{2,3},{3,2},{4,5},{5,4},{6,7},{7,6},{8,9},{9,8},{10,11... | collective-permute-start | bytes 393224 | tf_op jit(solution)/shard_map/ppermute | solution.py:192
  40.2 5.0 %collective-permute-start.8 = (bf16[128,512]{1,0:T(8,128)(2,1)S(1)}, bf16[128,512]{1,0:T(8,128)(2,1)S(1)}, u32[]{:S(2)}, u32[]{:S(2)}) collective-permute-start(bf16[128,512]{1,0:T(8,128)(2,1)S(1)} %get-tuple-element.30), channel_id=1, source_target_pairs={{0,2},{1,3},{2,0},{3,1},{4,6},{5,7},{6,4},{7,5},{8,10},{9,11},{10,... | collective-permute-start | bytes 393224 | tf_op jit(solution)/shard_map/ppermute | solution.py:192
  41.7 5.9 %collective-permute-start.9 = (bf16[128,512]{1,0:T(8,128)(2,1)S(1)}, bf16[128,512]{1,0:T(8,128)(2,1)S(1)}, u32[]{:S(2)}, u32[]{:S(2)}) collective-permute-start(bf16[128,512]{1,0:T(8,128)(2,1)S(1)} %get-tuple-element.31), channel_id=1, source_target_pairs={{0,3},{1,2},{2,1},{3,0},{4,7},{5,6},{6,5},{7,4},{8,11},{9,10},{10,... | collective-permute-start | bytes 393224 | tf_op jit(solution)/shard_map/ppermute | solution.py:192
  57.1 2.0 %collective-permute-start.12 = (f32[256,512]{1,0:T(8,128)S(1)}, f32[256,512]{1,0:T(8,128)S(1)}, u32[]{:S(2)}, u32[]{:S(2)}) collective-permute-start(f32[256,512]{1,0:T(8,128)S(1)} %drift.1), channel_id=1, source_target_pairs={{0,16},{16,0},{1,17},{17,1},{2,18},{18,2},{3,19},{19,3},{4,20},{20... | collective-permute-start | bytes 1572872 | tf_op jit(solution)/shard_map/ppermute | solution.py:198
  59.2 15.1 %collective-permute-start.16 = (bf16[256,512]{1,0:T(8,128)(2,1)S(1)}, bf16[256,512]{1,0:T(8,128)(2,1)S(1)}, u32[]{:S(2)}, u32[]{:S(2)}) collective-permute-start(bf16[256,512]{1,0:T(8,128)(2,1)S(1)} %outer.1.refs_8_), channel_id=1, source_target_pairs={{0,8},{1,9},{2,10},{3,11},{4,12},{5,13},{6,14},{7,15},{8,0},{9,1},... | collective-permute-start | bytes 786440 | tf_op jit(solution)/shard_map/ppermute | solution.py:189
  60.8 13.7 %collective-permute-start.14 = (bf16[256,512]{1,0:T(8,128)(2,1)S(1)}, bf16[256,512]{1,0:T(8,128)(2,1)S(1)}, u32[]{:S(2)}, u32[]{:S(2)}) collective-permute-start(bf16[256,512]{1,0:T(8,128)(2,1)S(1)} %outer.1.refs_8_), channel_id=1, source_target_pairs={{0,4},{1,5},{2,6},{3,7},{4,0},{5,1},{6,2},{7,3},{8,12},{9,13},{10,... | collective-permute-start | bytes 786440 | tf_op jit(solution)/shard_map/ppermute | solution.py:189
  74.4 7.6 %collective-permute-start.18 = (bf16[256,512]{1,0:T(8,128)(2,1)S(1)}, bf16[256,512]{1,0:T(8,128)(2,1)S(1)}, u32[]{:S(2)}, u32[]{:S(2)}) collective-permute-start(bf16[256,512]{1,0:T(8,128)(2,1)S(1)} %collective-permute-done.16.refs_12_), channel_id=1, source_target_pairs={{0,4},{1,5},{2,6},{3,7},{4,0},{5,1},{6,2},{7,3},{8,12},{9,13},{10,... | collective-permute-start | bytes 786440 | tf_op jit(solution)/shard_map/ppermute | solution.py:189
  74.4 7.6 %collective-permute-start.13 = (bf16[256,512]{1,0:T(8,128)(2,1)S(1)}, bf16[256,512]{1,0:T(8,128)(2,1)S(1)}, u32[]{:S(2)}, u32[]{:S(2)}) collective-permute-start(bf16[256,512]{1,0:T(8,128)(2,1)S(1)} %outer.1.refs_8_), channel_id=1, source_target_pairs={{0,16},{16,0},{1,17},{17,1},{2,18},{18,2},{3,19},{19,3},{4,20},{20... | collective-permute-start | bytes 786440 | tf_op jit(solution)/shard_map/ppermute | solution.py:198
  74.4 7.5 %collective-permute-start.15 = (bf16[256,512]{1,0:T(8,128)(2,1)S(1)}, bf16[256,512]{1,0:T(8,128)(2,1)S(1)}, u32[]{:S(2)}, u32[]{:S(2)}) collective-permute-start(bf16[256,512]{1,0:T(8,128)(2,1)S(1)} %collective-permute-done.14.refs_10_), channel_id=1, source_target_pairs={{0,16},{16,0},{1,17},{17,1},{2,18},{18,2},{3,19},{19,3},{4,20},{20... | collective-permute-start | bytes 786440 | tf_op jit(solution)/shard_map/ppermute | solution.py:198
  74.9 7.1 %collective-permute-start.17 = (bf16[256,512]{1,0:T(8,128)(2,1)S(1)}, bf16[256,512]{1,0:T(8,128)(2,1)S(1)}, u32[]{:S(2)}, u32[]{:S(2)}) collective-permute-start(bf16[256,512]{1,0:T(8,128)(2,1)S(1)} %collective-permute-done.16.refs_12_), channel_id=1, source_target_pairs={{0,16},{16,0},{1,17},{17,1},{2,18},{18,2},{3,19},{19,3},{4,20},{20... | collective-permute-start | bytes 786440 | tf_op jit(solution)/shard_map/ppermute | solution.py:198
  81.9 1.5 %collective-permute-start.19 = (bf16[256,512]{1,0:T(8,128)(2,1)S(1)}, bf16[256,512]{1,0:T(8,128)(2,1)S(1)}, u32[]{:S(2)}, u32[]{:S(2)}) collective-permute-start(bf16[256,512]{1,0:T(8,128)(2,1)S(1)} %collective-permute-done.18.refs_5_), channel_id=1, source_target_pairs={{0,16},{16,0},{1,17},{17,1},{2,18},{18,2},{3,19},{19,3},{4,20},{20... | collective-permute-start | bytes 786440 | tf_op jit(solution)/shard_map/ppermute | solution.py:198
  83.9 6.2 %collective-permute-start.20 = (bf16[128,512]{1,0:T(8,128)(2,1)S(1)}, bf16[128,512]{1,0:T(8,128)(2,1)S(1)}, u32[]{:S(2)}, u32[]{:S(2)}) collective-permute-start(bf16[128,512]{1,0:T(8,128)(2,1)S(1)} %get-tuple-element.35), channel_id=1, source_target_pairs={{0,1},{1,0},{2,3},{3,2},{4,5},{5,4},{6,7},{7,6},{8,9},{9,8},{10,11... | collective-permute-start | bytes 393224 | tf_op jit(solution)/shard_map/ppermute | solution.py:192
  86.2 8.1 %collective-permute-start.21 = (bf16[128,512]{1,0:T(8,128)(2,1)S(1)}, bf16[128,512]{1,0:T(8,128)(2,1)S(1)}, u32[]{:S(2)}, u32[]{:S(2)}) collective-permute-start(bf16[128,512]{1,0:T(8,128)(2,1)S(1)} %get-tuple-element.36), channel_id=1, source_target_pairs={{0,2},{1,3},{2,0},{3,1},{4,6},{5,7},{6,4},{7,5},{8,10},{9,11},{10,... | collective-permute-start | bytes 393224 | tf_op jit(solution)/shard_map/ppermute | solution.py:192
  87.9 6.3 %collective-permute-start.22 = (bf16[128,512]{1,0:T(8,128)(2,1)S(1)}, bf16[128,512]{1,0:T(8,128)(2,1)S(1)}, u32[]{:S(2)}, u32[]{:S(2)}) collective-permute-start(bf16[128,512]{1,0:T(8,128)(2,1)S(1)} %get-tuple-element.37), channel_id=1, source_target_pairs={{0,3},{1,2},{2,1},{3,0},{4,7},{5,6},{6,5},{7,4},{8,11},{9,10},{10,... | collective-permute-start | bytes 393224 | tf_op jit(solution)/shard_map/ppermute | solution.py:192
  (7 other events, 82.1 us)

commit v16 on v15

--- a/solution.py
+++ b/solution.py
@@ -17,6 +17,7 @@
 PLANES = 4
 CHUNK = 32
 CONTRACT_ROWS = (((0,), (0,)), ((), ()))
+AHEAD_FLOPS = 10**10
 VMEM_BYTES = 16 * 1024 * 1024
 
 
@@ -208,13 +209,12 @@
     full = jax.ShapeDtypeStruct((rows, width), jnp.float32)
     sent = jax.ShapeDtypeStruct((rows, width), jnp.bfloat16)
 
-    def gradient(message, at, out, arrived=()):
+    def gradient(message, at, out, arrived=(), flops=2 * inner * tokens * rows * width):
         kernel = partial(gradient_kernel, inner, rows, at)
-        flops = 2 * inner * tokens * rows * width
         return call(kernel, "gradient", [out], message + first + list(arrived), flops)[0]
 
     beside_far = planes(gradient(first, 0, sent), 1)
-    beside = planes(gradient(second, rows, sent), 1)
+    beside = planes(gradient(second, rows, sent, flops=AHEAD_FLOPS), 1)
     for_far = gradient(second, 0, sent, [beside_far])
     far = planes(for_far, 2)
     last = around(pack((0,), [for_far]))

time: 95.1 us -> 96.4 us (1.014)
  waiting for transfers between devices: 58.1 us -> 61.4 us
  starting transfers between devices: 27 us -> 24.9 us
    ppermute x6, waiting for transfers between devices: 24.7 us -> 33 us  [planes(): lax.ppermute(x, 'fsdp', [(p * inner + i, (p ^ bits) * inner + i) for p in...]
    ppermute x12, waiting for transfers between devices: 32.6 us -> 27.7 us  [across(): lax.ppermute(x, 'fsdp', [(p * inner + i, p * inner + (i ^ k)) for p in ra...]
    ppermute x6, starting transfers between devices: 10.8 us -> 9.04 us  [planes(): lax.ppermute(x, 'fsdp', [(p * inner + i, (p ^ bits) * inner + i) for p in...]
  transfers between devices with their start and end apart: 23 -> 23, of which waited for: 15 -> 18; matrix products, arithmetic and copies ran while one was open for 0% -> 0% of each run, Pallas kernels for 4% -> 5%
where the time goes in v16:
time: 96.4 us; the launch traced here: 96.3 us
  waiting for transfers between devices  61.4 us (64%)
  starting transfers between devices  24.9 us (26%)
  Pallas kernels  6.55 us (7%)
  local copies, waits for them, and re-layouts  2.53 us (3%)
    ppermute x6, waiting for transfers between devices, planes(): lax.ppermute(x, 'fsdp', [(p * inner + i, (p ^ bits) * inner + i) for p in...  33 us
    ppermute x12, waiting for transfers between devices, across(): lax.ppermute(x, 'fsdp', [(p * inner + i, p * inner + (i ^ k)) for p in ra...  27.7 us
    ppermute x12, starting transfers between devices, across(): lax.ppermute(x, 'fsdp', [(p * inner + i, p * inner + (i ^ k)) for p in ra...  15.3 us
    ppermute x6, starting transfers between devices, planes(): lax.ppermute(x, 'fsdp', [(p * inner + i, (p ^ bits) * inner + i) for p in...  9.04 us
    pallas_call x13, Pallas kernels, call(): pl.pallas_call(without_after, out_shape=out, in_specs=[pl.BlockSpec(memor...  6.55 us
    unnamed x16, local copies, waits for them, and re-layouts  2.53 us
  transfers between devices with their start and end apart: 23, of which 18 were waited for; matrix products, arithmetic and copies ran while one was open for 0% of the time, Pallas kernels for 5%

profile of v16, /device:TPU:0, one launch (start us, length us, event | category | flops | bytes accessed | tf_op | source)
XLA Modules:
  0.0 96.3 jit_solution(10841035461868924664)
XLA Ops:
  0.6 1.6 %copy-done = bf16[1,128,8192]{2,1,0:T(8,128)(2,1)S(1)} copy-done((bf16[1,128,8192]{2,1,0:T(8,128)(2,1)S(1)}, bf16[1,128,8192]{2,1,0:T(8,128)(2,1)}, u32[]{:S(2)}) %copy-start) | copy-done | bytes 2097176
  3.2 3.0 %collective-permute-start = (bf16[128,1024]{1,0:T(8,128)(2,1)S(1)}, bf16[128,1024]{1,0:T(8,128)(2,1)S(1)}, u32[]{:S(2)}, u32[]{:S(2)}) collective-permute-start(bf16[128,1024]{1,0:T(8,128)(2,1)S(1)} %get-tuple-element.20), channel_id=1, source_target_pairs={{0,1},{1,0},{2,3},{3,2},{4,5},{5,4},{6,7},{7,6},{8,9},{9,8},{10,11... | collective-permute-start | bytes 786440 | tf_op jit(solution)/shard_map/ppermute | solution.py:193
  6.2 1.5 %collective-permute-start.4 = (bf16[128,1024]{1,0:T(8,128)(2,1)S(1)}, bf16[128,1024]{1,0:T(8,128)(2,1)S(1)}, u32[]{:S(2)}, u32[]{:S(2)}) collective-permute-start(bf16[128,1024]{1,0:T(8,128)(2,1)S(1)} %get-tuple-element.26), channel_id=1, source_target_pairs={{0,2},{1,3},{2,0},{3,1},{4,6},{5,7},{6,4},{7,5},{8,10},{9,11},{10,... | collective-permute-start | bytes 786440 | tf_op jit(solution)/shard_map/ppermute | solution.py:193
  7.8 5.6 %collective-permute-done.refs_1_.refs_5_.refs_2_ = bf16[128,1024]{1,0:T(8,128)(2,1)S(1)} collective-permute-done((bf16[128,1024]{1,0:T(8,128)(2,1)S(1)}, bf16[128,1024]{1,0:T(8,128)(2,1)S(1)}, u32[]{:S(2)}, u32[]{:S(2)}) %collective-permute-start) | collective-permute-done | bytes 262176 | tf_op jit(solution)/shard_map/ppermute | solution.py:193
  13.4 2.1 %collective-permute-start.1 = (bf16[128,1024]{1,0:T(8,128)(2,1)S(1)}, bf16[128,1024]{1,0:T(8,128)(2,1)S(1)}, u32[]{:S(2)}, u32[]{:S(2)}) collective-permute-start(bf16[128,1024]{1,0:T(8,128)(2,1)S(1)} %get-tuple-element.22), channel_id=1, source_target_pairs={{0,1},{1,0},{2,3},{3,2},{4,5},{5,4},{6,7},{7,6},{8,9},{9,8},{10,11... | collective-permute-start | bytes 786440 | tf_op jit(solution)/shard_map/ppermute | solution.py:193
  15.6 1.5 %collective-permute-start.2 = (bf16[128,1024]{1,0:T(8,128)(2,1)S(1)}, bf16[128,1024]{1,0:T(8,128)(2,1)S(1)}, u32[]{:S(2)}, u32[]{:S(2)}) collective-permute-start(bf16[128,1024]{1,0:T(8,128)(2,1)S(1)} %get-tuple-element.23), channel_id=1, source_target_pairs={{0,2},{1,3},{2,0},{3,1},{4,6},{5,7},{6,4},{7,5},{8,10},{9,11},{10,... | collective-permute-start | bytes 786440 | tf_op jit(solution)/shard_map/ppermute | solution.py:193
  17.1 2.9 %collective-permute-done.4.refs_2_.refs_6_.refs_3_ = bf16[128,1024]{1,0:T(8,128)(2,1)S(1)} collective-permute-done((bf16[128,1024]{1,0:T(8,128)(2,1)S(1)}, bf16[128,1024]{1,0:T(8,128)(2,1)S(1)}, u32[]{:S(2)}, u32[]{:S(2)}) %collective-permute-start.4) | collective-permute-done | bytes 262176 | tf_op jit(solution)/shard_map/ppermute | solution.py:193
  21.0 1.6 %collective-permute-start.6 = (bf16[512,512]{1,0:T(8,128)(2,1)S(1)}, bf16[512,512]{1,0:T(8,128)(2,1)S(1)}, u32[]{:S(2)}, u32[]{:S(2)}) collective-permute-start(bf16[512,512]{1,0:T(8,128)(2,1)S(1)} %gradient.4), channel_id=1, source_target_pairs={{0,4},{1,5},{2,6},{3,7},{4,0},{5,1},{6,2},{7,3},{8,12},{9,13},{10,... | collective-permute-start | bytes 1572872 | tf_op jit(solution)/shard_map/ppermute | solution.py:190
  22.7 2.0 %collective-permute-done.1.refs_1_.refs_5_ = bf16[128,1024]{1,0:T(8,128)(2,1)S(1)} collective-permute-done((bf16[128,1024]{1,0:T(8,128)(2,1)S(1)}, bf16[128,1024]{1,0:T(8,128)(2,1)S(1)}, u32[]{:S(2)}, u32[]{:S(2)}) %collective-permute-start.1) | collective-permute-done | bytes 262176 | tf_op jit(solution)/shard_map/ppermute | solution.py:193
  24.6 6.2 %collective-permute-done.2.refs_2_.refs_6_ = bf16[128,1024]{1,0:T(8,128)(2,1)S(1)} collective-permute-done((bf16[128,1024]{1,0:T(8,128)(2,1)S(1)}, bf16[128,1024]{1,0:T(8,128)(2,1)S(1)}, u32[]{:S(2)}, u32[]{:S(2)}) %collective-permute-start.2) | collective-permute-done | bytes 262176 | tf_op jit(solution)/shard_map/ppermute | solution.py:193
  31.3 1.6 %collective-permute-start.10 = (bf16[512,512]{1,0:T(8,128)(2,1)S(1)}, bf16[512,512]{1,0:T(8,128)(2,1)S(1)}, u32[]{:S(2)}, u32[]{:S(2)}) collective-permute-start(bf16[512,512]{1,0:T(8,128)(2,1)S(1)} %gradient.7), channel_id=1, source_target_pairs={{0,4},{1,5},{2,6},{3,7},{4,0},{5,1},{6,2},{7,3},{8,12},{9,13},{10,... | collective-permute-start | bytes 1572872 | tf_op jit(solution)/shard_map/ppermute | solution.py:190
  33.5 2.7 %collective-permute-start.11 = (bf16[512,512]{1,0:T(8,128)(2,1)S(1)}, bf16[512,512]{1,0:T(8,128)(2,1)S(1)}, u32[]{:S(2)}, u32[]{:S(2)}) collective-permute-start(bf16[512,512]{1,0:T(8,128)(2,1)S(1)} %gradient.5.refs_1_), channel_id=1, source_target_pairs={{0,8},{1,9},{2,10},{3,11},{4,12},{5,13},{6,14},{7,15},{8,0},{9,1},... | collective-permute-start | bytes 1572872 | tf_op jit(solution)/shard_map/ppermute | solution.py:190
  39.8 2.5 %collective-permute-done.7.refs_1_ = bf16[128,512]{1,0:T(8,128)(2,1)S(1)} collective-permute-done((bf16[128,512]{1,0:T(8,128)(2,1)S(1)}, bf16[128,512]{1,0:T(8,128)(2,1)S(1)}, u32[]{:S(2)}, u32[]{:S(2)}) %collective-permute-start.7) | collective-permute-done | bytes 131104 | tf_op jit(solution)/shard_map/ppermute | solution.py:193
  42.6 1.6 %collective-permute-done.9.refs_3_ = bf16[128,512]{1,0:T(8,128)(2,1)S(1)} collective-permute-done((bf16[128,512]{1,0:T(8,128)(2,1)S(1)}, bf16[128,512]{1,0:T(8,128)(2,1)S(1)}, u32[]{:S(2)}, u32[]{:S(2)}) %collective-permute-start.9) | collective-permute-done | bytes 131104 | tf_op jit(solution)/shard_map/ppermute | solution.py:193
  44.7 9.9 %collective-permute-done.10.refs_1_ = bf16[512,512]{1,0:T(8,128)(2,1)S(1)} collective-permute-done((bf16[512,512]{1,0:T(8,128)(2,1)S(1)}, bf16[512,512]{1,0:T(8,128)(2,1)S(1)}, u32[]{:S(2)}, u32[]{:S(2)}) %collective-permute-start.10) | collective-permute-done | bytes 524320 | tf_op jit(solution)/shard_map/ppermute | solution.py:190
  54.5 3.5 %collective-permute-done.11.refs_2_ = bf16[512,512]{1,0:T(8,128)(2,1)S(1)} collective-permute-done((bf16[512,512]{1,0:T(8,128)(2,1)S(1)}, bf16[512,512]{1,0:T(8,128)(2,1)S(1)}, u32[]{:S(2)}, u32[]{:S(2)}) %collective-permute-start.11) | collective-permute-done | bytes 524320 | tf_op jit(solution)/shard_map/ppermute | solution.py:190
  58.7 1.7 %update.1 = (f32[512,512]{1,0:T(8,128)}, f32[256,512]{1,0:T(8,128)S(1)}) custom-call(f32[512,512]{1,0:T(8,128)S(1)} %gradient.6.refs_0_, bf16[512,512]{1,0:T(8,128)(2,1)S(1)} %collective-permute-done.10.refs_1_, bf16[512,512]{1,0:T(8,128)(2,1)S(1)} %collective-permute-done.11.refs_2_, f32[512,512]{1,0:T(8,128)S(1)} %bitcast.11, f32[512,512]{1,0:T(8,128)S(1)} %bitcast.13, ...), custom_call_target="tpu_custom_call" | custom-call | bytes 7864320 | tf_op jit(solution)/shard_map/update/pallas_call | solution.py:61
  60.9 3.0 %collective-permute-start.14 = (bf16[256,512]{1,0:T(8,128)(2,1)S(1)}, bf16[256,512]{1,0:T(8,128)(2,1)S(1)}, u32[]{:S(2)}, u32[]{:S(2)}) collective-permute-start(bf16[256,512]{1,0:T(8,128)(2,1)S(1)} %outer.1.refs_8_), channel_id=1, source_target_pairs={{0,4},{1,5},{2,6},{3,7},{4,0},{5,1},{6,2},{7,3},{8,12},{9,13},{10,... | collective-permute-start | bytes 786440 | tf_op jit(solution)/shard_map/ppermute | solution.py:190
  63.9 11.9 %collective-permute-done.16.refs_12_ = bf16[256,512]{1,0:T(8,128)(2,1)S(1)} collective-permute-done((bf16[256,512]{1,0:T(8,128)(2,1)S(1)}, bf16[256,512]{1,0:T(8,128)(2,1)S(1)}, u32[]{:S(2)}, u32[]{:S(2)}) %collective-permute-start.16) | collective-permute-done | bytes 262176 | tf_op jit(solution)/shard_map/ppermute | solution.py:190
  76.5 7.5 %collective-permute-done.18.refs_5_ = bf16[256,512]{1,0:T(8,128)(2,1)S(1)} collective-permute-done((bf16[256,512]{1,0:T(8,128)(2,1)S(1)}, bf16[256,512]{1,0:T(8,128)(2,1)S(1)}, u32[]{:S(2)}, u32[]{:S(2)}) %collective-permute-start.18) | collective-permute-done | bytes 262176 | tf_op jit(solution)/shard_map/ppermute | solution.py:190
  86.0 1.5 %collective-permute-start.20 = (bf16[128,512]{1,0:T(8,128)(2,1)S(1)}, bf16[128,512]{1,0:T(8,128)(2,1)S(1)}, u32[]{:S(2)}, u32[]{:S(2)}) collective-permute-start(bf16[128,512]{1,0:T(8,128)(2,1)S(1)} %get-tuple-element.35), channel_id=1, source_target_pairs={{0,1},{1,0},{2,3},{3,2},{4,5},{5,4},{6,7},{7,6},{8,9},{9,8},{10,11... | collective-permute-start | bytes 393224 | tf_op jit(solution)/shard_map/ppermute | solution.py:193
  89.5 2.4 %collective-permute-done.20.refs_1_ = bf16[128,512]{1,0:T(8,128)(2,1)S(1)} collective-permute-done((bf16[128,512]{1,0:T(8,128)(2,1)S(1)}, bf16[128,512]{1,0:T(8,128)(2,1)S(1)}, u32[]{:S(2)}, u32[]{:S(2)}) %collective-permute-start.20) | collective-permute-done | bytes 131104 | tf_op jit(solution)/shard_map/ppermute | solution.py:193
  91.9 1.8 %collective-permute-done.21.refs_2_ = bf16[128,512]{1,0:T(8,128)(2,1)S(1)} collective-permute-done((bf16[128,512]{1,0:T(8,128)(2,1)S(1)}, bf16[128,512]{1,0:T(8,128)(2,1)S(1)}, u32[]{:S(2)}, u32[]{:S(2)}) %collective-permute-start.21) | collective-permute-done | bytes 131104 | tf_op jit(solution)/shard_map/ppermute | solution.py:193
  93.7 1.8 %collective-permute-done.22.refs_3_ = bf16[128,512]{1,0:T(8,128)(2,1)S(1)} collective-permute-done((bf16[128,512]{1,0:T(8,128)(2,1)S(1)}, bf16[128,512]{1,0:T(8,128)(2,1)S(1)}, u32[]{:S(2)}, u32[]{:S(2)}) %collective-permute-start.22) | collective-permute-done | bytes 131104 | tf_op jit(solution)/shard_map/ppermute | solution.py:193
  (51 shorter events, 14.0 us)
Async XLA Ops:
  3.2 10.1 %collective-permute-start = (bf16[128,1024]{1,0:T(8,128)(2,1)S(1)}, bf16[128,1024]{1,0:T(8,128)(2,1)S(1)}, u32[]{:S(2)}, u32[]{:S(2)}) collective-permute-start(bf16[128,1024]{1,0:T(8,128)(2,1)S(1)} %get-tuple-element.20), channel_id=1, source_target_pairs={{0,1},{1,0},{2,3},{3,2},{4,5},{5,4},{6,7},{7,6},{8,9},{9,8},{10,11... | collective-permute-start | bytes 786440 | tf_op jit(solution)/shard_map/ppermute | solution.py:193
  6.2 13.8 %collective-permute-start.4 = (bf16[128,1024]{1,0:T(8,128)(2,1)S(1)}, bf16[128,1024]{1,0:T(8,128)(2,1)S(1)}, u32[]{:S(2)}, u32[]{:S(2)}) collective-permute-start(bf16[128,1024]{1,0:T(8,128)(2,1)S(1)} %get-tuple-element.26), channel_id=1, source_target_pairs={{0,2},{1,3},{2,0},{3,1},{4,6},{5,7},{6,4},{7,5},{8,10},{9,11},{10,... | collective-permute-start | bytes 786440 | tf_op jit(solution)/shard_map/ppermute | solution.py:193
  7.7 12.8 %collective-permute-start.5 = (bf16[128,1024]{1,0:T(8,128)(2,1)S(1)}, bf16[128,1024]{1,0:T(8,128)(2,1)S(1)}, u32[]{:S(2)}, u32[]{:S(2)}) collective-permute-start(bf16[128,1024]{1,0:T(8,128)(2,1)S(1)} %get-tuple-element.27), channel_id=1, source_target_pairs={{0,3},{1,2},{2,1},{3,0},{4,7},{5,6},{6,5},{7,4},{8,11},{9,10},{10,... | collective-permute-start | bytes 786440 | tf_op jit(solution)/shard_map/ppermute | solution.py:193
  13.4 11.2 %collective-permute-start.1 = (bf16[128,1024]{1,0:T(8,128)(2,1)S(1)}, bf16[128,1024]{1,0:T(8,128)(2,1)S(1)}, u32[]{:S(2)}, u32[]{:S(2)}) collective-permute-start(bf16[128,1024]{1,0:T(8,128)(2,1)S(1)} %get-tuple-element.22), channel_id=1, source_target_pairs={{0,1},{1,0},{2,3},{3,2},{4,5},{5,4},{6,7},{7,6},{8,9},{9,8},{10,11... | collective-permute-start | bytes 786440 | tf_op jit(solution)/shard_map/ppermute | solution.py:193
  15.6 15.3 %collective-permute-start.2 = (bf16[128,1024]{1,0:T(8,128)(2,1)S(1)}, bf16[128,1024]{1,0:T(8,128)(2,1)S(1)}, u32[]{:S(2)}, u32[]{:S(2)}) collective-permute-start(bf16[128,1024]{1,0:T(8,128)(2,1)S(1)} %get-tuple-element.23), channel_id=1, source_target_pairs={{0,2},{1,3},{2,0},{3,1},{4,6},{5,7},{6,4},{7,5},{8,10},{9,11},{10,... | collective-permute-start | bytes 786440 | tf_op jit(solution)/shard_map/ppermute | solution.py:193
  17.1 13.8 %collective-permute-start.3 = (bf16[128,1024]{1,0:T(8,128)(2,1)S(1)}, bf16[128,1024]{1,0:T(8,128)(2,1)S(1)}, u32[]{:S(2)}, u32[]{:S(2)}) collective-permute-start(bf16[128,1024]{1,0:T(8,128)(2,1)S(1)} %get-tuple-element.24), channel_id=1, source_target_pairs={{0,3},{1,2},{2,1},{3,0},{4,7},{5,6},{6,5},{7,4},{8,11},{9,10},{10,... | collective-permute-start | bytes 786440 | tf_op jit(solution)/shard_map/ppermute | solution.py:193
  21.0 12.0 %collective-permute-start.6 = (bf16[512,512]{1,0:T(8,128)(2,1)S(1)}, bf16[512,512]{1,0:T(8,128)(2,1)S(1)}, u32[]{:S(2)}, u32[]{:S(2)}) collective-permute-start(bf16[512,512]{1,0:T(8,128)(2,1)S(1)} %gradient.4), channel_id=1, source_target_pairs={{0,4},{1,5},{2,6},{3,7},{4,0},{5,1},{6,2},{7,3},{8,12},{9,13},{10,... | collective-permute-start | bytes 1572872 | tf_op jit(solution)/shard_map/ppermute | solution.py:190
  31.3 23.2 %collective-permute-start.10 = (bf16[512,512]{1,0:T(8,128)(2,1)S(1)}, bf16[512,512]{1,0:T(8,128)(2,1)S(1)}, u32[]{:S(2)}, u32[]{:S(2)}) collective-permute-start(bf16[512,512]{1,0:T(8,128)(2,1)S(1)} %gradient.7), channel_id=1, source_target_pairs={{0,4},{1,5},{2,6},{3,7},{4,0},{5,1},{6,2},{7,3},{8,12},{9,13},{10,... | collective-permute-start | bytes 1572872 | tf_op jit(solution)/shard_map/ppermute | solution.py:190
  33.5 24.6 %copy-start.2 = (f32[512,512]{1,0:T(8,128)S(1)}, f32[512,512]{1,0:T(8,128)}, u32[]{:S(2)}) copy-start(f32[512,512]{1,0:T(8,128)} %refs_2_.1) | copy-start | bytes 3145732
  33.5 24.6 %collective-permute-start.11 = (bf16[512,512]{1,0:T(8,128)(2,1)S(1)}, bf16[512,512]{1,0:T(8,128)(2,1)S(1)}, u32[]{:S(2)}, u32[]{:S(2)}) collective-permute-start(bf16[512,512]{1,0:T(8,128)(2,1)S(1)} %gradient.5.refs_1_), channel_id=1, source_target_pairs={{0,8},{1,9},{2,10},{3,11},{4,12},{5,13},{6,14},{7,15},{8,0},{9,1},... | collective-permute-start | bytes 1572872 | tf_op jit(solution)/shard_map/ppermute | solution.py:190
  36.2 6.1 %collective-permute-start.7 = (bf16[128,512]{1,0:T(8,128)(2,1)S(1)}, bf16[128,512]{1,0:T(8,128)(2,1)S(1)}, u32[]{:S(2)}, u32[]{:S(2)}) collective-permute-start(bf16[128,512]{1,0:T(8,128)(2,1)S(1)} %get-tuple-element.29), channel_id=1, source_target_pairs={{0,1},{1,0},{2,3},{3,2},{4,5},{5,4},{6,7},{7,6},{8,9},{9,8},{10,11... | collective-permute-start | bytes 393224 | tf_op jit(solution)/shard_map/ppermute | solution.py:193
  37.5 5.1 %collective-permute-start.8 = (bf16[128,512]{1,0:T(8,128)(2,1)S(1)}, bf16[128,512]{1,0:T(8,128)(2,1)S(1)}, u32[]{:S(2)}, u32[]{:S(2)}) collective-permute-start(bf16[128,512]{1,0:T(8,128)(2,1)S(1)} %get-tuple-element.30), channel_id=1, source_target_pairs={{0,2},{1,3},{2,0},{3,1},{4,6},{5,7},{6,4},{7,5},{8,10},{9,11},{10,... | collective-permute-start | bytes 393224 | tf_op jit(solution)/shard_map/ppermute | solution.py:193
  38.3 5.9 %collective-permute-start.9 = (bf16[128,512]{1,0:T(8,128)(2,1)S(1)}, bf16[128,512]{1,0:T(8,128)(2,1)S(1)}, u32[]{:S(2)}, u32[]{:S(2)}) collective-permute-start(bf16[128,512]{1,0:T(8,128)(2,1)S(1)} %get-tuple-element.31), channel_id=1, source_target_pairs={{0,3},{1,2},{2,1},{3,0},{4,7},{5,6},{6,5},{7,4},{8,11},{9,10},{10,... | collective-permute-start | bytes 393224 | tf_op jit(solution)/shard_map/ppermute | solution.py:193
  58.7 2.0 %collective-permute-start.12 = (f32[256,512]{1,0:T(8,128)S(1)}, f32[256,512]{1,0:T(8,128)S(1)}, u32[]{:S(2)}, u32[]{:S(2)}) collective-permute-start(f32[256,512]{1,0:T(8,128)S(1)} %drift.1), channel_id=1, source_target_pairs={{0,16},{16,0},{1,17},{17,1},{2,18},{18,2},{3,19},{19,3},{4,20},{20... | collective-permute-start | bytes 1572872 | tf_op jit(solution)/shard_map/ppermute | solution.py:199
  60.8 15.0 %collective-permute-start.16 = (bf16[256,512]{1,0:T(8,128)(2,1)S(1)}, bf16[256,512]{1,0:T(8,128)(2,1)S(1)}, u32[]{:S(2)}, u32[]{:S(2)}) collective-permute-start(bf16[256,512]{1,0:T(8,128)(2,1)S(1)} %outer.1.refs_8_), channel_id=1, source_target_pairs={{0,8},{1,9},{2,10},{3,11},{4,12},{5,13},{6,14},{7,15},{8,0},{9,1},... | collective-permute-start | bytes 786440 | tf_op jit(solution)/shard_map/ppermute | solution.py:190
  60.9 15.1 %collective-permute-start.14 = (bf16[256,512]{1,0:T(8,128)(2,1)S(1)}, bf16[256,512]{1,0:T(8,128)(2,1)S(1)}, u32[]{:S(2)}, u32[]{:S(2)}) collective-permute-start(bf16[256,512]{1,0:T(8,128)(2,1)S(1)} %outer.1.refs_8_), channel_id=1, source_target_pairs={{0,4},{1,5},{2,6},{3,7},{4,0},{5,1},{6,2},{7,3},{8,12},{9,13},{10,... | collective-permute-start | bytes 786440 | tf_op jit(solution)/shard_map/ppermute | solution.py:190
  75.8 8.2 %collective-permute-start.18 = (bf16[256,512]{1,0:T(8,128)(2,1)S(1)}, bf16[256,512]{1,0:T(8,128)(2,1)S(1)}, u32[]{:S(2)}, u32[]{:S(2)}) collective-permute-start(bf16[256,512]{1,0:T(8,128)(2,1)S(1)} %collective-permute-done.16.refs_12_), channel_id=1, source_target_pairs={{0,4},{1,5},{2,6},{3,7},{4,0},{5,1},{6,2},{7,3},{8,12},{9,13},{10,... | collective-permute-start | bytes 786440 | tf_op jit(solution)/shard_map/ppermute | solution.py:190
  75.8 8.2 %collective-permute-start.13 = (bf16[256,512]{1,0:T(8,128)(2,1)S(1)}, bf16[256,512]{1,0:T(8,128)(2,1)S(1)}, u32[]{:S(2)}, u32[]{:S(2)}) collective-permute-start(bf16[256,512]{1,0:T(8,128)(2,1)S(1)} %outer.1.refs_8_), channel_id=1, source_target_pairs={{0,16},{16,0},{1,17},{17,1},{2,18},{18,2},{3,19},{19,3},{4,20},{20... | collective-permute-start | bytes 786440 | tf_op jit(solution)/shard_map/ppermute | solution.py:199
  75.9 8.0 %collective-permute-start.15 = (bf16[256,512]{1,0:T(8,128)(2,1)S(1)}, bf16[256,512]{1,0:T(8,128)(2,1)S(1)}, u32[]{:S(2)}, u32[]{:S(2)}) collective-permute-start(bf16[256,512]{1,0:T(8,128)(2,1)S(1)} %collective-permute-done.14.refs_10_), channel_id=1, source_target_pairs={{0,16},{16,0},{1,17},{17,1},{2,18},{18,2},{3,19},{19,3},{4,20},{20... | collective-permute-start | bytes 786440 | tf_op jit(solution)/shard_map/ppermute | solution.py:199
  76.3 7.7 %collective-permute-start.17 = (bf16[256,512]{1,0:T(8,128)(2,1)S(1)}, bf16[256,512]{1,0:T(8,128)(2,1)S(1)}, u32[]{:S(2)}, u32[]{:S(2)}) collective-permute-start(bf16[256,512]{1,0:T(8,128)(2,1)S(1)} %collective-permute-done.16.refs_12_), channel_id=1, source_target_pairs={{0,16},{16,0},{1,17},{17,1},{2,18},{18,2},{3,19},{19,3},{4,20},{20... | collective-permute-start | bytes 786440 | tf_op jit(solution)/shard_map/ppermute | solution.py:199
  84.0 1.5 %collective-permute-start.19 = (bf16[256,512]{1,0:T(8,128)(2,1)S(1)}, bf16[256,512]{1,0:T(8,128)(2,1)S(1)}, u32[]{:S(2)}, u32[]{:S(2)}) collective-permute-start(bf16[256,512]{1,0:T(8,128)(2,1)S(1)} %collective-permute-done.18.refs_5_), channel_id=1, source_target_pairs={{0,16},{16,0},{1,17},{17,1},{2,18},{18,2},{3,19},{19,3},{4,20},{20... | collective-permute-start | bytes 786440 | tf_op jit(solution)/shard_map/ppermute | solution.py:199
  86.0 6.0 %collective-permute-start.20 = (bf16[128,512]{1,0:T(8,128)(2,1)S(1)}, bf16[128,512]{1,0:T(8,128)(2,1)S(1)}, u32[]{:S(2)}, u32[]{:S(2)}) collective-permute-start(bf16[128,512]{1,0:T(8,128)(2,1)S(1)} %get-tuple-element.35), channel_id=1, source_target_pairs={{0,1},{1,0},{2,3},{3,2},{4,5},{5,4},{6,7},{7,6},{8,9},{9,8},{10,11... | collective-permute-start | bytes 393224 | tf_op jit(solution)/shard_map/ppermute | solution.py:193
  87.5 6.2 %collective-permute-start.21 = (bf16[128,512]{1,0:T(8,128)(2,1)S(1)}, bf16[128,512]{1,0:T(8,128)(2,1)S(1)}, u32[]{:S(2)}, u32[]{:S(2)}) collective-permute-start(bf16[128,512]{1,0:T(8,128)(2,1)S(1)} %get-tuple-element.36), channel_id=1, source_target_pairs={{0,2},{1,3},{2,0},{3,1},{4,6},{5,7},{6,4},{7,5},{8,10},{9,11},{10,... | collective-permute-start | bytes 393224 | tf_op jit(solution)/shard_map/ppermute | solution.py:193
  88.0 7.5 %collective-permute-start.22 = (bf16[128,512]{1,0:T(8,128)(2,1)S(1)}, bf16[128,512]{1,0:T(8,128)(2,1)S(1)}, u32[]{:S(2)}, u32[]{:S(2)}) collective-permute-start(bf16[128,512]{1,0:T(8,128)(2,1)S(1)} %get-tuple-element.37), channel_id=1, source_target_pairs={{0,3},{1,2},{2,1},{3,0},{4,7},{5,6},{6,5},{7,4},{8,11},{9,10},{10,... | collective-permute-start | bytes 393224 | tf_op jit(solution)/shard_map/ppermute | solution.py:193
  (7 other events, 83.2 us)

commit v17 on v15

--- a/solution.py
+++ b/solution.py
@@ -86,19 +86,23 @@
             outs[k][:, slot * rows : (slot + 1) * rows] = acts_ref[:, pl.ds(block_start(inner, rows, bits, k), rows)]
 
 
-def gradient_kernel(inner, rows, acts_at, *refs):
-    acts_refs, cots_refs, arrived, out = refs[:inner], refs[inner : 2 * inner], refs[2 * inner : -1], refs[-1]
+def gradient_kernel(inner, rows, acts_at, arrived, *refs):
+    acts_refs, cots_refs, refs = refs[:inner], refs[inner : 2 * inner], refs[2 * inner :]
     columns = jnp.concatenate([ref[:, acts_at : acts_at + rows] for ref in acts_refs], axis=0)
     cots = jnp.concatenate([ref[:, rows:] for ref in cots_refs], axis=0)
     total = lax.dot_general(columns, cots, CONTRACT_ROWS, preferred_element_type=jnp.float32)
-    for ref in arrived:
+    for ref in refs[:arrived]:
         total += ref[...].astype(jnp.float32)
-    out[...] = total.astype(out.dtype)
+    at = 0
+    for out in refs[arrived:]:
+        out[...] = total[:, at : at + out.shape[1]].astype(out.dtype)
+        at += out.shape[1]
 
 
 def gradient_at(at, refs):
-    total, beside, far = refs
-    return total[at, :] + beside[at, :].astype(jnp.float32) + far[at, :].astype(jnp.float32)
+    total, far, *beside = refs
+    beside = jnp.concatenate([ref[at, :].astype(jnp.float32) for ref in beside], axis=1)
+    return total[at, :] + beside + far[at, :].astype(jnp.float32)
 
 
 def steps(half, which, body):
@@ -109,7 +113,7 @@
 
 
 def drift_kernel(*refs):
-    gradient_refs, (weights, first, second, anchor), drift_ref = refs[:3], refs[3:7], refs[7]
+    gradient_refs, (weights, first, second, anchor), drift_ref = refs[:-5], refs[-5:-1], refs[-1]
 
     def body(here, at):
         gradient = gradient_at(at, gradient_refs)
@@ -120,7 +124,7 @@
 
 
 def update_kernel(*refs):
-    gradient_refs, (weights, first, second, anchor), (first_ref, drift_ref) = refs[:3], refs[3:7], refs[7:]
+    gradient_refs, (weights, first, second, anchor), (first_ref, drift_ref) = refs[:-6], refs[-6:-2], refs[-2:]
     half = drift_ref.shape[0]
     r = lax.axis_index("rep")
 
@@ -180,7 +184,7 @@
 def on_device(acts, value_cots, inner_weights, first_moment, second_moment, anchor, outer_momentum):
     inner = lax.axis_size("fsdp") // PLANES
     rows, width = anchor.shape
-    if inner != 4 or lax.axis_size("rep") != 2 or rows % 256 or width % 128:
+    if inner != 4 or lax.axis_size("rep") != 2 or rows % 256 or width % 256:
         return general(acts, value_cots, inner_weights, first_moment, second_moment, anchor, outer_momentum)
     tokens = acts.shape[1]
     half = rows // 2
@@ -208,17 +212,19 @@
     full = jax.ShapeDtypeStruct((rows, width), jnp.float32)
     sent = jax.ShapeDtypeStruct((rows, width), jnp.bfloat16)
 
-    def gradient(message, at, out, arrived=()):
-        kernel = partial(gradient_kernel, inner, rows, at)
+    def gradient(message, at, out, arrived=(), after=()):
+        kernel = partial(gradient_kernel, inner, rows, at, len(arrived))
         flops = 2 * inner * tokens * rows * width
-        return call(kernel, "gradient", [out], message + first + list(arrived), flops)[0]
-
-    beside_far = planes(gradient(first, 0, sent), 1)
-    beside = planes(gradient(second, rows, sent), 1)
-    for_far = gradient(second, 0, sent, [beside_far])
+        return call(kernel, "gradient", out, message + first + list(arrived), flops, after=after)
+
+    piece = jax.ShapeDtypeStruct((rows, width // 2), jnp.bfloat16)
+    beside_far = planes(gradient(first, 0, [sent])[0], 1)
+    (for_far,) = gradient(second, 0, [sent], [beside_far])
     far = planes(for_far, 2)
-    last = around(pack((0,), [for_far]))
-    known = [gradient(last, 0, full), beside, far, inner_weights[0], first_moment[0], second_moment[0], anchor]
+    for_beside = gradient(second, rows, [piece] * 2, after=[for_far])
+    beside = [planes(x, 1) for x in for_beside]
+    last = around(pack((0,), for_beside[:1]))
+    known = [gradient(last, 0, [full])[0], far, *beside, inner_weights[0], first_moment[0], second_moment[0], anchor]
     half_block = jax.ShapeDtypeStruct((half, width), jnp.float32)
     (drift_out,) = call(drift_kernel, "drift", [half_block], known, 0)
     drift_in = swap(drift_out)

time: 95.1 us -> 98.8 us (1.039)
  waiting for transfers between devices: 58.1 us -> 64.8 us
  starting transfers between devices: 27 us -> 24 us
    ppermute x6 -> x7, waiting for transfers between devices: 24.7 us -> 29.3 us  [planes(): lax.ppermute(x, 'fsdp', [(p * inner + i, (p ^ bits) * inner + i) for p in...]
    ppermute x6 -> x7, starting transfers between devices: 10.8 us -> 7.81 us  [planes(): lax.ppermute(x, 'fsdp', [(p * inner + i, (p ^ bits) * inner + i) for p in...]
    ppermute x12, waiting for transfers between devices: 32.6 us -> 34.7 us  [across(): lax.ppermute(x, 'fsdp', [(p * inner + i, p * inner + (i ^ k)) for p in ra...]
  transfers between devices with their start and end apart: 23 -> 24, of which waited for: 15 -> 17; matrix products, arithmetic and copies ran while one was open for 0% -> 0% of each run, Pallas kernels for 4% -> 4%
where the time goes in v17:
time: 98.8 us; the launch traced here: 98.6 us
  waiting for transfers between devices  64.8 us (66%)
  starting transfers between devices  24 us (24%)
  Pallas kernels  6.56 us (7%)
  local copies, waits for them, and re-layouts  2.52 us (3%)
    ppermute x12, waiting for transfers between devices, across(): lax.ppermute(x, 'fsdp', [(p * inner + i, p * inner + (i ^ k)) for p in ra...  34.7 us
    ppermute x7, waiting for transfers between devices, planes(): lax.ppermute(x, 'fsdp', [(p * inner + i, (p ^ bits) * inner + i) for p in...  29.3 us
    ppermute x12, starting transfers between devices, across(): lax.ppermute(x, 'fsdp', [(p * inner + i, p * inner + (i ^ k)) for p in ra...  15.6 us
    ppermute x7, starting transfers between devices, planes(): lax.ppermute(x, 'fsdp', [(p * inner + i, (p ^ bits) * inner + i) for p in...  7.81 us
    pallas_call x13, Pallas kernels, call(): pl.pallas_call(without_after, out_shape=out, in_specs=[pl.BlockSpec(memor...  6.56 us
    unnamed x16, local copies, waits for them, and re-layouts  2.52 us
  transfers between devices with their start and end apart: 24, of which 17 were waited for; matrix products, arithmetic and copies ran while one was open for 0% of the time, Pallas kernels for 4%

profile of v17, /device:TPU:0, one launch (start us, length us, event | category | flops | bytes accessed | tf_op | source)
XLA Modules:
  0.0 98.6 jit_solution(520889749295976769)
XLA Ops:
  0.6 1.6 %copy-done = bf16[1,128,8192]{2,1,0:T(8,128)(2,1)S(1)} copy-done((bf16[1,128,8192]{2,1,0:T(8,128)(2,1)S(1)}, bf16[1,128,8192]{2,1,0:T(8,128)(2,1)}, u32[]{:S(2)}) %copy-start) | copy-done | bytes 2097176
  3.2 3.0 %collective-permute-start = (bf16[128,1024]{1,0:T(8,128)(2,1)S(1)}, bf16[128,1024]{1,0:T(8,128)(2,1)S(1)}, u32[]{:S(2)}, u32[]{:S(2)}) collective-permute-start(bf16[128,1024]{1,0:T(8,128)(2,1)S(1)} %get-tuple-element.22), channel_id=1, source_target_pairs={{0,1},{1,0},{2,3},{3,2},{4,5},{5,4},{6,7},{7,6},{8,9},{9,8},{10,11... | collective-permute-start | bytes 786440 | tf_op jit(solution)/shard_map/ppermute | solution.py:196
  6.2 1.5 %collective-permute-start.4 = (bf16[128,1024]{1,0:T(8,128)(2,1)S(1)}, bf16[128,1024]{1,0:T(8,128)(2,1)S(1)}, u32[]{:S(2)}, u32[]{:S(2)}) collective-permute-start(bf16[128,1024]{1,0:T(8,128)(2,1)S(1)} %get-tuple-element.28), channel_id=1, source_target_pairs={{0,2},{1,3},{2,0},{3,1},{4,6},{5,7},{6,4},{7,5},{8,10},{9,11},{10,... | collective-permute-start | bytes 786440 | tf_op jit(solution)/shard_map/ppermute | solution.py:196
  7.8 5.6 %collective-permute-done.refs_1_.refs_5_.refs_2_ = bf16[128,1024]{1,0:T(8,128)(2,1)S(1)} collective-permute-done((bf16[128,1024]{1,0:T(8,128)(2,1)S(1)}, bf16[128,1024]{1,0:T(8,128)(2,1)S(1)}, u32[]{:S(2)}, u32[]{:S(2)}) %collective-permute-start) | collective-permute-done | bytes 262176 | tf_op jit(solution)/shard_map/ppermute | solution.py:196
  13.4 6.2 %collective-permute-done.4.refs_2_.refs_6_.refs_3_ = bf16[128,1024]{1,0:T(8,128)(2,1)S(1)} collective-permute-done((bf16[128,1024]{1,0:T(8,128)(2,1)S(1)}, bf16[128,1024]{1,0:T(8,128)(2,1)S(1)}, u32[]{:S(2)}, u32[]{:S(2)}) %collective-permute-start.4) | collective-permute-done | bytes 262176 | tf_op jit(solution)/shard_map/ppermute | solution.py:196
  20.1 1.6 %collective-permute-start.6 = (bf16[512,512]{1,0:T(8,128)(2,1)S(1)}, bf16[512,512]{1,0:T(8,128)(2,1)S(1)}, u32[]{:S(2)}, u32[]{:S(2)}) collective-permute-start(bf16[512,512]{1,0:T(8,128)(2,1)S(1)} %gradient.4), channel_id=1, source_target_pairs={{0,4},{1,5},{2,6},{3,7},{4,0},{5,1},{6,2},{7,3},{8,12},{9,13},{10,... | collective-permute-start | bytes 1572872 | tf_op jit(solution)/shard_map/ppermute | solution.py:193
  23.9 1.4 %collective-permute-start.3 = (bf16[128,1024]{1,0:T(8,128)(2,1)S(1)}, bf16[128,1024]{1,0:T(8,128)(2,1)S(1)}, u32[]{:S(2)}, u32[]{:S(2)}) collective-permute-start(bf16[128,1024]{1,0:T(8,128)(2,1)S(1)} %get-tuple-element.26), channel_id=1, source_target_pairs={{0,3},{1,2},{2,1},{3,0},{4,7},{5,6},{6,5},{7,4},{8,11},{9,10},{10,... | collective-permute-start | bytes 786440 | tf_op jit(solution)/shard_map/ppermute | solution.py:196
  25.4 5.8 %collective-permute-done.1.refs_1_.refs_5_ = bf16[128,1024]{1,0:T(8,128)(2,1)S(1)} collective-permute-done((bf16[128,1024]{1,0:T(8,128)(2,1)S(1)}, bf16[128,1024]{1,0:T(8,128)(2,1)S(1)}, u32[]{:S(2)}, u32[]{:S(2)}) %collective-permute-start.1) | collective-permute-done | bytes 262176 | tf_op jit(solution)/shard_map/ppermute | solution.py:196
  31.1 4.2 %collective-permute-done.2.refs_2_.refs_6_ = bf16[128,1024]{1,0:T(8,128)(2,1)S(1)} collective-permute-done((bf16[128,1024]{1,0:T(8,128)(2,1)S(1)}, bf16[128,1024]{1,0:T(8,128)(2,1)S(1)}, u32[]{:S(2)}, u32[]{:S(2)}) %collective-permute-start.2) | collective-permute-done | bytes 262176 | tf_op jit(solution)/shard_map/ppermute | solution.py:196
  35.8 2.7 %collective-permute-start.10 = (bf16[512,512]{1,0:T(8,128)(2,1)S(1)}, bf16[512,512]{1,0:T(8,128)(2,1)S(1)}, u32[]{:S(2)}, u32[]{:S(2)}) collective-permute-start(bf16[512,512]{1,0:T(8,128)(2,1)S(1)} %gradient.5.refs_8_), channel_id=1, source_target_pairs={{0,8},{1,9},{2,10},{3,11},{4,12},{5,13},{6,14},{7,15},{8,0},{9,1},... | collective-permute-start | bytes 1572872 | tf_op jit(solution)/shard_map/ppermute | solution.py:193
  40.2 1.6 %collective-permute-start.12 = (bf16[512,256]{1,0:T(8,128)(2,1)S(1)}, bf16[512,256]{1,0:T(8,128)(2,1)S(1)}, u32[]{:S(2)}, u32[]{:S(2)}) collective-permute-start(bf16[512,256]{1,0:T(8,128)(2,1)S(1)} %get-tuple-element.35), channel_id=1, source_target_pairs={{0,4},{1,5},{2,6},{3,7},{4,0},{5,1},{6,2},{7,3},{8,12},{9,13},{10,... | collective-permute-start | bytes 786440 | tf_op jit(solution)/shard_map/ppermute | solution.py:193
  41.8 1.5 %collective-permute-start.8 = (bf16[128,512]{1,0:T(8,128)(2,1)S(1)}, bf16[128,512]{1,0:T(8,128)(2,1)S(1)}, u32[]{:S(2)}, u32[]{:S(2)}) collective-permute-start(bf16[128,512]{1,0:T(8,128)(2,1)S(1)} %get-tuple-element.33), channel_id=1, source_target_pairs={{0,2},{1,3},{2,0},{3,1},{4,6},{5,7},{6,4},{7,5},{8,10},{9,11},{10,... | collective-permute-start | bytes 393224 | tf_op jit(solution)/shard_map/ppermute | solution.py:196
  43.3 2.1 %collective-permute-done.7.refs_1_ = bf16[128,512]{1,0:T(8,128)(2,1)S(1)} collective-permute-done((bf16[128,512]{1,0:T(8,128)(2,1)S(1)}, bf16[128,512]{1,0:T(8,128)(2,1)S(1)}, u32[]{:S(2)}, u32[]{:S(2)}) %collective-permute-start.7) | collective-permute-done | bytes 131104 | tf_op jit(solution)/shard_map/ppermute | solution.py:196
  46.9 4.4 %collective-permute-done.9.refs_3_ = bf16[128,512]{1,0:T(8,128)(2,1)S(1)} collective-permute-done((bf16[128,512]{1,0:T(8,128)(2,1)S(1)}, bf16[128,512]{1,0:T(8,128)(2,1)S(1)}, u32[]{:S(2)}, u32[]{:S(2)}) %collective-permute-start.9) | collective-permute-done | bytes 131104 | tf_op jit(solution)/shard_map/ppermute | solution.py:196
  51.7 6.2 %collective-permute-done.11.refs_2_ = bf16[512,256]{1,0:T(8,128)(2,1)S(1)} collective-permute-done((bf16[512,256]{1,0:T(8,128)(2,1)S(1)}, bf16[512,256]{1,0:T(8,128)(2,1)S(1)}, u32[]{:S(2)}, u32[]{:S(2)}) %collective-permute-start.11) | collective-permute-done | bytes 262176 | tf_op jit(solution)/shard_map/ppermute | solution.py:193
  57.8 2.8 %collective-permute-done.12.refs_3_ = bf16[512,256]{1,0:T(8,128)(2,1)S(1)} collective-permute-done((bf16[512,256]{1,0:T(8,128)(2,1)S(1)}, bf16[512,256]{1,0:T(8,128)(2,1)S(1)}, u32[]{:S(2)}, u32[]{:S(2)}) %collective-permute-start.12) | collective-permute-done | bytes 262176 | tf_op jit(solution)/shard_map/ppermute | solution.py:193
  61.3 1.6 %update.1 = (f32[512,512]{1,0:T(8,128)}, f32[256,512]{1,0:T(8,128)S(1)}) custom-call(f32[512,512]{1,0:T(8,128)S(1)} %gradient.7.refs_0_, bf16[512,512]{1,0:T(8,128)(2,1)S(1)} %collective-permute-done.10.refs_1_, bf16[512,256]{1,0:T(8,128)(2,1)S(1)} %collective-permute-done.11.refs_2_, bf16[512,256]{1,0:T(8,128)(2,1)S(1)} %collective-permute-done.12.refs_3_, ...), custom_call_target="tpu_custom_call" | custom-call | bytes 7864320 | tf_op jit(solution)/shard_map/update/pallas_call | solution.py:60
  63.5 1.4 %collective-permute-start.15 = (bf16[256,512]{1,0:T(8,128)(2,1)S(1)}, bf16[256,512]{1,0:T(8,128)(2,1)S(1)}, u32[]{:S(2)}, u32[]{:S(2)}) collective-permute-start(bf16[256,512]{1,0:T(8,128)(2,1)S(1)} %outer.1.refs_8_), channel_id=1, source_target_pairs={{0,4},{1,5},{2,6},{3,7},{4,0},{5,1},{6,2},{7,3},{8,12},{9,13},{10,... | collective-permute-start | bytes 786440 | tf_op jit(solution)/shard_map/ppermute | solution.py:193
  64.9 12.6 %collective-permute-done.17.refs_12_ = bf16[256,512]{1,0:T(8,128)(2,1)S(1)} collective-permute-done((bf16[256,512]{1,0:T(8,128)(2,1)S(1)}, bf16[256,512]{1,0:T(8,128)(2,1)S(1)}, u32[]{:S(2)}, u32[]{:S(2)}) %collective-permute-start.17) | collective-permute-done | bytes 262176 | tf_op jit(solution)/shard_map/ppermute | solution.py:193
  78.1 7.6 %collective-permute-done.19.refs_5_ = bf16[256,512]{1,0:T(8,128)(2,1)S(1)} collective-permute-done((bf16[256,512]{1,0:T(8,128)(2,1)S(1)}, bf16[256,512]{1,0:T(8,128)(2,1)S(1)}, u32[]{:S(2)}, u32[]{:S(2)}) %collective-permute-start.19) | collective-permute-done | bytes 262176 | tf_op jit(solution)/shard_map/ppermute | solution.py:193
  88.8 1.8 %collective-permute-start.22 = (bf16[128,512]{1,0:T(8,128)(2,1)S(1)}, bf16[128,512]{1,0:T(8,128)(2,1)S(1)}, u32[]{:S(2)}, u32[]{:S(2)}) collective-permute-start(bf16[128,512]{1,0:T(8,128)(2,1)S(1)} %get-tuple-element.40), channel_id=1, source_target_pairs={{0,2},{1,3},{2,0},{3,1},{4,6},{5,7},{6,4},{7,5},{8,10},{9,11},{10,... | collective-permute-start | bytes 393224 | tf_op jit(solution)/shard_map/ppermute | solution.py:196
  91.6 2.3 %collective-permute-done.21.refs_1_ = bf16[128,512]{1,0:T(8,128)(2,1)S(1)} collective-permute-done((bf16[128,512]{1,0:T(8,128)(2,1)S(1)}, bf16[128,512]{1,0:T(8,128)(2,1)S(1)}, u32[]{:S(2)}, u32[]{:S(2)}) %collective-permute-start.21) | collective-permute-done | bytes 131104 | tf_op jit(solution)/shard_map/ppermute | solution.py:196
  93.9 2.3 %collective-permute-done.22.refs_2_ = bf16[128,512]{1,0:T(8,128)(2,1)S(1)} collective-permute-done((bf16[128,512]{1,0:T(8,128)(2,1)S(1)}, bf16[128,512]{1,0:T(8,128)(2,1)S(1)}, u32[]{:S(2)}, u32[]{:S(2)}) %collective-permute-start.22) | collective-permute-done | bytes 131104 | tf_op jit(solution)/shard_map/ppermute | solution.py:196
  96.2 1.7 %collective-permute-done.23.refs_3_ = bf16[128,512]{1,0:T(8,128)(2,1)S(1)} collective-permute-done((bf16[128,512]{1,0:T(8,128)(2,1)S(1)}, bf16[128,512]{1,0:T(8,128)(2,1)S(1)}, u32[]{:S(2)}, u32[]{:S(2)}) %collective-permute-start.23) | collective-permute-done | bytes 131104 | tf_op jit(solution)/shard_map/ppermute | solution.py:196
  (53 shorter events, 14.3 us)
Async XLA Ops:
  3.2 10.1 %collective-permute-start = (bf16[128,1024]{1,0:T(8,128)(2,1)S(1)}, bf16[128,1024]{1,0:T(8,128)(2,1)S(1)}, u32[]{:S(2)}, u32[]{:S(2)}) collective-permute-start(bf16[128,1024]{1,0:T(8,128)(2,1)S(1)} %get-tuple-element.22), channel_id=1, source_target_pairs={{0,1},{1,0},{2,3},{3,2},{4,5},{5,4},{6,7},{7,6},{8,9},{9,8},{10,11... | collective-permute-start | bytes 786440 | tf_op jit(solution)/shard_map/ppermute | solution.py:196
  6.2 13.4 %collective-permute-start.4 = (bf16[128,1024]{1,0:T(8,128)(2,1)S(1)}, bf16[128,1024]{1,0:T(8,128)(2,1)S(1)}, u32[]{:S(2)}, u32[]{:S(2)}) collective-permute-start(bf16[128,1024]{1,0:T(8,128)(2,1)S(1)} %get-tuple-element.28), channel_id=1, source_target_pairs={{0,2},{1,3},{2,0},{3,1},{4,6},{5,7},{6,4},{7,5},{8,10},{9,11},{10,... | collective-permute-start | bytes 786440 | tf_op jit(solution)/shard_map/ppermute | solution.py:196
  7.7 11.9 %collective-permute-start.5 = (bf16[128,1024]{1,0:T(8,128)(2,1)S(1)}, bf16[128,1024]{1,0:T(8,128)(2,1)S(1)}, u32[]{:S(2)}, u32[]{:S(2)}) collective-permute-start(bf16[128,1024]{1,0:T(8,128)(2,1)S(1)} %get-tuple-element.29), channel_id=1, source_target_pairs={{0,3},{1,2},{2,1},{3,0},{4,7},{5,6},{6,5},{7,4},{8,11},{9,10},{10,... | collective-permute-start | bytes 786440 | tf_op jit(solution)/shard_map/ppermute | solution.py:196
  20.1 15.3 %collective-permute-start.6 = (bf16[512,512]{1,0:T(8,128)(2,1)S(1)}, bf16[512,512]{1,0:T(8,128)(2,1)S(1)}, u32[]{:S(2)}, u32[]{:S(2)}) collective-permute-start(bf16[512,512]{1,0:T(8,128)(2,1)S(1)} %gradient.4), channel_id=1, source_target_pairs={{0,4},{1,5},{2,6},{3,7},{4,0},{5,1},{6,2},{7,3},{8,12},{9,13},{10,... | collective-permute-start | bytes 1572872 | tf_op jit(solution)/shard_map/ppermute | solution.py:193
  21.8 9.3 %collective-permute-start.1 = (bf16[128,1024]{1,0:T(8,128)(2,1)S(1)}, bf16[128,1024]{1,0:T(8,128)(2,1)S(1)}, u32[]{:S(2)}, u32[]{:S(2)}) collective-permute-start(bf16[128,1024]{1,0:T(8,128)(2,1)S(1)} %get-tuple-element.24), channel_id=1, source_target_pairs={{0,1},{1,0},{2,3},{3,2},{4,5},{5,4},{6,7},{7,6},{8,9},{9,8},{10,11... | collective-permute-start | bytes 786440 | tf_op jit(solution)/shard_map/ppermute | solution.py:196
  23.1 12.2 %collective-permute-start.2 = (bf16[128,1024]{1,0:T(8,128)(2,1)S(1)}, bf16[128,1024]{1,0:T(8,128)(2,1)S(1)}, u32[]{:S(2)}, u32[]{:S(2)}) collective-permute-start(bf16[128,1024]{1,0:T(8,128)(2,1)S(1)} %get-tuple-element.25), channel_id=1, source_target_pairs={{0,2},{1,3},{2,0},{3,1},{4,6},{5,7},{6,4},{7,5},{8,10},{9,11},{10,... | collective-permute-start | bytes 786440 | tf_op jit(solution)/shard_map/ppermute | solution.py:196
  23.9 11.4 %collective-permute-start.3 = (bf16[128,1024]{1,0:T(8,128)(2,1)S(1)}, bf16[128,1024]{1,0:T(8,128)(2,1)S(1)}, u32[]{:S(2)}, u32[]{:S(2)}) collective-permute-start(bf16[128,1024]{1,0:T(8,128)(2,1)S(1)} %get-tuple-element.26), channel_id=1, source_target_pairs={{0,3},{1,2},{2,1},{3,0},{4,7},{5,6},{6,5},{7,4},{8,11},{9,10},{10,... | collective-permute-start | bytes 786440 | tf_op jit(solution)/shard_map/ppermute | solution.py:196
  35.8 24.8 %collective-permute-start.10 = (bf16[512,512]{1,0:T(8,128)(2,1)S(1)}, bf16[512,512]{1,0:T(8,128)(2,1)S(1)}, u32[]{:S(2)}, u32[]{:S(2)}) collective-permute-start(bf16[512,512]{1,0:T(8,128)(2,1)S(1)} %gradient.5.refs_8_), channel_id=1, source_target_pairs={{0,8},{1,9},{2,10},{3,11},{4,12},{5,13},{6,14},{7,15},{8,0},{9,1},... | collective-permute-start | bytes 1572872 | tf_op jit(solution)/shard_map/ppermute | solution.py:193
  39.1 6.3 %collective-permute-start.7 = (bf16[128,512]{1,0:T(8,128)(2,1)S(1)}, bf16[128,512]{1,0:T(8,128)(2,1)S(1)}, u32[]{:S(2)}, u32[]{:S(2)}) collective-permute-start(bf16[128,512]{1,0:T(8,128)(2,1)S(1)} %get-tuple-element.32), channel_id=1, source_target_pairs={{0,1},{1,0},{2,3},{3,2},{4,5},{5,4},{6,7},{7,6},{8,9},{9,8},{10,11... | collective-permute-start | bytes 393224 | tf_op jit(solution)/shard_map/ppermute | solution.py:196
  39.7 18.1 %collective-permute-start.11 = (bf16[512,256]{1,0:T(8,128)(2,1)S(1)}, bf16[512,256]{1,0:T(8,128)(2,1)S(1)}, u32[]{:S(2)}, u32[]{:S(2)}) collective-permute-start(bf16[512,256]{1,0:T(8,128)(2,1)S(1)} %get-tuple-element.30.refs_1_), channel_id=1, source_target_pairs={{0,4},{1,5},{2,6},{3,7},{4,0},{5,1},{6,2},{7,3},{8,12},{9,13},{10,... | collective-permute-start | bytes 786440 | tf_op jit(solution)/shard_map/ppermute | solution.py:193
  40.2 20.5 %collective-permute-start.12 = (bf16[512,256]{1,0:T(8,128)(2,1)S(1)}, bf16[512,256]{1,0:T(8,128)(2,1)S(1)}, u32[]{:S(2)}, u32[]{:S(2)}) collective-permute-start(bf16[512,256]{1,0:T(8,128)(2,1)S(1)} %get-tuple-element.35), channel_id=1, source_target_pairs={{0,4},{1,5},{2,6},{3,7},{4,0},{5,1},{6,2},{7,3},{8,12},{9,13},{10,... | collective-permute-start | bytes 786440 | tf_op jit(solution)/shard_map/ppermute | solution.py:193
  41.8 5.1 %collective-permute-start.8 = (bf16[128,512]{1,0:T(8,128)(2,1)S(1)}, bf16[128,512]{1,0:T(8,128)(2,1)S(1)}, u32[]{:S(2)}, u32[]{:S(2)}) collective-permute-start(bf16[128,512]{1,0:T(8,128)(2,1)S(1)} %get-tuple-element.33), channel_id=1, source_target_pairs={{0,2},{1,3},{2,0},{3,1},{4,6},{5,7},{6,4},{7,5},{8,10},{9,11},{10,... | collective-permute-start | bytes 393224 | tf_op jit(solution)/shard_map/ppermute | solution.py:196
  45.4 5.9 %collective-permute-start.9 = (bf16[128,512]{1,0:T(8,128)(2,1)S(1)}, bf16[128,512]{1,0:T(8,128)(2,1)S(1)}, u32[]{:S(2)}, u32[]{:S(2)}) collective-permute-start(bf16[128,512]{1,0:T(8,128)(2,1)S(1)} %get-tuple-element.34), channel_id=1, source_target_pairs={{0,3},{1,2},{2,1},{3,0},{4,7},{5,6},{6,5},{7,4},{8,11},{9,10},{10,... | collective-permute-start | bytes 393224 | tf_op jit(solution)/shard_map/ppermute | solution.py:196
  61.2 2.0 %collective-permute-start.13 = (f32[256,512]{1,0:T(8,128)S(1)}, f32[256,512]{1,0:T(8,128)S(1)}, u32[]{:S(2)}, u32[]{:S(2)}) collective-permute-start(f32[256,512]{1,0:T(8,128)S(1)} %drift.1), channel_id=1, source_target_pairs={{0,16},{16,0},{1,17},{17,1},{2,18},{18,2},{3,19},{19,3},{4,20},{20... | collective-permute-start | bytes 1572872 | tf_op jit(solution)/shard_map/ppermute | solution.py:202
  63.4 14.1 %collective-permute-start.17 = (bf16[256,512]{1,0:T(8,128)(2,1)S(1)}, bf16[256,512]{1,0:T(8,128)(2,1)S(1)}, u32[]{:S(2)}, u32[]{:S(2)}) collective-permute-start(bf16[256,512]{1,0:T(8,128)(2,1)S(1)} %outer.1.refs_8_), channel_id=1, source_target_pairs={{0,8},{1,9},{2,10},{3,11},{4,12},{5,13},{6,14},{7,15},{8,0},{9,1},... | collective-permute-start | bytes 786440 | tf_op jit(solution)/shard_map/ppermute | solution.py:193
  63.5 14.1 %collective-permute-start.15 = (bf16[256,512]{1,0:T(8,128)(2,1)S(1)}, bf16[256,512]{1,0:T(8,128)(2,1)S(1)}, u32[]{:S(2)}, u32[]{:S(2)}) collective-permute-start(bf16[256,512]{1,0:T(8,128)(2,1)S(1)} %outer.1.refs_8_), channel_id=1, source_target_pairs={{0,4},{1,5},{2,6},{3,7},{4,0},{5,1},{6,2},{7,3},{8,12},{9,13},{10,... | collective-permute-start | bytes 786440 | tf_op jit(solution)/shard_map/ppermute | solution.py:193
  77.5 8.2 %collective-permute-start.19 = (bf16[256,512]{1,0:T(8,128)(2,1)S(1)}, bf16[256,512]{1,0:T(8,128)(2,1)S(1)}, u32[]{:S(2)}, u32[]{:S(2)}) collective-permute-start(bf16[256,512]{1,0:T(8,128)(2,1)S(1)} %collective-permute-done.17.refs_12_), channel_id=1, source_target_pairs={{0,4},{1,5},{2,6},{3,7},{4,0},{5,1},{6,2},{7,3},{8,12},{9,13},{10,... | collective-permute-start | bytes 786440 | tf_op jit(solution)/shard_map/ppermute | solution.py:193
  77.5 8.2 %collective-permute-start.14 = (bf16[256,512]{1,0:T(8,128)(2,1)S(1)}, bf16[256,512]{1,0:T(8,128)(2,1)S(1)}, u32[]{:S(2)}, u32[]{:S(2)}) collective-permute-start(bf16[256,512]{1,0:T(8,128)(2,1)S(1)} %outer.1.refs_8_), channel_id=1, source_target_pairs={{0,16},{16,0},{1,17},{17,1},{2,18},{18,2},{3,19},{19,3},{4,20},{20... | collective-permute-start | bytes 786440 | tf_op jit(solution)/shard_map/ppermute | solution.py:202
  77.6 8.1 %collective-permute-start.16 = (bf16[256,512]{1,0:T(8,128)(2,1)S(1)}, bf16[256,512]{1,0:T(8,128)(2,1)S(1)}, u32[]{:S(2)}, u32[]{:S(2)}) collective-permute-start(bf16[256,512]{1,0:T(8,128)(2,1)S(1)} %collective-permute-done.15.refs_10_), channel_id=1, source_target_pairs={{0,16},{16,0},{1,17},{17,1},{2,18},{18,2},{3,19},{19,3},{4,20},{20... | collective-permute-start | bytes 786440 | tf_op jit(solution)/shard_map/ppermute | solution.py:202
  78.0 7.7 %collective-permute-start.18 = (bf16[256,512]{1,0:T(8,128)(2,1)S(1)}, bf16[256,512]{1,0:T(8,128)(2,1)S(1)}, u32[]{:S(2)}, u32[]{:S(2)}) collective-permute-start(bf16[256,512]{1,0:T(8,128)(2,1)S(1)} %collective-permute-done.17.refs_12_), channel_id=1, source_target_pairs={{0,16},{16,0},{1,17},{17,1},{2,18},{18,2},{3,19},{19,3},{4,20},{20... | collective-permute-start | bytes 786440 | tf_op jit(solution)/shard_map/ppermute | solution.py:202
  85.7 1.5 %collective-permute-start.20 = (bf16[256,512]{1,0:T(8,128)(2,1)S(1)}, bf16[256,512]{1,0:T(8,128)(2,1)S(1)}, u32[]{:S(2)}, u32[]{:S(2)}) collective-permute-start(bf16[256,512]{1,0:T(8,128)(2,1)S(1)} %collective-permute-done.19.refs_5_), channel_id=1, source_target_pairs={{0,16},{16,0},{1,17},{17,1},{2,18},{18,2},{3,19},{19,3},{4,20},{20... | collective-permute-start | bytes 786440 | tf_op jit(solution)/shard_map/ppermute | solution.py:202
  87.7 6.2 %collective-permute-start.21 = (bf16[128,512]{1,0:T(8,128)(2,1)S(1)}, bf16[128,512]{1,0:T(8,128)(2,1)S(1)}, u32[]{:S(2)}, u32[]{:S(2)}) collective-permute-start(bf16[128,512]{1,0:T(8,128)(2,1)S(1)} %get-tuple-element.39), channel_id=1, source_target_pairs={{0,1},{1,0},{2,3},{3,2},{4,5},{5,4},{6,7},{7,6},{8,9},{9,8},{10,11... | collective-permute-start | bytes 393224 | tf_op jit(solution)/shard_map/ppermute | solution.py:196
  88.8 7.3 %collective-permute-start.22 = (bf16[128,512]{1,0:T(8,128)(2,1)S(1)}, bf16[128,512]{1,0:T(8,128)(2,1)S(1)}, u32[]{:S(2)}, u32[]{:S(2)}) collective-permute-start(bf16[128,512]{1,0:T(8,128)(2,1)S(1)} %get-tuple-element.40), channel_id=1, source_target_pairs={{0,2},{1,3},{2,0},{3,1},{4,6},{5,7},{6,4},{7,5},{8,10},{9,11},{10,... | collective-permute-start | bytes 393224 | tf_op jit(solution)/shard_map/ppermute | solution.py:196
  90.6 7.3 %collective-permute-start.23 = (bf16[128,512]{1,0:T(8,128)(2,1)S(1)}, bf16[128,512]{1,0:T(8,128)(2,1)S(1)}, u32[]{:S(2)}, u32[]{:S(2)}) collective-permute-start(bf16[128,512]{1,0:T(8,128)(2,1)S(1)} %get-tuple-element.41), channel_id=1, source_target_pairs={{0,3},{1,2},{2,1},{3,0},{4,7},{5,6},{6,5},{7,4},{8,11},{9,10},{10,... | collective-permute-start | bytes 393224 | tf_op jit(solution)/shard_map/ppermute | solution.py:196
  (8 other events, 109.8 us)

commit v18 on v15

--- a/solution.py
+++ b/solution.py
@@ -191,8 +191,10 @@
     def across(x, k):
         return lax.ppermute(x, "fsdp", [(p * inner + i, p * inner + (i ^ k)) for p in range(PLANES) for i in range(inner)])
 
+    order = list(reversed(range(1, inner)))
+
     def around(blocks):
-        return [blocks[0]] + [across(blocks[k], k) for k in range(1, inner)]
+        return [blocks[0]] + [across(blocks[k], k) for k in order]
 
     def swap(x):
         return lax.ppermute(x, "rep", [(0, 1), (1, 0)])
@@ -245,7 +247,7 @@
         [early] + first + [mine3, swap(mine3)],
         flops,
     )
-    terms = [own] + [across(sums[k - 1], k) for k in range(1, inner)]
+    terms = [own] + [across(x, k) for x, k in zip(sums, order)]
     (values,) = call(sum_kernel, "sum", [block], terms, 0)
     return (first_next[None], values[None])
 

time: 95.1 us -> 99.4 us (1.045)
  waiting for transfers between devices: 58.1 us -> 62.7 us
    ppermute x6, waiting for transfers between devices: 24.7 us -> 28.5 us  [planes(): lax.ppermute(x, 'fsdp', [(p * inner + i, (p ^ bits) * inner + i) for p in...]
  transfers between devices with their start and end apart: 23 -> 23, of which waited for: 15 -> 18; matrix products, arithmetic and copies ran while one was open for 0% -> 0% of each run, Pallas kernels for 4% -> 4%
where the time goes in v18:
time: 99.4 us; the launch traced here: 99.2 us
  waiting for transfers between devices  62.7 us (63%)
  starting transfers between devices  26.6 us (27%)
  Pallas kernels  6.55 us (7%)
  local copies, waits for them, and re-layouts  2.52 us (3%)
    ppermute x12, waiting for transfers between devices, across(): lax.ppermute(x, 'fsdp', [(p * inner + i, p * inner + (i ^ k)) for p in ra...  33.5 us
    ppermute x6, waiting for transfers between devices, planes(): lax.ppermute(x, 'fsdp', [(p * inner + i, (p ^ bits) * inner + i) for p in...  28.5 us
    ppermute x12, starting transfers between devices, across(): lax.ppermute(x, 'fsdp', [(p * inner + i, p * inner + (i ^ k)) for p in ra...  15.3 us
    ppermute x6, starting transfers between devices, planes(): lax.ppermute(x, 'fsdp', [(p * inner + i, (p ^ bits) * inner + i) for p in...  10.7 us
    pallas_call x13, Pallas kernels, call(): pl.pallas_call(without_after, out_shape=out, in_specs=[pl.BlockSpec(memor...  6.55 us
    unnamed x16, local copies, waits for them, and re-layouts  2.52 us
  transfers between devices with their start and end apart: 23, of which 18 were waited for; matrix products, arithmetic and copies ran while one was open for 0% of the time, Pallas kernels for 4%

profile of v18, /device:TPU:0, one launch (start us, length us, event | category | flops | bytes accessed | tf_op | source)
XLA Modules:
  0.0 99.2 jit_solution(15292497352335677563)
XLA Ops:
  0.6 1.6 %copy-done = bf16[1,128,8192]{2,1,0:T(8,128)(2,1)S(1)} copy-done((bf16[1,128,8192]{2,1,0:T(8,128)(2,1)S(1)}, bf16[1,128,8192]{2,1,0:T(8,128)(2,1)}, u32[]{:S(2)}) %copy-start) | copy-done | bytes 2097176
  3.2 4.0 %collective-permute-start = (bf16[128,1024]{1,0:T(8,128)(2,1)S(1)}, bf16[128,1024]{1,0:T(8,128)(2,1)S(1)}, u32[]{:S(2)}, u32[]{:S(2)}) collective-permute-start(bf16[128,1024]{1,0:T(8,128)(2,1)S(1)} %get-tuple-element.20), channel_id=1, source_target_pairs={{0,3},{1,2},{2,1},{3,0},{4,7},{5,6},{6,5},{7,4},{8,11},{9,10},{10,... | collective-permute-start | bytes 786440 | tf_op jit(solution)/shard_map/ppermute | solution.py:192
  7.8 6.5 %collective-permute-done.refs_1_.refs_5_.refs_2_ = bf16[128,1024]{1,0:T(8,128)(2,1)S(1)} collective-permute-done((bf16[128,1024]{1,0:T(8,128)(2,1)S(1)}, bf16[128,1024]{1,0:T(8,128)(2,1)S(1)}, u32[]{:S(2)}, u32[]{:S(2)}) %collective-permute-start) | collective-permute-done | bytes 262176 | tf_op jit(solution)/shard_map/ppermute | solution.py:192
  14.4 4.7 %collective-permute-done.4.refs_2_.refs_6_.refs_3_ = bf16[128,1024]{1,0:T(8,128)(2,1)S(1)} collective-permute-done((bf16[128,1024]{1,0:T(8,128)(2,1)S(1)}, bf16[128,1024]{1,0:T(8,128)(2,1)S(1)}, u32[]{:S(2)}, u32[]{:S(2)}) %collective-permute-start.4) | collective-permute-done | bytes 262176 | tf_op jit(solution)/shard_map/ppermute | solution.py:192
  19.9 1.6 %collective-permute-start.6 = (bf16[512,512]{1,0:T(8,128)(2,1)S(1)}, bf16[512,512]{1,0:T(8,128)(2,1)S(1)}, u32[]{:S(2)}, u32[]{:S(2)}) collective-permute-start(bf16[512,512]{1,0:T(8,128)(2,1)S(1)} %gradient.4), channel_id=1, source_target_pairs={{0,4},{1,5},{2,6},{3,7},{4,0},{5,1},{6,2},{7,3},{8,12},{9,13},{10,... | collective-permute-start | bytes 1572872 | tf_op jit(solution)/shard_map/ppermute | solution.py:189
  21.6 1.7 %collective-permute-start.1 = (bf16[128,1024]{1,0:T(8,128)(2,1)S(1)}, bf16[128,1024]{1,0:T(8,128)(2,1)S(1)}, u32[]{:S(2)}, u32[]{:S(2)}) collective-permute-start(bf16[128,1024]{1,0:T(8,128)(2,1)S(1)} %get-tuple-element.22), channel_id=1, source_target_pairs={{0,3},{1,2},{2,1},{3,0},{4,7},{5,6},{6,5},{7,4},{8,11},{9,10},{10,... | collective-permute-start | bytes 786440 | tf_op jit(solution)/shard_map/ppermute | solution.py:192
  23.3 1.3 %collective-permute-start.2 = (bf16[128,1024]{1,0:T(8,128)(2,1)S(1)}, bf16[128,1024]{1,0:T(8,128)(2,1)S(1)}, u32[]{:S(2)}, u32[]{:S(2)}) collective-permute-start(bf16[128,1024]{1,0:T(8,128)(2,1)S(1)} %get-tuple-element.23), channel_id=1, source_target_pairs={{0,2},{1,3},{2,0},{3,1},{4,6},{5,7},{6,4},{7,5},{8,10},{9,11},{10,... | collective-permute-start | bytes 786440 | tf_op jit(solution)/shard_map/ppermute | solution.py:192
  25.1 6.7 %collective-permute-done.1.refs_1_.refs_5_ = bf16[128,1024]{1,0:T(8,128)(2,1)S(1)} collective-permute-done((bf16[128,1024]{1,0:T(8,128)(2,1)S(1)}, bf16[128,1024]{1,0:T(8,128)(2,1)S(1)}, u32[]{:S(2)}, u32[]{:S(2)}) %collective-permute-start.1) | collective-permute-done | bytes 262176 | tf_op jit(solution)/shard_map/ppermute | solution.py:192
  31.8 4.2 %collective-permute-done.2.refs_2_.refs_6_ = bf16[128,1024]{1,0:T(8,128)(2,1)S(1)} collective-permute-done((bf16[128,1024]{1,0:T(8,128)(2,1)S(1)}, bf16[128,1024]{1,0:T(8,128)(2,1)S(1)}, u32[]{:S(2)}, u32[]{:S(2)}) %collective-permute-start.2) | collective-permute-done | bytes 262176 | tf_op jit(solution)/shard_map/ppermute | solution.py:192
  37.7 2.7 %collective-permute-start.11 = (bf16[512,512]{1,0:T(8,128)(2,1)S(1)}, bf16[512,512]{1,0:T(8,128)(2,1)S(1)}, u32[]{:S(2)}, u32[]{:S(2)}) collective-permute-start(bf16[512,512]{1,0:T(8,128)(2,1)S(1)} %gradient.5.refs_1_), channel_id=1, source_target_pairs={{0,8},{1,9},{2,10},{3,11},{4,12},{5,13},{6,14},{7,15},{8,0},{9,1},... | collective-permute-start | bytes 1572872 | tf_op jit(solution)/shard_map/ppermute | solution.py:189
  40.3 1.5 %collective-permute-start.7 = (bf16[128,512]{1,0:T(8,128)(2,1)S(1)}, bf16[128,512]{1,0:T(8,128)(2,1)S(1)}, u32[]{:S(2)}, u32[]{:S(2)}) collective-permute-start(bf16[128,512]{1,0:T(8,128)(2,1)S(1)} %get-tuple-element.29), channel_id=1, source_target_pairs={{0,3},{1,2},{2,1},{3,0},{4,7},{5,6},{6,5},{7,4},{8,11},{9,10},{10,... | collective-permute-start | bytes 393224 | tf_op jit(solution)/shard_map/ppermute | solution.py:192
  41.8 1.4 %collective-permute-start.8 = (bf16[128,512]{1,0:T(8,128)(2,1)S(1)}, bf16[128,512]{1,0:T(8,128)(2,1)S(1)}, u32[]{:S(2)}, u32[]{:S(2)}) collective-permute-start(bf16[128,512]{1,0:T(8,128)(2,1)S(1)} %get-tuple-element.30), channel_id=1, source_target_pairs={{0,2},{1,3},{2,0},{3,1},{4,6},{5,7},{6,4},{7,5},{8,10},{9,11},{10,... | collective-permute-start | bytes 393224 | tf_op jit(solution)/shard_map/ppermute | solution.py:192
  43.9 3.6 %collective-permute-done.7.refs_1_ = bf16[128,512]{1,0:T(8,128)(2,1)S(1)} collective-permute-done((bf16[128,512]{1,0:T(8,128)(2,1)S(1)}, bf16[128,512]{1,0:T(8,128)(2,1)S(1)}, u32[]{:S(2)}, u32[]{:S(2)}) %collective-permute-start.7) | collective-permute-done | bytes 131104 | tf_op jit(solution)/shard_map/ppermute | solution.py:192
  47.5 1.4 %collective-permute-done.8.refs_2_ = bf16[128,512]{1,0:T(8,128)(2,1)S(1)} collective-permute-done((bf16[128,512]{1,0:T(8,128)(2,1)S(1)}, bf16[128,512]{1,0:T(8,128)(2,1)S(1)}, u32[]{:S(2)}, u32[]{:S(2)}) %collective-permute-start.8) | collective-permute-done | bytes 131104 | tf_op jit(solution)/shard_map/ppermute | solution.py:192
  49.4 12.2 %collective-permute-done.10.refs_1_ = bf16[512,512]{1,0:T(8,128)(2,1)S(1)} collective-permute-done((bf16[512,512]{1,0:T(8,128)(2,1)S(1)}, bf16[512,512]{1,0:T(8,128)(2,1)S(1)}, u32[]{:S(2)}, u32[]{:S(2)}) %collective-permute-start.10) | collective-permute-done | bytes 524320 | tf_op jit(solution)/shard_map/ppermute | solution.py:189
  62.3 1.7 %update.1 = (f32[512,512]{1,0:T(8,128)}, f32[256,512]{1,0:T(8,128)S(1)}) custom-call(f32[512,512]{1,0:T(8,128)S(1)} %gradient.6.refs_0_, bf16[512,512]{1,0:T(8,128)(2,1)S(1)} %collective-permute-done.10.refs_1_, bf16[512,512]{1,0:T(8,128)(2,1)S(1)} %collective-permute-done.11.refs_2_, f32[512,512]{1,0:T(8,128)S(1)} %bitcast.11, f32[512,512]{1,0:T(8,128)S(1)} %bitcast.13, ...), custom_call_target="tpu_custom_call" | custom-call | bytes 7864320 | tf_op jit(solution)/shard_map/update/pallas_call | solution.py:60
  64.4 1.4 %collective-permute-start.16 = (bf16[256,512]{1,0:T(8,128)(2,1)S(1)}, bf16[256,512]{1,0:T(8,128)(2,1)S(1)}, u32[]{:S(2)}, u32[]{:S(2)}) collective-permute-start(bf16[256,512]{1,0:T(8,128)(2,1)S(1)} %outer.1.refs_8_), channel_id=1, source_target_pairs={{0,8},{1,9},{2,10},{3,11},{4,12},{5,13},{6,14},{7,15},{8,0},{9,1},... | collective-permute-start | bytes 786440 | tf_op jit(solution)/shard_map/ppermute | solution.py:189
  65.8 4.6 %collective-permute-start.14 = (bf16[256,512]{1,0:T(8,128)(2,1)S(1)}, bf16[256,512]{1,0:T(8,128)(2,1)S(1)}, u32[]{:S(2)}, u32[]{:S(2)}) collective-permute-start(bf16[256,512]{1,0:T(8,128)(2,1)S(1)} %outer.1.refs_8_), channel_id=1, source_target_pairs={{0,4},{1,5},{2,6},{3,7},{4,0},{5,1},{6,2},{7,3},{8,12},{9,13},{10,... | collective-permute-start | bytes 786440 | tf_op jit(solution)/shard_map/ppermute | solution.py:189
  70.3 9.2 %collective-permute-done.16.refs_12_ = bf16[256,512]{1,0:T(8,128)(2,1)S(1)} collective-permute-done((bf16[256,512]{1,0:T(8,128)(2,1)S(1)}, bf16[256,512]{1,0:T(8,128)(2,1)S(1)}, u32[]{:S(2)}, u32[]{:S(2)}) %collective-permute-start.16) | collective-permute-done | bytes 262176 | tf_op jit(solution)/shard_map/ppermute | solution.py:189
  80.1 7.0 %collective-permute-done.18.refs_5_ = bf16[256,512]{1,0:T(8,128)(2,1)S(1)} collective-permute-done((bf16[256,512]{1,0:T(8,128)(2,1)S(1)}, bf16[256,512]{1,0:T(8,128)(2,1)S(1)}, u32[]{:S(2)}, u32[]{:S(2)}) %collective-permute-start.18) | collective-permute-done | bytes 262176 | tf_op jit(solution)/shard_map/ppermute | solution.py:189
  89.1 1.1 %collective-permute-start.20 = (bf16[128,512]{1,0:T(8,128)(2,1)S(1)}, bf16[128,512]{1,0:T(8,128)(2,1)S(1)}, u32[]{:S(2)}, u32[]{:S(2)}) collective-permute-start(bf16[128,512]{1,0:T(8,128)(2,1)S(1)} %get-tuple-element.35), channel_id=1, source_target_pairs={{0,3},{1,2},{2,1},{3,0},{4,7},{5,6},{6,5},{7,4},{8,11},{9,10},{10,... | collective-permute-start | bytes 393224 | tf_op jit(solution)/shard_map/ppermute | solution.py:192
  90.1 2.0 %collective-permute-start.21 = (bf16[128,512]{1,0:T(8,128)(2,1)S(1)}, bf16[128,512]{1,0:T(8,128)(2,1)S(1)}, u32[]{:S(2)}, u32[]{:S(2)}) collective-permute-start(bf16[128,512]{1,0:T(8,128)(2,1)S(1)} %get-tuple-element.36), channel_id=1, source_target_pairs={{0,2},{1,3},{2,0},{3,1},{4,6},{5,7},{6,4},{7,5},{8,10},{9,11},{10,... | collective-permute-start | bytes 393224 | tf_op jit(solution)/shard_map/ppermute | solution.py:192
  92.6 3.8 %collective-permute-done.20.refs_1_ = bf16[128,512]{1,0:T(8,128)(2,1)S(1)} collective-permute-done((bf16[128,512]{1,0:T(8,128)(2,1)S(1)}, bf16[128,512]{1,0:T(8,128)(2,1)S(1)}, u32[]{:S(2)}, u32[]{:S(2)}) %collective-permute-start.20) | collective-permute-done | bytes 131104 | tf_op jit(solution)/shard_map/ppermute | solution.py:192
  96.4 2.0 %collective-permute-done.21.refs_2_ = bf16[128,512]{1,0:T(8,128)(2,1)S(1)} collective-permute-done((bf16[128,512]{1,0:T(8,128)(2,1)S(1)}, bf16[128,512]{1,0:T(8,128)(2,1)S(1)}, u32[]{:S(2)}, u32[]{:S(2)}) %collective-permute-start.21) | collective-permute-done | bytes 131104 | tf_op jit(solution)/shard_map/ppermute | solution.py:192
  (51 shorter events, 10.7 us)
Async XLA Ops:
  3.2 11.1 %collective-permute-start = (bf16[128,1024]{1,0:T(8,128)(2,1)S(1)}, bf16[128,1024]{1,0:T(8,128)(2,1)S(1)}, u32[]{:S(2)}, u32[]{:S(2)}) collective-permute-start(bf16[128,1024]{1,0:T(8,128)(2,1)S(1)} %get-tuple-element.20), channel_id=1, source_target_pairs={{0,3},{1,2},{2,1},{3,0},{4,7},{5,6},{6,5},{7,4},{8,11},{9,10},{10,... | collective-permute-start | bytes 786440 | tf_op jit(solution)/shard_map/ppermute | solution.py:192
  7.2 11.9 %collective-permute-start.4 = (bf16[128,1024]{1,0:T(8,128)(2,1)S(1)}, bf16[128,1024]{1,0:T(8,128)(2,1)S(1)}, u32[]{:S(2)}, u32[]{:S(2)}) collective-permute-start(bf16[128,1024]{1,0:T(8,128)(2,1)S(1)} %get-tuple-element.26), channel_id=1, source_target_pairs={{0,2},{1,3},{2,0},{3,1},{4,6},{5,7},{6,4},{7,5},{8,10},{9,11},{10,... | collective-permute-start | bytes 786440 | tf_op jit(solution)/shard_map/ppermute | solution.py:192
  7.7 11.7 %collective-permute-start.5 = (bf16[128,1024]{1,0:T(8,128)(2,1)S(1)}, bf16[128,1024]{1,0:T(8,128)(2,1)S(1)}, u32[]{:S(2)}, u32[]{:S(2)}) collective-permute-start(bf16[128,1024]{1,0:T(8,128)(2,1)S(1)} %get-tuple-element.27), channel_id=1, source_target_pairs={{0,1},{1,0},{2,3},{3,2},{4,5},{5,4},{6,7},{7,6},{8,9},{9,8},{10,11... | collective-permute-start | bytes 786440 | tf_op jit(solution)/shard_map/ppermute | solution.py:192
  19.9 17.3 %collective-permute-start.6 = (bf16[512,512]{1,0:T(8,128)(2,1)S(1)}, bf16[512,512]{1,0:T(8,128)(2,1)S(1)}, u32[]{:S(2)}, u32[]{:S(2)}) collective-permute-start(bf16[512,512]{1,0:T(8,128)(2,1)S(1)} %gradient.4), channel_id=1, source_target_pairs={{0,4},{1,5},{2,6},{3,7},{4,0},{5,1},{6,2},{7,3},{8,12},{9,13},{10,... | collective-permute-start | bytes 1572872 | tf_op jit(solution)/shard_map/ppermute | solution.py:189
  21.6 10.2 %collective-permute-start.1 = (bf16[128,1024]{1,0:T(8,128)(2,1)S(1)}, bf16[128,1024]{1,0:T(8,128)(2,1)S(1)}, u32[]{:S(2)}, u32[]{:S(2)}) collective-permute-start(bf16[128,1024]{1,0:T(8,128)(2,1)S(1)} %get-tuple-element.22), channel_id=1, source_target_pairs={{0,3},{1,2},{2,1},{3,0},{4,7},{5,6},{6,5},{7,4},{8,11},{9,10},{10,... | collective-permute-start | bytes 786440 | tf_op jit(solution)/shard_map/ppermute | solution.py:192
  23.3 12.7 %collective-permute-start.2 = (bf16[128,1024]{1,0:T(8,128)(2,1)S(1)}, bf16[128,1024]{1,0:T(8,128)(2,1)S(1)}, u32[]{:S(2)}, u32[]{:S(2)}) collective-permute-start(bf16[128,1024]{1,0:T(8,128)(2,1)S(1)} %get-tuple-element.23), channel_id=1, source_target_pairs={{0,2},{1,3},{2,0},{3,1},{4,6},{5,7},{6,4},{7,5},{8,10},{9,11},{10,... | collective-permute-start | bytes 786440 | tf_op jit(solution)/shard_map/ppermute | solution.py:192
  24.6 11.5 %collective-permute-start.3 = (bf16[128,1024]{1,0:T(8,128)(2,1)S(1)}, bf16[128,1024]{1,0:T(8,128)(2,1)S(1)}, u32[]{:S(2)}, u32[]{:S(2)}) collective-permute-start(bf16[128,1024]{1,0:T(8,128)(2,1)S(1)} %get-tuple-element.24), channel_id=1, source_target_pairs={{0,1},{1,0},{2,3},{3,2},{4,5},{5,4},{6,7},{7,6},{8,9},{9,8},{10,11... | collective-permute-start | bytes 786440 | tf_op jit(solution)/shard_map/ppermute | solution.py:192
  36.6 25.0 %collective-permute-start.10 = (bf16[512,512]{1,0:T(8,128)(2,1)S(1)}, bf16[512,512]{1,0:T(8,128)(2,1)S(1)}, u32[]{:S(2)}, u32[]{:S(2)}) collective-permute-start(bf16[512,512]{1,0:T(8,128)(2,1)S(1)} %gradient.7), channel_id=1, source_target_pairs={{0,4},{1,5},{2,6},{3,7},{4,0},{5,1},{6,2},{7,3},{8,12},{9,13},{10,... | collective-permute-start | bytes 1572872 | tf_op jit(solution)/shard_map/ppermute | solution.py:189
  37.6 24.1 %copy-start.2 = (f32[512,512]{1,0:T(8,128)S(1)}, f32[512,512]{1,0:T(8,128)}, u32[]{:S(2)}) copy-start(f32[512,512]{1,0:T(8,128)} %refs_2_.1) | copy-start | bytes 3145732
  37.7 24.0 %collective-permute-start.11 = (bf16[512,512]{1,0:T(8,128)(2,1)S(1)}, bf16[512,512]{1,0:T(8,128)(2,1)S(1)}, u32[]{:S(2)}, u32[]{:S(2)}) collective-permute-start(bf16[512,512]{1,0:T(8,128)(2,1)S(1)} %gradient.5.refs_1_), channel_id=1, source_target_pairs={{0,8},{1,9},{2,10},{3,11},{4,12},{5,13},{6,14},{7,15},{8,0},{9,1},... | collective-permute-start | bytes 1572872 | tf_op jit(solution)/shard_map/ppermute | solution.py:189
  40.3 7.2 %collective-permute-start.7 = (bf16[128,512]{1,0:T(8,128)(2,1)S(1)}, bf16[128,512]{1,0:T(8,128)(2,1)S(1)}, u32[]{:S(2)}, u32[]{:S(2)}) collective-permute-start(bf16[128,512]{1,0:T(8,128)(2,1)S(1)} %get-tuple-element.29), channel_id=1, source_target_pairs={{0,3},{1,2},{2,1},{3,0},{4,7},{5,6},{6,5},{7,4},{8,11},{9,10},{10,... | collective-permute-start | bytes 393224 | tf_op jit(solution)/shard_map/ppermute | solution.py:192
  41.8 7.0 %collective-permute-start.8 = (bf16[128,512]{1,0:T(8,128)(2,1)S(1)}, bf16[128,512]{1,0:T(8,128)(2,1)S(1)}, u32[]{:S(2)}, u32[]{:S(2)}) collective-permute-start(bf16[128,512]{1,0:T(8,128)(2,1)S(1)} %get-tuple-element.30), channel_id=1, source_target_pairs={{0,2},{1,3},{2,0},{3,1},{4,6},{5,7},{6,4},{7,5},{8,10},{9,11},{10,... | collective-permute-start | bytes 393224 | tf_op jit(solution)/shard_map/ppermute | solution.py:192
  43.3 5.7 %collective-permute-start.9 = (bf16[128,512]{1,0:T(8,128)(2,1)S(1)}, bf16[128,512]{1,0:T(8,128)(2,1)S(1)}, u32[]{:S(2)}, u32[]{:S(2)}) collective-permute-start(bf16[128,512]{1,0:T(8,128)(2,1)S(1)} %get-tuple-element.31), channel_id=1, source_target_pairs={{0,1},{1,0},{2,3},{3,2},{4,5},{5,4},{6,7},{7,6},{8,9},{9,8},{10,11... | collective-permute-start | bytes 393224 | tf_op jit(solution)/shard_map/ppermute | solution.py:192
  62.2 2.0 %collective-permute-start.12 = (f32[256,512]{1,0:T(8,128)S(1)}, f32[256,512]{1,0:T(8,128)S(1)}, u32[]{:S(2)}, u32[]{:S(2)}) collective-permute-start(f32[256,512]{1,0:T(8,128)S(1)} %drift.1), channel_id=1, source_target_pairs={{0,16},{16,0},{1,17},{17,1},{2,18},{18,2},{3,19},{19,3},{4,20},{20... | collective-permute-start | bytes 1572872 | tf_op jit(solution)/shard_map/ppermute | solution.py:200
  64.4 15.1 %collective-permute-start.16 = (bf16[256,512]{1,0:T(8,128)(2,1)S(1)}, bf16[256,512]{1,0:T(8,128)(2,1)S(1)}, u32[]{:S(2)}, u32[]{:S(2)}) collective-permute-start(bf16[256,512]{1,0:T(8,128)(2,1)S(1)} %outer.1.refs_8_), channel_id=1, source_target_pairs={{0,8},{1,9},{2,10},{3,11},{4,12},{5,13},{6,14},{7,15},{8,0},{9,1},... | collective-permute-start | bytes 786440 | tf_op jit(solution)/shard_map/ppermute | solution.py:189
  65.8 13.8 %collective-permute-start.14 = (bf16[256,512]{1,0:T(8,128)(2,1)S(1)}, bf16[256,512]{1,0:T(8,128)(2,1)S(1)}, u32[]{:S(2)}, u32[]{:S(2)}) collective-permute-start(bf16[256,512]{1,0:T(8,128)(2,1)S(1)} %outer.1.refs_8_), channel_id=1, source_target_pairs={{0,4},{1,5},{2,6},{3,7},{4,0},{5,1},{6,2},{7,3},{8,12},{9,13},{10,... | collective-permute-start | bytes 786440 | tf_op jit(solution)/shard_map/ppermute | solution.py:189
  79.5 7.6 %collective-permute-start.18 = (bf16[256,512]{1,0:T(8,128)(2,1)S(1)}, bf16[256,512]{1,0:T(8,128)(2,1)S(1)}, u32[]{:S(2)}, u32[]{:S(2)}) collective-permute-start(bf16[256,512]{1,0:T(8,128)(2,1)S(1)} %collective-permute-done.16.refs_12_), channel_id=1, source_target_pairs={{0,4},{1,5},{2,6},{3,7},{4,0},{5,1},{6,2},{7,3},{8,12},{9,13},{10,... | collective-permute-start | bytes 786440 | tf_op jit(solution)/shard_map/ppermute | solution.py:189
  79.5 7.6 %collective-permute-start.13 = (bf16[256,512]{1,0:T(8,128)(2,1)S(1)}, bf16[256,512]{1,0:T(8,128)(2,1)S(1)}, u32[]{:S(2)}, u32[]{:S(2)}) collective-permute-start(bf16[256,512]{1,0:T(8,128)(2,1)S(1)} %outer.1.refs_8_), channel_id=1, source_target_pairs={{0,16},{16,0},{1,17},{17,1},{2,18},{18,2},{3,19},{19,3},{4,20},{20... | collective-permute-start | bytes 786440 | tf_op jit(solution)/shard_map/ppermute | solution.py:200
  79.6 7.5 %collective-permute-start.15 = (bf16[256,512]{1,0:T(8,128)(2,1)S(1)}, bf16[256,512]{1,0:T(8,128)(2,1)S(1)}, u32[]{:S(2)}, u32[]{:S(2)}) collective-permute-start(bf16[256,512]{1,0:T(8,128)(2,1)S(1)} %collective-permute-done.14.refs_10_), channel_id=1, source_target_pairs={{0,16},{16,0},{1,17},{17,1},{2,18},{18,2},{3,19},{19,3},{4,20},{20... | collective-permute-start | bytes 786440 | tf_op jit(solution)/shard_map/ppermute | solution.py:200
  80.0 7.1 %collective-permute-start.17 = (bf16[256,512]{1,0:T(8,128)(2,1)S(1)}, bf16[256,512]{1,0:T(8,128)(2,1)S(1)}, u32[]{:S(2)}, u32[]{:S(2)}) collective-permute-start(bf16[256,512]{1,0:T(8,128)(2,1)S(1)} %collective-permute-done.16.refs_12_), channel_id=1, source_target_pairs={{0,16},{16,0},{1,17},{17,1},{2,18},{18,2},{3,19},{19,3},{4,20},{20... | collective-permute-start | bytes 786440 | tf_op jit(solution)/shard_map/ppermute | solution.py:200
  87.1 1.5 %collective-permute-start.19 = (bf16[256,512]{1,0:T(8,128)(2,1)S(1)}, bf16[256,512]{1,0:T(8,128)(2,1)S(1)}, u32[]{:S(2)}, u32[]{:S(2)}) collective-permute-start(bf16[256,512]{1,0:T(8,128)(2,1)S(1)} %collective-permute-done.18.refs_5_), channel_id=1, source_target_pairs={{0,16},{16,0},{1,17},{17,1},{2,18},{18,2},{3,19},{19,3},{4,20},{20... | collective-permute-start | bytes 786440 | tf_op jit(solution)/shard_map/ppermute | solution.py:200
  89.1 7.3 %collective-permute-start.20 = (bf16[128,512]{1,0:T(8,128)(2,1)S(1)}, bf16[128,512]{1,0:T(8,128)(2,1)S(1)}, u32[]{:S(2)}, u32[]{:S(2)}) collective-permute-start(bf16[128,512]{1,0:T(8,128)(2,1)S(1)} %get-tuple-element.35), channel_id=1, source_target_pairs={{0,3},{1,2},{2,1},{3,0},{4,7},{5,6},{6,5},{7,4},{8,11},{9,10},{10,... | collective-permute-start | bytes 393224 | tf_op jit(solution)/shard_map/ppermute | solution.py:192
  90.1 8.3 %collective-permute-start.21 = (bf16[128,512]{1,0:T(8,128)(2,1)S(1)}, bf16[128,512]{1,0:T(8,128)(2,1)S(1)}, u32[]{:S(2)}, u32[]{:S(2)}) collective-permute-start(bf16[128,512]{1,0:T(8,128)(2,1)S(1)} %get-tuple-element.36), channel_id=1, source_target_pairs={{0,2},{1,3},{2,0},{3,1},{4,6},{5,7},{6,4},{7,5},{8,10},{9,11},{10,... | collective-permute-start | bytes 393224 | tf_op jit(solution)/shard_map/ppermute | solution.py:192
  92.1 6.4 %collective-permute-start.22 = (bf16[128,512]{1,0:T(8,128)(2,1)S(1)}, bf16[128,512]{1,0:T(8,128)(2,1)S(1)}, u32[]{:S(2)}, u32[]{:S(2)}) collective-permute-start(bf16[128,512]{1,0:T(8,128)(2,1)S(1)} %get-tuple-element.37), channel_id=1, source_target_pairs={{0,1},{1,0},{2,3},{3,2},{4,5},{5,4},{6,7},{7,6},{8,9},{9,8},{10,11... | collective-permute-start | bytes 393224 | tf_op jit(solution)/shard_map/ppermute | solution.py:192
  (7 other events, 95.0 us)

commit v19 on v15

--- a/solution.py
+++ b/solution.py
@@ -245,7 +245,7 @@
         [early] + first + [mine3, swap(mine3)],
         flops,
     )
-    terms = [own] + [across(sums[k - 1], k) for k in range(1, inner)]
+    terms = [own] + [across(sums[k - 1], k) for k in reversed(range(1, inner))]
     (values,) = call(sum_kernel, "sum", [block], terms, 0)
     return (first_next[None], values[None])
 

time: 95.1 us -> 95 us (level)
  transfers between devices with their start and end apart: 23 -> 23, of which waited for: 15 -> 16; matrix products, arithmetic and copies ran while one was open for 0% -> 0% of each run, Pallas kernels for 4% -> 4%
where the time goes in v19:
time: 95 us; the launch traced here: 94.8 us
  waiting for transfers between devices  57.8 us (61%)
  starting transfers between devices  27.1 us (29%)
  Pallas kernels  6.54 us (7%)
  local copies, waits for them, and re-layouts  2.52 us (3%)
    ppermute x12, waiting for transfers between devices, across(): lax.ppermute(x, 'fsdp', [(p * inner + i, p * inner + (i ^ k)) for p in ra...  32.3 us
    ppermute x6, waiting for transfers between devices, planes(): lax.ppermute(x, 'fsdp', [(p * inner + i, (p ^ bits) * inner + i) for p in...  24.7 us
    ppermute x12, starting transfers between devices, across(): lax.ppermute(x, 'fsdp', [(p * inner + i, p * inner + (i ^ k)) for p in ra...  15.7 us
    ppermute x6, starting transfers between devices, planes(): lax.ppermute(x, 'fsdp', [(p * inner + i, (p ^ bits) * inner + i) for p in...  10.8 us
    pallas_call x13, Pallas kernels, call(): pl.pallas_call(without_after, out_shape=out, in_specs=[pl.BlockSpec(memor...  6.54 us
    unnamed x16, local copies, waits for them, and re-layouts  2.52 us
  transfers between devices with their start and end apart: 23, of which 16 were waited for; matrix products, arithmetic and copies ran while one was open for 0% of the time, Pallas kernels for 4%

profile of v19, /device:TPU:0, one launch (start us, length us, event | category | flops | bytes accessed | tf_op | source)
XLA Modules:
  0.0 94.8 jit_solution(7361322176297042135)
XLA Ops:
  0.6 1.6 %copy-done = bf16[1,128,8192]{2,1,0:T(8,128)(2,1)S(1)} copy-done((bf16[1,128,8192]{2,1,0:T(8,128)(2,1)S(1)}, bf16[1,128,8192]{2,1,0:T(8,128)(2,1)}, u32[]{:S(2)}) %copy-start) | copy-done | bytes 2097176
  3.2 3.0 %collective-permute-start = (bf16[128,1024]{1,0:T(8,128)(2,1)S(1)}, bf16[128,1024]{1,0:T(8,128)(2,1)S(1)}, u32[]{:S(2)}, u32[]{:S(2)}) collective-permute-start(bf16[128,1024]{1,0:T(8,128)(2,1)S(1)} %get-tuple-element.20), channel_id=1, source_target_pairs={{0,1},{1,0},{2,3},{3,2},{4,5},{5,4},{6,7},{7,6},{8,9},{9,8},{10,11... | collective-permute-start | bytes 786440 | tf_op jit(solution)/shard_map/ppermute | solution.py:192
  6.2 1.5 %collective-permute-start.4 = (bf16[128,1024]{1,0:T(8,128)(2,1)S(1)}, bf16[128,1024]{1,0:T(8,128)(2,1)S(1)}, u32[]{:S(2)}, u32[]{:S(2)}) collective-permute-start(bf16[128,1024]{1,0:T(8,128)(2,1)S(1)} %get-tuple-element.26), channel_id=1, source_target_pairs={{0,2},{1,3},{2,0},{3,1},{4,6},{5,7},{6,4},{7,5},{8,10},{9,11},{10,... | collective-permute-start | bytes 786440 | tf_op jit(solution)/shard_map/ppermute | solution.py:192
  7.8 5.6 %collective-permute-done.refs_1_.refs_5_.refs_2_ = bf16[128,1024]{1,0:T(8,128)(2,1)S(1)} collective-permute-done((bf16[128,1024]{1,0:T(8,128)(2,1)S(1)}, bf16[128,1024]{1,0:T(8,128)(2,1)S(1)}, u32[]{:S(2)}, u32[]{:S(2)}) %collective-permute-start) | collective-permute-done | bytes 262176 | tf_op jit(solution)/shard_map/ppermute | solution.py:192
  13.4 6.2 %collective-permute-done.4.refs_2_.refs_6_.refs_3_ = bf16[128,1024]{1,0:T(8,128)(2,1)S(1)} collective-permute-done((bf16[128,1024]{1,0:T(8,128)(2,1)S(1)}, bf16[128,1024]{1,0:T(8,128)(2,1)S(1)}, u32[]{:S(2)}, u32[]{:S(2)}) %collective-permute-start.4) | collective-permute-done | bytes 262176 | tf_op jit(solution)/shard_map/ppermute | solution.py:192
  20.1 1.6 %collective-permute-start.6 = (bf16[512,512]{1,0:T(8,128)(2,1)S(1)}, bf16[512,512]{1,0:T(8,128)(2,1)S(1)}, u32[]{:S(2)}, u32[]{:S(2)}) collective-permute-start(bf16[512,512]{1,0:T(8,128)(2,1)S(1)} %gradient.4), channel_id=1, source_target_pairs={{0,4},{1,5},{2,6},{3,7},{4,0},{5,1},{6,2},{7,3},{8,12},{9,13},{10,... | collective-permute-start | bytes 1572872 | tf_op jit(solution)/shard_map/ppermute | solution.py:189
  21.8 1.3 %collective-permute-start.1 = (bf16[128,1024]{1,0:T(8,128)(2,1)S(1)}, bf16[128,1024]{1,0:T(8,128)(2,1)S(1)}, u32[]{:S(2)}, u32[]{:S(2)}) collective-permute-start(bf16[128,1024]{1,0:T(8,128)(2,1)S(1)} %get-tuple-element.22), channel_id=1, source_target_pairs={{0,1},{1,0},{2,3},{3,2},{4,5},{5,4},{6,7},{7,6},{8,9},{9,8},{10,11... | collective-permute-start | bytes 786440 | tf_op jit(solution)/shard_map/ppermute | solution.py:192
  23.9 1.4 %collective-permute-start.3 = (bf16[128,1024]{1,0:T(8,128)(2,1)S(1)}, bf16[128,1024]{1,0:T(8,128)(2,1)S(1)}, u32[]{:S(2)}, u32[]{:S(2)}) collective-permute-start(bf16[128,1024]{1,0:T(8,128)(2,1)S(1)} %get-tuple-element.24), channel_id=1, source_target_pairs={{0,3},{1,2},{2,1},{3,0},{4,7},{5,6},{6,5},{7,4},{8,11},{9,10},{10,... | collective-permute-start | bytes 786440 | tf_op jit(solution)/shard_map/ppermute | solution.py:192
  25.4 5.8 %collective-permute-done.1.refs_1_.refs_5_ = bf16[128,1024]{1,0:T(8,128)(2,1)S(1)} collective-permute-done((bf16[128,1024]{1,0:T(8,128)(2,1)S(1)}, bf16[128,1024]{1,0:T(8,128)(2,1)S(1)}, u32[]{:S(2)}, u32[]{:S(2)}) %collective-permute-start.1) | collective-permute-done | bytes 262176 | tf_op jit(solution)/shard_map/ppermute | solution.py:192
  31.1 4.2 %collective-permute-done.2.refs_2_.refs_6_ = bf16[128,1024]{1,0:T(8,128)(2,1)S(1)} collective-permute-done((bf16[128,1024]{1,0:T(8,128)(2,1)S(1)}, bf16[128,1024]{1,0:T(8,128)(2,1)S(1)}, u32[]{:S(2)}, u32[]{:S(2)}) %collective-permute-start.2) | collective-permute-done | bytes 262176 | tf_op jit(solution)/shard_map/ppermute | solution.py:192
  36.9 2.7 %collective-permute-start.11 = (bf16[512,512]{1,0:T(8,128)(2,1)S(1)}, bf16[512,512]{1,0:T(8,128)(2,1)S(1)}, u32[]{:S(2)}, u32[]{:S(2)}) collective-permute-start(bf16[512,512]{1,0:T(8,128)(2,1)S(1)} %gradient.5.refs_1_), channel_id=1, source_target_pairs={{0,8},{1,9},{2,10},{3,11},{4,12},{5,13},{6,14},{7,15},{8,0},{9,1},... | collective-permute-start | bytes 1572872 | tf_op jit(solution)/shard_map/ppermute | solution.py:189
  40.2 1.5 %collective-permute-start.8 = (bf16[128,512]{1,0:T(8,128)(2,1)S(1)}, bf16[128,512]{1,0:T(8,128)(2,1)S(1)}, u32[]{:S(2)}, u32[]{:S(2)}) collective-permute-start(bf16[128,512]{1,0:T(8,128)(2,1)S(1)} %get-tuple-element.30), channel_id=1, source_target_pairs={{0,2},{1,3},{2,0},{3,1},{4,6},{5,7},{6,4},{7,5},{8,10},{9,11},{10,... | collective-permute-start | bytes 393224 | tf_op jit(solution)/shard_map/ppermute | solution.py:192
  41.7 1.4 %collective-permute-start.9 = (bf16[128,512]{1,0:T(8,128)(2,1)S(1)}, bf16[128,512]{1,0:T(8,128)(2,1)S(1)}, u32[]{:S(2)}, u32[]{:S(2)}) collective-permute-start(bf16[128,512]{1,0:T(8,128)(2,1)S(1)} %get-tuple-element.31), channel_id=1, source_target_pairs={{0,3},{1,2},{2,1},{3,0},{4,7},{5,6},{6,5},{7,4},{8,11},{9,10},{10,... | collective-permute-start | bytes 393224 | tf_op jit(solution)/shard_map/ppermute | solution.py:192
  43.1 1.5 %collective-permute-done.7.refs_1_ = bf16[128,512]{1,0:T(8,128)(2,1)S(1)} collective-permute-done((bf16[128,512]{1,0:T(8,128)(2,1)S(1)}, bf16[128,512]{1,0:T(8,128)(2,1)S(1)}, u32[]{:S(2)}, u32[]{:S(2)}) %collective-permute-start.7) | collective-permute-done | bytes 131104 | tf_op jit(solution)/shard_map/ppermute | solution.py:192
  45.2 2.4 %collective-permute-done.9.refs_3_ = bf16[128,512]{1,0:T(8,128)(2,1)S(1)} collective-permute-done((bf16[128,512]{1,0:T(8,128)(2,1)S(1)}, bf16[128,512]{1,0:T(8,128)(2,1)S(1)}, u32[]{:S(2)}, u32[]{:S(2)}) %collective-permute-start.9) | collective-permute-done | bytes 131104 | tf_op jit(solution)/shard_map/ppermute | solution.py:192
  48.0 8.5 %collective-permute-done.10.refs_1_ = bf16[512,512]{1,0:T(8,128)(2,1)S(1)} collective-permute-done((bf16[512,512]{1,0:T(8,128)(2,1)S(1)}, bf16[512,512]{1,0:T(8,128)(2,1)S(1)}, u32[]{:S(2)}, u32[]{:S(2)}) %collective-permute-start.10) | collective-permute-done | bytes 524320 | tf_op jit(solution)/shard_map/ppermute | solution.py:189
  57.2 1.7 %update.1 = (f32[512,512]{1,0:T(8,128)}, f32[256,512]{1,0:T(8,128)S(1)}) custom-call(f32[512,512]{1,0:T(8,128)S(1)} %gradient.6.refs_0_, bf16[512,512]{1,0:T(8,128)(2,1)S(1)} %collective-permute-done.10.refs_1_, bf16[512,512]{1,0:T(8,128)(2,1)S(1)} %collective-permute-done.11.refs_2_, f32[512,512]{1,0:T(8,128)S(1)} %bitcast.11, f32[512,512]{1,0:T(8,128)S(1)} %bitcast.13, ...), custom_call_target="tpu_custom_call" | custom-call | bytes 7864320 | tf_op jit(solution)/shard_map/update/pallas_call | solution.py:60
  59.2 1.5 %collective-permute-start.16 = (bf16[256,512]{1,0:T(8,128)(2,1)S(1)}, bf16[256,512]{1,0:T(8,128)(2,1)S(1)}, u32[]{:S(2)}, u32[]{:S(2)}) collective-permute-start(bf16[256,512]{1,0:T(8,128)(2,1)S(1)} %outer.1.refs_8_), channel_id=1, source_target_pairs={{0,8},{1,9},{2,10},{3,11},{4,12},{5,13},{6,14},{7,15},{8,0},{9,1},... | collective-permute-start | bytes 786440 | tf_op jit(solution)/shard_map/ppermute | solution.py:189
  60.8 4.4 %collective-permute-start.14 = (bf16[256,512]{1,0:T(8,128)(2,1)S(1)}, bf16[256,512]{1,0:T(8,128)(2,1)S(1)}, u32[]{:S(2)}, u32[]{:S(2)}) collective-permute-start(bf16[256,512]{1,0:T(8,128)(2,1)S(1)} %outer.1.refs_8_), channel_id=1, source_target_pairs={{0,4},{1,5},{2,6},{3,7},{4,0},{5,1},{6,2},{7,3},{8,12},{9,13},{10,... | collective-permute-start | bytes 786440 | tf_op jit(solution)/shard_map/ppermute | solution.py:189
  65.2 9.2 %collective-permute-done.16.refs_12_ = bf16[256,512]{1,0:T(8,128)(2,1)S(1)} collective-permute-done((bf16[256,512]{1,0:T(8,128)(2,1)S(1)}, bf16[256,512]{1,0:T(8,128)(2,1)S(1)}, u32[]{:S(2)}, u32[]{:S(2)}) %collective-permute-start.16) | collective-permute-done | bytes 262176 | tf_op jit(solution)/shard_map/ppermute | solution.py:189
  75.0 7.0 %collective-permute-done.18.refs_5_ = bf16[256,512]{1,0:T(8,128)(2,1)S(1)} collective-permute-done((bf16[256,512]{1,0:T(8,128)(2,1)S(1)}, bf16[256,512]{1,0:T(8,128)(2,1)S(1)}, u32[]{:S(2)}, u32[]{:S(2)}) %collective-permute-start.18) | collective-permute-done | bytes 262176 | tf_op jit(solution)/shard_map/ppermute | solution.py:189
  83.9 3.4 %collective-permute-start.20 = (bf16[128,512]{1,0:T(8,128)(2,1)S(1)}, bf16[128,512]{1,0:T(8,128)(2,1)S(1)}, u32[]{:S(2)}, u32[]{:S(2)}) collective-permute-start(bf16[128,512]{1,0:T(8,128)(2,1)S(1)} %get-tuple-element.35), channel_id=1, source_target_pairs={{0,3},{1,2},{2,1},{3,0},{4,7},{5,6},{6,5},{7,4},{8,11},{9,10},{10,... | collective-permute-start | bytes 393224 | tf_op jit(solution)/shard_map/ppermute | solution.py:192
  88.0 3.3 %collective-permute-done.20.refs_1_ = bf16[128,512]{1,0:T(8,128)(2,1)S(1)} collective-permute-done((bf16[128,512]{1,0:T(8,128)(2,1)S(1)}, bf16[128,512]{1,0:T(8,128)(2,1)S(1)}, u32[]{:S(2)}, u32[]{:S(2)}) %collective-permute-start.20) | collective-permute-done | bytes 131104 | tf_op jit(solution)/shard_map/ppermute | solution.py:192
  91.3 2.7 %collective-permute-done.21.refs_2_ = bf16[128,512]{1,0:T(8,128)(2,1)S(1)} collective-permute-done((bf16[128,512]{1,0:T(8,128)(2,1)S(1)}, bf16[128,512]{1,0:T(8,128)(2,1)S(1)}, u32[]{:S(2)}, u32[]{:S(2)}) %collective-permute-start.21) | collective-permute-done | bytes 131104 | tf_op jit(solution)/shard_map/ppermute | solution.py:192
  (51 shorter events, 10.6 us)
Async XLA Ops:
  3.2 10.1 %collective-permute-start = (bf16[128,1024]{1,0:T(8,128)(2,1)S(1)}, bf16[128,1024]{1,0:T(8,128)(2,1)S(1)}, u32[]{:S(2)}, u32[]{:S(2)}) collective-permute-start(bf16[128,1024]{1,0:T(8,128)(2,1)S(1)} %get-tuple-element.20), channel_id=1, source_target_pairs={{0,1},{1,0},{2,3},{3,2},{4,5},{5,4},{6,7},{7,6},{8,9},{9,8},{10,11... | collective-permute-start | bytes 786440 | tf_op jit(solution)/shard_map/ppermute | solution.py:192
  6.2 13.4 %collective-permute-start.4 = (bf16[128,1024]{1,0:T(8,128)(2,1)S(1)}, bf16[128,1024]{1,0:T(8,128)(2,1)S(1)}, u32[]{:S(2)}, u32[]{:S(2)}) collective-permute-start(bf16[128,1024]{1,0:T(8,128)(2,1)S(1)} %get-tuple-element.26), channel_id=1, source_target_pairs={{0,2},{1,3},{2,0},{3,1},{4,6},{5,7},{6,4},{7,5},{8,10},{9,11},{10,... | collective-permute-start | bytes 786440 | tf_op jit(solution)/shard_map/ppermute | solution.py:192
  7.7 11.9 %collective-permute-start.5 = (bf16[128,1024]{1,0:T(8,128)(2,1)S(1)}, bf16[128,1024]{1,0:T(8,128)(2,1)S(1)}, u32[]{:S(2)}, u32[]{:S(2)}) collective-permute-start(bf16[128,1024]{1,0:T(8,128)(2,1)S(1)} %get-tuple-element.27), channel_id=1, source_target_pairs={{0,3},{1,2},{2,1},{3,0},{4,7},{5,6},{6,5},{7,4},{8,11},{9,10},{10,... | collective-permute-start | bytes 786440 | tf_op jit(solution)/shard_map/ppermute | solution.py:192
  20.1 16.3 %collective-permute-start.6 = (bf16[512,512]{1,0:T(8,128)(2,1)S(1)}, bf16[512,512]{1,0:T(8,128)(2,1)S(1)}, u32[]{:S(2)}, u32[]{:S(2)}) collective-permute-start(bf16[512,512]{1,0:T(8,128)(2,1)S(1)} %gradient.4), channel_id=1, source_target_pairs={{0,4},{1,5},{2,6},{3,7},{4,0},{5,1},{6,2},{7,3},{8,12},{9,13},{10,... | collective-permute-start | bytes 1572872 | tf_op jit(solution)/shard_map/ppermute | solution.py:189
  21.8 9.3 %collective-permute-start.1 = (bf16[128,1024]{1,0:T(8,128)(2,1)S(1)}, bf16[128,1024]{1,0:T(8,128)(2,1)S(1)}, u32[]{:S(2)}, u32[]{:S(2)}) collective-permute-start(bf16[128,1024]{1,0:T(8,128)(2,1)S(1)} %get-tuple-element.22), channel_id=1, source_target_pairs={{0,1},{1,0},{2,3},{3,2},{4,5},{5,4},{6,7},{7,6},{8,9},{9,8},{10,11... | collective-permute-start | bytes 786440 | tf_op jit(solution)/shard_map/ppermute | solution.py:192
  23.1 12.2 %collective-permute-start.2 = (bf16[128,1024]{1,0:T(8,128)(2,1)S(1)}, bf16[128,1024]{1,0:T(8,128)(2,1)S(1)}, u32[]{:S(2)}, u32[]{:S(2)}) collective-permute-start(bf16[128,1024]{1,0:T(8,128)(2,1)S(1)} %get-tuple-element.23), channel_id=1, source_target_pairs={{0,2},{1,3},{2,0},{3,1},{4,6},{5,7},{6,4},{7,5},{8,10},{9,11},{10,... | collective-permute-start | bytes 786440 | tf_op jit(solution)/shard_map/ppermute | solution.py:192
  23.9 11.4 %collective-permute-start.3 = (bf16[128,1024]{1,0:T(8,128)(2,1)S(1)}, bf16[128,1024]{1,0:T(8,128)(2,1)S(1)}, u32[]{:S(2)}, u32[]{:S(2)}) collective-permute-start(bf16[128,1024]{1,0:T(8,128)(2,1)S(1)} %get-tuple-element.24), channel_id=1, source_target_pairs={{0,3},{1,2},{2,1},{3,0},{4,7},{5,6},{6,5},{7,4},{8,11},{9,10},{10,... | collective-permute-start | bytes 786440 | tf_op jit(solution)/shard_map/ppermute | solution.py:192
  35.8 20.7 %collective-permute-start.10 = (bf16[512,512]{1,0:T(8,128)(2,1)S(1)}, bf16[512,512]{1,0:T(8,128)(2,1)S(1)}, u32[]{:S(2)}, u32[]{:S(2)}) collective-permute-start(bf16[512,512]{1,0:T(8,128)(2,1)S(1)} %gradient.7), channel_id=1, source_target_pairs={{0,4},{1,5},{2,6},{3,7},{4,0},{5,1},{6,2},{7,3},{8,12},{9,13},{10,... | collective-permute-start | bytes 1572872 | tf_op jit(solution)/shard_map/ppermute | solution.py:189
  36.8 19.7 %copy-start.2 = (f32[512,512]{1,0:T(8,128)S(1)}, f32[512,512]{1,0:T(8,128)}, u32[]{:S(2)}) copy-start(f32[512,512]{1,0:T(8,128)} %refs_2_.1) | copy-start | bytes 3145732
  36.9 19.6 %collective-permute-start.11 = (bf16[512,512]{1,0:T(8,128)(2,1)S(1)}, bf16[512,512]{1,0:T(8,128)(2,1)S(1)}, u32[]{:S(2)}, u32[]{:S(2)}) collective-permute-start(bf16[512,512]{1,0:T(8,128)(2,1)S(1)} %gradient.5.refs_1_), channel_id=1, source_target_pairs={{0,8},{1,9},{2,10},{3,11},{4,12},{5,13},{6,14},{7,15},{8,0},{9,1},... | collective-permute-start | bytes 1572872 | tf_op jit(solution)/shard_map/ppermute | solution.py:189
  39.6 5.0 %collective-permute-start.7 = (bf16[128,512]{1,0:T(8,128)(2,1)S(1)}, bf16[128,512]{1,0:T(8,128)(2,1)S(1)}, u32[]{:S(2)}, u32[]{:S(2)}) collective-permute-start(bf16[128,512]{1,0:T(8,128)(2,1)S(1)} %get-tuple-element.29), channel_id=1, source_target_pairs={{0,1},{1,0},{2,3},{3,2},{4,5},{5,4},{6,7},{7,6},{8,9},{9,8},{10,11... | collective-permute-start | bytes 393224 | tf_op jit(solution)/shard_map/ppermute | solution.py:192
  40.2 5.0 %collective-permute-start.8 = (bf16[128,512]{1,0:T(8,128)(2,1)S(1)}, bf16[128,512]{1,0:T(8,128)(2,1)S(1)}, u32[]{:S(2)}, u32[]{:S(2)}) collective-permute-start(bf16[128,512]{1,0:T(8,128)(2,1)S(1)} %get-tuple-element.30), channel_id=1, source_target_pairs={{0,2},{1,3},{2,0},{3,1},{4,6},{5,7},{6,4},{7,5},{8,10},{9,11},{10,... | collective-permute-start | bytes 393224 | tf_op jit(solution)/shard_map/ppermute | solution.py:192
  41.7 5.9 %collective-permute-start.9 = (bf16[128,512]{1,0:T(8,128)(2,1)S(1)}, bf16[128,512]{1,0:T(8,128)(2,1)S(1)}, u32[]{:S(2)}, u32[]{:S(2)}) collective-permute-start(bf16[128,512]{1,0:T(8,128)(2,1)S(1)} %get-tuple-element.31), channel_id=1, source_target_pairs={{0,3},{1,2},{2,1},{3,0},{4,7},{5,6},{6,5},{7,4},{8,11},{9,10},{10,... | collective-permute-start | bytes 393224 | tf_op jit(solution)/shard_map/ppermute | solution.py:192
  57.1 2.0 %collective-permute-start.12 = (f32[256,512]{1,0:T(8,128)S(1)}, f32[256,512]{1,0:T(8,128)S(1)}, u32[]{:S(2)}, u32[]{:S(2)}) collective-permute-start(f32[256,512]{1,0:T(8,128)S(1)} %drift.1), channel_id=1, source_target_pairs={{0,16},{16,0},{1,17},{17,1},{2,18},{18,2},{3,19},{19,3},{4,20},{20... | collective-permute-start | bytes 1572872 | tf_op jit(solution)/shard_map/ppermute | solution.py:198
  59.2 15.1 %collective-permute-start.16 = (bf16[256,512]{1,0:T(8,128)(2,1)S(1)}, bf16[256,512]{1,0:T(8,128)(2,1)S(1)}, u32[]{:S(2)}, u32[]{:S(2)}) collective-permute-start(bf16[256,512]{1,0:T(8,128)(2,1)S(1)} %outer.1.refs_8_), channel_id=1, source_target_pairs={{0,8},{1,9},{2,10},{3,11},{4,12},{5,13},{6,14},{7,15},{8,0},{9,1},... | collective-permute-start | bytes 786440 | tf_op jit(solution)/shard_map/ppermute | solution.py:189
  60.8 13.7 %collective-permute-start.14 = (bf16[256,512]{1,0:T(8,128)(2,1)S(1)}, bf16[256,512]{1,0:T(8,128)(2,1)S(1)}, u32[]{:S(2)}, u32[]{:S(2)}) collective-permute-start(bf16[256,512]{1,0:T(8,128)(2,1)S(1)} %outer.1.refs_8_), channel_id=1, source_target_pairs={{0,4},{1,5},{2,6},{3,7},{4,0},{5,1},{6,2},{7,3},{8,12},{9,13},{10,... | collective-permute-start | bytes 786440 | tf_op jit(solution)/shard_map/ppermute | solution.py:189
  74.4 7.6 %collective-permute-start.18 = (bf16[256,512]{1,0:T(8,128)(2,1)S(1)}, bf16[256,512]{1,0:T(8,128)(2,1)S(1)}, u32[]{:S(2)}, u32[]{:S(2)}) collective-permute-start(bf16[256,512]{1,0:T(8,128)(2,1)S(1)} %collective-permute-done.16.refs_12_), channel_id=1, source_target_pairs={{0,4},{1,5},{2,6},{3,7},{4,0},{5,1},{6,2},{7,3},{8,12},{9,13},{10,... | collective-permute-start | bytes 786440 | tf_op jit(solution)/shard_map/ppermute | solution.py:189
  74.4 7.6 %collective-permute-start.13 = (bf16[256,512]{1,0:T(8,128)(2,1)S(1)}, bf16[256,512]{1,0:T(8,128)(2,1)S(1)}, u32[]{:S(2)}, u32[]{:S(2)}) collective-permute-start(bf16[256,512]{1,0:T(8,128)(2,1)S(1)} %outer.1.refs_8_), channel_id=1, source_target_pairs={{0,16},{16,0},{1,17},{17,1},{2,18},{18,2},{3,19},{19,3},{4,20},{20... | collective-permute-start | bytes 786440 | tf_op jit(solution)/shard_map/ppermute | solution.py:198
  74.4 7.5 %collective-permute-start.15 = (bf16[256,512]{1,0:T(8,128)(2,1)S(1)}, bf16[256,512]{1,0:T(8,128)(2,1)S(1)}, u32[]{:S(2)}, u32[]{:S(2)}) collective-permute-start(bf16[256,512]{1,0:T(8,128)(2,1)S(1)} %collective-permute-done.14.refs_10_), channel_id=1, source_target_pairs={{0,16},{16,0},{1,17},{17,1},{2,18},{18,2},{3,19},{19,3},{4,20},{20... | collective-permute-start | bytes 786440 | tf_op jit(solution)/shard_map/ppermute | solution.py:198
  74.9 7.1 %collective-permute-start.17 = (bf16[256,512]{1,0:T(8,128)(2,1)S(1)}, bf16[256,512]{1,0:T(8,128)(2,1)S(1)}, u32[]{:S(2)}, u32[]{:S(2)}) collective-permute-start(bf16[256,512]{1,0:T(8,128)(2,1)S(1)} %collective-permute-done.16.refs_12_), channel_id=1, source_target_pairs={{0,16},{16,0},{1,17},{17,1},{2,18},{18,2},{3,19},{19,3},{4,20},{20... | collective-permute-start | bytes 786440 | tf_op jit(solution)/shard_map/ppermute | solution.py:198
  81.9 1.5 %collective-permute-start.19 = (bf16[256,512]{1,0:T(8,128)(2,1)S(1)}, bf16[256,512]{1,0:T(8,128)(2,1)S(1)}, u32[]{:S(2)}, u32[]{:S(2)}) collective-permute-start(bf16[256,512]{1,0:T(8,128)(2,1)S(1)} %collective-permute-done.18.refs_5_), channel_id=1, source_target_pairs={{0,16},{16,0},{1,17},{17,1},{2,18},{18,2},{3,19},{19,3},{4,20},{20... | collective-permute-start | bytes 786440 | tf_op jit(solution)/shard_map/ppermute | solution.py:198
  83.9 7.4 %collective-permute-start.20 = (bf16[128,512]{1,0:T(8,128)(2,1)S(1)}, bf16[128,512]{1,0:T(8,128)(2,1)S(1)}, u32[]{:S(2)}, u32[]{:S(2)}) collective-permute-start(bf16[128,512]{1,0:T(8,128)(2,1)S(1)} %get-tuple-element.35), channel_id=1, source_target_pairs={{0,3},{1,2},{2,1},{3,0},{4,7},{5,6},{6,5},{7,4},{8,11},{9,10},{10,... | collective-permute-start | bytes 393224 | tf_op jit(solution)/shard_map/ppermute | solution.py:192
  87.4 6.6 %collective-permute-start.21 = (bf16[128,512]{1,0:T(8,128)(2,1)S(1)}, bf16[128,512]{1,0:T(8,128)(2,1)S(1)}, u32[]{:S(2)}, u32[]{:S(2)}) collective-permute-start(bf16[128,512]{1,0:T(8,128)(2,1)S(1)} %get-tuple-element.36), channel_id=1, source_target_pairs={{0,2},{1,3},{2,0},{3,1},{4,6},{5,7},{6,4},{7,5},{8,10},{9,11},{10,... | collective-permute-start | bytes 393224 | tf_op jit(solution)/shard_map/ppermute | solution.py:192
  87.7 6.4 %collective-permute-start.22 = (bf16[128,512]{1,0:T(8,128)(2,1)S(1)}, bf16[128,512]{1,0:T(8,128)(2,1)S(1)}, u32[]{:S(2)}, u32[]{:S(2)}) collective-permute-start(bf16[128,512]{1,0:T(8,128)(2,1)S(1)} %get-tuple-element.37), channel_id=1, source_target_pairs={{0,1},{1,0},{2,3},{3,2},{4,5},{5,4},{6,7},{7,6},{8,9},{9,8},{10,11... | collective-permute-start | bytes 393224 | tf_op jit(solution)/shard_map/ppermute | solution.py:192
  (7 other events, 82.1 us)
